TPU v7x, 128 devices: a whole 4x4x4 slice. The times are simulated.
128 devices in a mesh: fsdp: 8 (over z, core), ctx: 8 (over x, y_lo), tp: 2 (over y_hi).
Axes of the slice: x: 4, y: 4 (y_hi: 2, y_lo: 2; y = y_hi * 2 + y_lo), z: 4, core: 2. Of those that a mesh axis runs over, the one named last changes fastest.
Arguments:
- inputs: bfloat16 [8192, 2048], P(('fsdp', 'ctx')), may hold values from -6 to 6
- lengths: int32 [8], replicated, may hold values from 1 to 1024, 5120 in all
- routes: int32 [8192, 4], P(('fsdp', 'ctx')), may hold values from 0 to 7, all different within a row; in each aligned block of 128 rows (0 to 127, 128 to 255, ...) at most 80 rows name the same one
- norm_gains: bfloat16 [2, 2048], P(None, 'fsdp'), may hold values from 0.5 to 1.5
- w_qkv: bfloat16 [2048, 3, 2048], P('fsdp', None, 'tp'), may hold values from -0.125 to 0.125
- b_qkv: bfloat16 [3, 16, 128], P(None, 'tp', 'fsdp'), may hold values from -1.1953125 to 1.1953125
- w_o: bfloat16 [2048, 2048], P('fsdp', 'tp'), may hold values from -0.5 to 0.5
- w_router: bfloat16 [2048, 8], P('fsdp'), may hold values from -0.0625 to 0.0625
- w_sgate: bfloat16 [2048], P('fsdp'), may hold values from -0.125 to 0.125
- w_sgu: bfloat16 [2048, 2, 5632], P('fsdp', None, 'tp'), may hold values from -0.125 to 0.125
- w_sdown: bfloat16 [2048, 5632], P('fsdp', 'tp'), may hold values from -0.15625 to 0.15625
- w_egu: bfloat16 [2048, 8, 2, 1408], P('fsdp', None, None, 'tp'), may hold values from -0.125 to 0.125
- w_edown: bfloat16 [2048, 8, 1408], P('fsdp', None, 'tp'), may hold values from -0.4375 to 0.4375
- grad_out: bfloat16 [8192, 2048], P(('fsdp', 'ctx')), may hold values from -6 to 6
Outputs:
- output: bfloat16 [8192, 2048], P(('fsdp', 'ctx'))
- grad_inputs: bfloat16 [8192, 2048], P(('fsdp', 'ctx'))
- grad_norm_gains: float32 [2, 2048], P(None, 'fsdp')
- grad_w_qkv: float32 [2048, 3, 2048], P('fsdp', None, 'tp')
- grad_b_qkv: float32 [3, 16, 128], P(None, 'tp', 'fsdp')
- grad_w_o: float32 [2048, 2048], P('fsdp', 'tp')
- grad_w_router: float32 [2048, 8], P('fsdp')
- grad_w_sgate: float32 [2048], P('fsdp')
- grad_w_sgu: float32 [2048, 2, 5632], P('fsdp', None, 'tp')
- grad_w_sdown: float32 [2048, 5632], P('fsdp', 'tp')
- grad_w_egu: float32 [2048, 8, 2, 1408], P('fsdp', None, None, 'tp')
- grad_w_edown: float32 [2048, 8, 1408], P('fsdp', None, 'tp')
Inputs may be any that keep to these rules, and one draw needn't show every extreme that they name: `lengths`: each sequence's count of valid tokens; the longest has all 1024 slots. `routes`: each row names 4 different experts; within the rows of one device no expert is named by more than 80 rows, a bound that some block reaches.
All inputs are finite; a program needn't handle non-finite values.
Results may differ from a plain program's by a relative error of at most 0.029.
Values may be sent and summed in bfloat16 or wider, within the bound.
No kernel may reach another device: no remote copies, remote signals or barrier semaphores. Data moves between devices by JAX's collectives and lax.ppermute only.
A program may use at most 384 MiB of HBM per device.

v0:
```python
import jax
import jax.numpy as jnp
from jax import lax
from jax.sharding import PartitionSpec as P

EPSILON = 1e-06
ROPE_BASE = 1000000.0
MASKED_SCORE = -1e30


def rotary_tables(row_count, offset, head_size):
    middle = head_size // 2
    inverse = ROPE_BASE ** (-(jnp.arange(middle, dtype=jnp.float32) * 2.0) / head_size)
    places = (offset + jnp.arange(row_count, dtype=jnp.int32)).astype(jnp.float32)
    angles = places[:, None] * inverse[None, :]
    angles = jnp.concatenate([angles, angles], axis=-1)
    return (jnp.cos(angles), jnp.sin(angles))


def rotate(values, cosine_table, sine_table):
    middle = values.shape[-1] // 2
    turned = jnp.concatenate([-values[..., middle:], values[..., :middle]], axis=-1)
    return values * cosine_table[:, None, :] + turned * sine_table[:, None, :]


def rotate_back(grads, cosine_table, sine_table):
    middle = grads.shape[-1] // 2
    scaled = grads * sine_table[:, None, :]
    return grads * cosine_table[:, None, :] + jnp.concatenate(
        [scaled[..., middle:], -scaled[..., :middle]], axis=-1
    )


def inverse_rms(values):
    return lax.rsqrt(jnp.mean(values * values, axis=-1, keepdims=True) + EPSILON)


def norm_back(grad_norm, values, factor, gain_vector):
    gain_grad = jnp.sum(grad_norm * values * factor, axis=0)
    weighted = grad_norm * gain_vector
    inner_sum = jnp.mean(weighted * values, axis=-1, keepdims=True)
    return (weighted * factor - values * factor**3 * inner_sum, gain_grad)


def swiglu(pre_act):
    return jax.nn.silu(pre_act[:, 0]) * pre_act[:, 1]


def swiglu_back(pre_act, grad_hidden):
    return jax.vjp(swiglu, pre_act)[1](grad_hidden)[0]


def slot_table(column, capacity):
    slot_index = jnp.cumsum(column) - 1.0
    hits = (slot_index[None, :] == jnp.arange(capacity, dtype=jnp.float32)[:, None]) & (
        column[None, :] > 0
    )
    return hits.astype(jnp.float32)


def scatter_rows(selector, row_values):
    return lax.dot_general(
        selector, row_values, (((0,), (0,)), ((), ())), precision=lax.Precision.HIGHEST
    )


def pick_rows(selector, row_values):
    return jnp.dot(selector, row_values, precision=lax.Precision.HIGHEST)


def score_table(queries, keys_all, places):
    scaled = jnp.einsum(
        "qhe,khe->hqk", queries, keys_all, preferred_element_type=jnp.float32
    ) * queries.shape[-1] ** (-0.5)
    causal = jnp.arange(keys_all.shape[0], dtype=jnp.int32)[None, :] <= places[:, None]
    return jnp.where(causal[None], scaled, MASKED_SCORE)


def gather_keys(keys_local, values_local):
    return (
        lax.all_gather(keys_local, "ctx", axis=0, tiled=True),
        lax.all_gather(values_local, "ctx", axis=0, tiled=True),
    )


def gather_expert(w_egu, w_edown, expert):
    return (
        lax.all_gather(w_egu[:, expert], "fsdp", axis=0, tiled=True),
        lax.all_gather(w_edown[:, expert], "fsdp", axis=0, tiled=True),
    )


def reduce_expert(grad_gu, grad_down):
    shards = (
        lax.psum_scatter(
            grad_gu.astype(jnp.bfloat16), "fsdp", scatter_dimension=0, tiled=True
        ).astype(jnp.float32),
        lax.psum_scatter(
            grad_down.astype(jnp.bfloat16), "fsdp", scatter_dimension=0, tiled=True
        ).astype(jnp.float32),
    )
    return (
        lax.psum(shards[0].astype(jnp.bfloat16), "ctx").astype(jnp.float32),
        lax.psum(shards[1].astype(jnp.bfloat16), "ctx").astype(jnp.float32),
    )


def body(
    inputs,
    lengths,
    routes,
    norm_gains,
    w_qkv,
    b_qkv,
    w_o,
    w_router,
    w_sgate,
    w_sgu,
    w_sdown,
    w_egu,
    w_edown,
    grad_out,
):
    tok_count = inputs.shape[0]
    experts_count = w_egu.shape[1]
    capacity = tok_count * 5 // 8
    head_size = b_qkv.shape[2] * lax.axis_size("fsdp")
    group = lax.axis_index("fsdp")
    offset = lax.axis_index("ctx") * tok_count
    places = offset + jnp.arange(tok_count, dtype=jnp.int32)
    length_here = jnp.sum(
        jnp.where(jnp.arange(lengths.shape[0], dtype=jnp.int32) == group, lengths, 0)
    )
    valid_rows = (places < length_here).astype(jnp.float32)[:, None]
    cosine_table, sine_table = rotary_tables(tok_count, offset, head_size)
    (
        gathered_gains,
        gathered_qkv,
        gathered_bias,
        gathered_out,
        gathered_router,
        gathered_sgate,
        gathered_sgu,
        gathered_sdown,
    ) = (
        lax.all_gather(norm_gains, "fsdp", axis=1, tiled=True),
        lax.all_gather(w_qkv, "fsdp", axis=0, tiled=True),
        lax.all_gather(b_qkv, "fsdp", axis=2, tiled=True),
        lax.all_gather(w_o, "fsdp", axis=0, tiled=True),
        lax.all_gather(w_router, "fsdp", axis=0, tiled=True),
        lax.all_gather(w_sgate, "fsdp", axis=0, tiled=True),
        lax.all_gather(w_sgu, "fsdp", axis=0, tiled=True),
        lax.all_gather(w_sdown, "fsdp", axis=0, tiled=True),
    )
    gain_first = gathered_gains[0].astype(jnp.float32)
    gain_second = gathered_gains[1].astype(jnp.float32)
    heads_local = gathered_bias.shape[1]
    width_local = heads_local * head_size
    hidden_in = inputs.astype(jnp.float32)
    factor_first = inverse_rms(hidden_in)
    normed_first = (hidden_in * factor_first * gain_first).astype(jnp.bfloat16)
    projected = jnp.einsum(
        "td,dcf->tcf", normed_first, gathered_qkv, preferred_element_type=jnp.float32
    )
    projected = projected + gathered_bias.reshape(3, width_local).astype(jnp.float32)
    shaped = projected.reshape(tok_count, 3, heads_local, head_size)
    queries = rotate(shaped[:, 0], cosine_table, sine_table).astype(jnp.bfloat16)
    keys_local = rotate(shaped[:, 1], cosine_table, sine_table).astype(jnp.bfloat16)
    values_local = shaped[:, 2].astype(jnp.bfloat16)
    keys_all, values_all = gather_keys(keys_local, values_local)
    scores = score_table(queries, keys_all, places)
    peak = jnp.max(scores, axis=-1, keepdims=True)
    expons = jnp.exp(scores - peak)
    total = jnp.sum(expons, axis=-1, keepdims=True)
    att_probs = expons / total
    log_total = peak + jnp.log(total)
    probs_low = att_probs.astype(jnp.bfloat16)
    attended = jnp.einsum("hqk,khe->qhe", probs_low, values_all, preferred_element_type=jnp.float32)
    attended = attended.reshape(tok_count, width_local).astype(jnp.bfloat16)
    branch_part = jnp.einsum(
        "tf,df->td", attended, gathered_out, preferred_element_type=jnp.float32
    )
    branch = lax.psum(branch_part.astype(jnp.bfloat16), "tp").astype(jnp.float32)
    middle_state = hidden_in + branch
    factor_second = inverse_rms(middle_state)
    normed_second = (middle_state * factor_second * gain_second).astype(jnp.bfloat16)
    logits = jnp.dot(normed_second, gathered_router, preferred_element_type=jnp.float32)
    router_probs = jax.nn.softmax(logits, axis=-1)
    experts_range = jnp.arange(experts_count, dtype=jnp.int32)
    chosen = (
        jnp.any(routes[:, :, None] == experts_range[None, None, :], axis=1).astype(jnp.float32)
        * valid_rows
    )
    combine = chosen * router_probs
    shared_gate = jax.nn.sigmoid(
        jnp.dot(normed_second, gathered_sgate, preferred_element_type=jnp.float32)
    )
    shared_pre = jnp.einsum(
        "td,dcf->tcf", normed_second, gathered_sgu, preferred_element_type=jnp.float32
    )
    shared_hidden = swiglu(shared_pre).astype(jnp.bfloat16)
    shared_part = jnp.einsum(
        "tf,df->td", shared_hidden, gathered_sdown, preferred_element_type=jnp.float32
    )
    mixed_part = shared_gate[:, None] * shared_part
    grad_top = grad_out.astype(jnp.float32) * valid_rows
    grad_mix_part = jnp.zeros_like(grad_top)
    selectors = [slot_table(chosen[:, expert], capacity) for expert in range(experts_count)]
    combine_columns = []
    stored = []
    for expert in range(experts_count):
        weight_gu, weight_down = gather_expert(w_egu, w_edown, expert)
        selector = selectors[expert]
        expert_rows = jnp.dot(
            selector.astype(jnp.bfloat16), normed_second, preferred_element_type=jnp.float32
        ).astype(jnp.bfloat16)
        expert_pre = jnp.einsum(
            "cd,dgf->cgf", expert_rows, weight_gu, preferred_element_type=jnp.float32
        )
        expert_hidden = swiglu(expert_pre).astype(jnp.bfloat16)
        expert_out = jnp.einsum(
            "cf,df->cd", expert_hidden, weight_down, preferred_element_type=jnp.float32
        )
        mixed_part = mixed_part + combine[:, expert : expert + 1] * scatter_rows(
            selector, expert_out
        )
        stored.append((expert_rows, expert_pre, expert_hidden, expert_out))
    expert_gu_shards = []
    expert_down_shards = []
    for expert in range(experts_count):
        selector = selectors[expert]
        expert_rows, expert_pre, expert_hidden, expert_out = stored[expert]
        weight_gu, weight_down = gather_expert(w_egu, w_edown, expert)
        grad_rows = pick_rows(selector, grad_top)
        combine_columns.append(
            scatter_rows(selector, jnp.sum(grad_rows * expert_out, axis=-1, keepdims=True))[:, 0]
        )
        combine_slot = pick_rows(selector, combine[:, expert : expert + 1])
        grad_out_low = (grad_rows * combine_slot).astype(jnp.bfloat16)
        grad_hidden = jnp.einsum(
            "cd,df->cf", grad_out_low, weight_down, preferred_element_type=jnp.float32
        )
        grad_pre = swiglu_back(expert_pre, grad_hidden).astype(jnp.bfloat16)
        grad_expert_in = jnp.einsum(
            "cgf,dgf->cd", grad_pre, weight_gu, preferred_element_type=jnp.float32
        )
        grad_mix_part = grad_mix_part + scatter_rows(selector, grad_expert_in)
        grad_weight_gu = jnp.einsum(
            "cd,cgf->dgf", expert_rows, grad_pre, preferred_element_type=jnp.float32
        )
        grad_weight_down = jnp.einsum(
            "cd,cf->df", grad_out_low, expert_hidden, preferred_element_type=jnp.float32
        )
        reduced_gu, reduced_down = reduce_expert(grad_weight_gu, grad_weight_down)
        expert_gu_shards.append(reduced_gu)
        expert_down_shards.append(reduced_down)
    grad_egu = jnp.stack(expert_gu_shards, axis=1)
    grad_edown = jnp.stack(expert_down_shards, axis=1)
    mixed = lax.psum(mixed_part.astype(jnp.bfloat16), "tp").astype(jnp.float32)
    result = (valid_rows * (middle_state + mixed)).astype(jnp.bfloat16)
    grad_combine_part = jnp.stack(combine_columns, axis=1)
    grad_shared_gate = jnp.sum(grad_top * shared_part, axis=-1)
    grad_shared_low = (shared_gate[:, None] * grad_top).astype(jnp.bfloat16)
    grad_shared_hidden = jnp.einsum(
        "td,df->tf", grad_shared_low, gathered_sdown, preferred_element_type=jnp.float32
    )
    grad_shared_pre = swiglu_back(shared_pre, grad_shared_hidden).astype(jnp.bfloat16)
    grad_mix_part = grad_mix_part + jnp.einsum(
        "tgf,dgf->td", grad_shared_pre, gathered_sgu, preferred_element_type=jnp.float32
    )
    grad_sgu_full = jnp.einsum(
        "td,tgf->dgf", normed_second, grad_shared_pre, preferred_element_type=jnp.float32
    )
    grad_sdown_full = jnp.einsum(
        "td,tf->df", grad_shared_low, shared_hidden, preferred_element_type=jnp.float32
    )
    grad_normed, grad_combine, grad_gate_value = (
        lax.psum(grad_mix_part.astype(jnp.bfloat16), "tp").astype(jnp.float32),
        lax.psum(grad_combine_part.astype(jnp.bfloat16), "tp").astype(jnp.float32),
        lax.psum(grad_shared_gate.astype(jnp.bfloat16), "tp").astype(jnp.float32),
    )
    grad_router_probs = grad_combine * chosen
    grad_logits = router_probs * (
        grad_router_probs - jnp.sum(grad_router_probs * router_probs, axis=-1, keepdims=True)
    )
    grad_logits = grad_logits.astype(jnp.bfloat16)
    grad_normed = grad_normed + jnp.einsum(
        "te,de->td", grad_logits, gathered_router, preferred_element_type=jnp.float32
    )
    grad_router_full = jnp.einsum(
        "td,te->de", normed_second, grad_logits, preferred_element_type=jnp.float32
    )
    grad_gate_logit = (grad_gate_value * shared_gate * (1.0 - shared_gate)).astype(jnp.bfloat16)
    grad_normed = (
        grad_normed
        + grad_gate_logit.astype(jnp.float32)[:, None] * gathered_sgate.astype(jnp.float32)[None, :]
    )
    grad_sgate_full = jnp.einsum(
        "td,t->d", normed_second, grad_gate_logit, preferred_element_type=jnp.float32
    )
    grad_middle, grad_gain_second = norm_back(grad_normed, middle_state, factor_second, gain_second)
    grad_middle = grad_middle + grad_top
    grad_branch = grad_middle.astype(jnp.bfloat16)
    grad_attended = jnp.einsum(
        "td,df->tf", grad_branch, gathered_out, preferred_element_type=jnp.float32
    ).astype(jnp.bfloat16)
    grad_out_proj = jnp.einsum(
        "td,tf->df", grad_branch, attended, preferred_element_type=jnp.float32
    )
    grad_attended = grad_attended.reshape(tok_count, heads_local, head_size)
    keys_back, values_back = (keys_all, values_all)
    probs_again = jnp.exp(score_table(queries, keys_back, places) - log_total)
    grad_probs = jnp.einsum(
        "qhe,khe->hqk", grad_attended, values_back, preferred_element_type=jnp.float32
    )
    inner_sum = jnp.sum(probs_again * grad_probs, axis=-1, keepdims=True)
    grad_scores = (probs_again * (grad_probs - inner_sum)).astype(jnp.bfloat16)
    score_scale = head_size ** (-0.5)
    grad_queries = (
        jnp.einsum("hqk,khe->qhe", grad_scores, keys_back, preferred_element_type=jnp.float32)
        * score_scale
    )
    grad_keys_all = (
        jnp.einsum("hqk,qhe->khe", grad_scores, queries, preferred_element_type=jnp.float32)
        * score_scale
    )
    grad_values_all = jnp.einsum(
        "hqk,qhe->khe", probs_low, grad_attended, preferred_element_type=jnp.float32
    )
    grad_keys, grad_values = (
        lax.psum_scatter(
            grad_keys_all.astype(jnp.bfloat16), "ctx", scatter_dimension=0, tiled=True
        ).astype(jnp.float32),
        lax.psum_scatter(
            grad_values_all.astype(jnp.bfloat16), "ctx", scatter_dimension=0, tiled=True
        ).astype(jnp.float32),
    )
    grad_projected = jnp.stack(
        [
            rotate_back(grad_queries, cosine_table, sine_table),
            rotate_back(grad_keys, cosine_table, sine_table),
            grad_values,
        ],
        axis=1,
    )
    grad_projected = grad_projected.reshape(tok_count, 3, width_local).astype(jnp.bfloat16)
    grad_bias_full = jnp.sum(grad_projected.astype(jnp.float32), axis=0).reshape(
        3, heads_local, head_size
    )
    grad_qkv_full = jnp.einsum(
        "td,tcf->dcf", normed_first, grad_projected, preferred_element_type=jnp.float32
    )
    grad_first_part = jnp.einsum(
        "tcf,dcf->td", grad_projected, gathered_qkv, preferred_element_type=jnp.float32
    )
    grad_normed_first = lax.psum(grad_first_part.astype(jnp.bfloat16), "tp").astype(jnp.float32)
    grad_input, grad_gain_first = norm_back(grad_normed_first, hidden_in, factor_first, gain_first)
    grad_input = grad_input + grad_middle
    grad_gains = jnp.stack([grad_gain_first, grad_gain_second])
    shards = (
        lax.psum_scatter(
            grad_gains.astype(jnp.bfloat16), "fsdp", scatter_dimension=1, tiled=True
        ).astype(jnp.float32),
        lax.psum_scatter(
            grad_qkv_full.astype(jnp.bfloat16), "fsdp", scatter_dimension=0, tiled=True
        ).astype(jnp.float32),
        lax.psum_scatter(
            grad_bias_full.astype(jnp.bfloat16), "fsdp", scatter_dimension=2, tiled=True
        ).astype(jnp.float32),
        lax.psum_scatter(
            grad_out_proj.astype(jnp.bfloat16), "fsdp", scatter_dimension=0, tiled=True
        ).astype(jnp.float32),
        lax.psum_scatter(
            grad_router_full.astype(jnp.bfloat16), "fsdp", scatter_dimension=0, tiled=True
        ).astype(jnp.float32),
        lax.psum_scatter(
            grad_sgate_full.astype(jnp.bfloat16), "fsdp", scatter_dimension=0, tiled=True
        ).astype(jnp.float32),
        lax.psum_scatter(
            grad_sgu_full.astype(jnp.bfloat16), "fsdp", scatter_dimension=0, tiled=True
        ).astype(jnp.float32),
        lax.psum_scatter(
            grad_sdown_full.astype(jnp.bfloat16), "fsdp", scatter_dimension=0, tiled=True
        ).astype(jnp.float32),
    )
    reduced = (
        lax.psum(shards[0].astype(jnp.bfloat16), "ctx").astype(jnp.float32),
        lax.psum(shards[1].astype(jnp.bfloat16), "ctx").astype(jnp.float32),
        lax.psum(shards[2].astype(jnp.bfloat16), "ctx").astype(jnp.float32),
        lax.psum(shards[3].astype(jnp.bfloat16), "ctx").astype(jnp.float32),
        lax.psum(shards[4].astype(jnp.bfloat16), "ctx").astype(jnp.float32),
        lax.psum(shards[5].astype(jnp.bfloat16), "ctx").astype(jnp.float32),
        lax.psum(shards[6].astype(jnp.bfloat16), "ctx").astype(jnp.float32),
        lax.psum(shards[7].astype(jnp.bfloat16), "ctx").astype(jnp.float32),
    )
    return (
        result,
        grad_input.astype(jnp.bfloat16),
        reduced[0],
        reduced[1],
        reduced[2],
        reduced[3],
        reduced[4],
        reduced[5],
        reduced[6],
        reduced[7],
        grad_egu,
        grad_edown,
    )


def solution(mesh):
    return jax.shard_map(
        body,
        mesh=mesh,
        in_specs=(
            P(("fsdp", "ctx"), None),
            P(),
            P(("fsdp", "ctx"), None),
            P(None, "fsdp"),
            P("fsdp", None, "tp"),
            P(None, "tp", "fsdp"),
            P("fsdp", "tp"),
            P("fsdp", None),
            P("fsdp"),
            P("fsdp", None, "tp"),
            P("fsdp", "tp"),
            P("fsdp", None, None, "tp"),
            P("fsdp", None, "tp"),
            P(("fsdp", "ctx"), None),
        ),
        out_specs=(
            P(("fsdp", "ctx"), None),
            P(("fsdp", "ctx"), None),
            P(None, "fsdp"),
            P("fsdp", None, "tp"),
            P(None, "tp", "fsdp"),
            P("fsdp", "tp"),
            P("fsdp", None),
            P("fsdp"),
            P("fsdp", None, "tp"),
            P("fsdp", "tp"),
            P("fsdp", None, None, "tp"),
            P("fsdp", None, "tp"),
        ),
        check_vma=False,
    )
```

profile of v0, /device:TPU:0, one launch (start us, length us, event | category | flops | bytes accessed | tf_op | source)
XLA Modules:
  0.0 3026.7 jit_solution(3802281491616967726)
XLA Ops:
  8.7 14.0 all_gather.96
  22.9 10.9 all_gather.94
  36.1 43.6 %all-gather.41.cloned.1.call-done = bf16[2048,3,1024]{2,0,1:T(8,128)(2,1)} async-done(((bf16[256,3,1024]{2,0,1:T(8,128)(2,1)}), bf16[2048,3,1024]{2,0,1:T(8,128)(2,1)}) %all-gather.41.cloned.1.call-update) | async-done | bytes 12582928 | tf_op jit(solution)/shard_map/all_gather | solution.py:147
  79.8 6.7 convolution_add_fusion.8
  90.5 49.8 %all-gather.43.cloned.1.call-done = bf16[1024,8,128]{2,0,1:T(8,128)(2,1)} async-done(((bf16[128,8,128]{2,0,1:T(8,128)(2,1)}), bf16[1024,8,128]{2,0,1:T(8,128)(2,1)}) %all-gather.43.cloned.1.call-update) | async-done | bytes 2097168 | tf_op jit(solution)/shard_map/all_gather | solution.py:81
  145.7 54.7 %all-gather.51.cloned.1.call-done = bf16[1024,1,8,128]{0,3,2,1:T(8,128)(2,1)} async-done(((bf16[128,1,8,128]{0,3,2,1:T(8,128)(2,1)}), bf16[1024,1,8,128]{0,3,2,1:T(8,128)(2,1)}) %all-gather.51.cloned.1.call-update) | async-done | bytes 2097168 | tf_op jit(solution)/shard_map/all_gather | solution.py:82
  202.7 33.3 %all-gather.45.cloned.1.call-done = bf16[2048,1024]{1,0:T(8,128)(2,1)} async-done(((bf16[256,1024]{1,0:T(8,128)(2,1)}), bf16[2048,1024]{1,0:T(8,128)(2,1)}) %all-gather.45.cloned.1.call-update) | async-done | bytes 4194320 | tf_op jit(solution)/shard_map/all_gather | solution.py:149
  264.4 8.5 all-gather.17
  273.6 13.2 all_gather.103
  298.3 22.9 all-gather.77.cloned.1.call-done
  325.7 29.0 all-gather.79.cloned.1.call-done
  363.8 36.5 %all-gather.81.cloned.1.call-done = bf16[2048,1,2,704]{0,3,2,1:T(8,128)(2,1)} async-done(((bf16[256,1,2,704]{0,3,2,1:T(8,128)(2,1)}), bf16[2048,1,2,704]{0,3,2,1:T(8,128)(2,1)}) %all-gather.81.cloned.1.call-update) | async-done | bytes 5767184 | tf_op jit(solution)/shard_map/all_gather | solution.py:88
  405.5 28.2 all-gather.83.cloned.1.call-done
  441.8 37.3 %all-gather.57.cloned.1.call-done = bf16[2048,1,2,704]{0,3,2,1:T(8,128)(2,1)} async-done(((bf16[256,1,2,704]{0,3,2,1:T(8,128)(2,1)}), bf16[2048,1,2,704]{0,3,2,1:T(8,128)(2,1)}) %all-gather.57.cloned.1.call-update) | async-done | bytes 5767184 | tf_op jit(solution)/shard_map/all_gather | solution.py:88
  484.3 28.2 all-gather.59.cloned.1.call-done
  520.7 37.3 %all-gather.61.cloned.1.call-done = bf16[2048,1,2,704]{0,3,2,1:T(8,128)(2,1)} async-done(((bf16[256,1,2,704]{0,3,2,1:T(8,128)(2,1)}), bf16[2048,1,2,704]{0,3,2,1:T(8,128)(2,1)}) %all-gather.61.cloned.1.call-update) | async-done | bytes 5767184 | tf_op jit(solution)/shard_map/all_gather | solution.py:88
  563.2 28.2 all-gather.63.cloned.1.call-done
  599.4 37.5 %all-gather.65.cloned.1.call-done = bf16[2048,1,2,704]{0,3,2,1:T(8,128)(2,1)} async-done(((bf16[256,1,2,704]{0,3,2,1:T(8,128)(2,1)}), bf16[2048,1,2,704]{0,3,2,1:T(8,128)(2,1)}) %all-gather.65.cloned.1.call-update) | async-done | bytes 5767184 | tf_op jit(solution)/shard_map/all_gather | solution.py:88
  642.1 28.0 all-gather.67.cloned.1.call-done
  678.2 37.9 %all-gather.69.cloned.1.call-done = bf16[2048,1,2,704]{0,3,2,1:T(8,128)(2,1)} async-done(((bf16[256,1,2,704]{0,3,2,1:T(8,128)(2,1)}), bf16[2048,1,2,704]{0,3,2,1:T(8,128)(2,1)}) %all-gather.69.cloned.1.call-update) | async-done | bytes 5767184 | tf_op jit(solution)/shard_map/all_gather | solution.py:88
  721.4 28.0 all-gather.71.cloned.1.call-done
  757.4 38.0 %all-gather.73.cloned.1.call-done = bf16[2048,1,2,704]{0,3,2,1:T(8,128)(2,1)} async-done(((bf16[256,1,2,704]{0,3,2,1:T(8,128)(2,1)}), bf16[2048,1,2,704]{0,3,2,1:T(8,128)(2,1)}) %all-gather.73.cloned.1.call-update) | async-done | bytes 5767184 | tf_op jit(solution)/shard_map/all_gather | solution.py:88
  800.9 28.0 all-gather.75.cloned.1.call-done
  836.4 38.5 %all-gather.53.cloned.1.call-done = bf16[2048,1,2,704]{0,3,2,1:T(8,128)(2,1)} async-done(((bf16[256,1,2,704]{0,3,2,1:T(8,128)(2,1)}), bf16[2048,1,2,704]{0,3,2,1:T(8,128)(2,1)}) %all-gather.53.cloned.1.call-update) | async-done | bytes 5767184 | tf_op jit(solution)/shard_map/all_gather | solution.py:88
  880.2 28.7 all-gather.55.cloned.1.call-done
  941.7 81.9 %all-gather.47.cloned.1.call-done = bf16[2048,2,2816]{2,0,1:T(8,128)(2,1)} async-done(((bf16[256,2,2816]{2,0,1:T(8,128)(2,1)}), bf16[2048,2,2816]{2,0,1:T(8,128)(2,1)}) %all-gather.47.cloned.1.call-update) | async-done | bytes 23068688 | tf_op jit(solution)/shard_map/all_gather | solution.py:152
  1023.7 12.3 fusion.171
  1036.0 53.5 %all-gather.49.cloned.1.call-done = bf16[2048,2816]{1,0:T(8,128)(2,1)} async-done(((bf16[256,2816]{1,0:T(8,128)(2,1)}), bf16[2048,2816]{1,0:T(8,128)(2,1)}) %all-gather.49.cloned.1.call-update) | async-done | bytes 11534352 | tf_op jit(solution)/shard_map/all_gather | solution.py:153
  1089.5 8.6 multiply_bitcast_fusion
  1098.1 13.8 convolution_bitcast_fusion.1
  1115.0 9.3 multiply_reduce_fusion.3
  1124.3 6.5 all-reduce.21
  1130.8 21.1 all-reduce.30.cloned.1.call-done
  1191.6 26.1 reduce-scatter.76.cloned.1.call-done
  1221.3 51.4 %reduce-scatter.32.cloned.1.call-done = bf16[128,8,128]{2,0,1:T(8,128)(2,1)} async-done(((bf16[1024,8,128]{2,0,1:T(8,128)(2,1)}), bf16[128,8,128]{2,0,1:T(8,128)(2,1)}) %reduce-scatter.32.cloned.1.call-update) | async-done | bytes 262160 | tf_op jit(solution)/shard_map/reduce_scatter | solution.py:331
  1279.4 9.8 fusion.76
  1374.3 6.6 convolution_convert_fusion.2
  1381.0 12.8 convolution_convert_fusion
  1399.2 14.0 reduce-scatter.70.cloned.1.call-done
  1413.2 36.6 %reduce-scatter.68.cloned.1.call-done = bf16[256,704]{0,1:T(8,128)(2,1)} async-done(((bf16[2048,704]{0,1:T(8,128)(2,1)}), bf16[256,704]{0,1:T(8,128)(2,1)}) %reduce-scatter.68.cloned.1.call-update) | async-done | bytes 360464 | tf_op jit(solution)/shard_map/reduce_scatter | solution.py:98
  1449.8 36.7 %reduce-scatter.66.cloned.1.call-done = bf16[256,704]{0,1:T(8,128)(2,1)} async-done(((bf16[2048,704]{0,1:T(8,128)(2,1)}), bf16[256,704]{0,1:T(8,128)(2,1)}) %reduce-scatter.66.cloned.1.call-update) | async-done | bytes 360464 | tf_op jit(solution)/shard_map/reduce_scatter | solution.py:98
  1486.5 36.7 %reduce-scatter.64.cloned.1.call-done = bf16[256,704]{0,1:T(8,128)(2,1)} async-done(((bf16[2048,704]{0,1:T(8,128)(2,1)}), bf16[256,704]{0,1:T(8,128)(2,1)}) %reduce-scatter.64.cloned.1.call-update) | async-done | bytes 360464 | tf_op jit(solution)/shard_map/reduce_scatter | solution.py:98
  1523.2 37.1 %reduce-scatter.62.cloned.1.call-done = bf16[256,704]{0,1:T(8,128)(2,1)} async-done(((bf16[2048,704]{0,1:T(8,128)(2,1)}), bf16[256,704]{0,1:T(8,128)(2,1)}) %reduce-scatter.62.cloned.1.call-update) | async-done | bytes 360464 | tf_op jit(solution)/shard_map/reduce_scatter | solution.py:98
  1560.3 36.7 %reduce-scatter.74.cloned.1.call-done = bf16[256,704]{0,1:T(8,128)(2,1)} async-done(((bf16[2048,704]{0,1:T(8,128)(2,1)}), bf16[256,704]{0,1:T(8,128)(2,1)}) %reduce-scatter.74.cloned.1.call-update) | async-done | bytes 360464 | tf_op jit(solution)/shard_map/reduce_scatter | solution.py:98
  1596.9 36.7 %reduce-scatter.72.cloned.1.call-done = bf16[256,704]{0,1:T(8,128)(2,1)} async-done(((bf16[2048,704]{0,1:T(8,128)(2,1)}), bf16[256,704]{0,1:T(8,128)(2,1)}) %reduce-scatter.72.cloned.1.call-update) | async-done | bytes 360464 | tf_op jit(solution)/shard_map/reduce_scatter | solution.py:98
  1633.6 43.1 %reduce-scatter.44.cloned.1.call-done = bf16[256,2,704]{0,2,1:T(8,128)(2,1)} async-done(((bf16[2048,2,704]{0,2,1:T(8,128)(2,1)}), bf16[256,2,704]{0,2,1:T(8,128)(2,1)}) %reduce-scatter.44.cloned.1.call-update) | async-done | bytes 720912 | tf_op jit(solution)/shard_map/reduce_scatter | solution.py:95
  1676.7 43.6 %reduce-scatter.54.cloned.1.call-done = bf16[256,2,704]{0,2,1:T(8,128)(2,1)} async-done(((bf16[2048,2,704]{0,2,1:T(8,128)(2,1)}), bf16[256,2,704]{0,2,1:T(8,128)(2,1)}) %reduce-scatter.54.cloned.1.call-update) | async-done | bytes 720912 | tf_op jit(solution)/shard_map/reduce_scatter | solution.py:95
  1720.2 43.6 %reduce-scatter.52.cloned.1.call-done = bf16[256,2,704]{0,2,1:T(8,128)(2,1)} async-done(((bf16[2048,2,704]{0,2,1:T(8,128)(2,1)}), bf16[256,2,704]{0,2,1:T(8,128)(2,1)}) %reduce-scatter.52.cloned.1.call-update) | async-done | bytes 720912 | tf_op jit(solution)/shard_map/reduce_scatter | solution.py:95
  1763.9 43.6 %reduce-scatter.50.cloned.1.call-done = bf16[256,2,704]{0,2,1:T(8,128)(2,1)} async-done(((bf16[2048,2,704]{0,2,1:T(8,128)(2,1)}), bf16[256,2,704]{0,2,1:T(8,128)(2,1)}) %reduce-scatter.50.cloned.1.call-update) | async-done | bytes 720912 | tf_op jit(solution)/shard_map/reduce_scatter | solution.py:95
  1807.5 43.9 %reduce-scatter.48.cloned.1.call-done = bf16[256,2,704]{0,2,1:T(8,128)(2,1)} async-done(((bf16[2048,2,704]{0,2,1:T(8,128)(2,1)}), bf16[256,2,704]{0,2,1:T(8,128)(2,1)}) %reduce-scatter.48.cloned.1.call-update) | async-done | bytes 720912 | tf_op jit(solution)/shard_map/reduce_scatter | solution.py:95
  1851.4 44.3 %reduce-scatter.46.cloned.1.call-done = bf16[256,2,704]{0,2,1:T(8,128)(2,1)} async-done(((bf16[2048,2,704]{0,2,1:T(8,128)(2,1)}), bf16[256,2,704]{0,2,1:T(8,128)(2,1)}) %reduce-scatter.46.cloned.1.call-update) | async-done | bytes 720912 | tf_op jit(solution)/shard_map/reduce_scatter | solution.py:95
  1895.6 43.7 %reduce-scatter.58.cloned.1.call-done = bf16[256,2,704]{0,2,1:T(8,128)(2,1)} async-done(((bf16[2048,2,704]{0,2,1:T(8,128)(2,1)}), bf16[256,2,704]{0,2,1:T(8,128)(2,1)}) %reduce-scatter.58.cloned.1.call-update) | async-done | bytes 720912 | tf_op jit(solution)/shard_map/reduce_scatter | solution.py:95
  1939.3 43.3 %reduce-scatter.56.cloned.1.call-done = bf16[256,2,704]{0,2,1:T(8,128)(2,1)} async-done(((bf16[2048,2,704]{0,2,1:T(8,128)(2,1)}), bf16[256,2,704]{0,2,1:T(8,128)(2,1)}) %reduce-scatter.56.cloned.1.call-update) | async-done | bytes 720912 | tf_op jit(solution)/shard_map/reduce_scatter | solution.py:95
  1982.7 40.4 %reduce-scatter.36.cloned.1.call-done = bf16[256,1024]{1,0:T(8,128)(2,1)} async-done(((bf16[2048,1024]{1,0:T(8,128)(2,1)}), bf16[256,1024]{1,0:T(8,128)(2,1)}) %reduce-scatter.36.cloned.1.call-update) | async-done | bytes 524304 | tf_op jit(solution)/shard_map/reduce_scatter | solution.py:370
  2023.1 69.3 %reduce-scatter.42.cloned.1.call-done = bf16[256,2816]{1,0:T(8,128)(2,1)} async-done(((bf16[2048,2816]{1,0:T(8,128)(2,1)}), bf16[256,2816]{1,0:T(8,128)(2,1)}) %reduce-scatter.42.cloned.1.call-update) | async-done | bytes 1441808 | tf_op jit(solution)/shard_map/reduce_scatter | solution.py:382
  2092.4 74.5 %reduce-scatter.34.cloned.1.call-done = bf16[256,3,1024]{2,0,1:T(8,128)(2,1)} async-done(((bf16[2048,3,1024]{2,0,1:T(8,128)(2,1)}), bf16[256,3,1024]{2,0,1:T(8,128)(2,1)}) %reduce-scatter.34.cloned.1.call-update) | async-done | bytes 1572880 | tf_op jit(solution)/shard_map/reduce_scatter | solution.py:364
  2166.9 123.6 %reduce-scatter.40.cloned.1.call-done = bf16[256,2,2816]{2,0,1:T(8,128)(2,1)} async-done(((bf16[2048,2,2816]{2,0,1:T(8,128)(2,1)}), bf16[256,2,2816]{2,0,1:T(8,128)(2,1)}) %reduce-scatter.40.cloned.1.call-update) | async-done | bytes 2883600 | tf_op jit(solution)/shard_map/reduce_scatter | solution.py:379
  2292.6 12.4 all-reduce.18
  2305.1 17.6 reduce-scatter.80.cloned.1.call-done
  2326.0 29.2 reduce-scatter.78.cloned.1.call-done
  2356.1 30.6 %reduce-scatter.38.cloned.1.call-done = bf16[256,8]{0,1:T(8,128)(2,1)} async-done(((bf16[2048,8]{0,1:T(8,128)(2,1)}), bf16[256,8]{0,1:T(8,128)(2,1)}) %reduce-scatter.38.cloned.1.call-update) | async-done | bytes 4112 | tf_op jit(solution)/shard_map/reduce_scatter | solution.py:373
  2386.8 56.7 %all-reduce.19 = (bf16[2,256]{1,0:T(2,128)(2,1)S(1)}, bf16[3,8,16]{2,1,0:T(8,128)(2,1)S(1)}, bf16[256,8]{0,1:T(8,128)(2,1)S(1)}, bf16[256]{0:T(256)(128)(2,1)S(1)}) all-reduce(bf16[2,256]{1,0:T(2,128)(2,1)S(1)} %copy.257, bf16[3,8,16]{2,1,0:T(8,128)(2,1)S(1)} %copy.259, ...), channel_id=1, replica_groups=mesh['fsdp'=8,'ctx'=8,'tp'=2] {'ctx'}, use_global_device_ids=true, to_apply=%region_40.41 | all-reduce | flops 3200 | bytes 12800 | tf_op jit(solution)/shard_map/psum | solution.py:387
  2445.8 548.6 %all-reduce.32.cloned.1.call-done = (bf16[256,2,2816]{2,0,1:T(8,128)(2,1)}, bf16[256,3,1024]{2,0,1:T(8,128)(2,1)}, bf16[256,1024]{1,0:T(8,128)(2,1)}, bf16[256,2...) async-done(((bf16[256,2,2816]{2,0,1:T(8,128)(2,1)}, ...) | async-done | bytes 15073296 | tf_op jit(solution)/shard_map/psum | solution.py:393
  2996.5 7.4 copy.238
  (858 shorter events, 353.5 us)
Async XLA Ops:
  7.2 72.6 %all-gather.41.cloned.1.call-start = ((), (), s32[]{:S(2)}) async-start(), calls=%async_computation.25 | async-start | bytes 14155776 | tf_op jit(solution)/shard_map/all_gather | solution.py:147
  7.9 132.3 %all-gather.43.cloned.1.call-start = ((), (), s32[]{:S(2)}) async-start(), calls=%async_computation.26 | async-start | bytes 2359296 | tf_op jit(solution)/shard_map/all_gather | solution.py:81
  88.7 111.6 %all-gather.51.cloned.1.call-start = ((), (), s32[]{:S(2)}) async-start(), calls=%async_computation.54 | async-start | bytes 2359296 | tf_op jit(solution)/shard_map/all_gather | solution.py:82
  89.8 146.3 %all-gather.45.cloned.1.call-start = ((), (), s32[]{:S(2)}) async-start(), calls=%async_computation.27 | async-start | bytes 4718592 | tf_op jit(solution)/shard_map/all_gather | solution.py:149
  90.3 196.4 %all-reduce.28.cloned.1.call-start = ((), (), s32[]{:S(2)}) async-start(), calls=%async_computation.28 | async-start | bytes 1048576 | tf_op jit(solution)/shard_map/psum | solution.py:183
  145.7 94.8 %copy-start.4 = (bf16[8,128,1024]{1,2,0:T(8,128)(2,1)}, bf16[8,128,1024]{1,2,0:T(8,128)(2,1)S(1)}, u32[]{:S(2)}) copy-start(bf16[8,128,1024]{1,2,0:T(8,128)(2,1)S(1)} %divide_convert_fusion) | copy-start | bytes 6291460
  240.6 80.7 %all-gather.77.cloned.1.call-start = ((), (), s32[]{:S(2)}) async-start(), calls=%async_computation.67 | async-start | bytes 6488064 | tf_op jit(solution)/shard_map/all_gather | solution.py:88
  245.9 108.8 %all-gather.79.cloned.1.call-start = ((), (), s32[]{:S(2)}) async-start(), calls=%async_computation.68 | async-start | bytes 3244032 | tf_op jit(solution)/shard_map/all_gather | solution.py:89
  249.3 151.0 %all-gather.81.cloned.1.call-start = ((), (), s32[]{:S(2)}) async-start(), calls=%async_computation.69 | async-start | bytes 6488064 | tf_op jit(solution)/shard_map/all_gather | solution.py:88
  250.0 183.6 %all-gather.83.cloned.1.call-start = ((), (), s32[]{:S(2)}) async-start(), calls=%async_computation.70 | async-start | bytes 3244032 | tf_op jit(solution)/shard_map/all_gather | solution.py:89
  250.8 228.3 %all-gather.57.cloned.1.call-start = ((), (), s32[]{:S(2)}) async-start(), calls=%async_computation.57 | async-start | bytes 6488064 | tf_op jit(solution)/shard_map/all_gather | solution.py:88
  251.3 261.2 %all-gather.59.cloned.1.call-start = ((), (), s32[]{:S(2)}) async-start(), calls=%async_computation.58 | async-start | bytes 3244032 | tf_op jit(solution)/shard_map/all_gather | solution.py:89
  252.1 305.9 %all-gather.61.cloned.1.call-start = ((), (), s32[]{:S(2)}) async-start(), calls=%async_computation.59 | async-start | bytes 6488064 | tf_op jit(solution)/shard_map/all_gather | solution.py:88
  252.7 338.7 %all-gather.63.cloned.1.call-start = ((), (), s32[]{:S(2)}) async-start(), calls=%async_computation.60 | async-start | bytes 3244032 | tf_op jit(solution)/shard_map/all_gather | solution.py:89
  253.4 383.4 %all-gather.65.cloned.1.call-start = ((), (), s32[]{:S(2)}) async-start(), calls=%async_computation.61 | async-start | bytes 6488064 | tf_op jit(solution)/shard_map/all_gather | solution.py:88
  254.0 416.1 %all-gather.67.cloned.1.call-start = ((), (), s32[]{:S(2)}) async-start(), calls=%async_computation.62 | async-start | bytes 3244032 | tf_op jit(solution)/shard_map/all_gather | solution.py:89
  254.6 461.6 %all-gather.69.cloned.1.call-start = ((), (), s32[]{:S(2)}) async-start(), calls=%async_computation.63 | async-start | bytes 6488064 | tf_op jit(solution)/shard_map/all_gather | solution.py:88
  255.1 494.3 %all-gather.71.cloned.1.call-start = ((), (), s32[]{:S(2)}) async-start(), calls=%async_computation.64 | async-start | bytes 3244032 | tf_op jit(solution)/shard_map/all_gather | solution.py:89
  255.7 539.7 %all-gather.73.cloned.1.call-start = ((), (), s32[]{:S(2)}) async-start(), calls=%async_computation.65 | async-start | bytes 6488064 | tf_op jit(solution)/shard_map/all_gather | solution.py:88
  256.3 572.5 %all-gather.75.cloned.1.call-start = ((), (), s32[]{:S(2)}) async-start(), calls=%async_computation.66 | async-start | bytes 3244032 | tf_op jit(solution)/shard_map/all_gather | solution.py:89
  257.1 617.8 %all-gather.53.cloned.1.call-start = ((), (), s32[]{:S(2)}) async-start(), calls=%async_computation.55 | async-start | bytes 6488064 | tf_op jit(solution)/shard_map/all_gather | solution.py:88
  257.6 651.2 %all-gather.55.cloned.1.call-start = ((), (), s32[]{:S(2)}) async-start(), calls=%async_computation.56 | async-start | bytes 3244032 | tf_op jit(solution)/shard_map/all_gather | solution.py:89
  258.4 765.2 %all-gather.47.cloned.1.call-start = ((), (), s32[]{:S(2)}) async-start(), calls=%async_computation.29 | async-start | bytes 25952256 | tf_op jit(solution)/shard_map/all_gather | solution.py:152
  262.3 827.2 %all-gather.49.cloned.1.call-start = ((), (), s32[]{:S(2)}) async-start(), calls=%async_computation.30 | async-start | bytes 12976128 | tf_op jit(solution)/shard_map/all_gather | solution.py:153
  263.0 888.9 %all-reduce.30.cloned.1.call-start = ((), (), s32[]{:S(2)}) async-start(), calls=%async_computation.31 | async-start | bytes 1048576 | tf_op jit(solution)/shard_map/psum | solution.py:278
  362.4 75.1 %copy-start.31 = (bf16[80,2048,1]{1,0,2:T(8,128)(2,1)}, bf16[80,2048,1]{1,0,2:T(8,128)(2,1)S(1)}, u32[]{:S(2)}) copy-start(bf16[80,2048,1]{1,0,2:T(8,128)(2,1)S(1)} %fusion.109) | copy-start | bytes 983044
  441.1 75.3 %copy-start.33 = (bf16[80,2048,1]{1,0,2:T(8,128)(2,1)}, bf16[80,2048,1]{1,0,2:T(8,128)(2,1)S(1)}, u32[]{:S(2)}) copy-start(bf16[80,2048,1]{1,0,2:T(8,128)(2,1)S(1)} %fusion.103) | copy-start | bytes 983044
  520.0 75.3 %copy-start.35 = (bf16[80,2048,1]{1,0,2:T(8,128)(2,1)}, bf16[80,2048,1]{1,0,2:T(8,128)(2,1)S(1)}, u32[]{:S(2)}) copy-start(bf16[80,2048,1]{1,0,2:T(8,128)(2,1)S(1)} %fusion.104) | copy-start | bytes 983044
  598.7 75.3 %copy-start.37 = (bf16[80,2048,1]{1,0,2:T(8,128)(2,1)}, bf16[80,2048,1]{1,0,2:T(8,128)(2,1)S(1)}, u32[]{:S(2)}) copy-start(bf16[80,2048,1]{1,0,2:T(8,128)(2,1)S(1)} %fusion.105) | copy-start | bytes 983044
  677.5 75.8 %copy-start.39 = (bf16[80,2048,1]{1,0,2:T(8,128)(2,1)}, bf16[80,2048,1]{1,0,2:T(8,128)(2,1)S(1)}, u32[]{:S(2)}) copy-start(bf16[80,2048,1]{1,0,2:T(8,128)(2,1)S(1)} %fusion.106) | copy-start | bytes 983044
  678.2 75.0 %copy-start.20 = (f32[80,2048]{1,0:T(8,128)}, f32[80,2048]{1,0:T(8,128)S(1)}, u32[]{:S(2)}) copy-start(f32[80,2048]{1,0:T(8,128)S(1)} %fusion.157) | copy-start | bytes 1966084
  756.7 76.0 %copy-start.41 = (bf16[80,2048,1]{1,0,2:T(8,128)(2,1)}, bf16[80,2048,1]{1,0,2:T(8,128)(2,1)S(1)}, u32[]{:S(2)}) copy-start(bf16[80,2048,1]{1,0,2:T(8,128)(2,1)S(1)} %fusion.107) | copy-start | bytes 983044
  757.4 75.3 %copy-start.21 = (f32[80,2048]{1,0:T(8,128)}, f32[80,2048]{1,0:T(8,128)S(1)}, u32[]{:S(2)}) copy-start(f32[80,2048]{1,0:T(8,128)S(1)} %fusion.156) | copy-start | bytes 1966084
  835.7 77.1 %copy-start.43 = (bf16[80,2048,1]{1,0,2:T(8,128)(2,1)}, bf16[80,2048,1]{1,0,2:T(8,128)(2,1)S(1)}, u32[]{:S(2)}) copy-start(bf16[80,2048,1]{1,0,2:T(8,128)(2,1)S(1)} %fusion.102) | copy-start | bytes 983044
  836.4 76.4 %copy-start.22 = (f32[80,2048]{1,0:T(8,128)}, f32[80,2048]{1,0:T(8,128)S(1)}, u32[]{:S(2)}) copy-start(f32[80,2048]{1,0:T(8,128)S(1)} %fusion.161) | copy-start | bytes 1966084
  941.7 147.7 %copy-start.201 = (f32[128]{0:T(128)S(1)}, f32[128]{0:T(128)}, u32[]{:S(2)}) copy-start(f32[128]{0:T(128)} %fusion.143) | copy-start | bytes 1540
  1114.8 102.9 %reduce-scatter.76.cloned.1.call-start = ((), (), s32[]{:S(2)}) async-start(), calls=%async_computation.71 | async-start | bytes 2359296
  1167.0 105.7 %reduce-scatter.32.cloned.1.call-start = ((), (), s32[]{:S(2)}) async-start(), calls=%async_computation.32 | async-start | bytes 2359296 | tf_op jit(solution)/shard_map/reduce_scatter | solution.py:331
  1176.4 219.3 %all-reduce.34.cloned.1.call-start = ((), (), s32[]{:S(2)}) async-start(), calls=%async_computation.75 | async-start | bytes 2097152 | tf_op jit(solution)/shard_map/psum | solution.py:259
  1191.6 97.5 %copy-start.50 = (bf16[128,1,1024]{2,0,1:T(8,128)(2,1)}, bf16[128,1,1024]{2,0,1:T(8,128)(2,1)S(1)}, u32[]{:S(2)}) copy-start(bf16[128,1,1024]{2,0,1:T(8,128)(2,1)S(1)} %copy.234) | copy-start | bytes 786436
  1289.2 110.0 %reduce-scatter.60.cloned.1.call-start = ((), (), s32[]{:S(2)}) async-start(), calls=%async_computation.46 | async-start | bytes 3244032 | tf_op jit(solution)/shard_map/reduce_scatter | solution.py:98
  1292.9 120.3 %reduce-scatter.70.cloned.1.call-start = ((), (), s32[]{:S(2)}) async-start(), calls=%async_computation.51 | async-start | bytes 3244032 | tf_op jit(solution)/shard_map/reduce_scatter | solution.py:98
  1297.2 152.5 %reduce-scatter.68.cloned.1.call-start = ((), (), s32[]{:S(2)}) async-start(), calls=%async_computation.50 | async-start | bytes 3244032 | tf_op jit(solution)/shard_map/reduce_scatter | solution.py:98
  1301.0 185.5 %reduce-scatter.66.cloned.1.call-start = ((), (), s32[]{:S(2)}) async-start(), calls=%async_computation.49 | async-start | bytes 3244032 | tf_op jit(solution)/shard_map/reduce_scatter | solution.py:98
  1304.7 218.4 %reduce-scatter.64.cloned.1.call-start = ((), (), s32[]{:S(2)}) async-start(), calls=%async_computation.48 | async-start | bytes 3244032 | tf_op jit(solution)/shard_map/reduce_scatter | solution.py:98
  1308.5 251.8 %reduce-scatter.62.cloned.1.call-start = ((), (), s32[]{:S(2)}) async-start(), calls=%async_computation.47 | async-start | bytes 3244032 | tf_op jit(solution)/shard_map/reduce_scatter | solution.py:98
  1312.2 284.7 %reduce-scatter.74.cloned.1.call-start = ((), (), s32[]{:S(2)}) async-start(), calls=%async_computation.53 | async-start | bytes 3244032 | tf_op jit(solution)/shard_map/reduce_scatter | solution.py:98
  1315.9 317.7 %reduce-scatter.72.cloned.1.call-start = ((), (), s32[]{:S(2)}) async-start(), calls=%async_computation.52 | async-start | bytes 3244032 | tf_op jit(solution)/shard_map/reduce_scatter | solution.py:98
  1319.6 357.1 %reduce-scatter.44.cloned.1.call-start = ((), (), s32[]{:S(2)}) async-start(), calls=%async_computation.38 | async-start | bytes 6488064 | tf_op jit(solution)/shard_map/reduce_scatter | solution.py:95
  1325.0 395.3 %reduce-scatter.54.cloned.1.call-start = ((), (), s32[]{:S(2)}) async-start(), calls=%async_computation.43 | async-start | bytes 6488064 | tf_op jit(solution)/shard_map/reduce_scatter | solution.py:95
  1330.4 433.5 %reduce-scatter.52.cloned.1.call-start = ((), (), s32[]{:S(2)}) async-start(), calls=%async_computation.42 | async-start | bytes 6488064 | tf_op jit(solution)/shard_map/reduce_scatter | solution.py:95
  1335.7 471.7 %reduce-scatter.50.cloned.1.call-start = ((), (), s32[]{:S(2)}) async-start(), calls=%async_computation.41 | async-start | bytes 6488064 | tf_op jit(solution)/shard_map/reduce_scatter | solution.py:95
  1341.0 510.4 %reduce-scatter.48.cloned.1.call-start = ((), (), s32[]{:S(2)}) async-start(), calls=%async_computation.40 | async-start | bytes 6488064 | tf_op jit(solution)/shard_map/reduce_scatter | solution.py:95
  1346.4 549.3 %reduce-scatter.46.cloned.1.call-start = ((), (), s32[]{:S(2)}) async-start(), calls=%async_computation.39 | async-start | bytes 6488064 | tf_op jit(solution)/shard_map/reduce_scatter | solution.py:95
  1351.7 587.6 %reduce-scatter.58.cloned.1.call-start = ((), (), s32[]{:S(2)}) async-start(), calls=%async_computation.45 | async-start | bytes 6488064 | tf_op jit(solution)/shard_map/reduce_scatter | solution.py:95
  1357.1 625.6 %reduce-scatter.56.cloned.1.call-start = ((), (), s32[]{:S(2)}) async-start(), calls=%async_computation.44 | async-start | bytes 6488064 | tf_op jit(solution)/shard_map/reduce_scatter | solution.py:95
  1362.5 660.6 %reduce-scatter.36.cloned.1.call-start = ((), (), s32[]{:S(2)}) async-start(), calls=%async_computation.34 | async-start | bytes 4718592 | tf_op jit(solution)/shard_map/reduce_scatter | solution.py:370
  1366.9 725.5 %reduce-scatter.42.cloned.1.call-start = ((), (), s32[]{:S(2)}) async-start(), calls=%async_computation.37 | async-start | bytes 12976128 | tf_op jit(solution)/shard_map/reduce_scatter | solution.py:382
  1373.2 793.7 %reduce-scatter.34.cloned.1.call-start = ((), (), s32[]{:S(2)}) async-start(), calls=%async_computation.33 | async-start | bytes 14155776 | tf_op jit(solution)/shard_map/reduce_scatter | solution.py:364
  1380.9 909.6 %reduce-scatter.40.cloned.1.call-start = ((), (), s32[]{:S(2)}) async-start(), calls=%async_computation.36 | async-start | bytes 25952256 | tf_op jit(solution)/shard_map/reduce_scatter | solution.py:379
  1393.9 928.8 %reduce-scatter.80.cloned.1.call-start = ((), (), s32[]{:S(2)}) async-start(), calls=%async_computation.73 | async-start | bytes 36864
  1395.6 959.6 %reduce-scatter.78.cloned.1.call-start = ((), (), s32[]{:S(2)}) async-start(), calls=%async_computation.72 | async-start | bytes 589824
  1398.2 988.6 %reduce-scatter.38.cloned.1.call-start = ((), (), s32[]{:S(2)}) async-start(), calls=%async_computation.35 | async-start | bytes 36864 | tf_op jit(solution)/shard_map/reduce_scatter | solution.py:373
  1399.1 1595.3 %all-reduce.32.cloned.1.call-start = ((), (), s32[]{:S(2)}) async-start(), calls=%async_computation.74 | async-start | bytes 30146560 | tf_op jit(solution)/shard_map/psum | solution.py:393
  (241 other events, 2752.1 us)
Sparse Core Ops, SparseCore 0:
  9.7 70.0 all-gather.40
  88.9 51.3 all-gather.42
  142.4 57.9 all-gather.50
  202.0 34.0 all-gather.44
  240.7 36.4 all-reduce.27
  278.8 42.3 all-gather.76
  323.0 31.5 all-gather.78
  356.4 43.7 all-gather.80
  402.0 31.5 all-gather.82
  435.3 43.7 all-gather.56
  480.9 31.5 all-gather.58
  514.2 43.7 all-gather.60
  559.8 31.5 all-gather.62
  593.0 43.7 all-gather.64
  638.5 31.5 all-gather.66
  672.3 43.7 all-gather.68
  717.8 31.5 all-gather.70
  751.6 43.7 all-gather.72
  797.2 31.5 all-gather.74
  831.1 43.7 all-gather.52
  877.2 31.5 all-gather.54
  911.2 112.3 all-gather.46
  1025.5 63.9 all-gather.48
  1115.0 36.9 all-reduce.29
  1167.1 50.5 reduce-scatter.75
  1220.6 52.0 reduce-scatter.31
  1289.3 49.2 all-reduce.33
  1341.7 34.7 reduce-scatter.59
  1379.1 34.0 reduce-scatter.69
  1415.6 34.0 reduce-scatter.67
  1452.3 34.0 reduce-scatter.65
  1489.0 34.0 reduce-scatter.63
  1526.1 34.0 reduce-scatter.61
  1562.8 34.0 reduce-scatter.73
  1599.5 34.0 reduce-scatter.71
  1636.6 40.0 reduce-scatter.43
  1679.1 41.1 reduce-scatter.53
  1722.8 41.0 reduce-scatter.51
  1766.3 41.1 reduce-scatter.49
  1810.0 41.3 reduce-scatter.47
  1854.5 41.0 reduce-scatter.45
  1898.2 41.0 reduce-scatter.57
  1941.7 40.8 reduce-scatter.55
  1985.2 37.8 reduce-scatter.35
  2026.1 66.2 reduce-scatter.41
  2094.8 72.0 reduce-scatter.33
  2169.3 121.1 reduce-scatter.39
  2292.8 29.8 reduce-scatter.79
  2325.4 29.7 reduce-scatter.77
  2357.7 29.0 reduce-scatter.37
  2390.8 603.5 all-reduce.31
where the time goes:
time: 3040 us; the launch traced here: 3030 us
  waiting for transfers between devices  2460 us (81%)
  matrix products  322 us (11%)
  blocking collectives  122 us (4%)
  local copies, waits for them, and re-layouts  60.2 us (2%)
  other arithmetic  44.7 us (1%)
    psum x1, waiting for transfers between devices, body(): lax.psum(shards[6].astype(jnp.bfloat16), 'ctx').astype(jnp.float32)  549 us
    reduce_scatter x8, waiting for transfers between devices, reduce_expert(): lax.psum_scatter(grad_gu.astype(jnp.bfloat16), 'fsdp', scatter_dimension=...  349 us
    all_gather x8, waiting for transfers between devices, gather_expert(): lax.all_gather(w_egu[:, expert], 'fsdp', axis=0, tiled=True)  286 us
    reduce_scatter x8, waiting for transfers between devices, reduce_expert(): lax.psum_scatter(grad_down.astype(jnp.bfloat16), 'fsdp', scatter_dimensio...  234 us
    all_gather x8, waiting for transfers between devices, gather_expert(): lax.all_gather(w_edown[:, expert], 'fsdp', axis=0, tiled=True)  226 us
    reduce_scatter x1, waiting for transfers between devices, body(): lax.psum_scatter(grad_sgu_full.astype(jnp.bfloat16), 'fsdp', scatter_dime...  124 us
    unnamed x54, waiting for transfers between devices  83.7 us
    all_gather x1, waiting for transfers between devices, body(): lax.all_gather(w_sgu, 'fsdp', axis=0, tiled=True)  81.9 us
  transfers between devices with their start and end apart: 51, of which 48 were waited for; matrix products, arithmetic and copies ran while one was open for 10% of the time, Pallas kernels for 0%

commit v1 on v0

v1 whole, which is shorter than its diff:
```python
import jax
import jax.numpy as jnp
from jax import lax
from jax.experimental import pallas as pl
from jax.experimental.pallas import tpu as pltpu
from jax.sharding import PartitionSpec as P

EPSILON = 1e-06
ROPE_BASE = 1000000.0
MASKED_SCORE = -1e30
LOW = jnp.bfloat16
WIDE = jnp.float32
VMEM_BYTES = 56 * 1024 * 1024


def low(values):
    return values.astype(LOW)


def wide(values):
    return values.astype(WIDE)


def rotary_tables(row_count, head_size):
    middle = head_size // 2
    inverse = ROPE_BASE ** (-(jnp.arange(middle, dtype=WIDE) * 2.0) / head_size)
    places = jnp.arange(row_count, dtype=jnp.int32).astype(WIDE)
    angles = places[:, None] * inverse[None, :]
    cosine, sine = jnp.cos(angles), jnp.sin(angles)
    return (
        jnp.concatenate([cosine, cosine], axis=-1),
        jnp.concatenate([-sine, sine], axis=-1),
    )


def inverse_rms(values):
    return lax.rsqrt(jnp.mean(values * values, axis=-1, keepdims=True) + EPSILON)


def ring(step):
    return [(i, (i + step) % 8) for i in range(8)]


PAIR = [(i, i ^ 1) for i in range(8)]


def up(values):
    return lax.ppermute(values, "ctx", ring(2))


def down(values):
    return lax.ppermute(values, "ctx", ring(-2))


def swap(values):
    return lax.ppermute(values, "ctx", PAIR)


def relative_places():
    here = lax.axis_index("ctx")
    return [(here + step) % 8 for step in (0, 6, 2, 4)] + [
        ((here ^ 1) + step) % 8 for step in (0, 6, 2, 4)
    ]


def gather_relative(block):
    half = block.shape[0] // 2
    left, right, pair = up(block), down(block), swap(block)
    first, second = up(left[:half]), down(right[half:])
    pair_left, pair_right = up(pair), down(pair)
    opposite = jnp.concatenate([first, second], axis=0)
    pair_opposite = swap(opposite)
    return [block, left, right, opposite, pair, pair_left, pair_right, pair_opposite]


def in_order(blocks):
    placed = jnp.zeros((8,) + blocks[0].shape, blocks[0].dtype)
    for block, place in zip(blocks, relative_places()):
        placed = lax.dynamic_update_slice(placed, block[None], (place,) + (0,) * block.ndim)
    return placed


def scatter_relative(blocks):
    own, left, right, opposite, pair, pair_left, pair_right, pair_opposite = blocks
    half = own.shape[0] // 2
    from_pair = swap(low(pair_opposite))
    pair_up, pair_down = up(low(pair_right)), down(low(pair_left))
    opposite = wide(opposite) + wide(from_pair)
    first, second = up(low(opposite[:half])), down(low(opposite[half:]))
    crossing = swap(low(wide(pair) + wide(pair_up) + wide(pair_down)))
    right = jnp.concatenate([wide(right[:half]) + wide(first), wide(right[half:])], axis=0)
    left = jnp.concatenate([wide(left[:half]), wide(left[half:]) + wide(second)], axis=0)
    last_up, last_down = up(low(right)), down(low(left))
    return wide(own) + wide(crossing) + wide(last_up) + wide(last_down)


def add_halves(values):
    mine = low(values)
    return wide(mine) + wide(lax.ppermute(mine, "tp", [(0, 1), (1, 0)]))


QUERY_ROWS = 256


def turn(values, cosine, sine):
    return values * cosine + pltpu.roll(values, values.shape[-1] // 2, 1) * sine


def dot_rows(left, right):
    return lax.dot_general(left, right, (((1,), (1,)), ((), ())), preferred_element_type=WIDE)


def dot_columns(left, right):
    return lax.dot_general(left, right, (((0,), (0,)), ((), ())), preferred_element_type=WIDE)


def probabilities(queries, keys, start, scale):
    scores = dot_rows(queries, keys) * scale
    rows = start + lax.broadcasted_iota(jnp.int32, scores.shape, 0)
    columns = lax.broadcasted_iota(jnp.int32, scores.shape, 1)
    scores = jnp.where(columns <= rows, scores, MASKED_SCORE)
    expons = jnp.exp(scores - jnp.max(scores, axis=-1, keepdims=True))
    return expons / jnp.sum(expons, axis=-1, keepdims=True)


def attend_kernel(proj_ref, cos_ref, sin_ref, q_ref, k_ref, v_ref, out_ref):
    size = cos_ref.shape[1]
    scale = size ** (-0.5)
    cosine, sine = cos_ref[...], sin_ref[...]
    q_ref[...] = low(turn(proj_ref[:, :size], cosine, sine))
    k_ref[...] = low(turn(proj_ref[:, size : 2 * size], cosine, sine))
    v_ref[...] = low(proj_ref[:, 2 * size :])
    for start in range(0, q_ref.shape[0], QUERY_ROWS):
        end = start + QUERY_ROWS
        probs = low(probabilities(q_ref[start:end], k_ref[:end], start, scale))
        out_ref[start:end] = low(jnp.dot(probs, v_ref[:end], preferred_element_type=WIDE))


def attend_back_kernel(
    q_ref, k_ref, v_ref, grad_ref, cos_ref, sin_ref, out_ref, bias_ref, dk_ref, dv_ref
):
    size = cos_ref.shape[1]
    scale = size ** (-0.5)
    dk_ref[...] = jnp.zeros_like(dk_ref)
    dv_ref[...] = jnp.zeros_like(dv_ref)
    bias = jnp.zeros((1, size), WIDE)
    for start in range(0, q_ref.shape[0], QUERY_ROWS):
        end = start + QUERY_ROWS
        queries, grads = q_ref[start:end], grad_ref[start:end]
        probs = probabilities(queries, k_ref[:end], start, scale)
        grad_probs = dot_rows(grads, v_ref[:end])
        inner = jnp.sum(probs * grad_probs, axis=-1, keepdims=True)
        grad_scores = low(probs * (grad_probs - inner))
        grad_queries = jnp.dot(grad_scores, k_ref[:end], preferred_element_type=WIDE) * scale
        grad_queries = low(turn(grad_queries, cos_ref[start:end], -sin_ref[start:end]))
        out_ref[start:end, :size] = grad_queries
        bias = bias + jnp.sum(wide(grad_queries), axis=0, keepdims=True)
        dk_ref[:end] += dot_columns(grad_scores, queries) * scale
        dv_ref[:end] += dot_columns(low(probs), grads)
    bias_ref[:, :size] = bias
    grad_keys = low(turn(dk_ref[...], cos_ref[...], -sin_ref[...]))
    out_ref[:, size : 2 * size] = grad_keys
    bias_ref[:, size : 2 * size] = jnp.sum(wide(grad_keys), axis=0, keepdims=True)
    grad_values = low(dv_ref[...])
    out_ref[:, 2 * size :] = grad_values
    bias_ref[:, 2 * size :] = jnp.sum(wide(grad_values), axis=0, keepdims=True)


def attend(proj, cosine, sine):
    rows, size = cosine.shape
    one = jax.ShapeDtypeStruct((rows, size), LOW)
    return pl.pallas_call(
        attend_kernel,
        out_shape=(one, one, one, one),
        compiler_params=pltpu.CompilerParams(vmem_limit_bytes=VMEM_BYTES),
        name="attend",
    )(proj, cosine, sine)


def attend_back(queries, keys, values, grads, cosine, sine):
    rows, size = cosine.shape
    return pl.pallas_call(
        attend_back_kernel,
        out_shape=(
            jax.ShapeDtypeStruct((rows, 3 * size), LOW),
            jax.ShapeDtypeStruct((1, 3 * size), WIDE),
        ),
        scratch_shapes=[pltpu.VMEM((rows, size), WIDE), pltpu.VMEM((rows, size), WIDE)],
        compiler_params=pltpu.CompilerParams(vmem_limit_bytes=VMEM_BYTES),
        name="attend_back",
    )(queries, keys, values, grads, cosine, sine)


def gated_unit(normed, grad_top, weight_gate, weight_up, weight_down, scale):
    gate = jnp.dot(normed, weight_gate, preferred_element_type=WIDE)
    upper = jnp.dot(normed, weight_up, preferred_element_type=WIDE)
    back = jnp.dot(grad_top, weight_down, preferred_element_type=WIDE)
    sigmoid = jax.nn.sigmoid(gate)
    silu = gate * sigmoid
    hidden = silu * upper
    hidden_scaled = low(hidden * scale)
    grad_scale = jnp.sum(hidden * back, axis=-1, keepdims=True)
    grad_hidden = back * scale
    grad_gate = low(grad_hidden * upper * (sigmoid * (1.0 + gate * (1.0 - sigmoid))))
    grad_up = low(grad_hidden * silu)
    mixed = dot_rows(hidden_scaled, weight_down)
    grad_normed = dot_rows(grad_gate, weight_gate) + dot_rows(grad_up, weight_up)
    return (
        mixed,
        grad_normed,
        grad_scale,
        low(dot_columns(normed, grad_gate)),
        low(dot_columns(normed, grad_up)),
        low(dot_columns(grad_top, hidden_scaled)),
    )


def body(
    inputs,
    lengths,
    routes,
    norm_gains,
    w_qkv,
    b_qkv,
    w_o,
    w_router,
    w_sgate,
    w_sgu,
    w_sdown,
    w_egu,
    w_edown,
    grad_out,
):
    rows, width = inputs.shape
    shard = w_qkv.shape[0]
    experts = w_egu.shape[1]
    heads, bias_part = b_qkv.shape[1], b_qkv.shape[2]
    head_size = bias_part * 8
    expert_units = w_edown.shape[2]
    shared_units = w_sdown.shape[1] // 8
    group, here = lax.axis_index("fsdp"), lax.axis_index("ctx")
    places = here * rows + jnp.arange(rows, dtype=jnp.int32)
    length_here = lax.dynamic_index_in_dim(lengths, group, 0, keepdims=False)
    valid = (places < length_here).astype(WIDE)[:, None]
    experts_range = jnp.arange(experts, dtype=jnp.int32)
    chosen = (
        jnp.any(routes[:, :, None] == experts_range[None, None, :], axis=1).astype(WIDE) * valid
    )

    bias_here = lax.dynamic_slice(b_qkv, (0, here, 0), (3, 1, bias_part)).reshape(3 * bias_part)
    bias_column = jnp.pad(bias_here, (0, shard - 3 * bias_part))[:, None]
    small = jnp.concatenate(
        [norm_gains.T, w_sgate[:, None], w_router, bias_column], axis=1
    )
    small = jnp.pad(small, ((0, 0), (0, 128 - small.shape[1])))
    qkv_here = lax.dynamic_slice(
        w_qkv, (0, 0, here * head_size), (shard, 3, head_size)
    ).reshape(shard, 3 * head_size)
    first_pack = lax.all_gather(
        jnp.concatenate([qkv_here, small], axis=1), "fsdp", axis=0, tiled=True
    )
    weight_qkv, small_all = first_pack[:, : 3 * head_size], first_pack[:, 3 * head_size :]
    gain_first, gain_second = wide(small_all[:, 0]), wide(small_all[:, 1])
    weight_sgate, weight_router = small_all[:, 2:3], small_all[:, 3 : 3 + experts]
    bias_all = small_all[:, 3 + experts].reshape(8, shard)[:, : 3 * bias_part]
    bias_all = wide(bias_all.reshape(8, 3, bias_part).transpose(1, 0, 2).reshape(3 * head_size))
    weight_out = lax.all_gather(w_o, "fsdp", axis=0, tiled=True)
    shared_start = here * shared_units
    shared_gu = lax.dynamic_slice(w_sgu, (0, 0, shared_start), (shard, 2, shared_units))
    shared_down = lax.dynamic_slice(w_sdown, (0, shared_start), (shard, shared_units))
    expert_gu = lax.dynamic_slice(w_egu, (0, here, 0, 0), (shard, 1, 2, expert_units))
    expert_down = lax.dynamic_slice(w_edown, (0, here, 0), (shard, 1, expert_units))
    second_pack = lax.all_gather(
        jnp.concatenate(
            [
                expert_gu.reshape(shard, 2 * expert_units),
                expert_down.reshape(shard, expert_units),
                shared_gu.reshape(shard, 2 * shared_units),
                shared_down,
            ],
            axis=1,
        ),
        "fsdp",
        axis=0,
        tiled=True,
    )
    expert_columns = second_pack[:, : 3 * expert_units]
    shared_columns = second_pack[:, 3 * expert_units :]
    weight_qkv_all = lax.all_gather(w_qkv, "fsdp", axis=0, tiled=True)

    cosine, sine = rotary_tables(rows * 8, head_size)
    grad_own = low(wide(grad_out) * valid)
    hidden_in = wide(inputs)
    hidden_all = in_order(gather_relative(inputs)).reshape(rows * 8, width)
    hidden_wide = wide(hidden_all)
    normed_first = low(hidden_wide * inverse_rms(hidden_wide) * gain_first)
    proj = jnp.dot(normed_first, weight_qkv, preferred_element_type=WIDE) + bias_all
    queries, keys, values, attended = attend(proj, cosine, sine)
    attended_own = lax.all_to_all(attended, "ctx", 0, 1, tiled=True)
    grad_pack = jnp.concatenate(
        [grad_own, jnp.pad(low(chosen), ((0, 0), (0, 128 - experts)))], axis=1
    )
    grad_all = jnp.concatenate(gather_relative(grad_pack), axis=0)
    grad_top_all, chosen_all = grad_all[:, :width], wide(grad_all[:, width : width + experts])
    branch = add_halves(dot_rows(attended_own, weight_out))
    middle = hidden_in + branch
    factor_second = inverse_rms(middle)
    normed_own = low(middle * factor_second * gain_second)

    normed_all = jnp.concatenate(gather_relative(normed_own), axis=0)
    logits = jnp.dot(normed_all, weight_router, preferred_element_type=WIDE)
    router_probs = jax.nn.softmax(logits, axis=-1)
    shared_gate = jax.nn.sigmoid(jnp.dot(normed_all, weight_sgate, preferred_element_type=WIDE))
    mine = (experts_range == here).astype(WIDE)[None, :]
    combine = jnp.sum(chosen_all * router_probs * mine, axis=-1, keepdims=True)
    expert = gated_unit(
        normed_all,
        grad_top_all,
        expert_columns[:, :expert_units],
        expert_columns[:, expert_units : 2 * expert_units],
        expert_columns[:, 2 * expert_units :],
        combine,
    )
    shared = gated_unit(
        normed_all,
        grad_top_all,
        shared_columns[:, :shared_units],
        shared_columns[:, shared_units : 2 * shared_units],
        shared_columns[:, 2 * shared_units :],
        shared_gate,
    )
    mixed_all = expert[0] + shared[0]
    scales_all = jnp.concatenate([expert[2] * mine, shared[2]], axis=1)
    scales_all = jnp.pad(scales_all, ((0, 0), (0, 128 - experts - 1)))
    grad_normed_all = jnp.concatenate([expert[1] + shared[1], scales_all], axis=1)

    def split(values):
        return [values[index * rows : (index + 1) * rows] for index in range(8)]

    grad_sum = add_halves(scatter_relative(split(grad_normed_all)))
    mlp_grads = lax.psum_scatter(
        jnp.concatenate(list(expert[3:]) + list(shared[3:]), axis=1),
        "fsdp",
        scatter_dimension=0,
        tiled=True,
    )
    mixed = add_halves(scatter_relative(split(mixed_all)))
    result = low(valid * (middle + mixed))

    probs_own, gate_own = router_probs[:rows], shared_gate[:rows]
    grad_normed, grad_combine = grad_sum[:, :width], grad_sum[:, width : width + experts]
    grad_gate = grad_sum[:, width + experts : width + experts + 1]
    picked = grad_combine * chosen
    grad_logits = low(
        probs_own * (picked - jnp.sum(picked * probs_own, axis=-1, keepdims=True))
    )
    grad_gate_logit = low(grad_gate * gate_own * (1.0 - gate_own))
    both = jnp.concatenate([grad_logits, grad_gate_logit], axis=1)
    both_weights = jnp.concatenate([weight_router, weight_sgate], axis=1)
    grad_normed = grad_normed + dot_rows(both, both_weights)
    grad_both = dot_columns(normed_own, both)
    grad_top = wide(grad_own)
    grad_gain_second = jnp.sum(grad_normed * middle * factor_second, axis=0)
    weighted = grad_normed * gain_second
    inner = jnp.mean(weighted * middle, axis=-1, keepdims=True)
    grad_middle = grad_top + weighted * factor_second - middle * factor_second**3 * inner
    grad_branch = low(grad_middle)

    grad_attended = low(jnp.dot(grad_branch, weight_out, preferred_element_type=WIDE))
    grad_heads = lax.all_to_all(
        grad_attended.reshape(rows, heads, head_size).transpose(1, 0, 2), "ctx", 0, 0, tiled=True
    ).reshape(rows * 8, head_size)
    grad_proj, grad_bias = attend_back(queries, keys, values, grad_heads, cosine, sine)
    proj_own = lax.all_to_all(grad_proj.reshape(8, rows, 3 * head_size), "ctx", 0, 0, tiled=True)
    proj_own = proj_own.reshape(8, rows, 3, head_size).transpose(1, 2, 0, 3)
    grad_first = lax.dot_general(
        proj_own.reshape(rows, 3 * heads * head_size),
        weight_qkv_all.reshape(width, 3 * heads * head_size),
        (((1,), (1,)), ((), ())),
        preferred_element_type=WIDE,
    )
    grad_first = add_halves(grad_first)
    factor_first = inverse_rms(hidden_in)
    weighted = grad_first * gain_first
    inner = jnp.mean(weighted * hidden_in, axis=-1, keepdims=True)
    grad_input = grad_middle + weighted * factor_first - hidden_in * factor_first**3 * inner

    grad_out_part = lax.psum_scatter(
        low(dot_columns(grad_branch, attended_own)), "fsdp", scatter_dimension=0, tiled=True
    )
    grad_w_o_here = scatter_relative(
        [
            lax.dynamic_slice(grad_out_part, (0, place * head_size), (shard, head_size))
            for place in relative_places()
        ]
    )
    grad_qkv_here = low(dot_columns(normed_first, grad_proj))
    bias_rows = grad_bias.reshape(3, 8, bias_part).transpose(1, 0, 2).reshape(8, 3 * bias_part)
    bias_rows = jnp.pad(bias_rows, ((0, 0), (0, shard - 3 * bias_part))).reshape(width, 1)
    small_grads = low(jnp.concatenate([grad_both, grad_gain_second[:, None], bias_rows], axis=1))
    small_grads = jnp.pad(small_grads, ((0, 0), (0, 128 - small_grads.shape[1])))
    last_pack = lax.psum_scatter(
        jnp.concatenate([grad_qkv_here, small_grads], axis=1),
        "fsdp",
        scatter_dimension=0,
        tiled=True,
    )
    mlp_all = in_order(gather_relative(mlp_grads))
    last_all = in_order(
        gather_relative(jnp.concatenate([last_pack, low(grad_w_o_here)], axis=1))
    )
    expert_gu_all = wide(mlp_all[:, :, : 2 * expert_units])
    grad_w_egu = expert_gu_all.reshape(8, shard, 2, expert_units).transpose(1, 0, 2, 3)
    grad_w_edown = wide(mlp_all[:, :, 2 * expert_units : 3 * expert_units]).transpose(1, 0, 2)
    shared_gu_all = wide(mlp_all[:, :, 3 * expert_units : 3 * expert_units + 2 * shared_units])
    grad_w_sgu = (
        shared_gu_all.reshape(8, shard, 2, shared_units)
        .transpose(1, 2, 0, 3)
        .reshape(shard, 2, 8 * shared_units)
    )
    grad_w_sdown = (
        wide(mlp_all[:, :, 3 * expert_units + 2 * shared_units :])
        .transpose(1, 0, 2)
        .reshape(shard, 8 * shared_units)
    )
    qkv_size = 3 * head_size
    grad_w_qkv = (
        wide(last_all[:, :, :qkv_size])
        .reshape(8, shard, 3, head_size)
        .transpose(1, 2, 0, 3)
        .reshape(shard, 3, heads * head_size)
    )
    small_sums = wide(last_all[:, :, qkv_size : qkv_size + 128])
    grad_w_o = (
        wide(last_all[:, :, qkv_size + 128 :]).transpose(1, 0, 2).reshape(shard, heads * head_size)
    )
    summed = jnp.sum(small_sums[:, :, : experts + 2], axis=0)
    grad_b_qkv = (
        small_sums[:, : 3 * bias_part, experts + 2].reshape(8, 3, bias_part).transpose(1, 0, 2)
    )
    products = jnp.sum(grad_w_qkv * wide(w_qkv), axis=(1, 2))
    products = products + lax.ppermute(products, "tp", [(0, 1), (1, 0)])
    grad_gain_first = products / wide(norm_gains[0])
    return (
        result,
        low(grad_input),
        jnp.stack([grad_gain_first, summed[:, experts + 1]]),
        grad_w_qkv,
        grad_b_qkv,
        grad_w_o,
        summed[:, :experts],
        summed[:, experts],
        grad_w_sgu,
        grad_w_sdown,
        grad_w_egu,
        grad_w_edown,
    )


def solution(mesh):
    return jax.shard_map(
        body,
        mesh=mesh,
        in_specs=(
            P(("fsdp", "ctx"), None),
            P(),
            P(("fsdp", "ctx"), None),
            P(None, "fsdp"),
            P("fsdp", None, "tp"),
            P(None, "tp", "fsdp"),
            P("fsdp", "tp"),
            P("fsdp", None),
            P("fsdp"),
            P("fsdp", None, "tp"),
            P("fsdp", "tp"),
            P("fsdp", None, None, "tp"),
            P("fsdp", None, "tp"),
            P(("fsdp", "ctx"), None),
        ),
        out_specs=(
            P(("fsdp", "ctx"), None),
            P(("fsdp", "ctx"), None),
            P(None, "fsdp"),
            P("fsdp", None, "tp"),
            P(None, "tp", "fsdp"),
            P("fsdp", "tp"),
            P("fsdp", None),
            P("fsdp"),
            P("fsdp", None, "tp"),
            P("fsdp", "tp"),
            P("fsdp", None, None, "tp"),
            P("fsdp", None, "tp"),
        ),
        check_vma=False,
    )
```

time: 3040 us -> 658 us (0.22)
  waiting for transfers between devices: 2460 us -> 159 us
  matrix products: 322 us -> 129 us
  starting transfers between devices: 3.07 us -> 129 us
  blocking collectives: 122 us -> 12.8 us
  local copies, waits for them, and re-layouts: 60.2 us -> 126 us
    reduce_scatter x22 -> x3, waiting for transfers between devices: 973 us -> 0.04 us  [the longest x1 0.02 us: body(): lax.psum_scatter(jnp.concatenate([grad_qkv_here, small_grads], axis=1), '...]
    all_gather x22 -> x4, waiting for transfers between devices: 829 us -> 0.04 us  [the longest x1 0.02 us: body(): lax.all_gather(jnp.concatenate([qkv_here, small], axis=1), 'fsdp', axis=0...]
    psum x4 -> x0, waiting for transfers between devices: 570 us -> none  [the longest x1 549 us: body(): lax.psum(shards[6].astype(jnp.bfloat16), 'ctx').astype(jnp.float32)]
    dot_general x119 -> x28, matrix products: 322 us -> 129 us  [the longest x8 48.1 us: dot_rows(): lax.dot_general(left, right, (((1,), (1,)), ((), ())), preferred_element_...]
    ppermute x0 -> x69, waiting for transfers between devices: none -> 146 us  [the longest x24 99 us: up(): return lax.ppermute(values, 'ctx', ring(2))]
    ppermute x0 -> x69, starting transfers between devices: none -> 118 us  [the longest x24 67.9 us: down(): return lax.ppermute(values, 'ctx', ring(-2))]
    unnamed x54 -> x7, waiting for transfers between devices: 83.7 us -> 0.79 us
    psum x2 -> x0, blocking collectives: 63.2 us -> none  [the longest x1 56.7 us: body(): lax.psum(shards[0].astype(jnp.bfloat16), 'ctx').astype(jnp.float32)]
  transfers between devices with their start and end apart: 51 -> 78, of which waited for: 48 -> 33; matrix products, arithmetic and copies ran while one was open for 10% -> 42% of each run, Pallas kernels for 0% -> 2%
where the time goes in v1:
time: 658 us; the launch traced here: 647 us
  waiting for transfers between devices  159 us (24%)
  starting transfers between devices  129 us (20%)
  matrix products  129 us (20%)
  local copies, waits for them, and re-layouts  126 us (19%)
  other arithmetic  64.8 us (10%)
  between operations  15.9 us (2%)
  blocking collectives  12.8 us (2%)
  Pallas kernels  10.9 us (2%)
    ppermute x24, waiting for transfers between devices, up(): return lax.ppermute(values, 'ctx', ring(2))  99 us
    ppermute x24, starting transfers between devices, down(): return lax.ppermute(values, 'ctx', ring(-2))  67.9 us
    dot_general x8, matrix products, dot_rows(): lax.dot_general(left, right, (((1,), (1,)), ((), ())), preferred_element_...  48.1 us
    dot_general x9, matrix products, dot_columns(): lax.dot_general(left, right, (((0,), (0,)), ((), ())), preferred_element_...  34.4 us
    unnamed x130, local copies, waits for them, and re-layouts  33 us
    ppermute x16, starting transfers between devices, swap(): return lax.ppermute(values, 'ctx', PAIR)  26 us
    ppermute x4, waiting for transfers between devices, add_halves(): return wide(mine) + wide(lax.ppermute(mine, 'tp', [(0, 1), (1, 0)]))  22.5 us
    dynamic_update_slice x23, local copies, waits for them, and re-layouts, in_order(): lax.dynamic_update_slice(placed, block[None], (place,) + (0,) * block.ndim)  18.8 us
  transfers between devices with their start and end apart: 78, of which 33 were waited for; matrix products, arithmetic and copies ran while one was open for 42% of the time, Pallas kernels for 2%

profile of v1, /device:TPU:0, one launch (start us, length us, event | category | flops | bytes accessed | tf_op | source)
XLA Modules:
  0.0 646.8 jit_solution(5999207729768566770)
XLA Ops:
  31.5 3.4 collective-permute-done
  46.0 13.5 %collective-permute-start.7 = (bf16[128,2048]{1,0:T(8,128)(2,1)S(1)}, bf16[128,2048]{1,0:T(8,128)(2,1)S(1)}, u32[]{:S(2)}, u32[]{:S(2)}) collective-permute-start(bf16[128,2048]{1,0:T(8,128)(2,1)S(1)} %constant_dynamic-update-slice_fusion), channel_id=1, source_target_pairs={{0,2},{2,0},{4,6},{6,4},{8,10},{10,8},{12,14},{14,12},{1,3},{3,1},... | collective-permute-start | bytes 1572872 | tf_op jit(solution)/shard_map/ppermute | solution.py:56
  60.9 6.3 collective-permute-done.7
  71.3 3.4 fusion.2
  74.8 3.5 fusion.30.proj_ref
  78.3 4.8 attend.1
  84.9 6.0 all-to-all-start
  91.1 6.8 %all-to-all-done = bf16[8,128,128]{1,2,0:T(8,128)(2,1)S(1)} async-done(((bf16[8,128,128]{1,2,0:T(8,128)(2,1)}), bf16[8,128,128]{1,2,0:T(8,128)(2,1)S(1)}, u32[]{:S(2)}, u32[]{:S(2)}) %all-to-all-start) | async-done | bytes 262176 | tf_op jit(solution)/shard_map/all_to_all | solution.py:299
  97.8 3.6 convolution_convert_fusion.8
  108.7 8.1 %collective-permute-done.8 = bf16[128,2048]{0,1:T(8,128)(2,1)} collective-permute-done((bf16[128,2048]{0,1:T(8,128)(2,1)S(1)}, bf16[128,2048]{0,1:T(8,128)(2,1)}, u32[]{:S(2)}, u32[]{:S(2)}) %collective-permute-start.8) | collective-permute-done | bytes 524320 | tf_op jit(solution)/shard_map/ppermute | solution.py:99
  133.1 4.8 collective-permute-done.19
  139.5 3.7 collective-permute-start.23
  145.8 3.3 collective-permute-start.12
  151.3 10.6 %collective-permute-done.11 = bf16[64,2048]{0,1:T(8,128)(2,1)S(1)} collective-permute-done((bf16[64,2048]{0,1:T(8,128)(2,1)}, bf16[64,2048]{0,1:T(8,128)(2,1)S(1)}, u32[]{:S(2)}, u32[]{:S(2)}) %collective-permute-start.11) | collective-permute-done | bytes 262176 | tf_op jit(solution)/shard_map/ppermute | solution.py:48
  161.9 3.5 collective-permute-start.15
  168.0 7.8 %concatenate.100 = bf16[1024,2176]{0,1:T(8,128)(2,1)} concatenate(bf16[128,2176]{0,1:T(8,128)(2,1)} %copy-done.15, bf16[128,2176]{0,1:T(8,128)(2,1)} %collective-permute-done.17, bf16[128,2176]{0,1:T(8,128)(2,1)} %collective-permute-done.18, bf16[64,2176]{0,1:T(8,128)(2,1)S(1)} %copy.199, bf16[64,2176]{0,1:T(8,128)(2,1)S(1)} %copy.200, ...), dimensions={0} | concatenate | bytes 8912896 | tf_op jit(solution)/shard_map/concatenate | solution.py:303
  175.9 7.6 %concatenate.96 = bf16[1024,2048]{0,1:T(8,128)(2,1)} concatenate(bf16[128,2048]{0,1:T(8,128)(2,1)} %multiply_convert_fusion.8, bf16[128,2048]{0,1:T(8,128)(2,1)} %collective-permute-done.9, bf16[128,2048]{0,1:T(8,128)(2,1)} %collective-permute-done.10, bf16[64,2048]{0,1:T(8,128)(2,1)} %copy-done.20, bf16[64,2048]{0,1:T(8,128)(2,1)} %copy-done.21, ...), dimensions={0} | concatenate | bytes 8388608 | tf_op jit(solution)/shard_map/concatenate | solution.py:310
  189.5 5.5 fusion.36
  195.1 4.9 fusion.40
  206.3 6.3 multiply_reduce_fusion.2
  212.7 5.2 fusion.17
  220.3 5.9 fusion.121
  230.9 3.9 fusion.38
  234.9 7.9 %fusion.23 = f32[1024,2048]{0,1:T(8,128)} fusion(bf16[1024,704]{0,1:T(8,128)(2,1)S(1)} %copy-done.52, bf16[2048,3168]{0,1:T(8,128)(2,1)} %all-gather.9.cloned.1.call-done), kind=kOutput, calls=%fused_computation.56 | convolution fusion | flops 2952790016 | bytes 12713984 | tf_op jit(solution)/shard_map/dot_general | solution.py:110
  242.8 7.6 %fusion.19 = f32[1024,2048]{0,1:T(8,128)} fusion(bf16[1024,704]{0,1:T(8,128)(2,1)S(1)} %copy-done.50, bf16[2048,3168]{0,1:T(8,128)(2,1)} %all-gather.9.cloned.1.call-done), kind=kOutput, calls=%fused_computation.52 | convolution fusion | flops 2952790016 | bytes 12713984 | tf_op jit(solution)/shard_map/dot_general | solution.py:110
  250.4 13.0 %add_add_fusion = f32[1024,2048]{0,1:T(8,128)} fusion(f32[1024,2048]{0,1:T(8,128)S(1)} %fusion.38, f32[1024,2048]{0,1:T(8,128)} %fusion.23, f32[1024,2048]{0,1:T(8,128)} %fusion.19, bf16[1024,352]{0,1:T(8,128)(2,1)S(1)} %get-tuple-element.131, bf16[2048,3168]{0,1:T(8,128)(2,1)} %all-gather.9.cloned.1.call-done), kind=kOutput, calls=%fused_computation.11 | convolution fusion | flops 1482686464 | bytes 35717120 | tf_op jit(solution)/shard_map/dot_general | solution.py:110
  263.4 6.2 fusion
  279.1 3.3 fusion.74
  282.4 3.5 collective-permute-done.35
  285.9 4.7 collective-permute-done.34
  296.1 3.3 collective-permute-start.40
  314.3 3.9 collective-permute-done.29
  320.8 3.3 collective-permute-start.32
  324.4 3.9 collective-permute-done.36
  330.6 3.8 collective-permute-start.42
  335.3 3.3 collective-permute-done.30
  340.3 4.5 collective-permute-start.33
  345.9 7.5 %collective-permute-done.33 = bf16[128,2048]{0,1:T(8,128)(2,1)S(1)} collective-permute-done((bf16[128,2048]{0,1:T(8,128)(2,1)S(1)}, bf16[128,2048]{0,1:T(8,128)(2,1)S(1)}, u32[]{:S(2)}, u32[]{:S(2)}) %collective-permute-start.33) | collective-permute-done | bytes 524320 | tf_op jit(solution)/shard_map/ppermute | solution.py:99
  354.7 3.3 convolution_convert_fusion
  361.7 3.4 all-to-all-start.1
  366.6 5.4 all-to-all-done.1
  372.7 6.1 attend_back.1
  379.8 4.4 convolution_convert_fusion.4
  386.0 7.6 %fusion.5 = bf16[2048,3168]{0,1:T(8,128)(2,1)} fusion(bf16[1024,2048]{0,1:T(8,128)(2,1)} %concatenate.96, bf16[1024,704]{0,1:T(8,128)(2,1)} %get-tuple-element.111), kind=kOutput, calls=%fused_computation.27 | convolution fusion | flops 2954231808 | bytes 8519680 | tf_op jit(solution)/shard_map/dot_general | solution.py:114
  393.7 4.7 fusion.4
  398.4 4.7 fusion.3
  413.1 12.8 %all_to_all.29 = bf16[8,128,384]{1,2,0:T(8,128)(2,1)S(1)} all-to-all(bf16[8,128,384]{1,2,0:T(8,128)(2,1)S(1)} %copy.213), channel_id=1, replica_groups=mesh['fsdp'=8,'ctx'=8,'tp'=2] {'ctx'}, dimensions={0} | all-to-all | bytes 1572864 | tf_op jit(solution)/shard_map/all_to_all | solution.py:374
  426.9 9.9 %convolution_convert_fusion.9 = bf16[128,2048]{0,1:T(8,128)(2,1)S(1)} fusion(bf16[128,3072]{0,1:T(8,128)(2,1)} %bitcast.179, bf16[2048,3072]{0,1:T(8,128)(2,1)} %bitcast.169), kind=kOutput, calls=%fused_computation.61 | convolution fusion | flops 1610874880 | bytes 13893632 | tf_op jit(solution)/shard_map/dot_general | solution.py:376
  436.9 3.7 collective-permute-start.43
  441.6 6.8 %collective-permute-done.43 = bf16[128,2048]{0,1:T(8,128)(2,1)S(1)} collective-permute-done((bf16[128,2048]{0,1:T(8,128)(2,1)S(1)}, bf16[128,2048]{0,1:T(8,128)(2,1)S(1)}, u32[]{:S(2)}, u32[]{:S(2)}) %collective-permute-start.43) | collective-permute-done | bytes 524320 | tf_op jit(solution)/shard_map/ppermute | solution.py:99
  454.1 3.8 collective-permute-done.44
  464.9 3.3 collective-permute-start.51
  470.7 3.4 collective-permute-done.49
  481.6 3.7 collective-permute-done.52
  487.3 3.3 collective-permute-start.55
  499.3 3.9 collective-permute-done.59
  515.3 3.5 copy.224
  521.4 5.5 broadcast_in_dim.137
  528.2 17.5 %collective-permute-done.61 = bf16[256,3168]{0,1:T(8,128)(2,1)S(1)} collective-permute-done((bf16[256,3168]{0,1:T(8,128)(2,1)}, bf16[256,3168]{0,1:T(8,128)(2,1)S(1)}, u32[]{:S(2)}, u32[]{:S(2)}) %collective-permute-start.61) | collective-permute-done | bytes 1622048 | tf_op jit(solution)/shard_map/ppermute | solution.py:48
  557.7 10.3 %collective-permute-done.63 = bf16[128,3168]{0,1:T(8,128)(2,1)S(1)} collective-permute-done((bf16[128,3168]{0,1:T(8,128)(2,1)S(1)}, bf16[128,3168]{0,1:T(8,128)(2,1)S(1)}, u32[]{:S(2)}, u32[]{:S(2)}) %collective-permute-start.63) | collective-permute-done | bytes 811040 | tf_op jit(solution)/shard_map/ppermute | solution.py:48
  574.7 23.8 %collective-permute-done.66 = bf16[256,3168]{0,1:T(8,128)(2,1)S(1)} collective-permute-done((bf16[256,3168]{0,1:T(8,128)(2,1)}, bf16[256,3168]{0,1:T(8,128)(2,1)S(1)}, u32[]{:S(2)}, u32[]{:S(2)}) %collective-permute-start.66) | collective-permute-done | bytes 1622048 | tf_op jit(solution)/shard_map/ppermute | solution.py:48
  602.4 6.5 convert_bitcast_fusion.2
  619.3 9.7 %copy.227 = f32[256,2,2816]{2,1,0:T(2,128)} copy(f32[256,2,2816]{0,2,1:T(8,128)} %bitcast.168) | data formatting | bytes 11534336
  631.3 8.5 %convert_bitcast_fusion = f32[256,8,2,704]{0,3,2,1:T(8,128)} fusion(bf16[8,256,2,704]{1,3,2,0:T(8,128)(2,1)} %bitcast.167), kind=kLoop, calls=%fused_computation.6 | loop fusion | flops 2883584 | bytes 17301504 | tf_op jit(solution)/shard_map/transpose | solution.py:413
  (421 shorter events, 239.2 us)
Async XLA Ops:
  7.2 63.0 %all-gather.5.cloned.1.call-start = ((), (), s32[]{:S(2)}) async-start(), calls=%async_computation.6 | async-start | bytes 2359296 | tf_op jit(solution)/shard_map/all_gather | solution.py:259
  13.2 84.6 %all-gather.7.cloned.1.call-start = ((), (), s32[]{:S(2)}) async-start(), calls=%async_computation.7 | async-start | bytes 4718592 | tf_op jit(solution)/shard_map/all_gather | solution.py:267
  14.0 175.5 %all-gather.9.cloned.1.call-start = ((), (), s32[]{:S(2)}) async-start(), calls=%async_computation.8 | async-start | bytes 14598144 | tf_op jit(solution)/shard_map/all_gather | solution.py:273
  20.0 14.9 %collective-permute-start = (bf16[128,2048]{1,0:T(8,128)(2,1)S(1)}, bf16[128,2048]{1,0:T(8,128)(2,1)S(1)}, u32[]{:S(2)}, u32[]{:S(2)}) collective-permute-start(bf16[128,2048]{1,0:T(8,128)(2,1)S(1)} %copy-done.23), channel_id=1, source_target_pairs={{0,4},{2,6},{4,8},{6,10},{8,12},{10,14},{12,0},{14,2},{1,5},{3,7},... | collective-permute-start | bytes 1572872 | tf_op jit(solution)/shard_map/ppermute | solution.py:48
  21.7 13.8 %collective-permute-start.1 = (bf16[128,2048]{1,0:T(8,128)(2,1)S(1)}, bf16[128,2048]{1,0:T(8,128)(2,1)}, u32[]{:S(2)}, u32[]{:S(2)}) collective-permute-start(bf16[128,2048]{1,0:T(8,128)(2,1)S(1)} %copy-done.23), channel_id=1, source_target_pairs={{0,12},{2,14},{4,0},{6,2},{8,4},{10,6},{12,8},{14,10},{1,13},{3,15... | collective-permute-start | bytes 1572872 | tf_op jit(solution)/shard_map/ppermute | solution.py:52
  23.3 15.9 %collective-permute-start.4 = (bf16[128,2048]{1,0:T(8,128)(2,1)S(1)}, bf16[128,2048]{1,0:T(8,128)(2,1)}, u32[]{:S(2)}, u32[]{:S(2)}) collective-permute-start(bf16[128,2048]{1,0:T(8,128)(2,1)S(1)} %copy-done.23), channel_id=1, source_target_pairs={{0,2},{2,0},{4,6},{6,4},{8,10},{10,8},{12,14},{14,12},{1,3},{3,1},... | collective-permute-start | bytes 1572872 | tf_op jit(solution)/shard_map/ppermute | solution.py:56
  34.9 10.0 %collective-permute-start.2 = (bf16[64,2048]{1,0:T(8,128)(2,1)S(1)}, bf16[64,2048]{1,0:T(8,128)(2,1)S(1)}, u32[]{:S(2)}, u32[]{:S(2)}) collective-permute-start(bf16[64,2048]{1,0:T(8,128)(2,1)S(1)} %slice.338), channel_id=1, source_target_pairs={{0,4},{2,6},{4,8},{6,10},{8,12},{10,14},{12,0},{14,2},{1,5},{3,7},... | collective-permute-start | bytes 786440 | tf_op jit(solution)/shard_map/ppermute | solution.py:48
  36.4 9.6 %collective-permute-start.3 = (bf16[64,2048]{1,0:T(8,128)(2,1)S(1)}, bf16[64,2048]{1,0:T(8,128)(2,1)S(1)}, u32[]{:S(2)}, u32[]{:S(2)}) collective-permute-start(bf16[64,2048]{1,0:T(8,128)(2,1)S(1)} %slice.339), channel_id=1, source_target_pairs={{0,12},{2,14},{4,0},{6,2},{8,4},{10,6},{12,8},{14,10},{1,13},{3,15... | collective-permute-start | bytes 786440 | tf_op jit(solution)/shard_map/ppermute | solution.py:52
  39.3 21.5 %collective-permute-start.5 = (bf16[128,2048]{1,0:T(8,128)(2,1)}, bf16[128,2048]{1,0:T(8,128)(2,1)S(1)}, u32[]{:S(2)}, u32[]{:S(2)}) collective-permute-start(bf16[128,2048]{1,0:T(8,128)(2,1)} %collective-permute-done.4), channel_id=1, source_target_pairs={{0,4},{2,6},{4,8},{6,10},{8,12},{10,14},{12,0},{14,2},{1,5},{3,7},... | collective-permute-start | bytes 1572872 | tf_op jit(solution)/shard_map/ppermute | solution.py:48
  39.3 21.5 %collective-permute-start.6 = (bf16[128,2048]{1,0:T(8,128)(2,1)}, bf16[128,2048]{1,0:T(8,128)(2,1)S(1)}, u32[]{:S(2)}, u32[]{:S(2)}) collective-permute-start(bf16[128,2048]{1,0:T(8,128)(2,1)} %collective-permute-done.4), channel_id=1, source_target_pairs={{0,12},{2,14},{4,0},{6,2},{8,4},{10,6},{12,8},{14,10},{1,13},{3,15... | collective-permute-start | bytes 1572872 | tf_op jit(solution)/shard_map/ppermute | solution.py:52
  46.0 21.1 %collective-permute-start.7 = (bf16[128,2048]{1,0:T(8,128)(2,1)S(1)}, bf16[128,2048]{1,0:T(8,128)(2,1)S(1)}, u32[]{:S(2)}, u32[]{:S(2)}) collective-permute-start(bf16[128,2048]{1,0:T(8,128)(2,1)S(1)} %constant_dynamic-update-slice_fusion), channel_id=1, source_target_pairs={{0,2},{2,0},{4,6},{6,4},{8,10},{10,8},{12,14},{14,12},{1,3},{3,1},... | collective-permute-start | bytes 1572872 | tf_op jit(solution)/shard_map/ppermute | solution.py:56
  84.9 12.9 %all-to-all-start = ((bf16[8,128,128]{1,2,0:T(8,128)(2,1)}), bf16[8,128,128]{1,2,0:T(8,128)(2,1)S(1)}, u32[]{:S(2)}, u32[]{:S(2)}) async-start(bf16[8,128,128]{1,2,0:T(8,128)(2,1)} %copy.190), calls=%async_computation | async-start | bytes 524288 | tf_op jit(solution)/shard_map/all_to_all | solution.py:299
  90.9 336.0 %all-gather.11.cloned.1.call-start = ((), (), s32[]{:S(2)}) async-start(), calls=%async_computation.9 | async-start | bytes 14155776 | tf_op jit(solution)/shard_map/all_gather | solution.py:289
  101.5 15.4 %collective-permute-start.8 = (bf16[128,2048]{0,1:T(8,128)(2,1)S(1)}, bf16[128,2048]{0,1:T(8,128)(2,1)}, u32[]{:S(2)}, u32[]{:S(2)}) collective-permute-start(bf16[128,2048]{0,1:T(8,128)(2,1)S(1)} %convolution_convert_fusion.8), channel_id=1, source_target_pairs={{0,1},{1,0},{2,3},{3,2},{4,5},{5,4},{6,7},{7,6},{8,9},{9,8},{10,11... | collective-permute-start | bytes 1572872 | tf_op jit(solution)/shard_map/ppermute | solution.py:99
  104.5 18.2 %collective-permute-start.17 = (bf16[128,2176]{0,1:T(8,128)(2,1)S(1)}, bf16[128,2176]{0,1:T(8,128)(2,1)}, u32[]{:S(2)}, u32[]{:S(2)}) collective-permute-start(bf16[128,2176]{0,1:T(8,128)(2,1)S(1)} %fusion.78), channel_id=1, source_target_pairs={{0,4},{2,6},{4,8},{6,10},{8,12},{10,14},{12,0},{14,2},{1,5},{3,7},... | collective-permute-start | bytes 1671176 | tf_op jit(solution)/shard_map/ppermute | solution.py:48
  104.9 19.8 %collective-permute-start.18 = (bf16[128,2176]{0,1:T(8,128)(2,1)S(1)}, bf16[128,2176]{0,1:T(8,128)(2,1)}, u32[]{:S(2)}, u32[]{:S(2)}) collective-permute-start(bf16[128,2176]{0,1:T(8,128)(2,1)S(1)} %fusion.78), channel_id=1, source_target_pairs={{0,12},{2,14},{4,0},{6,2},{8,4},{10,6},{12,8},{14,10},{1,13},{3,15... | collective-permute-start | bytes 1671176 | tf_op jit(solution)/shard_map/ppermute | solution.py:52
  107.8 24.2 %collective-permute-start.21 = (bf16[128,2176]{0,1:T(8,128)(2,1)S(1)}, bf16[128,2176]{0,1:T(8,128)(2,1)}, u32[]{:S(2)}, u32[]{:S(2)}) collective-permute-start(bf16[128,2176]{0,1:T(8,128)(2,1)S(1)} %fusion.78), channel_id=1, source_target_pairs={{0,2},{2,0},{4,6},{6,4},{8,10},{10,8},{12,14},{14,12},{1,3},{3,1},... | collective-permute-start | bytes 1671176 | tf_op jit(solution)/shard_map/ppermute | solution.py:56
  119.5 24.9 %collective-permute-start.9 = (bf16[128,2048]{0,1:T(8,128)(2,1)}, bf16[128,2048]{0,1:T(8,128)(2,1)}, u32[]{:S(2)}, u32[]{:S(2)}) collective-permute-start(bf16[128,2048]{0,1:T(8,128)(2,1)} %multiply_convert_fusion.8), channel_id=1, source_target_pairs={{0,4},{2,6},{4,8},{6,10},{8,12},{10,14},{12,0},{14,2},{1,5},{3,7},... | collective-permute-start | bytes 1572872 | tf_op jit(solution)/shard_map/ppermute | solution.py:48
  119.9 24.6 %collective-permute-start.10 = (bf16[128,2048]{0,1:T(8,128)(2,1)}, bf16[128,2048]{0,1:T(8,128)(2,1)}, u32[]{:S(2)}, u32[]{:S(2)}) collective-permute-start(bf16[128,2048]{0,1:T(8,128)(2,1)} %multiply_convert_fusion.8), channel_id=1, source_target_pairs={{0,12},{2,14},{4,0},{6,2},{8,4},{10,6},{12,8},{14,10},{1,13},{3,15... | collective-permute-start | bytes 1572872 | tf_op jit(solution)/shard_map/ppermute | solution.py:52
  124.7 13.2 %collective-permute-start.19 = (bf16[64,2176]{1,0:T(8,128)(2,1)}, bf16[64,2176]{1,0:T(8,128)(2,1)S(1)}, u32[]{:S(2)}, u32[]{:S(2)}) collective-permute-start(bf16[64,2176]{1,0:T(8,128)(2,1)} %copy.195), channel_id=1, source_target_pairs={{0,4},{2,6},{4,8},{6,10},{8,12},{10,14},{12,0},{14,2},{1,5},{3,7},... | collective-permute-start | bytes 835592 | tf_op jit(solution)/shard_map/ppermute | solution.py:48
  128.8 10.7 %collective-permute-start.20 = (bf16[64,2176]{1,0:T(8,128)(2,1)}, bf16[64,2176]{1,0:T(8,128)(2,1)}, u32[]{:S(2)}, u32[]{:S(2)}) collective-permute-start(bf16[64,2176]{1,0:T(8,128)(2,1)} %copy.196), channel_id=1, source_target_pairs={{0,12},{2,14},{4,0},{6,2},{8,4},{10,6},{12,8},{14,10},{1,13},{3,15... | collective-permute-start | bytes 835592 | tf_op jit(solution)/shard_map/ppermute | solution.py:52
  132.0 18.1 %collective-permute-start.13 = (bf16[128,2048]{0,1:T(8,128)(2,1)}, bf16[128,2048]{0,1:T(8,128)(2,1)}, u32[]{:S(2)}, u32[]{:S(2)}) collective-permute-start(bf16[128,2048]{0,1:T(8,128)(2,1)} %multiply_convert_fusion.8), channel_id=1, source_target_pairs={{0,2},{2,0},{4,6},{6,4},{8,10},{10,8},{12,14},{14,12},{1,3},{3,1},... | collective-permute-start | bytes 1572872 | tf_op jit(solution)/shard_map/ppermute | solution.py:56
  137.9 28.5 %collective-permute-start.22 = (bf16[128,2176]{0,1:T(8,128)(2,1)}, bf16[128,2176]{0,1:T(8,128)(2,1)}, u32[]{:S(2)}, u32[]{:S(2)}) collective-permute-start(bf16[128,2176]{0,1:T(8,128)(2,1)} %collective-permute-done.21), channel_id=1, source_target_pairs={{0,4},{2,6},{4,8},{6,10},{8,12},{10,14},{12,0},{14,2},{1,5},{3,7},... | collective-permute-start | bytes 1671176 | tf_op jit(solution)/shard_map/ppermute | solution.py:48
  139.5 28.6 %collective-permute-start.23 = (bf16[128,2176]{0,1:T(8,128)(2,1)}, bf16[128,2176]{0,1:T(8,128)(2,1)}, u32[]{:S(2)}, u32[]{:S(2)}) collective-permute-start(bf16[128,2176]{0,1:T(8,128)(2,1)} %collective-permute-done.21), channel_id=1, source_target_pairs={{0,12},{2,14},{4,0},{6,2},{8,4},{10,6},{12,8},{14,10},{1,13},{3,15... | collective-permute-start | bytes 1671176 | tf_op jit(solution)/shard_map/ppermute | solution.py:52
  144.4 17.4 %collective-permute-start.11 = (bf16[64,2048]{0,1:T(8,128)(2,1)}, bf16[64,2048]{0,1:T(8,128)(2,1)S(1)}, u32[]{:S(2)}, u32[]{:S(2)}) collective-permute-start(bf16[64,2048]{0,1:T(8,128)(2,1)} %bitcast.164), channel_id=1, source_target_pairs={{0,4},{2,6},{4,8},{6,10},{8,12},{10,14},{12,0},{14,2},{1,5},{3,7},... | collective-permute-start | bytes 786440 | tf_op jit(solution)/shard_map/ppermute | solution.py:48
  145.8 16.1 %collective-permute-start.12 = (bf16[64,2048]{0,1:T(8,128)(2,1)S(1)}, bf16[64,2048]{0,1:T(8,128)(2,1)S(1)}, u32[]{:S(2)}, u32[]{:S(2)}) collective-permute-start(bf16[64,2048]{0,1:T(8,128)(2,1)S(1)} %slice.347), channel_id=1, source_target_pairs={{0,12},{2,14},{4,0},{6,2},{8,4},{10,6},{12,8},{14,10},{1,13},{3,15... | collective-permute-start | bytes 786440 | tf_op jit(solution)/shard_map/ppermute | solution.py:52
  150.2 17.8 %collective-permute-start.24 = (bf16[128,2176]{0,1:T(8,128)(2,1)}, bf16[128,2176]{0,1:T(8,128)(2,1)}, u32[]{:S(2)}, u32[]{:S(2)}) collective-permute-start(bf16[128,2176]{0,1:T(8,128)(2,1)} %pad_maximum_fusion.3), channel_id=1, source_target_pairs={{0,2},{2,0},{4,6},{6,4},{8,10},{10,8},{12,14},{14,12},{1,3},{3,1},... | collective-permute-start | bytes 1671176 | tf_op jit(solution)/shard_map/ppermute | solution.py:56
  161.9 13.9 %collective-permute-start.14 = (bf16[128,2048]{0,1:T(8,128)(2,1)}, bf16[128,2048]{0,1:T(8,128)(2,1)}, u32[]{:S(2)}, u32[]{:S(2)}) collective-permute-start(bf16[128,2048]{0,1:T(8,128)(2,1)} %collective-permute-done.13), channel_id=1, source_target_pairs={{0,4},{2,6},{4,8},{6,10},{8,12},{10,14},{12,0},{14,2},{1,5},{3,7},... | collective-permute-start | bytes 1572872 | tf_op jit(solution)/shard_map/ppermute | solution.py:48
  161.9 13.9 %collective-permute-start.15 = (bf16[128,2048]{0,1:T(8,128)(2,1)}, bf16[128,2048]{0,1:T(8,128)(2,1)}, u32[]{:S(2)}, u32[]{:S(2)}) collective-permute-start(bf16[128,2048]{0,1:T(8,128)(2,1)} %collective-permute-done.13), channel_id=1, source_target_pairs={{0,12},{2,14},{4,0},{6,2},{8,4},{10,6},{12,8},{14,10},{1,13},{3,15... | collective-permute-start | bytes 1572872 | tf_op jit(solution)/shard_map/ppermute | solution.py:52
  167.5 281.3 %reduce-scatter.6.cloned.1.call-start = ((), (), s32[]{:S(2)}) async-start(), calls=%async_computation.11 | async-start | bytes 4718592 | tf_op jit(solution)/shard_map/reduce_scatter | solution.py:388
  227.7 48.0 %collective-permute-start.26 = (bf16[128,2048]{0,1:T(8,128)(2,1)}, bf16[128,2048]{0,1:T(8,128)(2,1)}, u32[]{:S(2)}, u32[]{:S(2)}) collective-permute-start(bf16[128,2048]{0,1:T(8,128)(2,1)} %get-tuple-element.127), channel_id=1, source_target_pairs={{0,12},{2,14},{4,0},{6,2},{8,4},{10,6},{12,8},{14,10},{1,13},{3,15... | collective-permute-start | bytes 1572872 | tf_op jit(solution)/shard_map/ppermute | solution.py:52
  227.8 51.4 %collective-permute-start.25 = (bf16[128,2048]{0,1:T(8,128)(2,1)}, bf16[128,2048]{0,1:T(8,128)(2,1)}, u32[]{:S(2)}, u32[]{:S(2)}) collective-permute-start(bf16[128,2048]{0,1:T(8,128)(2,1)} %get-tuple-element.125), channel_id=1, source_target_pairs={{0,4},{2,6},{4,8},{6,10},{8,12},{10,14},{12,0},{14,2},{1,5},{3,7},... | collective-permute-start | bytes 1572872 | tf_op jit(solution)/shard_map/ppermute | solution.py:48
  229.7 49.4 %collective-permute-start.28 = (bf16[128,2048]{0,1:T(8,128)(2,1)}, bf16[128,2048]{0,1:T(8,128)(2,1)}, u32[]{:S(2)}, u32[]{:S(2)}) collective-permute-start(bf16[128,2048]{0,1:T(8,128)(2,1)} %get-tuple-element.126), channel_id=1, source_target_pairs={{0,2},{2,0},{4,6},{6,4},{8,10},{10,8},{12,14},{14,12},{1,3},{3,1},... | collective-permute-start | bytes 1572872 | tf_op jit(solution)/shard_map/ppermute | solution.py:56
  273.7 12.2 %collective-permute-start.35 = (bf16[128,2176]{0,1:T(8,128)(2,1)S(1)}, bf16[128,2176]{0,1:T(8,128)(2,1)S(1)}, u32[]{:S(2)}, u32[]{:S(2)}) collective-permute-start(bf16[128,2176]{0,1:T(8,128)(2,1)S(1)} %get-tuple-element.120), channel_id=1, source_target_pairs={{0,12},{2,14},{4,0},{6,2},{8,4},{10,6},{12,8},{14,10},{1,13},{3,15... | collective-permute-start | bytes 1671176 | tf_op jit(solution)/shard_map/ppermute | solution.py:52
  275.1 15.5 %collective-permute-start.34 = (bf16[128,2176]{0,1:T(8,128)(2,1)S(1)}, bf16[128,2176]{0,1:T(8,128)(2,1)S(1)}, u32[]{:S(2)}, u32[]{:S(2)}) collective-permute-start(bf16[128,2176]{0,1:T(8,128)(2,1)S(1)} %get-tuple-element.118), channel_id=1, source_target_pairs={{0,4},{2,6},{4,8},{6,10},{8,12},{10,14},{12,0},{14,2},{1,5},{3,7},... | collective-permute-start | bytes 1671176 | tf_op jit(solution)/shard_map/ppermute | solution.py:48
  275.7 14.8 %collective-permute-start.37 = (bf16[128,2176]{0,1:T(8,128)(2,1)S(1)}, bf16[128,2176]{0,1:T(8,128)(2,1)S(1)}, u32[]{:S(2)}, u32[]{:S(2)}) collective-permute-start(bf16[128,2176]{0,1:T(8,128)(2,1)S(1)} %get-tuple-element.119), channel_id=1, source_target_pairs={{0,2},{2,0},{4,6},{6,4},{8,10},{10,8},{12,14},{14,12},{1,3},{3,1},... | collective-permute-start | bytes 1671176 | tf_op jit(solution)/shard_map/ppermute | solution.py:56
  294.8 11.0 %collective-permute-start.38 = (bf16[64,2176]{1,0:T(8,128)(2,1)}, bf16[64,2176]{1,0:T(8,128)(2,1)S(1)}, u32[]{:S(2)}, u32[]{:S(2)}) collective-permute-start(bf16[64,2176]{1,0:T(8,128)(2,1)} %copy.207), channel_id=1, source_target_pairs={{0,4},{2,6},{4,8},{6,10},{8,12},{10,14},{12,0},{14,2},{1,5},{3,7},... | collective-permute-start | bytes 835592 | tf_op jit(solution)/shard_map/ppermute | solution.py:48
  296.1 12.4 %collective-permute-start.40 = (bf16[64,2176]{1,0:T(8,128)(2,1)S(1)}, bf16[64,2176]{1,0:T(8,128)(2,1)S(1)}, u32[]{:S(2)}, u32[]{:S(2)}) collective-permute-start(bf16[64,2176]{1,0:T(8,128)(2,1)S(1)} %copy.209), channel_id=1, source_target_pairs={{0,12},{2,14},{4,0},{6,2},{8,4},{10,6},{12,8},{14,10},{1,13},{3,15... | collective-permute-start | bytes 835592 | tf_op jit(solution)/shard_map/ppermute | solution.py:52
  301.8 16.4 %collective-permute-start.29 = (bf16[64,2048]{0,1:T(8,128)(2,1)}, bf16[64,2048]{0,1:T(8,128)(2,1)}, u32[]{:S(2)}, u32[]{:S(2)}) collective-permute-start(bf16[64,2048]{0,1:T(8,128)(2,1)} %get-tuple-element.151), channel_id=1, source_target_pairs={{0,4},{2,6},{4,8},{6,10},{8,12},{10,14},{12,0},{14,2},{1,5},{3,7},... | collective-permute-start | bytes 786440 | tf_op jit(solution)/shard_map/ppermute | solution.py:48
  301.8 16.4 %collective-permute-start.31 = (bf16[64,2048]{0,1:T(8,128)(2,1)}, bf16[64,2048]{0,1:T(8,128)(2,1)}, u32[]{:S(2)}, u32[]{:S(2)}) collective-permute-start(bf16[64,2048]{0,1:T(8,128)(2,1)} %get-tuple-element.152), channel_id=1, source_target_pairs={{0,12},{2,14},{4,0},{6,2},{8,4},{10,6},{12,8},{14,10},{1,13},{3,15... | collective-permute-start | bytes 786440 | tf_op jit(solution)/shard_map/ppermute | solution.py:52
  305.1 30.3 %collective-permute-start.27 = (bf16[128,2048]{0,1:T(8,128)(2,1)}, bf16[128,2048]{0,1:T(8,128)(2,1)}, u32[]{:S(2)}, u32[]{:S(2)}) collective-permute-start(bf16[128,2048]{0,1:T(8,128)(2,1)} %get-tuple-element.112), channel_id=1, source_target_pairs={{0,2},{2,0},{4,6},{6,4},{8,10},{10,8},{12,14},{14,12},{1,3},{3,1},... | collective-permute-start | bytes 1572872 | tf_op jit(solution)/shard_map/ppermute | solution.py:56
  305.9 22.4 %collective-permute-start.36 = (bf16[128,2176]{0,1:T(8,128)(2,1)}, bf16[128,2176]{0,1:T(8,128)(2,1)}, u32[]{:S(2)}, u32[]{:S(2)}) collective-permute-start(bf16[128,2176]{0,1:T(8,128)(2,1)} %get-tuple-element.106), channel_id=1, source_target_pairs={{0,2},{2,0},{4,6},{6,4},{8,10},{10,8},{12,14},{14,12},{1,3},{3,1},... | collective-permute-start | bytes 1671176 | tf_op jit(solution)/shard_map/ppermute | solution.py:56
  312.3 15.9 %collective-permute-start.41 = (bf16[128,2176]{0,1:T(8,128)(2,1)S(1)}, bf16[128,2176]{0,1:T(8,128)(2,1)S(1)}, u32[]{:S(2)}, u32[]{:S(2)}) collective-permute-start(bf16[128,2176]{0,1:T(8,128)(2,1)S(1)} %pad_maximum_fusion.5), channel_id=1, source_target_pairs={{0,12},{2,14},{4,0},{6,2},{8,4},{10,6},{12,8},{14,10},{1,13},{3,15... | collective-permute-start | bytes 1671176 | tf_op jit(solution)/shard_map/ppermute | solution.py:52
  318.2 10.7 %collective-permute-start.39 = (bf16[128,2176]{0,1:T(8,128)(2,1)S(1)}, bf16[128,2176]{0,1:T(8,128)(2,1)S(1)}, u32[]{:S(2)}, u32[]{:S(2)}) collective-permute-start(bf16[128,2176]{0,1:T(8,128)(2,1)S(1)} %pad_maximum_fusion.4), channel_id=1, source_target_pairs={{0,4},{2,6},{4,8},{6,10},{8,12},{10,14},{12,0},{14,2},{1,5},{3,7},... | collective-permute-start | bytes 1671176 | tf_op jit(solution)/shard_map/ppermute | solution.py:48
  320.8 14.5 %collective-permute-start.32 = (bf16[128,2048]{0,1:T(8,128)(2,1)S(1)}, bf16[128,2048]{0,1:T(8,128)(2,1)S(1)}, u32[]{:S(2)}, u32[]{:S(2)}) collective-permute-start(bf16[128,2048]{0,1:T(8,128)(2,1)S(1)} %pad_maximum_fusion.10), channel_id=1, source_target_pairs={{0,12},{2,14},{4,0},{6,2},{8,4},{10,6},{12,8},{14,10},{1,13},{3,15... | collective-permute-start | bytes 1572872 | tf_op jit(solution)/shard_map/ppermute | solution.py:52
  328.2 10.4 %collective-permute-start.30 = (bf16[128,2048]{0,1:T(8,128)(2,1)S(1)}, bf16[128,2048]{0,1:T(8,128)(2,1)S(1)}, u32[]{:S(2)}, u32[]{:S(2)}) collective-permute-start(bf16[128,2048]{0,1:T(8,128)(2,1)S(1)} %pad_maximum_fusion.9), channel_id=1, source_target_pairs={{0,4},{2,6},{4,8},{6,10},{8,12},{10,14},{12,0},{14,2},{1,5},{3,7},... | collective-permute-start | bytes 1572872 | tf_op jit(solution)/shard_map/ppermute | solution.py:48
  330.6 14.2 %collective-permute-start.42 = (bf16[128,2176]{0,1:T(8,128)(2,1)S(1)}, bf16[128,2176]{0,1:T(8,128)(2,1)S(1)}, u32[]{:S(2)}, u32[]{:S(2)}) collective-permute-start(bf16[128,2176]{0,1:T(8,128)(2,1)S(1)} %fusion.60), channel_id=1, source_target_pairs={{0,1},{1,0},{2,3},{3,2},{4,5},{5,4},{6,7},{7,6},{8,9},{9,8},{10,11... | collective-permute-start | bytes 1671176 | tf_op jit(solution)/shard_map/ppermute | solution.py:99
  340.3 13.1 %collective-permute-start.33 = (bf16[128,2048]{0,1:T(8,128)(2,1)S(1)}, bf16[128,2048]{0,1:T(8,128)(2,1)S(1)}, u32[]{:S(2)}, u32[]{:S(2)}) collective-permute-start(bf16[128,2048]{0,1:T(8,128)(2,1)S(1)} %fusion.77), channel_id=1, source_target_pairs={{0,1},{1,0},{2,3},{3,2},{4,5},{5,4},{6,7},{7,6},{8,9},{9,8},{10,11... | collective-permute-start | bytes 1572872 | tf_op jit(solution)/shard_map/ppermute | solution.py:99
  361.7 10.3 %all-to-all-start.1 = ((bf16[8,128,128]{2,1,0:T(8,128)(2,1)}), bf16[8,128,128]{2,1,0:T(8,128)(2,1)S(1)}, u32[]{:S(2)}, u32[]{:S(2)}) async-start(bf16[8,128,128]{2,1,0:T(8,128)(2,1)} %bitcast.162), calls=%async_computation.1 | async-start | bytes 524288 | tf_op jit(solution)/shard_map/all_to_all | solution.py:370
  365.1 109.9 %reduce-scatter.4.cloned.1.call-start = ((), (), s32[]{:S(2)}) async-start(), calls=%async_computation.10 | async-start | bytes 2359296 | tf_op jit(solution)/shard_map/reduce_scatter | solution.py:402
  385.7 123.9 %reduce-scatter.8.cloned.1.call-start = ((), (), s32[]{:S(2)}) async-start(), calls=%async_computation.12 | async-start | bytes 14598144 | tf_op jit(solution)/shard_map/reduce_scatter | solution.py:341
  436.9 11.6 %collective-permute-start.43 = (bf16[128,2048]{0,1:T(8,128)(2,1)S(1)}, bf16[128,2048]{0,1:T(8,128)(2,1)S(1)}, u32[]{:S(2)}, u32[]{:S(2)}) collective-permute-start(bf16[128,2048]{0,1:T(8,128)(2,1)S(1)} %convolution_convert_fusion.9), channel_id=1, source_target_pairs={{0,1},{1,0},{2,3},{3,2},{4,5},{5,4},{6,7},{7,6},{8,9},{9,8},{10,11... | collective-permute-start | bytes 1572872 | tf_op jit(solution)/shard_map/ppermute | solution.py:99
  476.8 9.6 %collective-permute-start.53 = (bf16[256,640]{0,1:T(8,128)(2,1)}, bf16[256,640]{0,1:T(8,128)(2,1)}, u32[]{:S(2)}, u32[]{:S(2)}) collective-permute-start(bf16[256,640]{0,1:T(8,128)(2,1)} %pad_maximum_fusion.11), channel_id=1, source_target_pairs={{0,12},{2,14},{4,0},{6,2},{8,4},{10,6},{12,8},{14,10},{1,13},{3,15... | collective-permute-start | bytes 983048 | tf_op jit(solution)/shard_map/ppermute | solution.py:52
  480.0 10.6 %collective-permute-start.56 = (bf16[256,640]{0,1:T(8,128)(2,1)}, bf16[256,640]{0,1:T(8,128)(2,1)}, u32[]{:S(2)}, u32[]{:S(2)}) collective-permute-start(bf16[256,640]{0,1:T(8,128)(2,1)} %pad_maximum_fusion.11), channel_id=1, source_target_pairs={{0,2},{2,0},{4,6},{6,4},{8,10},{10,8},{12,14},{14,12},{1,3},{3,1},... | collective-permute-start | bytes 983048 | tf_op jit(solution)/shard_map/ppermute | solution.py:56
  486.3 9.7 %collective-permute-start.54 = (bf16[128,640]{0,1:T(8,128)(2,1)S(1)}, bf16[128,640]{0,1:T(8,128)(2,1)S(1)}, u32[]{:S(2)}, u32[]{:S(2)}) collective-permute-start(bf16[128,640]{0,1:T(8,128)(2,1)S(1)} %slice.394), channel_id=1, source_target_pairs={{0,4},{2,6},{4,8},{6,10},{8,12},{10,14},{12,0},{14,2},{1,5},{3,7},... | collective-permute-start | bytes 491528 | tf_op jit(solution)/shard_map/ppermute | solution.py:48
  505.8 15.0 %collective-permute-start.60 = (f32[256]{0:T(256)S(1)}, f32[256]{0:T(256)S(1)}, u32[]{:S(2)}, u32[]{:S(2)}) collective-permute-start(f32[256]{0:T(256)S(1)} %multiply_reduce_fusion.1), channel_id=1, source_target_pairs={{0,1},{1,0},{2,3},{3,2},{4,5},{5,4},{6,7},{7,6},{8,9},{9,8},{10,11... | collective-permute-start | bytes 3080 | tf_op jit(solution)/shard_map/ppermute | solution.py:442
  509.6 36.1 %collective-permute-start.61 = (bf16[256,3168]{0,1:T(8,128)(2,1)}, bf16[256,3168]{0,1:T(8,128)(2,1)S(1)}, u32[]{:S(2)}, u32[]{:S(2)}) collective-permute-start(bf16[256,3168]{0,1:T(8,128)(2,1)} %reduce-scatter.8.cloned.1.call-done), channel_id=1, source_target_pairs={{0,4},{2,6},{4,8},{6,10},{8,12},{10,14},{12,0},{14,2},{1,5},{3,7},... | collective-permute-start | bytes 4866056 | tf_op jit(solution)/shard_map/ppermute | solution.py:48
  509.6 36.5 %collective-permute-start.62 = (bf16[256,3168]{0,1:T(8,128)(2,1)}, bf16[256,3168]{0,1:T(8,128)(2,1)}, u32[]{:S(2)}, u32[]{:S(2)}) collective-permute-start(bf16[256,3168]{0,1:T(8,128)(2,1)} %reduce-scatter.8.cloned.1.call-done), channel_id=1, source_target_pairs={{0,12},{2,14},{4,0},{6,2},{8,4},{10,6},{12,8},{14,10},{1,13},{3,15... | collective-permute-start | bytes 4866056 | tf_op jit(solution)/shard_map/ppermute | solution.py:52
  512.9 37.5 %collective-permute-start.65 = (bf16[256,3168]{0,1:T(8,128)(2,1)}, bf16[256,3168]{0,1:T(8,128)(2,1)}, u32[]{:S(2)}, u32[]{:S(2)}) collective-permute-start(bf16[256,3168]{0,1:T(8,128)(2,1)} %reduce-scatter.8.cloned.1.call-done), channel_id=1, source_target_pairs={{0,2},{2,0},{4,6},{6,4},{8,10},{10,8},{12,14},{14,12},{1,3},{3,1},... | collective-permute-start | bytes 4866056 | tf_op jit(solution)/shard_map/ppermute | solution.py:56
  545.8 22.3 %collective-permute-start.63 = (bf16[128,3168]{0,1:T(8,128)(2,1)S(1)}, bf16[128,3168]{0,1:T(8,128)(2,1)S(1)}, u32[]{:S(2)}, u32[]{:S(2)}) collective-permute-start(bf16[128,3168]{0,1:T(8,128)(2,1)S(1)} %slice.404), channel_id=1, source_target_pairs={{0,4},{2,6},{4,8},{6,10},{8,12},{10,14},{12,0},{14,2},{1,5},{3,7},... | collective-permute-start | bytes 2433032 | tf_op jit(solution)/shard_map/ppermute | solution.py:48
  547.3 21.6 %collective-permute-start.64 = (bf16[128,3168]{0,1:T(8,128)(2,1)S(1)}, bf16[128,3168]{0,1:T(8,128)(2,1)S(1)}, u32[]{:S(2)}, u32[]{:S(2)}) collective-permute-start(bf16[128,3168]{0,1:T(8,128)(2,1)S(1)} %slice.405), channel_id=1, source_target_pairs={{0,12},{2,14},{4,0},{6,2},{8,4},{10,6},{12,8},{14,10},{1,13},{3,15... | collective-permute-start | bytes 2433032 | tf_op jit(solution)/shard_map/ppermute | solution.py:52
  550.3 48.1 %collective-permute-start.66 = (bf16[256,3168]{0,1:T(8,128)(2,1)}, bf16[256,3168]{0,1:T(8,128)(2,1)S(1)}, u32[]{:S(2)}, u32[]{:S(2)}) collective-permute-start(bf16[256,3168]{0,1:T(8,128)(2,1)} %collective-permute-done.65), channel_id=1, source_target_pairs={{0,4},{2,6},{4,8},{6,10},{8,12},{10,14},{12,0},{14,2},{1,5},{3,7},... | collective-permute-start | bytes 4866056 | tf_op jit(solution)/shard_map/ppermute | solution.py:48
  550.4 49.5 %collective-permute-start.67 = (bf16[256,3168]{0,1:T(8,128)(2,1)}, bf16[256,3168]{0,1:T(8,128)(2,1)S(1)}, u32[]{:S(2)}, u32[]{:S(2)}) collective-permute-start(bf16[256,3168]{0,1:T(8,128)(2,1)} %collective-permute-done.65), channel_id=1, source_target_pairs={{0,12},{2,14},{4,0},{6,2},{8,4},{10,6},{12,8},{14,10},{1,13},{3,15... | collective-permute-start | bytes 4866056 | tf_op jit(solution)/shard_map/ppermute | solution.py:52
  569.1 32.1 %collective-permute-start.68 = (bf16[256,3168]{0,1:T(8,128)(2,1)S(1)}, bf16[256,3168]{0,1:T(8,128)(2,1)S(1)}, u32[]{:S(2)}, u32[]{:S(2)}) collective-permute-start(bf16[256,3168]{0,1:T(8,128)(2,1)S(1)} %constant_dynamic-update-slice_fusion.4), channel_id=1, source_target_pairs={{0,2},{2,0},{4,6},{6,4},{8,10},{10,8},{12,14},{14,12},{1,3},{3,1},... | collective-permute-start | bytes 4866056 | tf_op jit(solution)/shard_map/ppermute | solution.py:56
  (71 other events, 532.9 us)
Sparse Core Ops, SparseCore 0:
  13.3 29.9 all-gather.4
  45.0 33.1 all-gather.6
  80.5 73.7 all-gather.8
  167.7 72.2 all-gather.10
  358.1 38.7 reduce-scatter.5
  399.7 32.6 reduce-scatter.3
  434.9 72.9 reduce-scatter.7

commit v2 on v1

v2 whole, which is shorter than its diff:
```python
import jax
import jax.numpy as jnp
import numpy as np
from jax import lax
from jax.experimental import pallas as pl
from jax.experimental.pallas import tpu as pltpu
from jax.sharding import PartitionSpec as P

EPSILON = 1e-06
ROPE_BASE = 1000000.0
MASKED_SCORE = -1e30
LOW = jnp.bfloat16
WIDE = jnp.float32
VMEM_BYTES = 56 * 1024 * 1024


def low(values):
    return values.astype(LOW)


def wide(values):
    return values.astype(WIDE)


def rotary_tables(row_count, head_size):
    middle = head_size // 2
    powers = -(np.arange(middle, dtype=np.float32) * np.float32(2.0)) / np.float32(head_size)
    inverse = np.power(np.float32(ROPE_BASE), powers).astype(np.float32)
    places = np.arange(row_count, dtype=np.float32)
    angles = (places[:, None] * inverse[None, :]).astype(np.float32)
    cosine, sine = np.cos(angles), np.sin(angles)
    return (
        jnp.asarray(np.concatenate([cosine, cosine], axis=-1)),
        jnp.asarray(np.concatenate([-sine, sine], axis=-1)),
    )


def inverse_rms(values):
    return lax.rsqrt(jnp.mean(values * values, axis=-1, keepdims=True) + EPSILON)


def ring(step):
    return [(i, (i + step) % 8) for i in range(8)]


PAIR = [(i, i ^ 1) for i in range(8)]


def up(values):
    return lax.ppermute(values, "ctx", ring(2))


def down(values):
    return lax.ppermute(values, "ctx", ring(-2))


def swap(values):
    return lax.ppermute(values, "ctx", PAIR)


def relative_places():
    here = lax.axis_index("ctx")
    return [(here + step) % 8 for step in (0, 6, 2, 4)] + [
        ((here ^ 1) + step) % 8 for step in (0, 6, 2, 4)
    ]


def across(values):
    return lax.ppermute(values, "ctx", ring(4))


def gather_first(block):
    return up(block), down(block), swap(block), across(block)


def gather_second(first):
    _, _, pair, opposite = first
    return up(pair), down(pair), swap(opposite)


def gather_blocks(block, first, second):
    left, right, pair, opposite = first
    return [block, left, right, opposite, pair, *second]


def gather_relative(block):
    first = gather_first(block)
    return gather_blocks(block, first, gather_second(first))


def large_first(block):
    return up(block), down(block), swap(block)


def large_second(first):
    left, right, pair = first
    half = left.shape[0] // 2
    return up(left[:half]), down(right[half:]), up(pair), down(pair)


def large_third(second):
    _, _, pair_left, pair_right = second
    half = pair_left.shape[0] // 2
    return up(pair_left[:half]), down(pair_right[half:])


def large_blocks(block, first, second, third):
    left, right, pair = first
    opposite = jnp.concatenate(second[:2], axis=0)
    pair_opposite = jnp.concatenate(third, axis=0)
    return [block, left, right, opposite, pair, second[2], second[3], pair_opposite]


def scatter_first(blocks):
    _, _, _, _, _, pair_left, pair_right, pair_opposite = blocks
    return swap(low(pair_opposite)), up(low(pair_right)), down(low(pair_left))


def scatter_second(blocks, first):
    _, left, right, opposite, pair, _, _, _ = blocks
    from_pair, pair_up, pair_down = first
    return (
        across(low(wide(opposite) + wide(from_pair))),
        swap(low(wide(pair) + wide(pair_up) + wide(pair_down))),
        up(low(right)),
        down(low(left)),
    )


def scatter_sum(own, second):
    far, crossing, last_up, last_down = second
    return wide(own) + wide(far) + wide(crossing) + wide(last_up) + wide(last_down)


def scatter_relative(blocks):
    return scatter_sum(blocks[0], scatter_second(blocks, scatter_first(blocks)))


def add_halves(values):
    mine = low(values)
    return wide(mine) + wide(lax.ppermute(mine, "tp", [(0, 1), (1, 0)]))


QUERY_ROWS = 256


def estimate(flops, bytes_accessed):
    return pl.CostEstimate(
        flops=flops // 1000, bytes_accessed=bytes_accessed // 1000, transcendentals=0
    )


def params():
    return pltpu.CompilerParams(vmem_limit_bytes=VMEM_BYTES)


def turn(values, cosine, sine):
    return values * cosine + pltpu.roll(values, values.shape[-1] // 2, 1) * sine


def dot_plain(left, right):
    return jnp.dot(left, right, preferred_element_type=WIDE)


def dot_rows(left, right):
    return lax.dot_general(left, right, (((1,), (1,)), ((), ())), preferred_element_type=WIDE)


def dot_columns(left, right):
    return lax.dot_general(left, right, (((0,), (0,)), ((), ())), preferred_element_type=WIDE)


def probabilities(queries, keys, start, scale):
    scores = dot_rows(queries, keys) * scale
    rows = start + lax.broadcasted_iota(jnp.int32, scores.shape, 0)
    columns = lax.broadcasted_iota(jnp.int32, scores.shape, 1)
    scores = jnp.where(columns <= rows, scores, MASKED_SCORE)
    expons = jnp.exp(scores - jnp.max(scores, axis=-1, keepdims=True))
    return expons / jnp.sum(expons, axis=-1, keepdims=True)


def block_rows(place, rows):
    return pl.ds(pl.multiple_of(place * rows, rows), rows)


def attend_kernel(places_ref, *refs):
    blocks = refs[:8]
    weight_ref, gain_ref, bias_ref, cos_ref, sin_ref = refs[8:13]
    q_ref, k_ref, v_ref, out_ref, normed_ref = refs[13:]
    size = cos_ref.shape[1]
    scale = size ** (-0.5)
    gain = gain_ref[...]
    for index, block in enumerate(blocks):
        values = wide(block[...])
        normed = low(values * inverse_rms(values) * gain)
        normed_ref[block_rows(places_ref[index], block.shape[0]), :] = normed
    for start in range(0, q_ref.shape[0], QUERY_ROWS):
        end = start + QUERY_ROWS
        proj = dot_plain(normed_ref[start:end], weight_ref[:, : 3 * size]) + bias_ref[...]
        cosine, sine = cos_ref[start:end], sin_ref[start:end]
        q_ref[start:end] = low(turn(proj[:, :size], cosine, sine))
        k_ref[start:end] = low(turn(proj[:, size : 2 * size], cosine, sine))
        v_ref[start:end] = low(proj[:, 2 * size :])
    for start in range(0, q_ref.shape[0], QUERY_ROWS):
        end = start + QUERY_ROWS
        probs = low(probabilities(q_ref[start:end], k_ref[:end], start, scale))
        out_ref[start:end] = low(dot_plain(probs, v_ref[:end]))


def attend(places, blocks, pack, gain, bias, cosine, sine):
    rows, size = cosine.shape
    width = blocks[0].shape[1]
    one = jax.ShapeDtypeStruct((rows, size), LOW)
    whole = pl.BlockSpec(memory_space=pltpu.VMEM)
    part = pl.BlockSpec((width, 512), lambda step: (0, 2))
    whole_of = lambda shape: pl.BlockSpec(shape, lambda step: (0, 0))
    return pl.pallas_call(
        attend_kernel,
        grid=(1,),
        in_specs=[pl.BlockSpec(memory_space=pltpu.SMEM)]
        + [whole_of(block.shape) for block in blocks]
        + [part]
        + [whole_of(value.shape) for value in (gain, bias, cosine, sine)],
        out_specs=[whole_of((rows, size))] * 4 + [whole_of((rows, width))],
        out_shape=(one, one, one, one, jax.ShapeDtypeStruct((rows, width), LOW)),
        compiler_params=params(),
        cost_estimate=estimate(9_000_000_000, 12_000_000),
        name="attend",
    )(places, *blocks, pack, gain, bias, cosine, sine)


def attend_back_kernel(
    q_ref, k_ref, v_ref, grad_ref, cos_ref, sin_ref, out_ref, bias_ref, dk_ref, dv_ref
):
    size = cos_ref.shape[1]
    scale = size ** (-0.5)
    dk_ref[...] = jnp.zeros_like(dk_ref)
    dv_ref[...] = jnp.zeros_like(dv_ref)
    bias = jnp.zeros((1, size), WIDE)
    for start in range(0, q_ref.shape[0], QUERY_ROWS):
        end = start + QUERY_ROWS
        queries, grads = q_ref[start:end], grad_ref[start:end]
        probs = probabilities(queries, k_ref[:end], start, scale)
        grad_probs = dot_rows(grads, v_ref[:end])
        inner = jnp.sum(probs * grad_probs, axis=-1, keepdims=True)
        grad_scores = low(probs * (grad_probs - inner))
        grad_queries = dot_plain(grad_scores, k_ref[:end]) * scale
        grad_queries = low(turn(grad_queries, cos_ref[start:end], -sin_ref[start:end]))
        out_ref[start:end, :size] = grad_queries
        bias = bias + jnp.sum(wide(grad_queries), axis=0, keepdims=True)
        dk_ref[:end] += dot_columns(grad_scores, queries) * scale
        dv_ref[:end] += dot_columns(low(probs), grads)
    bias_ref[:, :size] = bias
    grad_keys = low(turn(dk_ref[...], cos_ref[...], -sin_ref[...]))
    out_ref[:, size : 2 * size] = grad_keys
    bias_ref[:, size : 2 * size] = jnp.sum(wide(grad_keys), axis=0, keepdims=True)
    grad_values = low(dv_ref[...])
    out_ref[:, 2 * size :] = grad_values
    bias_ref[:, 2 * size :] = jnp.sum(wide(grad_values), axis=0, keepdims=True)


def attend_back(queries, keys, values, grads, cosine, sine):
    rows, size = cosine.shape
    return pl.pallas_call(
        attend_back_kernel,
        out_shape=(
            jax.ShapeDtypeStruct((rows, 3 * size), LOW),
            jax.ShapeDtypeStruct((1, 3 * size), WIDE),
        ),
        scratch_shapes=[pltpu.VMEM((rows, size), WIDE), pltpu.VMEM((rows, size), WIDE)],
        compiler_params=params(),
        cost_estimate=estimate(7_000_000_000, 6_000_000),
        name="attend_back",
    )(queries, keys, values, grads, cosine, sine)


UNIT_ROWS = 16


def units_kernel(*refs):
    x_hbm, g_hbm = refs[:4], refs[4:8]
    small_ref, mine_ref, weight_hbm = refs[8:11]
    d_hbm, back_hbm, hidden_hbm = refs[11:15], refs[15], refs[16]
    weight_ref, x_ref, g_ref, tail_ref, gate_ref, up_ref, down_ref = refs[17:24]
    back_ref, hidden_ref, turned_ref, flat_ref, d_ref, sems = refs[24:]
    units, tokens = hidden_ref.shape
    rows, width = x_hbm[0].shape
    expert_units = units * 2 // 3
    count = 0
    started = {}

    def start(name, source, target):
        nonlocal count
        copy = pltpu.make_async_copy(source, target, sems.at[count])
        copy.start()
        count += 1
        started.setdefault(name, []).append(copy)

    def finish(name):
        for copy in started[name]:
            copy.wait()

    def start_weights(part):
        group = pl.ds(part * units, units)
        for index in range(8):
            columns = pl.ds(index * (width // 8), width // 8)
            start(part, weight_hbm.at[index, group, :], weight_ref.at[group, columns])

    block = lambda index: pl.ds(index * rows, rows)
    for index in range(4):
        start("x", x_hbm[index], x_ref.at[block(index)])
    start_weights(0)
    start_weights(1)
    for index in range(4):
        start("tail", g_hbm[index].at[:, pl.ds(width, 128)], tail_ref.at[block(index)])
        start("g", g_hbm[index].at[:, pl.ds(0, width)], g_ref.at[block(index)])
    start_weights(2)
    finish("x")
    logits = dot_rows(small_ref[...], x_ref[...])
    places = lax.broadcasted_iota(jnp.int32, logits.shape, 0)
    routed = jnp.where(places < 8, logits, MASKED_SCORE)
    expons = jnp.exp(routed - jnp.max(routed, axis=0, keepdims=True))
    probs = expons / jnp.sum(expons, axis=0, keepdims=True)
    shared_gate = jax.nn.sigmoid(
        jnp.sum(jnp.where(places == 8, logits, 0.0), axis=0, keepdims=True)
    )
    for part, (target, source) in enumerate(((gate_ref, x_ref), (up_ref, x_ref), (down_ref, g_ref))):
        if part == 2:
            finish("g")
        finish(part)
        target[...] = dot_rows(weight_ref[part * units : (part + 1) * units], source[...])
    finish("tail")
    chosen = wide(tail_ref[...]).T[: places.shape[0]]
    mine = mine_ref[...]
    combine = jnp.sum(probs * chosen * mine, axis=0, keepdims=True)

    def unit_rows(scale):
        def step(index, total):
            chunk = pl.ds(pl.multiple_of(index * UNIT_ROWS, UNIT_ROWS), UNIT_ROWS)
            after = pl.ds(pl.multiple_of(units + index * UNIT_ROWS, UNIT_ROWS), UNIT_ROWS)
            gate, upper, back = gate_ref[chunk, :], up_ref[chunk, :], down_ref[chunk, :]
            sigmoid = jax.nn.sigmoid(gate)
            silu = gate * sigmoid
            hidden = silu * upper
            hidden_ref[chunk, :] = low(hidden * scale)
            grad_hidden = back * scale
            back_ref[chunk, :] = low(grad_hidden * upper * (sigmoid + silu * (1.0 - sigmoid)))
            back_ref[after, :] = low(grad_hidden * silu)
            return total + hidden * back

        return step

    zeros = jnp.zeros((UNIT_ROWS, tokens), WIDE)
    middle, last = expert_units // UNIT_ROWS, units // UNIT_ROWS
    expert_sum = lax.fori_loop(0, middle, unit_rows(combine), zeros)
    shared_sum = lax.fori_loop(middle, last, unit_rows(shared_gate), zeros)
    start("out", hidden_ref, hidden_hbm)
    start("out", back_ref, back_hbm)
    expert_sum = jnp.sum(expert_sum, axis=0, keepdims=True)
    shared_sum = jnp.sum(shared_sum, axis=0, keepdims=True)
    sums = mine * expert_sum + jnp.where(places == 8, shared_sum, 0.0)
    sums = jnp.concatenate([sums, jnp.zeros((128 - sums.shape[0], tokens), WIDE)], axis=0)
    d_ref[:, width : width + 128] = low(sums.T)
    turned_ref[...] = back_ref[...].T
    step = width // 4

    def send(begin, size):
        for index in range(4):
            source = d_ref.at[block(index), pl.ds(begin, size)]
            start("out", source, d_hbm[index].at[:, pl.ds(begin, size)])

    for part in range(4):
        columns = slice(part * step, (part + 1) * step)
        d_ref[:, columns] = low(dot_plain(turned_ref[...], weight_ref[: 2 * units, columns]))
        send(part * step, step if part < 3 else step + 128)
    flat_ref[...] = hidden_ref[...].T
    for part in range(4):
        columns = slice(part * step, (part + 1) * step)
        begin = width + 128 + part * step
        d_ref[:, begin : begin + step] = low(
            dot_plain(flat_ref[...], weight_ref[2 * units :, columns])
        )
        send(begin, step)
    finish("out")


def units_forward_back(x_blocks, g_blocks, small_rows, mine, weights):
    rows, width = x_blocks[0].shape
    tokens = 4 * rows
    units = weights.shape[1] // 3
    vmem = pl.BlockSpec(memory_space=pltpu.VMEM)
    anywhere = pl.BlockSpec(memory_space=pl.ANY)
    return pl.pallas_call(
        units_kernel,
        in_specs=[anywhere] * 8 + [vmem] * 2 + [anywhere],
        out_specs=[anywhere] * 6,
        out_shape=[jax.ShapeDtypeStruct((rows, 2 * width + 128), LOW)] * 4
        + [
            jax.ShapeDtypeStruct((2 * units, tokens), LOW),
            jax.ShapeDtypeStruct((units, tokens), LOW),
        ],
        scratch_shapes=[
            pltpu.VMEM((3 * units, width), LOW),
            pltpu.VMEM((tokens, width), LOW),
            pltpu.VMEM((tokens, width), LOW),
            pltpu.VMEM((tokens, 128), LOW),
            pltpu.VMEM((units, tokens), WIDE),
            pltpu.VMEM((units, tokens), WIDE),
            pltpu.VMEM((units, tokens), WIDE),
            pltpu.VMEM((2 * units, tokens), LOW),
            pltpu.VMEM((units, tokens), LOW),
            pltpu.VMEM((tokens, 2 * units), LOW),
            pltpu.VMEM((tokens, units), LOW),
            pltpu.VMEM((tokens, 2 * width + 128), LOW),
            pltpu.SemaphoreType.DMA((70,)),
        ],
        compiler_params=params(),
        cost_estimate=estimate(11_000_000_000, 20_000_000),
        name="units",
    )(*x_blocks, *g_blocks, small_rows, mine, weights)


def outer_kernel(*refs):
    back_refs, hidden_refs, x_refs, g_refs, out_ref = (
        refs[:2],
        refs[2:4],
        refs[4:12],
        refs[12:20],
        refs[20],
    )
    units = hidden_refs[0].shape[0]

    def product(lefts, rights):
        halves = [
            jnp.concatenate([ref[...] for ref in rights[half : half + 4]], axis=0)
            for half in (0, 4)
        ]
        return low(dot_plain(lefts[0][...], halves[0]) + dot_plain(lefts[1][...], halves[1]))

    back, hidden = product(back_refs, x_refs), product(hidden_refs, g_refs)
    for index in range(out_ref.shape[0]):
        columns = slice(index * 256, (index + 1) * 256)
        out_ref[index, : 2 * units] = back[:, columns]
        out_ref[index, 2 * units :] = hidden[:, columns]


def outer_products(backs, hiddens, x_blocks, g_blocks):
    units, tokens = hiddens[0].shape
    rows = x_blocks[0].shape[0]
    whole = lambda value: pl.BlockSpec(value.shape, lambda step: (0, 0))
    return pl.pallas_call(
        outer_kernel,
        grid=(4,),
        in_specs=[whole(value) for value in (*backs, *hiddens)]
        + [pl.BlockSpec((rows, 512), lambda step: (0, step))] * 16,
        out_specs=pl.BlockSpec((2, 3 * units, 256), lambda step: (step, 0, 0)),
        out_shape=jax.ShapeDtypeStruct((8, 3 * units, 256), LOW),
        compiler_params=params(),
        cost_estimate=estimate(units * 2 * 1024 * 2048, 10_000_000),
        name="outer",
    )(*backs, *hiddens, *x_blocks, *g_blocks)


def pack_kernel(here_ref, qkv_ref, out_weight_ref, small_ref, out_ref):
    width, size = out_weight_ref.shape[1], qkv_ref.shape[2]
    out_ref[:, :width] = out_weight_ref[...]
    for index in range(3):
        out_ref[:, width + index * size : width + (index + 1) * size] = qkv_ref[index]
    out_ref[:, width + 3 * size :] = jnp.zeros_like(out_ref[:, width + 3 * size :])
    out_ref[: small_ref.shape[0], width + 3 * size :] = small_ref[...]


def pack_first(here, qkv, out_weight, small):
    shard, width = out_weight.shape
    return pl.pallas_call(
        pack_kernel,
        grid_spec=pltpu.PrefetchScalarGridSpec(
            num_scalar_prefetch=1,
            grid=(1,),
            in_specs=[
                pl.BlockSpec((3, shard, 128), lambda step, here_ref: (0, 0, here_ref[0])),
                pl.BlockSpec((shard, width), lambda step, here_ref: (0, 0)),
                pl.BlockSpec(small.shape, lambda step, here_ref: (0, 0)),
            ],
            out_specs=pl.BlockSpec((shard, width + 512), lambda step, here_ref: (0, 0)),
        ),
        out_shape=jax.ShapeDtypeStruct((shard, width + 512), LOW),
        cost_estimate=estimate(1000, 1000),
        name="pack",
    )(here, qkv, out_weight, small)


def branch_kernel(left_ref, weight_ref, out_ref):
    out_ref[...] = low(dot_rows(left_ref[...], weight_ref[...]))


def branch_part(attended, pack):
    rows, units = attended.shape
    width = pack.shape[0]
    return pl.pallas_call(
        branch_kernel,
        grid=(4,),
        in_specs=[
            pl.BlockSpec((rows, units), lambda step: (0, 0)),
            pl.BlockSpec((width // 4, units), lambda step: (step, 0)),
        ],
        out_specs=pl.BlockSpec((rows, width // 4), lambda step: (0, step)),
        out_shape=jax.ShapeDtypeStruct((rows, width), LOW),
        cost_estimate=estimate(600_000_000, 5_000_000),
        name="branch",
    )(attended, pack)


def branch_back_kernel(left_ref, weight_ref, out_ref):
    out_ref[...] = low(dot_plain(left_ref[...], weight_ref[...]))


def branch_back(grads, pack, units):
    rows, width = grads.shape
    return pl.pallas_call(
        branch_back_kernel,
        grid=(4,),
        in_specs=[
            pl.BlockSpec((rows, width), lambda step: (0, 0)),
            pl.BlockSpec((width, units // 4), lambda step: (0, step)),
        ],
        out_specs=pl.BlockSpec((rows, units // 4), lambda step: (0, step)),
        out_shape=jax.ShapeDtypeStruct((rows, units), LOW),
        cost_estimate=estimate(600_000_000, 5_000_000),
        name="branch_back",
    )(grads, pack)


def first_back_kernel(left_ref, weight_ref, out_ref):
    total = dot_rows(left_ref[0], weight_ref[0, 0])
    for part in (1, 2):
        total = total + dot_rows(left_ref[part], weight_ref[0, part])
    out_ref[...] = low(total)


def first_back(grads, weights):
    parts, rows, units = grads.shape
    shards, _, shard, _ = weights.shape
    return pl.pallas_call(
        first_back_kernel,
        grid=(shards,),
        in_specs=[
            pl.BlockSpec((parts, rows, units), lambda step: (0, 0, 0)),
            pl.BlockSpec((1, parts, shard, units), lambda step: (step, 0, 0, 0)),
        ],
        out_specs=pl.BlockSpec((rows, shard), lambda step: (0, step)),
        out_shape=jax.ShapeDtypeStruct((rows, shards * shard), LOW),
        cost_estimate=estimate(1_700_000_000, 13_000_000),
        name="first_back",
    )(grads, weights)


def place_kernel(places_ref, *refs):
    blocks = refs[:8]
    qkv_ref, out_ref, small_ref = refs[8:]
    for index, block in enumerate(blocks):
        columns = block_rows(places_ref[index], 128)
        for part in range(3):
            qkv_ref[part, :, columns] = wide(block[:, part * 128 : (part + 1) * 128])
        out_ref[:, columns] = wide(block[:, 512:640])
        small_ref[places_ref[index]] = wide(block[:, 384:512])


def place_last(places, blocks):
    shard = blocks[0].shape[0]
    vmem = pl.BlockSpec(memory_space=pltpu.VMEM)
    return pl.pallas_call(
        place_kernel,
        in_specs=[pl.BlockSpec(memory_space=pltpu.SMEM)] + [vmem] * 8,
        out_specs=[vmem] * 3,
        out_shape=(
            jax.ShapeDtypeStruct((3, shard, 1024), WIDE),
            jax.ShapeDtypeStruct((shard, 1024), WIDE),
            jax.ShapeDtypeStruct((8, shard, 128), WIDE),
        ),
        compiler_params=params(),
        cost_estimate=estimate(1000, 1000),
        name="place",
    )(places, *blocks)


def place_units_kernel(places_ref, *refs):
    blocks, (gate_ref, down_ref, shared_ref) = refs[:4], refs[-3:]
    expert_units = down_ref.shape[1]
    units = blocks[0].shape[0] // 3
    step = pl.program_id(0)
    for index, block in enumerate(blocks):

        @pl.when(step == index)
        def _(block=block):
            for part in range(3):
                start = part * units
                expert = wide(block[start : start + expert_units])
                if part < 2:
                    gate_ref[0, part] = expert
                else:
                    down_ref[0] = expert
                shared_ref[part, 0] = block[start + expert_units : start + units]


def place_units(places, blocks, expert_units, earlier):
    total, shard = blocks[0].shape
    shared_units = total // 3 - expert_units
    outs = (
        jax.ShapeDtypeStruct((8, 2, expert_units, shard), WIDE),
        jax.ShapeDtypeStruct((8, expert_units, shard), WIDE),
        jax.ShapeDtypeStruct((3, 8, shared_units, shard), LOW),
    )
    anywhere = pl.BlockSpec(memory_space=pl.ANY)
    return pl.pallas_call(
        place_units_kernel,
        grid_spec=pltpu.PrefetchScalarGridSpec(
            num_scalar_prefetch=1,
            grid=(4,),
            in_specs=[pl.BlockSpec((total, shard), lambda step, places_ref: (0, 0))] * 4
            + [anywhere] * len(earlier),
            out_specs=[
                pl.BlockSpec(
                    (1, 2, expert_units, shard),
                    lambda step, places_ref: (places_ref[step], 0, 0, 0),
                ),
                pl.BlockSpec(
                    (1, expert_units, shard),
                    lambda step, places_ref: (places_ref[step], 0, 0),
                ),
                pl.BlockSpec(
                    (3, 1, shared_units, shard),
                    lambda step, places_ref: (0, places_ref[step], 0, 0),
                ),
            ],
        ),
        out_shape=outs,
        input_output_aliases={5 + index: index for index in range(len(earlier))},
        compiler_params=params(),
        cost_estimate=estimate(1000, 1000),
        name="place_units",
    )(places, *blocks, *earlier)


def flip_kernel(one_ref, in_ref, gate_ref, down_ref):
    for part in range(2):
        gate_ref[:, part, :] = dot_rows(one_ref[...], in_ref[part])
    down_ref[...] = dot_rows(one_ref[...], in_ref[2])


def flip(values):
    parts, units, shard = values.shape
    return pl.pallas_call(
        flip_kernel,
        grid=(2,),
        in_specs=[
            pl.BlockSpec((shard, shard), lambda step: (0, 0)),
            pl.BlockSpec((parts, units // 2, shard), lambda step: (0, step, 0)),
        ],
        out_specs=[
            pl.BlockSpec((shard, 2, units // 2), lambda step: (0, 0, step)),
            pl.BlockSpec((shard, units // 2), lambda step: (0, step)),
        ],
        out_shape=(
            jax.ShapeDtypeStruct((shard, 2, units), WIDE),
            jax.ShapeDtypeStruct((shard, units), WIDE),
        ),
        compiler_params=params(),
        cost_estimate=estimate(1000, 1000),
        name="flip",
    )(jnp.eye(shard, dtype=LOW), values)


def after(values, earlier):
    return lax.optimization_barrier((values, earlier))[0]


def body(
    inputs,
    lengths,
    routes,
    norm_gains,
    w_qkv,
    b_qkv,
    w_o,
    w_router,
    w_sgate,
    w_sgu,
    w_sdown,
    w_egu,
    w_edown,
    grad_out,
):
    rows, width = inputs.shape
    shard = w_qkv.shape[0]
    experts = w_egu.shape[1]
    heads, bias_part = b_qkv.shape[1], b_qkv.shape[2]
    head_size = bias_part * 8
    expert_units = w_edown.shape[2]
    shared_units = w_sdown.shape[1] // 8
    units = expert_units + shared_units
    group, here = lax.axis_index("fsdp"), lax.axis_index("ctx")
    places = here * rows + jnp.arange(rows, dtype=jnp.int32)
    length_here = lax.dynamic_index_in_dim(lengths, group, 0, keepdims=False)
    valid = (places < length_here).astype(WIDE)[:, None]
    experts_range = jnp.arange(experts, dtype=jnp.int32)
    chosen = (
        jnp.any(routes[:, :, None] == experts_range[None, None, :], axis=1).astype(WIDE) * valid
    )
    block_places = jnp.stack(relative_places()).astype(jnp.int32)

    bias_here = lax.dynamic_slice(b_qkv, (0, here, 0), (3, 1, bias_part)).reshape(1, 3 * bias_part)
    small = jnp.concatenate(
        [
            w_router.T,
            w_sgate[None],
            norm_gains,
            jnp.pad(bias_here, ((0, 0), (0, shard - 3 * bias_part))),
            jnp.zeros((4, shard), LOW),
        ],
        axis=0,
    )
    first_pack = lax.all_gather(
        pack_first(
            here.astype(jnp.int32).reshape(1),
            w_qkv.transpose(1, 0, 2),
            w_o,
            small.reshape(32, 128),
        ),
        "fsdp",
        axis=0,
        tiled=True,
    )
    small_all = first_pack[:, 1408:].reshape(8, shard, 128)[:, :32].reshape(8, 16, shard)
    small_all = small_all.transpose(1, 0, 2)
    bias_all = small_all[11, :, : 3 * bias_part].reshape(8, 3, bias_part)
    bias_all = wide(bias_all.transpose(1, 0, 2).reshape(1, 3 * head_size))
    small_all = small_all.reshape(16, width)
    gain_first, gain_second = wide(small_all[9]), wide(small_all[10])
    gate_rows = small_all[: experts + 1]
    small_rows = jnp.pad(gate_rows, ((0, 16 - experts - 1), (0, 0)))
    x_first = gather_first(inputs)
    x_second = gather_second(x_first)
    here_late = after(here, (x_first, x_second))
    shared_start = here_late * shared_units
    shared_gu = lax.dynamic_slice(w_sgu, (0, 0, shared_start), (shard, 2, shared_units))
    shared_gu = shared_gu.transpose(1, 2, 0)
    shared_down = lax.dynamic_slice(w_sdown, (0, shared_start), (shard, shared_units)).T
    expert_gu = lax.dynamic_index_in_dim(w_egu.transpose(1, 2, 3, 0), here_late, 0, keepdims=False)
    expert_down = lax.dynamic_index_in_dim(w_edown.transpose(1, 2, 0), here_late, 0, keepdims=False)
    unit_weights = lax.all_gather(
        jnp.concatenate(
            [expert_gu[0], shared_gu[0], expert_gu[1], shared_gu[1], expert_down, shared_down],
            axis=0,
        ),
        "fsdp",
        axis=0,
        tiled=False,
    )

    cosine, sine = rotary_tables(rows * 8, head_size)
    grad_own = low(wide(grad_out) * valid)
    hidden_in = wide(inputs)
    x_blocks = gather_blocks(inputs, x_first, x_second)
    grad_pack = jnp.concatenate(
        [grad_own, jnp.pad(low(chosen), ((0, 0), (0, 128 - experts)))], axis=1
    )
    grad_pack = after(grad_pack, x_second)
    g_first = gather_first(grad_pack)
    g_second = gather_second(g_first)
    g_blocks = gather_blocks(grad_pack, g_first, g_second)
    queries, keys, values, attended, normed_first = attend(
        block_places, x_blocks, first_pack, gain_first[None], bias_all, cosine, sine
    )
    attended_own = lax.all_to_all(attended, "ctx", 0, 1, tiled=True)
    branch = add_halves(after(branch_part(attended_own, first_pack), g_first))
    middle = hidden_in + branch
    factor_second = inverse_rms(middle)
    normed_own = low(middle * factor_second * gain_second)

    n_first = gather_first(normed_own)
    n_second = gather_second(n_first)
    n_blocks = gather_blocks(normed_own, n_first, n_second)
    mine = (jnp.arange(16, dtype=jnp.int32) == here).astype(WIDE)[:, None]
    first_half, second_half = (0, 1, 2, 4), (3, 5, 6, 7)
    pick = lambda blocks, half: [blocks[index] for index in half]
    results = []
    for half in (first_half, second_half):
        mine_here = after(mine, [result[5] for result in results])
        results.append(
            units_forward_back(
                pick(n_blocks, half), pick(g_blocks, half), small_rows, mine_here, unit_weights
            )
        )
    d_blocks = [None] * 8
    for half, result in zip((first_half, second_half), results):
        for place, index in enumerate(half):
            d_blocks[index] = result[place]
    (back_first, hidden_first), (back_second, hidden_second) = (
        results[0][4:],
        results[1][4:],
    )
    in_halves = lambda blocks: pick(blocks, first_half) + pick(blocks, second_half)
    weight_qkv_all = lax.all_gather(
        after(w_qkv.transpose(1, 0, 2), branch), "fsdp", axis=0, tiled=False
    )
    d_first = scatter_first(d_blocks)
    d_second = scatter_second(d_blocks, d_first)
    unit_part = outer_products(
        (back_first, back_second),
        (hidden_first, hidden_second),
        in_halves(n_blocks),
        in_halves(g_blocks),
    )
    unit_grads = lax.psum_scatter(unit_part, "fsdp", scatter_dimension=0, tiled=False)
    sums = scatter_sum(d_blocks[0], after(d_second, (unit_part, weight_qkv_all)))
    grad_sum = add_halves(sums[:, : width + 128])
    unit_first = large_first(unit_grads)

    logits = dot_rows(normed_own, gate_rows)
    probs_own = jax.nn.softmax(logits[:, :experts], axis=-1)
    gate_own = jax.nn.sigmoid(logits[:, experts : experts + 1])
    grad_normed, grad_combine = grad_sum[:, :width], grad_sum[:, width : width + experts]
    grad_gate = grad_sum[:, width + experts : width + experts + 1]
    picked = grad_combine * chosen
    grad_logits = low(
        probs_own * (picked - jnp.sum(picked * probs_own, axis=-1, keepdims=True))
    )
    grad_gate_logit = low(grad_gate * gate_own * (1.0 - gate_own))
    both = jnp.concatenate([grad_logits, grad_gate_logit], axis=1)
    grad_normed = grad_normed + dot_plain(both, gate_rows)
    grad_both = dot_columns(normed_own, both)
    grad_top = wide(grad_own)
    grad_gain_second = jnp.sum(grad_normed * middle * factor_second, axis=0)
    weighted = grad_normed * gain_second
    inner = jnp.mean(weighted * middle, axis=-1, keepdims=True)
    grad_middle = grad_top + weighted * factor_second - middle * factor_second**3 * inner
    grad_branch = low(grad_middle)

    grad_attended = branch_back(grad_branch, first_pack, heads * head_size)
    grad_heads = lax.all_to_all(
        grad_attended.reshape(rows, heads, head_size).transpose(1, 0, 2), "ctx", 0, 0, tiled=True
    ).reshape(rows * 8, head_size)
    grad_heads = after(grad_heads, unit_first)
    unit_second = large_second(unit_first)
    mixed = add_halves(after(sums[:, width + 128 :], grad_heads))
    result = low(valid * (middle + mixed))
    out_part = lax.psum_scatter(
        low(dot_columns(grad_branch, attended_own)), "fsdp", scatter_dimension=0, tiled=True
    )
    grad_proj, grad_bias = attend_back(queries, keys, values, grad_heads, cosine, sine)
    proj_own = lax.all_to_all(
        grad_proj.reshape(8, rows, 3 * head_size), "ctx", 0, 0, tiled=True
    )
    grad_qkv_here = low(dot_columns(normed_first, grad_proj))
    bias_rows = grad_bias.reshape(3, 8, bias_part).transpose(1, 0, 2).reshape(8, 3 * bias_part)
    bias_rows = jnp.pad(bias_rows, ((0, 0), (0, shard - 3 * bias_part))).reshape(width, 1)
    small_grads = low(jnp.concatenate([grad_both, grad_gain_second[:, None], bias_rows], axis=1))
    small_grads = jnp.pad(small_grads, ((0, 0), (0, 128 - small_grads.shape[1])))
    last_part = jnp.concatenate([grad_qkv_here, small_grads], axis=1)
    proj_own = after(proj_own, (last_part, unit_second))
    proj_own = proj_own.reshape(8, rows, 3, head_size).transpose(2, 1, 0, 3)
    proj_own = proj_own.reshape(3, rows, heads * head_size)
    first_part = first_back(proj_own, weight_qkv_all)
    grad_first = after(add_halves(first_part), result)
    unit_third = large_third(unit_second)
    factor_first = inverse_rms(hidden_in)
    weighted = grad_first * gain_first
    inner = jnp.mean(weighted * hidden_in, axis=-1, keepdims=True)
    grad_input = grad_middle + weighted * factor_first - hidden_in * factor_first**3 * inner

    last_pack = lax.psum_scatter(last_part, "fsdp", scatter_dimension=0, tiled=True)
    out_parts = out_part.reshape(shard, heads, head_size).transpose(1, 0, 2)
    out_parts = lax.all_to_all(after(out_parts, unit_second), "ctx", 0, 0, tiled=True)
    grad_w_o_here = low(jnp.sum(wide(out_parts), axis=0))
    unit_blocks = large_blocks(unit_grads, unit_first, unit_second, unit_third)
    early, late = (0, 1, 2, 4), (3, 5, 6, 7)
    placed = ()
    for half in (early, late):
        block_half = after(block_places, unit_second)[jnp.array(half)]
        placed = place_units(block_half, pick(unit_blocks, half), expert_units, placed)
    grad_egu, grad_edown, shared_grads = placed
    grad_w_sgu, grad_w_sdown = flip(shared_grads.reshape(3, 8 * shared_units, shard))
    weights_here = lax.dynamic_slice(
        w_qkv, (0, 0, here * head_size), (shard, 3, head_size)
    ).reshape(shard, 3 * head_size)
    products = jnp.sum(wide(weights_here) * wide(last_pack[:, : 3 * head_size]), axis=1)
    products = products + lax.ppermute(products, "tp", [(0, 1), (1, 0)])
    spare = 3 * head_size + experts + 3
    last_blocks = gather_relative(
        jnp.concatenate(
            [
                last_pack[:, :spare],
                low(products)[:, None],
                last_pack[:, spare + 1 :],
                grad_w_o_here,
            ],
            axis=1,
        )
    )
    grad_qkv, grad_w_o, small_sums = place_last(block_places, last_blocks)
    grad_w_qkv = grad_qkv.transpose(1, 0, 2)
    summed = jnp.sum(small_sums[:, :, : experts + 4], axis=0)
    grad_b_qkv = (
        small_sums[:, : 3 * bias_part, experts + 2].reshape(8, 3, bias_part).transpose(1, 0, 2)
    )
    grad_gain_first = summed[:, experts + 3] / wide(norm_gains[0])
    return (
        result,
        low(grad_input),
        jnp.stack([grad_gain_first, summed[:, experts + 1]]),
        grad_w_qkv,
        grad_b_qkv,
        grad_w_o,
        summed[:, :experts],
        summed[:, experts],
        grad_w_sgu,
        grad_w_sdown,
        grad_egu.transpose(3, 0, 1, 2),
        grad_edown.transpose(2, 0, 1),
    )


def solution(mesh):
    return jax.shard_map(
        body,
        mesh=mesh,
        in_specs=(
            P(("fsdp", "ctx"), None),
            P(),
            P(("fsdp", "ctx"), None),
            P(None, "fsdp"),
            P("fsdp", None, "tp"),
            P(None, "tp", "fsdp"),
            P("fsdp", "tp"),
            P("fsdp", None),
            P("fsdp"),
            P("fsdp", None, "tp"),
            P("fsdp", "tp"),
            P("fsdp", None, None, "tp"),
            P("fsdp", None, "tp"),
            P(("fsdp", "ctx"), None),
        ),
        out_specs=(
            P(("fsdp", "ctx"), None),
            P(("fsdp", "ctx"), None),
            P(None, "fsdp"),
            P("fsdp", None, "tp"),
            P(None, "tp", "fsdp"),
            P("fsdp", "tp"),
            P("fsdp", None),
            P("fsdp"),
            P("fsdp", None, "tp"),
            P("fsdp", "tp"),
            P("fsdp", None, None, "tp"),
            P("fsdp", None, "tp"),
        ),
        check_vma=False,
    )
```

time: 658 us -> 535 us (0.81)
  Pallas kernels: 10.9 us -> 132 us
  matrix products: 129 us -> 10.4 us
  local copies, waits for them, and re-layouts: 126 us -> 50.5 us
  starting transfers between devices: 129 us -> 89.7 us
  other arithmetic: 64.8 us -> 32.7 us
  waiting for transfers between devices: 159 us -> 186 us
    pallas_call x1 -> x12, Pallas kernels: 4.75 us -> 126 us  [the longest x2 44.5 us: units_forward_back(): pl.pallas_call(units_kernel, in_specs=[anywhere] * 8 + [vmem] * 2 + [anyw...]
    dot_general x8 -> x1, matrix products: 48.1 us -> 0.27 us  [dot_rows(): lax.dot_general(left, right, (((1,), (1,)), ((), ())), preferred_element_...]
    dot_general x11 -> x1, matrix products: 46.3 us -> 1.82 us  [dot_plain(): return jnp.dot(left, right, preferred_element_type=WIDE)]
    ppermute x24 -> x14, starting transfers between devices: 67.9 us -> 30.6 us  [down(): return lax.ppermute(values, 'ctx', ring(-2))]
    dot_general x9 -> x3, matrix products: 34.4 us -> 8.26 us  [dot_columns(): lax.dot_general(left, right, (((0,), (0,)), ((), ())), preferred_element_...]
    unnamed x130 -> x112, local copies, waits for them, and re-layouts: 33 us -> 12.4 us
    ppermute x24 -> x14, waiting for transfers between devices: 99 us -> 79.5 us  [up(): return lax.ppermute(values, 'ctx', ring(2))]
    slice x24 -> x12, local copies, waits for them, and re-layouts: 31.5 us -> 12.4 us  [the longest x2 4.18 us: large_third(): return (up(pair_left[:half]), down(pair_right[half:]))]
  transfers between devices with their start and end apart: 78 -> 58, of which waited for: 33 -> 19; matrix products, arithmetic and copies ran while one was open for 42% -> 14% of each run, Pallas kernels for 2% -> 24%
where the time goes in v2:
time: 535 us; the launch traced here: 528 us
  waiting for transfers between devices  186 us (35%)
  Pallas kernels  132 us (25%)
  starting transfers between devices  89.7 us (17%)
  local copies, waits for them, and re-layouts  50.5 us (9%)
  other arithmetic  32.7 us (6%)
  between operations  15.6 us (3%)
  blocking collectives  11.6 us (2%)
  matrix products  10.4 us (2%)
    ppermute x14, waiting for transfers between devices, up(): return lax.ppermute(values, 'ctx', ring(2))  79.5 us
    pallas_call x2, Pallas kernels, units_forward_back(): pl.pallas_call(units_kernel, in_specs=[anywhere] * 8 + [vmem] * 2 + [anyw...  44.5 us
    ppermute x14, starting transfers between devices, down(): return lax.ppermute(values, 'ctx', ring(-2))  30.6 us
    ppermute x11, waiting for transfers between devices, swap(): return lax.ppermute(values, 'ctx', PAIR)  25.5 us
    all_to_all x1, waiting for transfers between devices, body(): lax.all_to_all(grad_attended.reshape(rows, heads, head_size).transpose(1,...  23.7 us
    all_to_all x1, waiting for transfers between devices, body(): lax.all_to_all(grad_proj.reshape(8, rows, 3 * head_size), 'ctx', 0, 0, ti...  23.4 us
    pallas_call x1, Pallas kernels, outer_products(): pl.pallas_call(outer_kernel, grid=(4,), in_specs=[whole(value) for value...  20 us
    ppermute x4, waiting for transfers between devices, add_halves(): return wide(mine) + wide(lax.ppermute(mine, 'tp', [(0, 1), (1, 0)]))  18 us
  transfers between devices with their start and end apart: 58, of which 19 were waited for; matrix products, arithmetic and copies ran while one was open for 14% of the time, Pallas kernels for 24%

profile of v2, /device:TPU:0, one launch (start us, length us, event | category | flops | bytes accessed | tf_op | source)
XLA Modules:
  0.0 528.3 jit_solution(9492971525622422412)
XLA Ops:
  10.9 2.1 pack.1
  14.8 3.0 collective-permute-start.2
  18.4 2.6 collective-permute-start.1
  21.1 5.7 %collective-permute-done.3.refs_4_ = bf16[128,2048]{1,0:T(8,128)(2,1)S(1)} collective-permute-done((bf16[128,2048]{1,0:T(8,128)(2,1)S(1)}, bf16[128,2048]{1,0:T(8,128)(2,1)S(1)}, u32[]{:S(2)}, u32[]{:S(2)}) %collective-permute-start.3) | collective-permute-done | bytes 524320 | tf_op jit(solution)/shard_map/ppermute | solution.py:58
  31.7 9.7 %collective-permute-done.refs_1_ = bf16[128,2048]{1,0:T(8,128)(2,1)S(1)} collective-permute-done((bf16[128,2048]{1,0:T(8,128)(2,1)S(1)}, bf16[128,2048]{1,0:T(8,128)(2,1)S(1)}, u32[]{:S(2)}, u32[]{:S(2)}) %collective-permute-start) | collective-permute-done | bytes 524320 | tf_op jit(solution)/shard_map/ppermute | solution.py:50
  42.5 9.6 %collective-permute-done.4.refs_5_ = bf16[128,2048]{1,0:T(8,128)(2,1)S(1)} collective-permute-done((bf16[128,2048]{1,0:T(8,128)(2,1)S(1)}, bf16[128,2048]{1,0:T(8,128)(2,1)S(1)}, u32[]{:S(2)}, u32[]{:S(2)}) %collective-permute-start.4) | collective-permute-done | bytes 524320 | tf_op jit(solution)/shard_map/ppermute | solution.py:50
  70.9 12.8 %attend.1 = (bf16[1024,128]{1,0:T(8,128)(2,1)}, bf16[1024,128]{1,0:T(8,128)(2,1)}, bf16[1024,128]{1,0:T(8,128)(2,1)}, bf16[1024,128]{1,0:T(8,128)(2,1)}, bf16[1024,2048]{1,0:T(8,128)(2,1)}) custom-call(s32[8]{0:T(128)} %stack.39.places_ref, bf16[128,2048]{1,0:T(8,128)(2,1)} %refs_0_.1, bf16[128,2048]{1,0:T(8,128)(2,1)} %copy-done.32, ...), custom_call_target="tpu_custom_call" | custom-call | flops 9000000 | bytes 12000 | tf_op jit(solution)/shard_map/attend/pallas_call | solution.py:217
  83.7 11.6 %all_to_all.34 = bf16[8,128,128]{2,1,0:T(8,128)(2,1)S(1)} all-to-all(bf16[8,128,128]{2,1,0:T(8,128)(2,1)} %bitcast.135), channel_id=1, replica_groups=mesh['fsdp'=8,'ctx'=8,'tp'=2] {'ctx'}, dimensions={0} | all-to-all | bytes 524288 | tf_op jit(solution)/shard_map/all_to_all | solution.py:775
  96.0 5.1 branch.1
  101.2 3.1 collective-permute-start.11
  104.4 9.9 %collective-permute-done.11 = bf16[128,2048]{1,0:T(8,128)(2,1)S(1)} collective-permute-done((bf16[128,2048]{1,0:T(8,128)(2,1)}, bf16[128,2048]{1,0:T(8,128)(2,1)S(1)}, u32[]{:S(2)}, u32[]{:S(2)}) %collective-permute-start.11) | collective-permute-done | bytes 524320 | tf_op jit(solution)/shard_map/ppermute | solution.py:141
  118.0 1.9 collective-permute-start.12
  122.9 9.4 %collective-permute-done.15.refs_0_.refs_8_ = bf16[128,2048]{1,0:T(8,128)(2,1)S(1)} collective-permute-done((bf16[128,2048]{1,0:T(8,128)(2,1)S(1)}, bf16[128,2048]{1,0:T(8,128)(2,1)S(1)}, u32[]{:S(2)}, u32[]{:S(2)}) %collective-permute-start.15) | collective-permute-done | bytes 524320 | tf_op jit(solution)/shard_map/ppermute | solution.py:69
  134.6 6.6 %collective-permute-done.12.refs_1_.refs_5_ = bf16[128,2048]{1,0:T(8,128)(2,1)S(1)} collective-permute-done((bf16[128,2048]{1,0:T(8,128)(2,1)S(1)}, bf16[128,2048]{1,0:T(8,128)(2,1)S(1)}, u32[]{:S(2)}, u32[]{:S(2)}) %collective-permute-start.12) | collective-permute-done | bytes 524320 | tf_op jit(solution)/shard_map/ppermute | solution.py:50
  141.2 3.0 collective-permute-start.17
  147.9 22.1 %units.2 = (bf16[128,4224]{1,0:T(8,128)(2,1)}, bf16[128,4224]{1,0:T(8,128)(2,1)}, bf16[128,4224]{1,0:T(8,128)(2,1)}, bf16[128,4224]{1,0:T(8,128)(2,1)}, bf16[211...) custom-call(bf16[128,2048]{1,0:T(8,128)(2,1)} %copy-done.3, bf16[128,2048]{1,0:T(8,128)(2,1)} %copy-done.19, ...), custom_call_target="tpu_custom_call" | custom-call | flops 11000000 | bytes 20000 | tf_op jit(solution)/shard_map/units/pallas_call | solution.py:393
  170.8 22.4 %units.3 = (bf16[128,4224]{1,0:T(8,128)(2,1)}, bf16[128,4224]{1,0:T(8,128)(2,1)}, bf16[128,4224]{1,0:T(8,128)(2,1)}, bf16[128,4224]{1,0:T(8,128)(2,1)}, bf16[211...) custom-call(bf16[128,2048]{1,0:T(8,128)(2,1)} %copy-done.18, bf16[128,2048]{1,0:T(8,128)(2,1)} %collective-permute-done.16.refs_1_.refs_9_, ...), custom_call_target="tpu_custom_call" | custom-call | flops 11000000 | bytes 20000 | tf_op jit(solution)/shard_map/units/pallas_call | solution.py:393
  193.2 20.0 %outer.1 = bf16[8,3168,256]{2,1,0:T(8,128)(2,1)} custom-call(bf16[2112,512]{1,0:T(8,128)(2,1)} %get-tuple-element.71.refs_0_, bf16[2112,512]{1,0:T(8,128)(2,1)} %get-tuple-element.72.refs_1_, bf16[1056,512]{1,0:T(8,128)(2,1)} %get-tuple-element.62.refs_2_, bf16[1056,512]{1,0:T(8,128)(2,1)} %get-tuple-element.73.refs_3_, bf16[128,2048]{1,0:T(8,128)(2,1)} %copy-done.3, ...), custom_call_target="tpu_custom_call" | custom-call | flops 4429185 | bytes 10000 | tf_op jit(solution)/shard_map/outer/pallas_call | solution.py:451
  216.4 3.0 collective-permute-start.28
  219.4 16.4 %collective-permute-done.22 = bf16[128,4224]{1,0:T(8,128)(2,1)S(1)} collective-permute-done((bf16[128,4224]{1,0:T(8,128)(2,1)}, bf16[128,4224]{1,0:T(8,128)(2,1)S(1)}, u32[]{:S(2)}, u32[]{:S(2)}) %collective-permute-start.22) | collective-permute-done | bytes 1081376 | tf_op jit(solution)/shard_map/ppermute | solution.py:58
  235.8 2.6 add_convert_fusion.1
  238.3 2.0 collective-permute-start.23
  241.1 2.1 collective-permute-done.24
  246.3 40.8 %collective-permute-done.27 = bf16[128,4224]{1,0:T(8,128)(2,1)} collective-permute-done((bf16[128,4224]{1,0:T(8,128)(2,1)}, bf16[128,4224]{1,0:T(8,128)(2,1)}, u32[]{:S(2)}, u32[]{:S(2)}) %collective-permute-start.27) | collective-permute-done | bytes 1081376 | tf_op jit(solution)/shard_map/ppermute | solution.py:50
  287.1 3.3 convert_add_fusion
  292.3 2.8 collective-permute-start.29
  295.6 8.0 %collective-permute-done.29 = bf16[128,2176]{1,0:T(8,128)(2,1)S(1)} collective-permute-done((bf16[128,2176]{1,0:T(8,128)(2,1)}, bf16[128,2176]{1,0:T(8,128)(2,1)S(1)}, u32[]{:S(2)}, u32[]{:S(2)}) %collective-permute-start.29) | collective-permute-done | bytes 557088 | tf_op jit(solution)/shard_map/ppermute | solution.py:141
  307.0 1.8 multiply_reduce_fusion
  310.2 3.3 convolution_convert_fusion
  313.6 3.2 collective-permute-start.31
  317.1 4.6 branch_back.1
  323.4 3.4 all-to-all-start.1
  327.1 23.7 %all-to-all-done.1 = bf16[8,128,128]{2,1,0:T(8,128)(2,1)S(1)} async-done(((bf16[8,128,128]{2,1,0:T(8,128)(2,1)}), bf16[8,128,128]{2,1,0:T(8,128)(2,1)S(1)}, u32[]{:S(2)}, u32[]{:S(2)}) %all-to-all-start.1) | async-done | bytes 262176 | tf_op jit(solution)/shard_map/all_to_all | solution.py:841
  351.5 6.1 %attend_back.1 = (bf16[1024,384]{1,0:T(8,128)(2,1)}, f32[1,384]{1,0:T(1,128)}) custom-call(bf16[1024,128]{1,0:T(8,128)(2,1)} %get-tuple-element.81.q_ref, bf16[1024,128]{1,0:T(8,128)(2,1)} %get-tuple-element.82.k_ref, bf16[1024,128]{1,0:T(8,128)(2,1)} %get-tuple-element.83.v_ref, bf16[1024,128]{1,0:T(8,128)(2,1)} %bitcast.129, ...), custom_call_target="tpu_custom_call" | custom-call | flops 7000000 | bytes 6000 | tf_op jit(solution)/shard_map/attend_back/pallas_call | solution.py:264
  358.8 4.8 convolution_convert_fusion.1
  366.1 2.7 collective-permute-start.37
  371.1 3.5 all-to-all-start.2
  374.6 2.1 slice.154
  376.7 1.9 collective-permute-start.34
  378.6 2.1 slice.155
  383.9 2.4 collective-permute-start.33
  388.2 1.9 bitcast_bitcast_fusion
  390.2 23.4 %all-to-all-done.2 = bf16[8,128,384]{1,2,0:T(8,128)(2,1)S(1)} async-done(((bf16[8,128,384]{1,2,0:T(8,128)(2,1)}), bf16[8,128,384]{1,2,0:T(8,128)(2,1)S(1)}, u32[]{:S(2)}, u32[]{:S(2)}) %all-to-all-start.2) | async-done | bytes 786464 | tf_op jit(solution)/shard_map/all_to_all | solution.py:852
  413.6 10.6 %collective-permute-done.34 = bf16[1584,256]{1,0:T(8,128)(2,1)} collective-permute-done((bf16[1584,256]{1,0:T(8,128)(2,1)}, bf16[1584,256]{1,0:T(8,128)(2,1)}, u32[]{:S(2)}, u32[]{:S(2)}) %collective-permute-start.34) | collective-permute-done | bytes 811040 | tf_op jit(solution)/shard_map/ppermute | solution.py:50
  425.5 2.1 reshape.196.left_ref
  427.6 10.1 %first_back.1 = bf16[128,2048]{1,0:T(8,128)(2,1)} custom-call(bf16[3,128,1024]{2,1,0:T(8,128)(2,1)} %reshape.196.left_ref, bf16[8,3,256,1024]{3,2,1,0:T(8,128)(2,1)} %bitcast.112), custom_call_target="tpu_custom_call" | custom-call | flops 1700000 | bytes 13000 | tf_op jit(solution)/shard_map/first_back/pallas_call | solution.py:544
  437.7 2.6 collective-permute-start.38
  440.3 2.1 multiply_convert_fusion
  442.4 4.5 all-to-all-start.3
  446.8 2.7 pad_maximum_fusion.refs_0_
  449.5 2.1 slice.164
  451.6 3.2 collective-permute-start.48
  455.9 2.1 slice.163
  458.0 8.0 %place_units.2 = (f32[8,2,704,256]{3,2,1,0:T(8,128)}, f32[8,704,256]{2,1,0:T(8,128)}, bf16[3,8,352,256]{3,2,1,0:T(8,128)(2,1)}) custom-call(s32[4]{0:T(128)} %gather_fusion.1, bf16[3168,256]{1,0:T(8,128)(2,1)} %bitcast.122, bf16[3168,256]{1,0:T(8,128)(2,1)} %collective-permute-done.30.refs_1_, bf16[3168,256]{1,0:T(8,128)(2,1)} %collective-permute-done.31.refs_2_, ...), custom_call_target="tpu_custom_call" | custom-call | flops 1 | bytes 1 | tf_op jit(solution)/shard_map/place_units/pallas_call | solution.py:615
  469.8 1.8 collective-permute-start.39
  472.6 2.5 collective-permute-done.39
  476.3 2.3 collective-permute-start.42
  481.1 1.8 collective-permute-start.40
  484.3 3.5 collective-permute-done.43.refs_4_
  488.1 3.0 collective-permute-start.45
  492.7 2.6 pad_maximum_fusion.1.refs_3_
  495.3 7.9 %place_units.3 = (f32[8,2,704,256]{3,2,1,0:T(8,128)}, f32[8,704,256]{2,1,0:T(8,128)}, bf16[3,8,352,256]{3,2,1,0:T(8,128)(2,1)}) custom-call(s32[4]{0:T(128)} %gather_fusion, bf16[3168,256]{1,0:T(8,128)(2,1)} %pad_maximum_fusion.refs_0_, ...), custom_call_target="tpu_custom_call", output_to_operand_aliasing={{0}: (5, {}), {1}: (6, {}), {2}: (7, {})} | custom-call | flops 1 | bytes 1 | tf_op jit(solution)/shard_map/place_units/pallas_call | solution.py:615
  503.2 5.9 %flip.1 = (f32[256,2,2816]{2,1,0:T(2,128)}, f32[256,2816]{1,0:T(8,128)}) custom-call(bf16[256,256]{1,0:T(8,128)(2,1)} %fusion.11.one_ref, bf16[3,2816,256]{2,1,0:T(8,128)(2,1)} %bitcast.111), custom_call_target="tpu_custom_call" | custom-call | flops 1 | bytes 1 | tf_op jit(solution)/shard_map/flip/pallas_call | solution.py:653
  510.9 4.8 place.1
  (291 shorter events, 94.0 us)
Async XLA Ops:
  7.2 46.6 %copy-start = (bf16[256,2,2816]{2,1,0:T(2,128)(2,1)S(1)}, bf16[256,2,2816]{2,1,0:T(2,128)(2,1)}, u32[]{:S(2)}) copy-start(bf16[256,2,2816]{2,1,0:T(2,128)(2,1)} %param.27) | copy-start | bytes 8650756
  7.2 61.2 %all-gather.6.cloned.1.call-start = ((), (), s32[]{:S(2)}) async-start(), calls=%async_computation.7 | async-start | bytes 7077888 | tf_op jit(solution)/shard_map/all_gather | solution.py:723
  13.0 134.9 %all-gather.8.cloned.1.call-start = ((), (), s32[]{:S(2)}) async-start(), calls=%async_computation.11 | async-start | bytes 14598144 | tf_op jit(solution)/shard_map/all_gather | solution.py:751
  13.1 13.7 %collective-permute-start.3 = (bf16[128,2048]{1,0:T(8,128)(2,1)S(1)}, bf16[128,2048]{1,0:T(8,128)(2,1)S(1)}, u32[]{:S(2)}, u32[]{:S(2)}) collective-permute-start(bf16[128,2048]{1,0:T(8,128)(2,1)S(1)} %copy-done.5), channel_id=1, source_target_pairs={{0,2},{2,0},{4,6},{6,4},{8,10},{10,8},{12,14},{14,12},{1,3},{3,1},... | collective-permute-start | bytes 1572872 | tf_op jit(solution)/shard_map/ppermute | solution.py:58
  14.8 16.4 %collective-permute-start.2 = (bf16[128,2048]{1,0:T(8,128)(2,1)S(1)}, bf16[128,2048]{1,0:T(8,128)(2,1)S(1)}, u32[]{:S(2)}, u32[]{:S(2)}) collective-permute-start(bf16[128,2048]{1,0:T(8,128)(2,1)S(1)} %copy-done.5), channel_id=1, source_target_pairs={{0,8},{2,10},{4,12},{6,14},{8,0},{10,2},{12,4},{14,6},{1,9},{3,11}... | collective-permute-start | bytes 1572872 | tf_op jit(solution)/shard_map/ppermute | solution.py:69
  17.8 23.6 %collective-permute-start = (bf16[128,2048]{1,0:T(8,128)(2,1)S(1)}, bf16[128,2048]{1,0:T(8,128)(2,1)S(1)}, u32[]{:S(2)}, u32[]{:S(2)}) collective-permute-start(bf16[128,2048]{1,0:T(8,128)(2,1)S(1)} %copy-done.5), channel_id=1, source_target_pairs={{0,4},{2,6},{4,8},{6,10},{8,12},{10,14},{12,0},{14,2},{1,5},{3,7},... | collective-permute-start | bytes 1572872 | tf_op jit(solution)/shard_map/ppermute | solution.py:50
  18.4 24.1 %collective-permute-start.1 = (bf16[128,2048]{1,0:T(8,128)(2,1)S(1)}, bf16[128,2048]{1,0:T(8,128)(2,1)S(1)}, u32[]{:S(2)}, u32[]{:S(2)}) collective-permute-start(bf16[128,2048]{1,0:T(8,128)(2,1)S(1)} %copy-done.5), channel_id=1, source_target_pairs={{0,12},{2,14},{4,0},{6,2},{8,4},{10,6},{12,8},{14,10},{1,13},{3,15... | collective-permute-start | bytes 1572872 | tf_op jit(solution)/shard_map/ppermute | solution.py:54
  26.7 25.4 %collective-permute-start.4 = (bf16[128,2048]{1,0:T(8,128)(2,1)S(1)}, bf16[128,2048]{1,0:T(8,128)(2,1)S(1)}, u32[]{:S(2)}, u32[]{:S(2)}) collective-permute-start(bf16[128,2048]{1,0:T(8,128)(2,1)S(1)} %collective-permute-done.3.refs_4_), channel_id=1, source_target_pairs={{0,4},{2,6},{4,8},{6,10},{8,12},{10,14},{12,0},{14,2},{1,5},{3,7},... | collective-permute-start | bytes 1572872 | tf_op jit(solution)/shard_map/ppermute | solution.py:50
  28.4 23.9 %collective-permute-start.5 = (bf16[128,2048]{1,0:T(8,128)(2,1)S(1)}, bf16[128,2048]{1,0:T(8,128)(2,1)S(1)}, u32[]{:S(2)}, u32[]{:S(2)}) collective-permute-start(bf16[128,2048]{1,0:T(8,128)(2,1)S(1)} %collective-permute-done.3.refs_4_), channel_id=1, source_target_pairs={{0,12},{2,14},{4,0},{6,2},{8,4},{10,6},{12,8},{14,10},{1,13},{3,15... | collective-permute-start | bytes 1572872 | tf_op jit(solution)/shard_map/ppermute | solution.py:54
  31.2 21.1 %copy-start.31 = (bf16[128,2048]{1,0:T(8,128)(2,1)}, bf16[128,2048]{1,0:T(8,128)(2,1)S(1)}, u32[]{:S(2)}) copy-start(bf16[128,2048]{1,0:T(8,128)(2,1)S(1)} %collective-permute-done.2.refs_3_) | copy-start | bytes 1572868
  31.2 22.5 %collective-permute-start.6 = (bf16[128,2048]{1,0:T(8,128)(2,1)S(1)}, bf16[128,2048]{1,0:T(8,128)(2,1)}, u32[]{:S(2)}, u32[]{:S(2)}) collective-permute-start(bf16[128,2048]{1,0:T(8,128)(2,1)S(1)} %collective-permute-done.2.refs_3_), channel_id=1, source_target_pairs={{0,2},{2,0},{4,6},{6,4},{8,10},{10,8},{12,14},{14,12},{1,3},{3,1},... | collective-permute-start | bytes 1572872 | tf_op jit(solution)/shard_map/ppermute | solution.py:58
  59.7 186.6 %all-gather.10.cloned.1.call-start = ((), (), s32[]{:S(2)}) async-start(), calls=%async_computation.12 | async-start | bytes 14155776 | tf_op jit(solution)/shard_map/all_gather | solution.py:804
  60.4 253.1 %reduce-scatter.4.cloned.1.call-start = ((), (), s32[]{:S(2)}) async-start(), calls=%async_computation.8 | async-start | bytes 14598144 | tf_op jit(solution)/shard_map/reduce_scatter | solution.py:815
  63.4 20.3 %copy-start.9 = (bf16[128,2176]{1,0:T(8,128)(2,1)}, bf16[128,2176]{1,0:T(8,128)(2,1)S(1)}, u32[]{:S(2)}) copy-start(bf16[128,2176]{1,0:T(8,128)(2,1)S(1)} %fusion.8.refs_4_.refs_12_) | copy-start | bytes 1671172
  63.4 37.7 %collective-permute-start.7 = (bf16[128,2176]{1,0:T(8,128)(2,1)S(1)}, bf16[128,2176]{1,0:T(8,128)(2,1)S(1)}, u32[]{:S(2)}, u32[]{:S(2)}) collective-permute-start(bf16[128,2176]{1,0:T(8,128)(2,1)S(1)} %fusion.8.refs_4_.refs_12_), channel_id=1, source_target_pairs={{0,4},{2,6},{4,8},{6,10},{8,12},{10,14},{12,0},{14,2},{1,5},{3,7},... | collective-permute-start | bytes 1671176 | tf_op jit(solution)/shard_map/ppermute | solution.py:50
  65.1 36.1 %collective-permute-start.8 = (bf16[128,2176]{1,0:T(8,128)(2,1)S(1)}, bf16[128,2176]{1,0:T(8,128)(2,1)S(1)}, u32[]{:S(2)}, u32[]{:S(2)}) collective-permute-start(bf16[128,2176]{1,0:T(8,128)(2,1)S(1)} %fusion.8.refs_4_.refs_12_), channel_id=1, source_target_pairs={{0,12},{2,14},{4,0},{6,2},{8,4},{10,6},{12,8},{14,10},{1,13},{3,15... | collective-permute-start | bytes 1671176 | tf_op jit(solution)/shard_map/ppermute | solution.py:54
  66.7 34.4 %collective-permute-start.9 = (bf16[128,2176]{1,0:T(8,128)(2,1)S(1)}, bf16[128,2176]{1,0:T(8,128)(2,1)}, u32[]{:S(2)}, u32[]{:S(2)}) collective-permute-start(bf16[128,2176]{1,0:T(8,128)(2,1)S(1)} %fusion.8.refs_4_.refs_12_), channel_id=1, source_target_pairs={{0,2},{2,0},{4,6},{6,4},{8,10},{10,8},{12,14},{14,12},{1,3},{3,1},... | collective-permute-start | bytes 1671176 | tf_op jit(solution)/shard_map/ppermute | solution.py:58
  67.1 34.0 %collective-permute-start.10 = (bf16[128,2176]{1,0:T(8,128)(2,1)S(1)}, bf16[128,2176]{1,0:T(8,128)(2,1)S(1)}, u32[]{:S(2)}, u32[]{:S(2)}) collective-permute-start(bf16[128,2176]{1,0:T(8,128)(2,1)S(1)} %fusion.8.refs_4_.refs_12_), channel_id=1, source_target_pairs={{0,8},{2,10},{4,12},{6,14},{8,0},{10,2},{12,4},{14,6},{1,9},{3,11}... | collective-permute-start | bytes 1671176 | tf_op jit(solution)/shard_map/ppermute | solution.py:69
  101.2 13.1 %collective-permute-start.11 = (bf16[128,2048]{1,0:T(8,128)(2,1)}, bf16[128,2048]{1,0:T(8,128)(2,1)S(1)}, u32[]{:S(2)}, u32[]{:S(2)}) collective-permute-start(bf16[128,2048]{1,0:T(8,128)(2,1)} %branch.1), channel_id=1, source_target_pairs={{0,1},{1,0},{2,3},{3,2},{4,5},{5,4},{6,7},{7,6},{8,9},{9,8},{10,11... | collective-permute-start | bytes 1572872 | tf_op jit(solution)/shard_map/ppermute | solution.py:141
  104.2 17.1 %collective-permute-start.19 = (bf16[128,2176]{1,0:T(8,128)(2,1)}, bf16[128,2176]{1,0:T(8,128)(2,1)S(1)}, u32[]{:S(2)}, u32[]{:S(2)}) collective-permute-start(bf16[128,2176]{1,0:T(8,128)(2,1)} %collective-permute-done.9.refs_7_.refs_15_), channel_id=1, source_target_pairs={{0,4},{2,6},{4,8},{6,10},{8,12},{10,14},{12,0},{14,2},{1,5},{3,7},... | collective-permute-start | bytes 1671176 | tf_op jit(solution)/shard_map/ppermute | solution.py:50
  115.9 32.0 %copy-start.3 = (bf16[128,2048]{1,0:T(8,128)(2,1)}, bf16[128,2048]{1,0:T(8,128)(2,1)S(1)}, u32[]{:S(2)}) copy-start(bf16[128,2048]{1,0:T(8,128)(2,1)S(1)} %multiply_convert_fusion.1.refs_0_.refs_4_) | copy-start | bytes 1572868
  115.9 16.5 %collective-permute-start.15 = (bf16[128,2048]{1,0:T(8,128)(2,1)S(1)}, bf16[128,2048]{1,0:T(8,128)(2,1)S(1)}, u32[]{:S(2)}, u32[]{:S(2)}) collective-permute-start(bf16[128,2048]{1,0:T(8,128)(2,1)S(1)} %multiply_convert_fusion.1.refs_0_.refs_4_), channel_id=1, source_target_pairs={{0,8},{2,10},{4,12},{6,14},{8,0},{10,2},{12,4},{14,6},{1,9},{3,11}... | collective-permute-start | bytes 1572872 | tf_op jit(solution)/shard_map/ppermute | solution.py:69
  117.6 15.9 %collective-permute-start.14 = (bf16[128,2048]{1,0:T(8,128)(2,1)S(1)}, bf16[128,2048]{1,0:T(8,128)(2,1)}, u32[]{:S(2)}, u32[]{:S(2)}) collective-permute-start(bf16[128,2048]{1,0:T(8,128)(2,1)S(1)} %multiply_convert_fusion.1.refs_0_.refs_4_), channel_id=1, source_target_pairs={{0,2},{2,0},{4,6},{6,4},{8,10},{10,8},{12,14},{14,12},{1,3},{3,1},... | collective-permute-start | bytes 1572872 | tf_op jit(solution)/shard_map/ppermute | solution.py:58
  118.0 23.1 %collective-permute-start.12 = (bf16[128,2048]{1,0:T(8,128)(2,1)S(1)}, bf16[128,2048]{1,0:T(8,128)(2,1)S(1)}, u32[]{:S(2)}, u32[]{:S(2)}) collective-permute-start(bf16[128,2048]{1,0:T(8,128)(2,1)S(1)} %multiply_convert_fusion.1.refs_0_.refs_4_), channel_id=1, source_target_pairs={{0,4},{2,6},{4,8},{6,10},{8,12},{10,14},{12,0},{14,2},{1,5},{3,7},... | collective-permute-start | bytes 1572872 | tf_op jit(solution)/shard_map/ppermute | solution.py:50
  120.0 24.2 %collective-permute-start.13 = (bf16[128,2048]{1,0:T(8,128)(2,1)S(1)}, bf16[128,2048]{1,0:T(8,128)(2,1)S(1)}, u32[]{:S(2)}, u32[]{:S(2)}) collective-permute-start(bf16[128,2048]{1,0:T(8,128)(2,1)S(1)} %multiply_convert_fusion.1.refs_0_.refs_4_), channel_id=1, source_target_pairs={{0,12},{2,14},{4,0},{6,2},{8,4},{10,6},{12,8},{14,10},{1,13},{3,15... | collective-permute-start | bytes 1572872 | tf_op jit(solution)/shard_map/ppermute | solution.py:54
  121.3 22.9 %copy-start.16 = (bf16[128,2176]{1,0:T(8,128)(2,1)}, bf16[128,2176]{1,0:T(8,128)(2,1)S(1)}, u32[]{:S(2)}) copy-start(bf16[128,2176]{1,0:T(8,128)(2,1)S(1)} %collective-permute-done.19.refs_5_.refs_17_) | copy-start | bytes 1671172
  121.3 48.7 %collective-permute-start.20 = (bf16[128,2176]{1,0:T(8,128)(2,1)}, bf16[128,2176]{1,0:T(8,128)(2,1)S(1)}, u32[]{:S(2)}, u32[]{:S(2)}) collective-permute-start(bf16[128,2176]{1,0:T(8,128)(2,1)} %collective-permute-done.9.refs_7_.refs_15_), channel_id=1, source_target_pairs={{0,12},{2,14},{4,0},{6,2},{8,4},{10,6},{12,8},{14,10},{1,13},{3,15... | collective-permute-start | bytes 1671176 | tf_op jit(solution)/shard_map/ppermute | solution.py:54
  132.4 37.6 %copy-start.18 = (bf16[128,2048]{1,0:T(8,128)(2,1)}, bf16[128,2048]{1,0:T(8,128)(2,1)S(1)}, u32[]{:S(2)}) copy-start(bf16[128,2048]{1,0:T(8,128)(2,1)S(1)} %collective-permute-done.15.refs_0_.refs_8_) | copy-start | bytes 1572868
  132.4 37.6 %collective-permute-start.21 = (bf16[128,2176]{1,0:T(8,128)(2,1)}, bf16[128,2176]{1,0:T(8,128)(2,1)}, u32[]{:S(2)}, u32[]{:S(2)}) collective-permute-start(bf16[128,2176]{1,0:T(8,128)(2,1)} %copy-done.15), channel_id=1, source_target_pairs={{0,2},{2,0},{4,6},{6,4},{8,10},{10,8},{12,14},{14,12},{1,3},{3,1},... | collective-permute-start | bytes 1671176 | tf_op jit(solution)/shard_map/ppermute | solution.py:58
  133.5 36.5 %collective-permute-start.16 = (bf16[128,2048]{1,0:T(8,128)(2,1)}, bf16[128,2048]{1,0:T(8,128)(2,1)}, u32[]{:S(2)}, u32[]{:S(2)}) collective-permute-start(bf16[128,2048]{1,0:T(8,128)(2,1)} %collective-permute-done.14.refs_3_.refs_7_), channel_id=1, source_target_pairs={{0,4},{2,6},{4,8},{6,10},{8,12},{10,14},{12,0},{14,2},{1,5},{3,7},... | collective-permute-start | bytes 1572872 | tf_op jit(solution)/shard_map/ppermute | solution.py:50
  141.2 28.8 %collective-permute-start.17 = (bf16[128,2048]{1,0:T(8,128)(2,1)}, bf16[128,2048]{1,0:T(8,128)(2,1)}, u32[]{:S(2)}, u32[]{:S(2)}) collective-permute-start(bf16[128,2048]{1,0:T(8,128)(2,1)} %collective-permute-done.14.refs_3_.refs_7_), channel_id=1, source_target_pairs={{0,12},{2,14},{4,0},{6,2},{8,4},{10,6},{12,8},{14,10},{1,13},{3,15... | collective-permute-start | bytes 1572872 | tf_op jit(solution)/shard_map/ppermute | solution.py:54
  145.0 25.0 %collective-permute-start.18 = (bf16[128,2048]{1,0:T(8,128)(2,1)S(1)}, bf16[128,2048]{1,0:T(8,128)(2,1)}, u32[]{:S(2)}, u32[]{:S(2)}) collective-permute-start(bf16[128,2048]{1,0:T(8,128)(2,1)S(1)} %collective-permute-done.15.refs_0_.refs_8_), channel_id=1, source_target_pairs={{0,2},{2,0},{4,6},{6,4},{8,10},{10,8},{12,14},{14,12},{1,3},{3,1},... | collective-permute-start | bytes 1572872 | tf_op jit(solution)/shard_map/ppermute | solution.py:58
  213.3 175.0 %reduce-scatter.8.cloned.1.call-start = ((), (), s32[]{:S(2)}) async-start(), calls=%async_computation.10 | async-start | bytes 4718592 | tf_op jit(solution)/shard_map/reduce_scatter | solution.py:848
  213.3 22.5 %collective-permute-start.22 = (bf16[128,4224]{1,0:T(8,128)(2,1)}, bf16[128,4224]{1,0:T(8,128)(2,1)S(1)}, u32[]{:S(2)}, u32[]{:S(2)}) collective-permute-start(bf16[128,4224]{1,0:T(8,128)(2,1)} %get-tuple-element.65), channel_id=1, source_target_pairs={{0,2},{2,0},{4,6},{6,4},{8,10},{10,8},{12,14},{14,12},{1,3},{3,1},... | collective-permute-start | bytes 3244040 | tf_op jit(solution)/shard_map/ppermute | solution.py:58
  214.1 27.0 %collective-permute-start.25 = (bf16[128,4224]{1,0:T(8,128)(2,1)}, bf16[128,4224]{1,0:T(8,128)(2,1)S(1)}, u32[]{:S(2)}, u32[]{:S(2)}) collective-permute-start(bf16[128,4224]{1,0:T(8,128)(2,1)} %get-tuple-element.68), channel_id=1, source_target_pairs={{0,12},{2,14},{4,0},{6,2},{8,4},{10,6},{12,8},{14,10},{1,13},{3,15... | collective-permute-start | bytes 3244040 | tf_op jit(solution)/shard_map/ppermute | solution.py:54
  215.0 28.2 %collective-permute-start.24 = (bf16[128,4224]{1,0:T(8,128)(2,1)}, bf16[128,4224]{1,0:T(8,128)(2,1)S(1)}, u32[]{:S(2)}, u32[]{:S(2)}) collective-permute-start(bf16[128,4224]{1,0:T(8,128)(2,1)} %get-tuple-element.67), channel_id=1, source_target_pairs={{0,4},{2,6},{4,8},{6,10},{8,12},{10,14},{12,0},{14,2},{1,5},{3,7},... | collective-permute-start | bytes 3244040 | tf_op jit(solution)/shard_map/ppermute | solution.py:50
  216.1 71.0 %collective-permute-start.27 = (bf16[128,4224]{1,0:T(8,128)(2,1)}, bf16[128,4224]{1,0:T(8,128)(2,1)}, u32[]{:S(2)}, u32[]{:S(2)}) collective-permute-start(bf16[128,4224]{1,0:T(8,128)(2,1)} %get-tuple-element.69), channel_id=1, source_target_pairs={{0,4},{2,6},{4,8},{6,10},{8,12},{10,14},{12,0},{14,2},{1,5},{3,7},... | collective-permute-start | bytes 3244040 | tf_op jit(solution)/shard_map/ppermute | solution.py:50
  216.4 70.7 %collective-permute-start.28 = (bf16[128,4224]{1,0:T(8,128)(2,1)}, bf16[128,4224]{1,0:T(8,128)(2,1)}, u32[]{:S(2)}, u32[]{:S(2)}) collective-permute-start(bf16[128,4224]{1,0:T(8,128)(2,1)} %get-tuple-element.70), channel_id=1, source_target_pairs={{0,12},{2,14},{4,0},{6,2},{8,4},{10,6},{12,8},{14,10},{1,13},{3,15... | collective-permute-start | bytes 3244040 | tf_op jit(solution)/shard_map/ppermute | solution.py:54
  238.3 48.8 %collective-permute-start.23 = (bf16[128,4224]{1,0:T(8,128)(2,1)}, bf16[128,4224]{1,0:T(8,128)(2,1)}, u32[]{:S(2)}, u32[]{:S(2)}) collective-permute-start(bf16[128,4224]{1,0:T(8,128)(2,1)} %add_convert_fusion.1), channel_id=1, source_target_pairs={{0,8},{2,10},{4,12},{6,14},{8,0},{10,2},{12,4},{14,6},{1,9},{3,11}... | collective-permute-start | bytes 3244040 | tf_op jit(solution)/shard_map/ppermute | solution.py:69
  244.6 42.5 %collective-permute-start.26 = (bf16[128,4224]{1,0:T(8,128)(2,1)}, bf16[128,4224]{1,0:T(8,128)(2,1)}, u32[]{:S(2)}, u32[]{:S(2)}) collective-permute-start(bf16[128,4224]{1,0:T(8,128)(2,1)} %add_convert_fusion), channel_id=1, source_target_pairs={{0,2},{2,0},{4,6},{6,4},{8,10},{10,8},{12,14},{14,12},{1,3},{3,1},... | collective-permute-start | bytes 3244040 | tf_op jit(solution)/shard_map/ppermute | solution.py:58
  292.3 11.3 %collective-permute-start.29 = (bf16[128,2176]{1,0:T(8,128)(2,1)}, bf16[128,2176]{1,0:T(8,128)(2,1)S(1)}, u32[]{:S(2)}, u32[]{:S(2)}) collective-permute-start(bf16[128,2176]{1,0:T(8,128)(2,1)} %slice.203), channel_id=1, source_target_pairs={{0,1},{1,0},{2,3},{3,2},{4,5},{5,4},{6,7},{7,6},{8,9},{9,8},{10,11... | collective-permute-start | bytes 1671176 | tf_op jit(solution)/shard_map/ppermute | solution.py:141
  313.5 37.3 %collective-permute-start.30 = (bf16[3168,256]{1,0:T(8,128)(2,1)}, bf16[3168,256]{1,0:T(8,128)(2,1)}, u32[]{:S(2)}, u32[]{:S(2)}) collective-permute-start(bf16[3168,256]{1,0:T(8,128)(2,1)} %bitcast.119), channel_id=1, source_target_pairs={{0,4},{2,6},{4,8},{6,10},{8,12},{10,14},{12,0},{14,2},{1,5},{3,7},... | collective-permute-start | bytes 4866056 | tf_op jit(solution)/shard_map/ppermute | solution.py:50
  313.6 37.2 %collective-permute-start.31 = (bf16[3168,256]{1,0:T(8,128)(2,1)}, bf16[3168,256]{1,0:T(8,128)(2,1)}, u32[]{:S(2)}, u32[]{:S(2)}) collective-permute-start(bf16[3168,256]{1,0:T(8,128)(2,1)} %bitcast.120), channel_id=1, source_target_pairs={{0,12},{2,14},{4,0},{6,2},{8,4},{10,6},{12,8},{14,10},{1,13},{3,15... | collective-permute-start | bytes 4866056 | tf_op jit(solution)/shard_map/ppermute | solution.py:54
  316.8 34.0 %collective-permute-start.32 = (bf16[3168,256]{1,0:T(8,128)(2,1)}, bf16[3168,256]{1,0:T(8,128)(2,1)}, u32[]{:S(2)}, u32[]{:S(2)}) collective-permute-start(bf16[3168,256]{1,0:T(8,128)(2,1)} %bitcast.121), channel_id=1, source_target_pairs={{0,2},{2,0},{4,6},{6,4},{8,10},{10,8},{12,14},{14,12},{1,3},{3,1},... | collective-permute-start | bytes 4866056 | tf_op jit(solution)/shard_map/ppermute | solution.py:58
  323.4 27.4 %all-to-all-start.1 = ((bf16[8,128,128]{2,1,0:T(8,128)(2,1)}), bf16[8,128,128]{2,1,0:T(8,128)(2,1)S(1)}, u32[]{:S(2)}, u32[]{:S(2)}) async-start(bf16[8,128,128]{2,1,0:T(8,128)(2,1)} %bitcast_bitcast_fusion.1), calls=%async_computation.1 | async-start | bytes 524288 | tf_op jit(solution)/shard_map/all_to_all | solution.py:841
  326.8 142.0 %reduce-scatter.6.cloned.1.call-start = ((), (), s32[]{:S(2)}) async-start(), calls=%async_computation.9 | async-start | bytes 2359296 | tf_op jit(solution)/shard_map/reduce_scatter | solution.py:872
  365.3 59.0 %collective-permute-start.36 = (bf16[3168,256]{1,0:T(8,128)(2,1)}, bf16[3168,256]{1,0:T(8,128)(2,1)}, u32[]{:S(2)}, u32[]{:S(2)}) collective-permute-start(bf16[3168,256]{1,0:T(8,128)(2,1)} %collective-permute-done.32.refs_3_), channel_id=1, source_target_pairs={{0,4},{2,6},{4,8},{6,10},{8,12},{10,14},{12,0},{14,2},{1,5},{3,7},... | collective-permute-start | bytes 4866056 | tf_op jit(solution)/shard_map/ppermute | solution.py:50
  366.1 58.1 %collective-permute-start.37 = (bf16[3168,256]{1,0:T(8,128)(2,1)}, bf16[3168,256]{1,0:T(8,128)(2,1)}, u32[]{:S(2)}, u32[]{:S(2)}) collective-permute-start(bf16[3168,256]{1,0:T(8,128)(2,1)} %collective-permute-done.32.refs_3_), channel_id=1, source_target_pairs={{0,12},{2,14},{4,0},{6,2},{8,4},{10,6},{12,8},{14,10},{1,13},{3,15... | collective-permute-start | bytes 4866056 | tf_op jit(solution)/shard_map/ppermute | solution.py:54
  371.1 42.5 %all-to-all-start.2 = ((bf16[8,128,384]{1,2,0:T(8,128)(2,1)}), bf16[8,128,384]{1,2,0:T(8,128)(2,1)S(1)}, u32[]{:S(2)}, u32[]{:S(2)}) async-start(bf16[8,128,384]{1,2,0:T(8,128)(2,1)} %copy.193), calls=%async_computation.3 | async-start | bytes 1572864 | tf_op jit(solution)/shard_map/all_to_all | solution.py:852
  376.7 47.5 %collective-permute-start.34 = (bf16[1584,256]{1,0:T(8,128)(2,1)}, bf16[1584,256]{1,0:T(8,128)(2,1)}, u32[]{:S(2)}, u32[]{:S(2)}) collective-permute-start(bf16[1584,256]{1,0:T(8,128)(2,1)} %slice.154), channel_id=1, source_target_pairs={{0,4},{2,6},{4,8},{6,10},{8,12},{10,14},{12,0},{14,2},{1,5},{3,7},... | collective-permute-start | bytes 2433032 | tf_op jit(solution)/shard_map/ppermute | solution.py:50
  380.7 43.5 %collective-permute-start.35 = (bf16[1584,256]{1,0:T(8,128)(2,1)}, bf16[1584,256]{1,0:T(8,128)(2,1)}, u32[]{:S(2)}, u32[]{:S(2)}) collective-permute-start(bf16[1584,256]{1,0:T(8,128)(2,1)} %slice.155), channel_id=1, source_target_pairs={{0,12},{2,14},{4,0},{6,2},{8,4},{10,6},{12,8},{14,10},{1,13},{3,15... | collective-permute-start | bytes 2433032 | tf_op jit(solution)/shard_map/ppermute | solution.py:54
  383.9 56.4 %collective-permute-start.33 = (bf16[128,2048]{1,0:T(8,128)(2,1)S(1)}, bf16[128,2048]{1,0:T(8,128)(2,1)}, u32[]{:S(2)}, u32[]{:S(2)}) collective-permute-start(bf16[128,2048]{1,0:T(8,128)(2,1)S(1)} %slice.147), channel_id=1, source_target_pairs={{0,1},{1,0},{2,3},{3,2},{4,5},{5,4},{6,7},{7,6},{8,9},{9,8},{10,11... | collective-permute-start | bytes 1572872 | tf_op jit(solution)/shard_map/ppermute | solution.py:141
  437.7 29.5 %collective-permute-start.38 = (bf16[128,2048]{1,0:T(8,128)(2,1)}, bf16[128,2048]{1,0:T(8,128)(2,1)}, u32[]{:S(2)}, u32[]{:S(2)}) collective-permute-start(bf16[128,2048]{1,0:T(8,128)(2,1)} %first_back.1), channel_id=1, source_target_pairs={{0,1},{1,0},{2,3},{3,2},{4,5},{5,4},{6,7},{7,6},{8,9},{9,8},{10,11... | collective-permute-start | bytes 1572872 | tf_op jit(solution)/shard_map/ppermute | solution.py:141
  442.4 24.8 %all-to-all-start.3 = ((bf16[8,256,128]{2,1,0:T(8,128)(2,1)}), bf16[8,256,128]{2,1,0:T(8,128)(2,1)S(1)}, u32[]{:S(2)}, u32[]{:S(2)}) async-start(bf16[8,256,128]{2,1,0:T(8,128)(2,1)} %bitcast_bitcast_fusion), calls=%async_computation.6 | async-start | bytes 1048576 | tf_op jit(solution)/shard_map/all_to_all | solution.py:874
  451.6 31.3 %collective-permute-start.48 = (bf16[1584,256]{1,0:T(8,128)(2,1)}, bf16[1584,256]{1,0:T(8,128)(2,1)}, u32[]{:S(2)}, u32[]{:S(2)}) collective-permute-start(bf16[1584,256]{1,0:T(8,128)(2,1)} %slice.164), channel_id=1, source_target_pairs={{0,12},{2,14},{4,0},{6,2},{8,4},{10,6},{12,8},{14,10},{1,13},{3,15... | collective-permute-start | bytes 2433032 | tf_op jit(solution)/shard_map/ppermute | solution.py:54
  458.0 30.0 %collective-permute-start.47 = (bf16[1584,256]{1,0:T(8,128)(2,1)}, bf16[1584,256]{1,0:T(8,128)(2,1)}, u32[]{:S(2)}, u32[]{:S(2)}) collective-permute-start(bf16[1584,256]{1,0:T(8,128)(2,1)} %slice.163), channel_id=1, source_target_pairs={{0,4},{2,6},{4,8},{6,10},{8,12},{10,14},{12,0},{14,2},{1,5},{3,7},... | collective-permute-start | bytes 2433032 | tf_op jit(solution)/shard_map/ppermute | solution.py:50
  469.8 5.2 collective-permute-start.39
  476.3 14.8 %collective-permute-start.42 = (bf16[256,640]{1,0:T(8,128)(2,1)S(1)}, bf16[256,640]{1,0:T(8,128)(2,1)S(1)}, u32[]{:S(2)}, u32[]{:S(2)}) collective-permute-start(bf16[256,640]{1,0:T(8,128)(2,1)S(1)} %pad_maximum_fusion.2.refs_0_), channel_id=1, source_target_pairs={{0,8},{2,10},{4,12},{6,14},{8,0},{10,2},{12,4},{14,6},{1,9},{3,11}... | collective-permute-start | bytes 983048 | tf_op jit(solution)/shard_map/ppermute | solution.py:69
  478.6 9.2 %collective-permute-start.43 = (bf16[256,640]{1,0:T(8,128)(2,1)S(1)}, bf16[256,640]{1,0:T(8,128)(2,1)S(1)}, u32[]{:S(2)}, u32[]{:S(2)}) collective-permute-start(bf16[256,640]{1,0:T(8,128)(2,1)S(1)} %pad_maximum_fusion.2.refs_0_), channel_id=1, source_target_pairs={{0,2},{2,0},{4,6},{6,4},{8,10},{10,8},{12,14},{14,12},{1,3},{3,1},... | collective-permute-start | bytes 983048 | tf_op jit(solution)/shard_map/ppermute | solution.py:58
  481.1 28.0 %collective-permute-start.40 = (bf16[256,640]{1,0:T(8,128)(2,1)S(1)}, bf16[256,640]{1,0:T(8,128)(2,1)S(1)}, u32[]{:S(2)}, u32[]{:S(2)}) collective-permute-start(bf16[256,640]{1,0:T(8,128)(2,1)S(1)} %pad_maximum_fusion.2.refs_0_), channel_id=1, source_target_pairs={{0,4},{2,6},{4,8},{6,10},{8,12},{10,14},{12,0},{14,2},{1,5},{3,7},... | collective-permute-start | bytes 983048 | tf_op jit(solution)/shard_map/ppermute | solution.py:50
  482.9 26.3 %collective-permute-start.41 = (bf16[256,640]{1,0:T(8,128)(2,1)S(1)}, bf16[256,640]{1,0:T(8,128)(2,1)S(1)}, u32[]{:S(2)}, u32[]{:S(2)}) collective-permute-start(bf16[256,640]{1,0:T(8,128)(2,1)S(1)} %pad_maximum_fusion.2.refs_0_), channel_id=1, source_target_pairs={{0,12},{2,14},{4,0},{6,2},{8,4},{10,6},{12,8},{14,10},{1,13},{3,15... | collective-permute-start | bytes 983048 | tf_op jit(solution)/shard_map/ppermute | solution.py:54
  487.8 21.3 %collective-permute-start.44 = (bf16[256,640]{1,0:T(8,128)(2,1)S(1)}, bf16[256,640]{1,0:T(8,128)(2,1)S(1)}, u32[]{:S(2)}, u32[]{:S(2)}) collective-permute-start(bf16[256,640]{1,0:T(8,128)(2,1)S(1)} %collective-permute-done.43.refs_4_), channel_id=1, source_target_pairs={{0,4},{2,6},{4,8},{6,10},{8,12},{10,14},{12,0},{14,2},{1,5},{3,7},... | collective-permute-start | bytes 983048 | tf_op jit(solution)/shard_map/ppermute | solution.py:50
  488.1 21.1 %collective-permute-start.45 = (bf16[256,640]{1,0:T(8,128)(2,1)S(1)}, bf16[256,640]{1,0:T(8,128)(2,1)S(1)}, u32[]{:S(2)}, u32[]{:S(2)}) collective-permute-start(bf16[256,640]{1,0:T(8,128)(2,1)S(1)} %collective-permute-done.43.refs_4_), channel_id=1, source_target_pairs={{0,12},{2,14},{4,0},{6,2},{8,4},{10,6},{12,8},{14,10},{1,13},{3,15... | collective-permute-start | bytes 983048 | tf_op jit(solution)/shard_map/ppermute | solution.py:54
  491.0 18.1 %collective-permute-start.46 = (bf16[256,640]{1,0:T(8,128)(2,1)S(1)}, bf16[256,640]{1,0:T(8,128)(2,1)S(1)}, u32[]{:S(2)}, u32[]{:S(2)}) collective-permute-start(bf16[256,640]{1,0:T(8,128)(2,1)S(1)} %collective-permute-done.42.refs_3_), channel_id=1, source_target_pairs={{0,2},{2,0},{4,6},{6,4},{8,10},{10,8},{12,14},{14,12},{1,3},{3,1},... | collective-permute-start | bytes 983048 | tf_op jit(solution)/shard_map/ppermute | solution.py:58
  (43 other events, 250.2 us)
Sparse Core Ops, SparseCore 0:
  13.1 43.5 all-gather.5
  59.8 70.4 all-gather.7
  132.0 67.7 all-gather.9
  213.4 74.7 reduce-scatter.3
  313.6 38.3 reduce-scatter.7
  365.4 33.4 reduce-scatter.5

commit v3 on v2

--- a/solution.py
+++ b/solution.py
@@ -741,7 +741,11 @@
     small_rows = jnp.pad(gate_rows, ((0, 16 - experts - 1), (0, 0)))
     x_first = gather_first(inputs)
     x_second = gather_second(x_first)
-    here_late = after(here, (x_first, x_second))
+    grad_own = low(wide(grad_out) * valid)
+    grad_pack = jnp.concatenate(
+        [grad_own, jnp.pad(low(chosen), ((0, 0), (0, 128 - experts)))], axis=1
+    )
+    here_late = after(here, (x_first, x_second, grad_pack, block_places))
     shared_start = here_late * shared_units
     shared_gu = lax.dynamic_slice(w_sgu, (0, 0, shared_start), (shard, 2, shared_units))
     shared_gu = shared_gu.transpose(1, 2, 0)
@@ -759,12 +763,8 @@
     )
 
     cosine, sine = rotary_tables(rows * 8, head_size)
-    grad_own = low(wide(grad_out) * valid)
     hidden_in = wide(inputs)
     x_blocks = gather_blocks(inputs, x_first, x_second)
-    grad_pack = jnp.concatenate(
-        [grad_own, jnp.pad(low(chosen), ((0, 0), (0, 128 - experts)))], axis=1
-    )
     grad_pack = after(grad_pack, x_second)
     g_first = gather_first(grad_pack)
     g_second = gather_second(g_first)
@@ -849,6 +849,9 @@
         low(dot_columns(grad_branch, attended_own)), "fsdp", scatter_dimension=0, tiled=True
     )
     grad_proj, grad_bias = attend_back(queries, keys, values, grad_heads, cosine, sine)
+    out_parts = out_part.reshape(shard, heads, head_size).transpose(1, 0, 2)
+    out_parts = lax.all_to_all(after(out_parts, grad_proj), "ctx", 0, 0, tiled=True)
+    grad_w_o_here = low(jnp.sum(wide(out_parts), axis=0))
     proj_own = lax.all_to_all(
         grad_proj.reshape(8, rows, 3 * head_size), "ctx", 0, 0, tiled=True
     )
@@ -858,36 +861,18 @@
     small_grads = low(jnp.concatenate([grad_both, grad_gain_second[:, None], bias_rows], axis=1))
     small_grads = jnp.pad(small_grads, ((0, 0), (0, 128 - small_grads.shape[1])))
     last_part = jnp.concatenate([grad_qkv_here, small_grads], axis=1)
-    proj_own = after(proj_own, (last_part, unit_second))
+    proj_own = after(proj_own, (last_part, unit_second, grad_w_o_here))
     proj_own = proj_own.reshape(8, rows, 3, head_size).transpose(2, 1, 0, 3)
     proj_own = proj_own.reshape(3, rows, heads * head_size)
     first_part = first_back(proj_own, weight_qkv_all)
-    grad_first = after(add_halves(first_part), result)
-    unit_third = large_third(unit_second)
-    factor_first = inverse_rms(hidden_in)
-    weighted = grad_first * gain_first
-    inner = jnp.mean(weighted * hidden_in, axis=-1, keepdims=True)
-    grad_input = grad_middle + weighted * factor_first - hidden_in * factor_first**3 * inner
-
     last_pack = lax.psum_scatter(last_part, "fsdp", scatter_dimension=0, tiled=True)
-    out_parts = out_part.reshape(shard, heads, head_size).transpose(1, 0, 2)
-    out_parts = lax.all_to_all(after(out_parts, unit_second), "ctx", 0, 0, tiled=True)
-    grad_w_o_here = low(jnp.sum(wide(out_parts), axis=0))
-    unit_blocks = large_blocks(unit_grads, unit_first, unit_second, unit_third)
-    early, late = (0, 1, 2, 4), (3, 5, 6, 7)
-    placed = ()
-    for half in (early, late):
-        block_half = after(block_places, unit_second)[jnp.array(half)]
-        placed = place_units(block_half, pick(unit_blocks, half), expert_units, placed)
-    grad_egu, grad_edown, shared_grads = placed
-    grad_w_sgu, grad_w_sdown = flip(shared_grads.reshape(3, 8 * shared_units, shard))
     weights_here = lax.dynamic_slice(
         w_qkv, (0, 0, here * head_size), (shard, 3, head_size)
     ).reshape(shard, 3 * head_size)
     products = jnp.sum(wide(weights_here) * wide(last_pack[:, : 3 * head_size]), axis=1)
     products = products + lax.ppermute(products, "tp", [(0, 1), (1, 0)])
     spare = 3 * head_size + experts + 3
-    last_blocks = gather_relative(
+    last_block = (
         jnp.concatenate(
             [
                 last_pack[:, :spare],
@@ -898,6 +883,23 @@
             axis=1,
         )
     )
+    last_first = gather_first(last_block)
+    unit_third = large_third(unit_second)
+    grad_first = after(add_halves(after(first_part, last_first)), (result, unit_third))
+    last_blocks = gather_blocks(last_block, last_first, gather_second(last_first))
+    factor_first = inverse_rms(hidden_in)
+    weighted = grad_first * gain_first
+    inner = jnp.mean(weighted * hidden_in, axis=-1, keepdims=True)
+    grad_input = grad_middle + weighted * factor_first - hidden_in * factor_first**3 * inner
+
+    unit_blocks = large_blocks(unit_grads, unit_first, unit_second, unit_third)
+    early, late = (0, 1, 2, 4), (3, 5, 6, 7)
+    placed = ()
+    for half in (early, late):
+        block_half = after(block_places, unit_second)[jnp.array(half)]
+        placed = place_units(block_half, pick(unit_blocks, half), expert_units, placed)
+    grad_egu, grad_edown, shared_grads = placed
+    grad_w_sgu, grad_w_sdown = flip(shared_grads.reshape(3, 8 * shared_units, shard))
     grad_qkv, grad_w_o, small_sums = place_last(block_places, last_blocks)
     grad_w_qkv = grad_qkv.transpose(1, 0, 2)
     summed = jnp.sum(small_sums[:, :, : experts + 4], axis=0)

time: 535 us -> 508 us (0.950)
  waiting for transfers between devices: 186 us -> 154 us
    ppermute x14, waiting for transfers between devices: 79.5 us -> 53.9 us  [up(): return lax.ppermute(values, 'ctx', ring(2))]
    all_to_all x1, waiting for transfers between devices: 23.4 us -> 0.01 us  [body(): lax.all_to_all(grad_proj.reshape(8, rows, 3 * head_size), 'ctx', 0, 0, ti...]
    all_to_all x1, waiting for transfers between devices: 0.01 us -> 17.2 us  [body(): lax.all_to_all(after(out_parts, grad_proj), 'ctx', 0, 0, tiled=True)]
    ppermute x5, waiting for transfers between devices: 10.7 us -> 16.9 us  [across(): return lax.ppermute(values, 'ctx', ring(4))]
    unnamed x112 -> x110, local copies, waits for them, and re-layouts: 12.4 us -> 11.8 us
  transfers between devices with their start and end apart: 58 -> 58, of which waited for: 19 -> 15; matrix products, arithmetic and copies ran while one was open for 14% -> 17% of each run, Pallas kernels for 24% -> 26%
where the time goes in v3:
time: 508 us; the launch traced here: 501 us
  waiting for transfers between devices  154 us (30%)
  Pallas kernels  131 us (26%)
  starting transfers between devices  90.1 us (18%)
  local copies, waits for them, and re-layouts  50.3 us (10%)
  other arithmetic  37 us (7%)
  between operations  15.6 us (3%)
  blocking collectives  11.7 us (2%)
  matrix products  10.3 us (2%)
    ppermute x14, waiting for transfers between devices, up(): return lax.ppermute(values, 'ctx', ring(2))  53.9 us
    pallas_call x2, Pallas kernels, units_forward_back(): pl.pallas_call(units_kernel, in_specs=[anywhere] * 8 + [vmem] * 2 + [anyw...  44.8 us
    ppermute x14, starting transfers between devices, down(): return lax.ppermute(values, 'ctx', ring(-2))  27 us
    ppermute x11, waiting for transfers between devices, swap(): return lax.ppermute(values, 'ctx', PAIR)  24.8 us
    all_to_all x1, waiting for transfers between devices, body(): lax.all_to_all(grad_attended.reshape(rows, heads, head_size).transpose(1,...  21 us
    pallas_call x1, Pallas kernels, outer_products(): pl.pallas_call(outer_kernel, grid=(4,), in_specs=[whole(value) for value...  19.9 us
    all_to_all x1, waiting for transfers between devices, body(): lax.all_to_all(after(out_parts, grad_proj), 'ctx', 0, 0, tiled=True)  17.2 us
    ppermute x14, starting transfers between devices, up(): return lax.ppermute(values, 'ctx', ring(2))  17.1 us
  transfers between devices with their start and end apart: 58, of which 15 were waited for; matrix products, arithmetic and copies ran while one was open for 17% of the time, Pallas kernels for 26%

profile of v3, /device:TPU:0, one launch (start us, length us, event | category | flops | bytes accessed | tf_op | source)
XLA Modules:
  0.0 500.6 jit_solution(11249250149163694493)
XLA Ops:
  10.9 2.1 pack.1
  16.4 1.9 collective-permute-start.2
  21.2 2.0 multiply_convert_fusion.2
  23.2 8.0 %collective-permute-done.3.refs_4_ = bf16[128,2048]{1,0:T(8,128)(2,1)} collective-permute-done((bf16[128,2048]{1,0:T(8,128)(2,1)S(1)}, bf16[128,2048]{1,0:T(8,128)(2,1)}, u32[]{:S(2)}, u32[]{:S(2)}) %collective-permute-start.3) | collective-permute-done | bytes 524320 | tf_op jit(solution)/shard_map/ppermute | solution.py:58
  31.8 2.6 collective-permute-start.5
  34.4 7.2 %collective-permute-done.2.refs_3_ = bf16[128,2048]{1,0:T(8,128)(2,1)} collective-permute-done((bf16[128,2048]{1,0:T(8,128)(2,1)S(1)}, bf16[128,2048]{1,0:T(8,128)(2,1)}, u32[]{:S(2)}, u32[]{:S(2)}) %collective-permute-start.2) | collective-permute-done | bytes 524320 | tf_op jit(solution)/shard_map/ppermute | solution.py:69
  44.0 1.9 fusion.8.refs_4_.refs_12_
  45.9 5.7 %collective-permute-done.4.refs_5_ = bf16[128,2048]{1,0:T(8,128)(2,1)} collective-permute-done((bf16[128,2048]{1,0:T(8,128)(2,1)}, bf16[128,2048]{1,0:T(8,128)(2,1)}, u32[]{:S(2)}, u32[]{:S(2)}) %collective-permute-start.4) | collective-permute-done | bytes 524320 | tf_op jit(solution)/shard_map/ppermute | solution.py:50
  51.7 1.9 collective-permute-done.6.refs_7_
  61.3 2.3 collective-permute-start.8
  67.9 12.5 %attend.1 = (bf16[1024,128]{1,0:T(8,128)(2,1)}, bf16[1024,128]{1,0:T(8,128)(2,1)}, bf16[1024,128]{1,0:T(8,128)(2,1)}, bf16[1024,128]{1,0:T(8,128)(2,1)}, bf16[1024,2048]{1,0:T(8,128)(2,1)}) custom-call(s32[8]{0:T(128)} %stack.39.places_ref, bf16[128,2048]{1,0:T(8,128)(2,1)} %refs_0_.1, bf16[128,2048]{1,0:T(8,128)(2,1)} %collective-permute-done.refs_1_, ...), custom_call_target="tpu_custom_call" | custom-call | flops 9000000 | bytes 12000 | tf_op jit(solution)/shard_map/attend/pallas_call | solution.py:217
  80.4 11.7 %all_to_all.34 = bf16[8,128,128]{2,1,0:T(8,128)(2,1)S(1)} all-to-all(bf16[8,128,128]{2,1,0:T(8,128)(2,1)} %bitcast.134), channel_id=1, replica_groups=mesh['fsdp'=8,'ctx'=8,'tp'=2] {'ctx'}, dimensions={0} | all-to-all | bytes 524288 | tf_op jit(solution)/shard_map/all_to_all | solution.py:775
  92.9 4.9 branch.1
  97.9 3.1 collective-permute-start.11
  101.2 8.4 %collective-permute-done.11 = bf16[128,2048]{1,0:T(8,128)(2,1)S(1)} collective-permute-done((bf16[128,2048]{1,0:T(8,128)(2,1)}, bf16[128,2048]{1,0:T(8,128)(2,1)S(1)}, u32[]{:S(2)}, u32[]{:S(2)}) %collective-permute-start.11) | collective-permute-done | bytes 524320 | tf_op jit(solution)/shard_map/ppermute | solution.py:141
  114.0 2.4 collective-permute-start.12
  118.7 9.7 %collective-permute-done.15.refs_0_.refs_8_ = bf16[128,2048]{1,0:T(8,128)(2,1)} collective-permute-done((bf16[128,2048]{1,0:T(8,128)(2,1)S(1)}, bf16[128,2048]{1,0:T(8,128)(2,1)}, u32[]{:S(2)}, u32[]{:S(2)}) %collective-permute-start.15) | collective-permute-done | bytes 524320 | tf_op jit(solution)/shard_map/ppermute | solution.py:69
  130.5 6.5 %collective-permute-done.12.refs_1_.refs_5_ = bf16[128,2048]{1,0:T(8,128)(2,1)S(1)} collective-permute-done((bf16[128,2048]{1,0:T(8,128)(2,1)S(1)}, bf16[128,2048]{1,0:T(8,128)(2,1)S(1)}, u32[]{:S(2)}, u32[]{:S(2)}) %collective-permute-start.12) | collective-permute-done | bytes 524320 | tf_op jit(solution)/shard_map/ppermute | solution.py:50
  137.0 3.1 collective-permute-start.17
  143.6 22.3 %units.2 = (bf16[128,4224]{1,0:T(8,128)(2,1)}, bf16[128,4224]{1,0:T(8,128)(2,1)}, bf16[128,4224]{1,0:T(8,128)(2,1)}, bf16[128,4224]{1,0:T(8,128)(2,1)}, bf16[211...) custom-call(bf16[128,2048]{1,0:T(8,128)(2,1)} %copy-done.3, bf16[128,2048]{1,0:T(8,128)(2,1)} %copy-done.21, ...), custom_call_target="tpu_custom_call" | custom-call | flops 11000000 | bytes 20000 | tf_op jit(solution)/shard_map/units/pallas_call | solution.py:393
  167.0 22.5 %units.3 = (bf16[128,4224]{1,0:T(8,128)(2,1)}, bf16[128,4224]{1,0:T(8,128)(2,1)}, bf16[128,4224]{1,0:T(8,128)(2,1)}, bf16[128,4224]{1,0:T(8,128)(2,1)}, bf16[211...) custom-call(bf16[128,2048]{1,0:T(8,128)(2,1)} %collective-permute-done.15.refs_0_.refs_8_, ...), custom_call_target="tpu_custom_call" | custom-call | flops 11000000 | bytes 20000 | tf_op jit(solution)/shard_map/units/pallas_call | solution.py:393
  189.5 19.9 %outer.1 = bf16[8,3168,256]{2,1,0:T(8,128)(2,1)} custom-call(bf16[2112,512]{1,0:T(8,128)(2,1)} %get-tuple-element.72.refs_0_, bf16[2112,512]{1,0:T(8,128)(2,1)} %get-tuple-element.73.refs_1_, bf16[1056,512]{1,0:T(8,128)(2,1)} %get-tuple-element.63.refs_2_, bf16[1056,512]{1,0:T(8,128)(2,1)} %get-tuple-element.74.refs_3_, bf16[128,2048]{1,0:T(8,128)(2,1)} %copy-done.3, ...), custom_call_target="tpu_custom_call" | custom-call | flops 4429185 | bytes 10000 | tf_op jit(solution)/shard_map/outer/pallas_call | solution.py:451
  213.7 2.4 collective-permute-start.28
  216.1 14.8 %collective-permute-done.22 = bf16[128,4224]{1,0:T(8,128)(2,1)S(1)} collective-permute-done((bf16[128,4224]{1,0:T(8,128)(2,1)}, bf16[128,4224]{1,0:T(8,128)(2,1)S(1)}, u32[]{:S(2)}, u32[]{:S(2)}) %collective-permute-start.22) | collective-permute-done | bytes 1081376 | tf_op jit(solution)/shard_map/ppermute | solution.py:58
  231.0 2.6 add_convert_fusion.1
  234.7 3.1 collective-permute-done.25
  237.9 2.5 collective-permute-done.24
  243.5 39.0 %collective-permute-done.27 = bf16[128,4224]{1,0:T(8,128)(2,1)S(1)} collective-permute-done((bf16[128,4224]{1,0:T(8,128)(2,1)}, bf16[128,4224]{1,0:T(8,128)(2,1)S(1)}, u32[]{:S(2)}, u32[]{:S(2)}) %collective-permute-start.27) | collective-permute-done | bytes 1081376 | tf_op jit(solution)/shard_map/ppermute | solution.py:50
  283.5 3.3 convert_add_fusion
  287.8 2.9 collective-permute-start.29
  291.2 8.0 %collective-permute-done.29 = bf16[128,2176]{1,0:T(8,128)(2,1)} collective-permute-done((bf16[128,2176]{1,0:T(8,128)(2,1)}, bf16[128,2176]{1,0:T(8,128)(2,1)}, u32[]{:S(2)}, u32[]{:S(2)}) %collective-permute-start.29) | collective-permute-done | bytes 557088 | tf_op jit(solution)/shard_map/ppermute | solution.py:141
  303.3 1.8 multiply_reduce_fusion
  306.5 3.3 convolution_convert_fusion
  310.0 3.2 collective-permute-start.31
  313.5 4.6 branch_back.1
  319.8 3.4 all-to-all-start.1
  323.4 21.0 %all-to-all-done.1 = bf16[8,128,128]{2,1,0:T(8,128)(2,1)S(1)} async-done(((bf16[8,128,128]{2,1,0:T(8,128)(2,1)}), bf16[8,128,128]{2,1,0:T(8,128)(2,1)S(1)}, u32[]{:S(2)}, u32[]{:S(2)}) %all-to-all-start.1) | async-done | bytes 262176 | tf_op jit(solution)/shard_map/all_to_all | solution.py:841
  345.1 6.1 %attend_back.1 = (bf16[1024,384]{1,0:T(8,128)(2,1)}, f32[1,384]{1,0:T(1,128)}) custom-call(bf16[1024,128]{1,0:T(8,128)(2,1)} %get-tuple-element.82.q_ref, bf16[1024,128]{1,0:T(8,128)(2,1)} %get-tuple-element.83.k_ref, bf16[1024,128]{1,0:T(8,128)(2,1)} %get-tuple-element.84.v_ref, bf16[1024,128]{1,0:T(8,128)(2,1)} %bitcast.128, ...), custom_call_target="tpu_custom_call" | custom-call | flops 7000000 | bytes 6000 | tf_op jit(solution)/shard_map/attend_back/pallas_call | solution.py:264
  352.5 4.8 convolution_convert_fusion.1
  359.4 3.0 collective-permute-start.37
  364.2 1.9 slice.147
  366.1 1.9 bitcast_bitcast_fusion
  368.1 2.7 collective-permute-start.33
  370.7 4.1 all-to-all-start.3
  375.7 2.1 slice.154
  377.8 1.9 collective-permute-start.34
  379.7 2.1 slice.155
  383.1 1.9 copy.200
  385.7 2.3 copy.193
  388.0 17.2 %all-to-all-done.3 = bf16[8,256,128]{2,1,0:T(8,128)(2,1)} async-done(((bf16[8,256,128]{2,1,0:T(8,128)(2,1)}), bf16[8,256,128]{2,1,0:T(8,128)(2,1)}, u32[]{:S(2)}, u32[]{:S(2)}) %all-to-all-start.3) | async-done | bytes 524320 | tf_op jit(solution)/shard_map/all_to_all | solution.py:853
  405.3 5.0 all-to-all-start.2
  412.6 2.7 collective-permute-start.38
  415.2 2.2 multiply_convert_fusion
  418.5 2.0 collective-permute-start.44
  420.5 2.1 slice.160
  428.6 2.6 pad_maximum_fusion.refs_0_
  431.3 7.8 %place_units.2 = (f32[8,2,704,256]{3,2,1,0:T(8,128)}, f32[8,704,256]{2,1,0:T(8,128)}, bf16[3,8,352,256]{3,2,1,0:T(8,128)(2,1)}) custom-call(s32[4]{0:T(128)} %gather_fusion.1, bf16[3168,256]{1,0:T(8,128)(2,1)} %bitcast.121, bf16[3168,256]{1,0:T(8,128)(2,1)} %collective-permute-done.30.refs_1_, bf16[3168,256]{1,0:T(8,128)(2,1)} %collective-permute-done.31.refs_2_, ...), custom_call_target="tpu_custom_call" | custom-call | flops 1 | bytes 1 | tf_op jit(solution)/shard_map/place_units/pallas_call | solution.py:615
  443.0 10.1 %first_back.1 = bf16[128,2048]{1,0:T(8,128)(2,1)} custom-call(bf16[3,128,1024]{2,1,0:T(8,128)(2,1)} %reshape.197.left_ref, bf16[8,3,256,1024]{3,2,1,0:T(8,128)(2,1)} %bitcast.112), custom_call_target="tpu_custom_call" | custom-call | flops 1700000 | bytes 13000 | tf_op jit(solution)/shard_map/first_back/pallas_call | solution.py:544
  453.1 2.7 collective-permute-start.39
  460.8 2.6 pad_maximum_fusion.1.refs_3_
  463.5 7.9 %place_units.3 = (f32[8,2,704,256]{3,2,1,0:T(8,128)}, f32[8,704,256]{2,1,0:T(8,128)}, bf16[3,8,352,256]{3,2,1,0:T(8,128)(2,1)}) custom-call(s32[4]{0:T(128)} %gather_fusion, bf16[3168,256]{1,0:T(8,128)(2,1)} %pad_maximum_fusion.refs_0_, bf16[3168,256]{1,0:T(8,128)(2,1)} %copy-done.12, ...), custom_call_target="tpu_custom_call", output_to_operand_aliasing={{0}: (5, {}), {1}: (6, {}), {2}: (7, {})} | custom-call | flops 1 | bytes 1 | tf_op jit(solution)/shard_map/place_units/pallas_call | solution.py:615
  471.4 5.9 %flip.1 = (f32[256,2,2816]{2,1,0:T(2,128)}, f32[256,2816]{1,0:T(8,128)}) custom-call(bf16[256,256]{1,0:T(8,128)(2,1)} %fusion.11.one_ref, bf16[3,2816,256]{2,1,0:T(8,128)(2,1)} %bitcast.111), custom_call_target="tpu_custom_call" | custom-call | flops 1 | bytes 1 | tf_op jit(solution)/shard_map/flip/pallas_call | solution.py:653
  477.3 2.1 collective-permute-start.43
  481.0 4.6 place.1
  (289 shorter events, 93.7 us)
Async XLA Ops:
  7.2 46.4 %copy-start = (bf16[256,2,2816]{2,1,0:T(2,128)(2,1)S(1)}, bf16[256,2,2816]{2,1,0:T(2,128)(2,1)}, u32[]{:S(2)}) copy-start(bf16[256,2,2816]{2,1,0:T(2,128)(2,1)} %param.27) | copy-start | bytes 8650756
  7.2 58.2 %all-gather.6.cloned.1.call-start = ((), (), s32[]{:S(2)}) async-start(), calls=%async_computation.7 | async-start | bytes 7077888 | tf_op jit(solution)/shard_map/all_gather | solution.py:723
  13.0 130.6 %all-gather.8.cloned.1.call-start = ((), (), s32[]{:S(2)}) async-start(), calls=%async_computation.11 | async-start | bytes 14598144 | tf_op jit(solution)/shard_map/all_gather | solution.py:755
  13.1 32.9 %collective-permute-start = (bf16[128,2048]{1,0:T(8,128)(2,1)S(1)}, bf16[128,2048]{1,0:T(8,128)(2,1)}, u32[]{:S(2)}, u32[]{:S(2)}) collective-permute-start(bf16[128,2048]{1,0:T(8,128)(2,1)S(1)} %copy-done.5), channel_id=1, source_target_pairs={{0,4},{2,6},{4,8},{6,10},{8,12},{10,14},{12,0},{14,2},{1,5},{3,7},... | collective-permute-start | bytes 1572872 | tf_op jit(solution)/shard_map/ppermute | solution.py:50
  14.7 31.2 %collective-permute-start.1 = (bf16[128,2048]{1,0:T(8,128)(2,1)S(1)}, bf16[128,2048]{1,0:T(8,128)(2,1)}, u32[]{:S(2)}, u32[]{:S(2)}) collective-permute-start(bf16[128,2048]{1,0:T(8,128)(2,1)S(1)} %copy-done.5), channel_id=1, source_target_pairs={{0,12},{2,14},{4,0},{6,2},{8,4},{10,6},{12,8},{14,10},{1,13},{3,15... | collective-permute-start | bytes 1572872 | tf_op jit(solution)/shard_map/ppermute | solution.py:54
  16.4 25.2 %collective-permute-start.2 = (bf16[128,2048]{1,0:T(8,128)(2,1)S(1)}, bf16[128,2048]{1,0:T(8,128)(2,1)}, u32[]{:S(2)}, u32[]{:S(2)}) collective-permute-start(bf16[128,2048]{1,0:T(8,128)(2,1)S(1)} %copy-done.5), channel_id=1, source_target_pairs={{0,8},{2,10},{4,12},{6,14},{8,0},{10,2},{12,4},{14,6},{1,9},{3,11}... | collective-permute-start | bytes 1572872 | tf_op jit(solution)/shard_map/ppermute | solution.py:69
  18.3 12.9 %collective-permute-start.3 = (bf16[128,2048]{1,0:T(8,128)(2,1)S(1)}, bf16[128,2048]{1,0:T(8,128)(2,1)}, u32[]{:S(2)}, u32[]{:S(2)}) collective-permute-start(bf16[128,2048]{1,0:T(8,128)(2,1)S(1)} %copy-done.5), channel_id=1, source_target_pairs={{0,2},{2,0},{4,6},{6,4},{8,10},{10,8},{12,14},{14,12},{1,3},{3,1},... | collective-permute-start | bytes 1572872 | tf_op jit(solution)/shard_map/ppermute | solution.py:58
  31.2 20.5 %collective-permute-start.4 = (bf16[128,2048]{1,0:T(8,128)(2,1)}, bf16[128,2048]{1,0:T(8,128)(2,1)}, u32[]{:S(2)}, u32[]{:S(2)}) collective-permute-start(bf16[128,2048]{1,0:T(8,128)(2,1)} %collective-permute-done.3.refs_4_), channel_id=1, source_target_pairs={{0,4},{2,6},{4,8},{6,10},{8,12},{10,14},{12,0},{14,2},{1,5},{3,7},... | collective-permute-start | bytes 1572872 | tf_op jit(solution)/shard_map/ppermute | solution.py:50
  31.8 19.9 %collective-permute-start.5 = (bf16[128,2048]{1,0:T(8,128)(2,1)}, bf16[128,2048]{1,0:T(8,128)(2,1)}, u32[]{:S(2)}, u32[]{:S(2)}) collective-permute-start(bf16[128,2048]{1,0:T(8,128)(2,1)} %collective-permute-done.3.refs_4_), channel_id=1, source_target_pairs={{0,12},{2,14},{4,0},{6,2},{8,4},{10,6},{12,8},{14,10},{1,13},{3,15... | collective-permute-start | bytes 1572872 | tf_op jit(solution)/shard_map/ppermute | solution.py:54
  41.6 12.0 %collective-permute-start.6 = (bf16[128,2048]{1,0:T(8,128)(2,1)}, bf16[128,2048]{1,0:T(8,128)(2,1)}, u32[]{:S(2)}, u32[]{:S(2)}) collective-permute-start(bf16[128,2048]{1,0:T(8,128)(2,1)} %collective-permute-done.2.refs_3_), channel_id=1, source_target_pairs={{0,2},{2,0},{4,6},{6,4},{8,10},{10,8},{12,14},{14,12},{1,3},{3,1},... | collective-permute-start | bytes 1572872 | tf_op jit(solution)/shard_map/ppermute | solution.py:58
  59.5 184.0 %all-gather.10.cloned.1.call-start = ((), (), s32[]{:S(2)}) async-start(), calls=%async_computation.12 | async-start | bytes 14155776 | tf_op jit(solution)/shard_map/all_gather | solution.py:804
  60.2 249.6 %reduce-scatter.4.cloned.1.call-start = ((), (), s32[]{:S(2)}) async-start(), calls=%async_computation.8 | async-start | bytes 14598144 | tf_op jit(solution)/shard_map/reduce_scatter | solution.py:815
  60.3 37.5 %collective-permute-start.7 = (bf16[128,2176]{1,0:T(8,128)(2,1)S(1)}, bf16[128,2176]{1,0:T(8,128)(2,1)S(1)}, u32[]{:S(2)}, u32[]{:S(2)}) collective-permute-start(bf16[128,2176]{1,0:T(8,128)(2,1)S(1)} %copy-done.9), channel_id=1, source_target_pairs={{0,4},{2,6},{4,8},{6,10},{8,12},{10,14},{12,0},{14,2},{1,5},{3,7},... | collective-permute-start | bytes 1671176 | tf_op jit(solution)/shard_map/ppermute | solution.py:50
  61.3 36.6 %collective-permute-start.8 = (bf16[128,2176]{1,0:T(8,128)(2,1)S(1)}, bf16[128,2176]{1,0:T(8,128)(2,1)S(1)}, u32[]{:S(2)}, u32[]{:S(2)}) collective-permute-start(bf16[128,2176]{1,0:T(8,128)(2,1)S(1)} %copy-done.9), channel_id=1, source_target_pairs={{0,12},{2,14},{4,0},{6,2},{8,4},{10,6},{12,8},{14,10},{1,13},{3,15... | collective-permute-start | bytes 1671176 | tf_op jit(solution)/shard_map/ppermute | solution.py:54
  63.6 34.2 %collective-permute-start.9 = (bf16[128,2176]{1,0:T(8,128)(2,1)S(1)}, bf16[128,2176]{1,0:T(8,128)(2,1)}, u32[]{:S(2)}, u32[]{:S(2)}) collective-permute-start(bf16[128,2176]{1,0:T(8,128)(2,1)S(1)} %copy-done.9), channel_id=1, source_target_pairs={{0,2},{2,0},{4,6},{6,4},{8,10},{10,8},{12,14},{14,12},{1,3},{3,1},... | collective-permute-start | bytes 1671176 | tf_op jit(solution)/shard_map/ppermute | solution.py:58
  65.2 32.7 %collective-permute-start.10 = (bf16[128,2176]{1,0:T(8,128)(2,1)S(1)}, bf16[128,2176]{1,0:T(8,128)(2,1)}, u32[]{:S(2)}, u32[]{:S(2)}) collective-permute-start(bf16[128,2176]{1,0:T(8,128)(2,1)S(1)} %copy-done.9), channel_id=1, source_target_pairs={{0,8},{2,10},{4,12},{6,14},{8,0},{10,2},{12,4},{14,6},{1,9},{3,11}... | collective-permute-start | bytes 1671176 | tf_op jit(solution)/shard_map/ppermute | solution.py:69
  92.9 16.8 %copy-start.6 = (bf16[128,2048]{1,0:T(8,128)(2,1)S(1)}, bf16[128,2048]{1,0:T(8,128)(2,1)}, u32[]{:S(2)}) copy-start(bf16[128,2048]{1,0:T(8,128)(2,1)} %refs_0_.1) | copy-start | bytes 1572868
  97.9 11.8 %collective-permute-start.11 = (bf16[128,2048]{1,0:T(8,128)(2,1)}, bf16[128,2048]{1,0:T(8,128)(2,1)S(1)}, u32[]{:S(2)}, u32[]{:S(2)}) collective-permute-start(bf16[128,2048]{1,0:T(8,128)(2,1)} %branch.1), channel_id=1, source_target_pairs={{0,1},{1,0},{2,3},{3,2},{4,5},{5,4},{6,7},{7,6},{8,9},{9,8},{10,11... | collective-permute-start | bytes 1572872 | tf_op jit(solution)/shard_map/ppermute | solution.py:141
  100.9 16.3 %collective-permute-start.19 = (bf16[128,2176]{1,0:T(8,128)(2,1)}, bf16[128,2176]{1,0:T(8,128)(2,1)S(1)}, u32[]{:S(2)}, u32[]{:S(2)}) collective-permute-start(bf16[128,2176]{1,0:T(8,128)(2,1)} %collective-permute-done.9.refs_7_.refs_15_), channel_id=1, source_target_pairs={{0,4},{2,6},{4,8},{6,10},{8,12},{10,14},{12,0},{14,2},{1,5},{3,7},... | collective-permute-start | bytes 1671176 | tf_op jit(solution)/shard_map/ppermute | solution.py:50
  111.6 54.4 %copy-start.40 = (f32[128]{0:T(128)}, f32[128]{0:T(128)S(1)}, u32[]{:S(2)}) copy-start(f32[128]{0:T(128)S(1)} %get-tuple-element.198) | copy-start | bytes 1540
  111.7 31.9 %copy-start.3 = (bf16[128,2048]{1,0:T(8,128)(2,1)}, bf16[128,2048]{1,0:T(8,128)(2,1)S(1)}, u32[]{:S(2)}) copy-start(bf16[128,2048]{1,0:T(8,128)(2,1)S(1)} %multiply_convert_fusion.1.refs_0_.refs_4_) | copy-start | bytes 1572868
  111.7 16.7 %collective-permute-start.15 = (bf16[128,2048]{1,0:T(8,128)(2,1)S(1)}, bf16[128,2048]{1,0:T(8,128)(2,1)}, u32[]{:S(2)}, u32[]{:S(2)}) collective-permute-start(bf16[128,2048]{1,0:T(8,128)(2,1)S(1)} %multiply_convert_fusion.1.refs_0_.refs_4_), channel_id=1, source_target_pairs={{0,8},{2,10},{4,12},{6,14},{8,0},{10,2},{12,4},{14,6},{1,9},{3,11}... | collective-permute-start | bytes 1572872 | tf_op jit(solution)/shard_map/ppermute | solution.py:69
  113.4 16.0 %collective-permute-start.14 = (bf16[128,2048]{1,0:T(8,128)(2,1)S(1)}, bf16[128,2048]{1,0:T(8,128)(2,1)}, u32[]{:S(2)}, u32[]{:S(2)}) collective-permute-start(bf16[128,2048]{1,0:T(8,128)(2,1)S(1)} %multiply_convert_fusion.1.refs_0_.refs_4_), channel_id=1, source_target_pairs={{0,2},{2,0},{4,6},{6,4},{8,10},{10,8},{12,14},{14,12},{1,3},{3,1},... | collective-permute-start | bytes 1572872 | tf_op jit(solution)/shard_map/ppermute | solution.py:58
  114.0 23.0 %collective-permute-start.12 = (bf16[128,2048]{1,0:T(8,128)(2,1)S(1)}, bf16[128,2048]{1,0:T(8,128)(2,1)S(1)}, u32[]{:S(2)}, u32[]{:S(2)}) collective-permute-start(bf16[128,2048]{1,0:T(8,128)(2,1)S(1)} %multiply_convert_fusion.1.refs_0_.refs_4_), channel_id=1, source_target_pairs={{0,4},{2,6},{4,8},{6,10},{8,12},{10,14},{12,0},{14,2},{1,5},{3,7},... | collective-permute-start | bytes 1572872 | tf_op jit(solution)/shard_map/ppermute | solution.py:50
  116.4 23.7 %collective-permute-start.13 = (bf16[128,2048]{1,0:T(8,128)(2,1)S(1)}, bf16[128,2048]{1,0:T(8,128)(2,1)S(1)}, u32[]{:S(2)}, u32[]{:S(2)}) collective-permute-start(bf16[128,2048]{1,0:T(8,128)(2,1)S(1)} %multiply_convert_fusion.1.refs_0_.refs_4_), channel_id=1, source_target_pairs={{0,12},{2,14},{4,0},{6,2},{8,4},{10,6},{12,8},{14,10},{1,13},{3,15... | collective-permute-start | bytes 1572872 | tf_op jit(solution)/shard_map/ppermute | solution.py:54
  117.3 22.9 %copy-start.18 = (bf16[128,2176]{1,0:T(8,128)(2,1)}, bf16[128,2176]{1,0:T(8,128)(2,1)S(1)}, u32[]{:S(2)}) copy-start(bf16[128,2176]{1,0:T(8,128)(2,1)S(1)} %collective-permute-done.19.refs_5_.refs_17_) | copy-start | bytes 1671172
  117.3 48.7 %collective-permute-start.20 = (bf16[128,2176]{1,0:T(8,128)(2,1)}, bf16[128,2176]{1,0:T(8,128)(2,1)S(1)}, u32[]{:S(2)}, u32[]{:S(2)}) collective-permute-start(bf16[128,2176]{1,0:T(8,128)(2,1)} %collective-permute-done.9.refs_7_.refs_15_), channel_id=1, source_target_pairs={{0,12},{2,14},{4,0},{6,2},{8,4},{10,6},{12,8},{14,10},{1,13},{3,15... | collective-permute-start | bytes 1671176 | tf_op jit(solution)/shard_map/ppermute | solution.py:54
  128.4 37.6 %collective-permute-start.21 = (bf16[128,2176]{1,0:T(8,128)(2,1)}, bf16[128,2176]{1,0:T(8,128)(2,1)S(1)}, u32[]{:S(2)}, u32[]{:S(2)}) collective-permute-start(bf16[128,2176]{1,0:T(8,128)(2,1)} %collective-permute-done.10.refs_4_.refs_16_), channel_id=1, source_target_pairs={{0,2},{2,0},{4,6},{6,4},{8,10},{10,8},{12,14},{14,12},{1,3},{3,1},... | collective-permute-start | bytes 1671176 | tf_op jit(solution)/shard_map/ppermute | solution.py:58
  129.4 36.6 %collective-permute-start.16 = (bf16[128,2048]{1,0:T(8,128)(2,1)}, bf16[128,2048]{1,0:T(8,128)(2,1)}, u32[]{:S(2)}, u32[]{:S(2)}) collective-permute-start(bf16[128,2048]{1,0:T(8,128)(2,1)} %collective-permute-done.14.refs_3_.refs_7_), channel_id=1, source_target_pairs={{0,4},{2,6},{4,8},{6,10},{8,12},{10,14},{12,0},{14,2},{1,5},{3,7},... | collective-permute-start | bytes 1572872 | tf_op jit(solution)/shard_map/ppermute | solution.py:50
  137.0 29.0 %collective-permute-start.17 = (bf16[128,2048]{1,0:T(8,128)(2,1)}, bf16[128,2048]{1,0:T(8,128)(2,1)}, u32[]{:S(2)}, u32[]{:S(2)}) collective-permute-start(bf16[128,2048]{1,0:T(8,128)(2,1)} %collective-permute-done.14.refs_3_.refs_7_), channel_id=1, source_target_pairs={{0,12},{2,14},{4,0},{6,2},{8,4},{10,6},{12,8},{14,10},{1,13},{3,15... | collective-permute-start | bytes 1572872 | tf_op jit(solution)/shard_map/ppermute | solution.py:54
  140.9 25.1 %collective-permute-start.18 = (bf16[128,2048]{1,0:T(8,128)(2,1)}, bf16[128,2048]{1,0:T(8,128)(2,1)}, u32[]{:S(2)}, u32[]{:S(2)}) collective-permute-start(bf16[128,2048]{1,0:T(8,128)(2,1)} %collective-permute-done.15.refs_0_.refs_8_), channel_id=1, source_target_pairs={{0,2},{2,0},{4,6},{6,4},{8,10},{10,8},{12,14},{14,12},{1,3},{3,1},... | collective-permute-start | bytes 1572872 | tf_op jit(solution)/shard_map/ppermute | solution.py:58
  209.4 156.7 %reduce-scatter.6.cloned.1.call-start = ((), (), s32[]{:S(2)}) async-start(), calls=%async_computation.9 | async-start | bytes 4718592 | tf_op jit(solution)/shard_map/reduce_scatter | solution.py:848
  209.5 21.5 %collective-permute-start.22 = (bf16[128,4224]{1,0:T(8,128)(2,1)}, bf16[128,4224]{1,0:T(8,128)(2,1)S(1)}, u32[]{:S(2)}, u32[]{:S(2)}) collective-permute-start(bf16[128,4224]{1,0:T(8,128)(2,1)} %get-tuple-element.66), channel_id=1, source_target_pairs={{0,2},{2,0},{4,6},{6,4},{8,10},{10,8},{12,14},{14,12},{1,3},{3,1},... | collective-permute-start | bytes 3244040 | tf_op jit(solution)/shard_map/ppermute | solution.py:58
  210.8 27.0 %collective-permute-start.25 = (bf16[128,4224]{1,0:T(8,128)(2,1)}, bf16[128,4224]{1,0:T(8,128)(2,1)S(1)}, u32[]{:S(2)}, u32[]{:S(2)}) collective-permute-start(bf16[128,4224]{1,0:T(8,128)(2,1)} %get-tuple-element.69), channel_id=1, source_target_pairs={{0,12},{2,14},{4,0},{6,2},{8,4},{10,6},{12,8},{14,10},{1,13},{3,15... | collective-permute-start | bytes 3244040 | tf_op jit(solution)/shard_map/ppermute | solution.py:54
  212.2 28.2 %collective-permute-start.24 = (bf16[128,4224]{1,0:T(8,128)(2,1)}, bf16[128,4224]{1,0:T(8,128)(2,1)S(1)}, u32[]{:S(2)}, u32[]{:S(2)}) collective-permute-start(bf16[128,4224]{1,0:T(8,128)(2,1)} %get-tuple-element.68), channel_id=1, source_target_pairs={{0,4},{2,6},{4,8},{6,10},{8,12},{10,14},{12,0},{14,2},{1,5},{3,7},... | collective-permute-start | bytes 3244040 | tf_op jit(solution)/shard_map/ppermute | solution.py:50
  212.9 69.7 %collective-permute-start.27 = (bf16[128,4224]{1,0:T(8,128)(2,1)}, bf16[128,4224]{1,0:T(8,128)(2,1)S(1)}, u32[]{:S(2)}, u32[]{:S(2)}) collective-permute-start(bf16[128,4224]{1,0:T(8,128)(2,1)} %get-tuple-element.70), channel_id=1, source_target_pairs={{0,4},{2,6},{4,8},{6,10},{8,12},{10,14},{12,0},{14,2},{1,5},{3,7},... | collective-permute-start | bytes 3244040 | tf_op jit(solution)/shard_map/ppermute | solution.py:50
  213.7 68.9 %collective-permute-start.28 = (bf16[128,4224]{1,0:T(8,128)(2,1)}, bf16[128,4224]{1,0:T(8,128)(2,1)}, u32[]{:S(2)}, u32[]{:S(2)}) collective-permute-start(bf16[128,4224]{1,0:T(8,128)(2,1)} %get-tuple-element.71), channel_id=1, source_target_pairs={{0,12},{2,14},{4,0},{6,2},{8,4},{10,6},{12,8},{14,10},{1,13},{3,15... | collective-permute-start | bytes 3244040 | tf_op jit(solution)/shard_map/ppermute | solution.py:54
  233.5 49.0 %collective-permute-start.23 = (bf16[128,4224]{1,0:T(8,128)(2,1)}, bf16[128,4224]{1,0:T(8,128)(2,1)}, u32[]{:S(2)}, u32[]{:S(2)}) collective-permute-start(bf16[128,4224]{1,0:T(8,128)(2,1)} %add_convert_fusion.1), channel_id=1, source_target_pairs={{0,8},{2,10},{4,12},{6,14},{8,0},{10,2},{12,4},{14,6},{1,9},{3,11}... | collective-permute-start | bytes 3244040 | tf_op jit(solution)/shard_map/ppermute | solution.py:69
  241.8 40.8 %collective-permute-start.26 = (bf16[128,4224]{1,0:T(8,128)(2,1)}, bf16[128,4224]{1,0:T(8,128)(2,1)}, u32[]{:S(2)}, u32[]{:S(2)}) collective-permute-start(bf16[128,4224]{1,0:T(8,128)(2,1)} %add_convert_fusion), channel_id=1, source_target_pairs={{0,2},{2,0},{4,6},{6,4},{8,10},{10,8},{12,14},{14,12},{1,3},{3,1},... | collective-permute-start | bytes 3244040 | tf_op jit(solution)/shard_map/ppermute | solution.py:58
  287.8 11.4 %collective-permute-start.29 = (bf16[128,2176]{1,0:T(8,128)(2,1)}, bf16[128,2176]{1,0:T(8,128)(2,1)}, u32[]{:S(2)}, u32[]{:S(2)}) collective-permute-start(bf16[128,2176]{1,0:T(8,128)(2,1)} %slice.203), channel_id=1, source_target_pairs={{0,1},{1,0},{2,3},{3,2},{4,5},{5,4},{6,7},{7,6},{8,9},{9,8},{10,11... | collective-permute-start | bytes 1671176 | tf_op jit(solution)/shard_map/ppermute | solution.py:141
  309.9 34.5 %collective-permute-start.30 = (bf16[3168,256]{1,0:T(8,128)(2,1)}, bf16[3168,256]{1,0:T(8,128)(2,1)}, u32[]{:S(2)}, u32[]{:S(2)}) collective-permute-start(bf16[3168,256]{1,0:T(8,128)(2,1)} %bitcast.118), channel_id=1, source_target_pairs={{0,4},{2,6},{4,8},{6,10},{8,12},{10,14},{12,0},{14,2},{1,5},{3,7},... | collective-permute-start | bytes 4866056 | tf_op jit(solution)/shard_map/ppermute | solution.py:50
  310.0 34.5 %collective-permute-start.31 = (bf16[3168,256]{1,0:T(8,128)(2,1)}, bf16[3168,256]{1,0:T(8,128)(2,1)}, u32[]{:S(2)}, u32[]{:S(2)}) collective-permute-start(bf16[3168,256]{1,0:T(8,128)(2,1)} %bitcast.119), channel_id=1, source_target_pairs={{0,12},{2,14},{4,0},{6,2},{8,4},{10,6},{12,8},{14,10},{1,13},{3,15... | collective-permute-start | bytes 4866056 | tf_op jit(solution)/shard_map/ppermute | solution.py:54
  313.2 31.2 %collective-permute-start.32 = (bf16[3168,256]{1,0:T(8,128)(2,1)}, bf16[3168,256]{1,0:T(8,128)(2,1)}, u32[]{:S(2)}, u32[]{:S(2)}) collective-permute-start(bf16[3168,256]{1,0:T(8,128)(2,1)} %bitcast.120), channel_id=1, source_target_pairs={{0,2},{2,0},{4,6},{6,4},{8,10},{10,8},{12,14},{14,12},{1,3},{3,1},... | collective-permute-start | bytes 4866056 | tf_op jit(solution)/shard_map/ppermute | solution.py:58
  319.8 24.7 %all-to-all-start.1 = ((bf16[8,128,128]{2,1,0:T(8,128)(2,1)}), bf16[8,128,128]{2,1,0:T(8,128)(2,1)S(1)}, u32[]{:S(2)}, u32[]{:S(2)}) async-start(bf16[8,128,128]{2,1,0:T(8,128)(2,1)} %bitcast_bitcast_fusion.1), calls=%async_computation.1 | async-start | bytes 524288 | tf_op jit(solution)/shard_map/all_to_all | solution.py:841
  323.2 88.2 %reduce-scatter.8.cloned.1.call-start = ((), (), s32[]{:S(2)}) async-start(), calls=%async_computation.10 | async-start | bytes 2359296 | tf_op jit(solution)/shard_map/reduce_scatter | solution.py:868
  358.9 58.6 %collective-permute-start.36 = (bf16[3168,256]{1,0:T(8,128)(2,1)}, bf16[3168,256]{1,0:T(8,128)(2,1)S(1)}, u32[]{:S(2)}, u32[]{:S(2)}) collective-permute-start(bf16[3168,256]{1,0:T(8,128)(2,1)} %collective-permute-done.32.refs_3_), channel_id=1, source_target_pairs={{0,4},{2,6},{4,8},{6,10},{8,12},{10,14},{12,0},{14,2},{1,5},{3,7},... | collective-permute-start | bytes 4866056 | tf_op jit(solution)/shard_map/ppermute | solution.py:50
  359.4 61.1 %collective-permute-start.37 = (bf16[3168,256]{1,0:T(8,128)(2,1)}, bf16[3168,256]{1,0:T(8,128)(2,1)}, u32[]{:S(2)}, u32[]{:S(2)}) collective-permute-start(bf16[3168,256]{1,0:T(8,128)(2,1)} %collective-permute-done.32.refs_3_), channel_id=1, source_target_pairs={{0,12},{2,14},{4,0},{6,2},{8,4},{10,6},{12,8},{14,10},{1,13},{3,15... | collective-permute-start | bytes 4866056 | tf_op jit(solution)/shard_map/ppermute | solution.py:54
  368.1 44.5 %collective-permute-start.33 = (bf16[128,2048]{1,0:T(8,128)(2,1)}, bf16[128,2048]{1,0:T(8,128)(2,1)}, u32[]{:S(2)}, u32[]{:S(2)}) collective-permute-start(bf16[128,2048]{1,0:T(8,128)(2,1)} %slice.147), channel_id=1, source_target_pairs={{0,1},{1,0},{2,3},{3,2},{4,5},{5,4},{6,7},{7,6},{8,9},{9,8},{10,11... | collective-permute-start | bytes 1572872 | tf_op jit(solution)/shard_map/ppermute | solution.py:141
  370.7 34.6 %all-to-all-start.3 = ((bf16[8,256,128]{2,1,0:T(8,128)(2,1)}), bf16[8,256,128]{2,1,0:T(8,128)(2,1)}, u32[]{:S(2)}, u32[]{:S(2)}) async-start(bf16[8,256,128]{2,1,0:T(8,128)(2,1)} %bitcast_bitcast_fusion), calls=%async_computation.5 | async-start | bytes 1048576 | tf_op jit(solution)/shard_map/all_to_all | solution.py:853
  377.8 46.2 %collective-permute-start.34 = (bf16[1584,256]{1,0:T(8,128)(2,1)}, bf16[1584,256]{1,0:T(8,128)(2,1)}, u32[]{:S(2)}, u32[]{:S(2)}) collective-permute-start(bf16[1584,256]{1,0:T(8,128)(2,1)} %slice.154), channel_id=1, source_target_pairs={{0,4},{2,6},{4,8},{6,10},{8,12},{10,14},{12,0},{14,2},{1,5},{3,7},... | collective-permute-start | bytes 2433032 | tf_op jit(solution)/shard_map/ppermute | solution.py:50
  381.8 42.2 %collective-permute-start.35 = (bf16[1584,256]{1,0:T(8,128)(2,1)}, bf16[1584,256]{1,0:T(8,128)(2,1)}, u32[]{:S(2)}, u32[]{:S(2)}) collective-permute-start(bf16[1584,256]{1,0:T(8,128)(2,1)} %slice.155), channel_id=1, source_target_pairs={{0,12},{2,14},{4,0},{6,2},{8,4},{10,6},{12,8},{14,10},{1,13},{3,15... | collective-permute-start | bytes 2433032 | tf_op jit(solution)/shard_map/ppermute | solution.py:54
  405.3 33.8 %all-to-all-start.2 = ((bf16[8,128,384]{1,2,0:T(8,128)(2,1)}), bf16[8,128,384]{1,2,0:T(8,128)(2,1)}, u32[]{:S(2)}, u32[]{:S(2)}) async-start(bf16[8,128,384]{1,2,0:T(8,128)(2,1)} %copy.193), calls=%async_computation.3 | async-start | bytes 1572864 | tf_op jit(solution)/shard_map/all_to_all | solution.py:855
  412.6 12.6 %collective-permute-start.38 = (f32[256]{0:T(256)S(1)}, f32[256]{0:T(256)S(1)}, u32[]{:S(2)}, u32[]{:S(2)}) collective-permute-start(f32[256]{0:T(256)S(1)} %multiply_reduce_fusion.3), channel_id=1, source_target_pairs={{0,1},{1,0},{2,3},{3,2},{4,5},{5,4},{6,7},{7,6},{8,9},{9,8},{10,11... | collective-permute-start | bytes 3080 | tf_op jit(solution)/shard_map/ppermute | solution.py:873
  418.5 37.3 %collective-permute-start.44 = (bf16[1584,256]{1,0:T(8,128)(2,1)}, bf16[1584,256]{1,0:T(8,128)(2,1)}, u32[]{:S(2)}, u32[]{:S(2)}) collective-permute-start(bf16[1584,256]{1,0:T(8,128)(2,1)} %slice.159), channel_id=1, source_target_pairs={{0,4},{2,6},{4,8},{6,10},{8,12},{10,14},{12,0},{14,2},{1,5},{3,7},... | collective-permute-start | bytes 2433032 | tf_op jit(solution)/shard_map/ppermute | solution.py:50
  422.6 35.2 %collective-permute-start.45 = (bf16[1584,256]{1,0:T(8,128)(2,1)}, bf16[1584,256]{1,0:T(8,128)(2,1)}, u32[]{:S(2)}, u32[]{:S(2)}) collective-permute-start(bf16[1584,256]{1,0:T(8,128)(2,1)} %slice.160), channel_id=1, source_target_pairs={{0,12},{2,14},{4,0},{6,2},{8,4},{10,6},{12,8},{14,10},{1,13},{3,15... | collective-permute-start | bytes 2433032 | tf_op jit(solution)/shard_map/ppermute | solution.py:54
  425.5 30.3 %copy-start.25 = (bf16[256,640]{1,0:T(8,128)(2,1)}, bf16[256,640]{1,0:T(8,128)(2,1)S(1)}, u32[]{:S(2)}) copy-start(bf16[256,640]{1,0:T(8,128)(2,1)S(1)} %pad_maximum_fusion.2.refs_0_) | copy-start | bytes 983044
  425.5 30.8 %collective-permute-start.41 = (bf16[256,640]{1,0:T(8,128)(2,1)S(1)}, bf16[256,640]{1,0:T(8,128)(2,1)S(1)}, u32[]{:S(2)}, u32[]{:S(2)}) collective-permute-start(bf16[256,640]{1,0:T(8,128)(2,1)S(1)} %pad_maximum_fusion.2.refs_0_), channel_id=1, source_target_pairs={{0,2},{2,0},{4,6},{6,4},{8,10},{10,8},{12,14},{14,12},{1,3},{3,1},... | collective-permute-start | bytes 983048 | tf_op jit(solution)/shard_map/ppermute | solution.py:58
  427.0 32.7 %collective-permute-start.42 = (bf16[256,640]{1,0:T(8,128)(2,1)S(1)}, bf16[256,640]{1,0:T(8,128)(2,1)S(1)}, u32[]{:S(2)}, u32[]{:S(2)}) collective-permute-start(bf16[256,640]{1,0:T(8,128)(2,1)S(1)} %pad_maximum_fusion.2.refs_0_), channel_id=1, source_target_pairs={{0,8},{2,10},{4,12},{6,14},{8,0},{10,2},{12,4},{14,6},{1,9},{3,11}... | collective-permute-start | bytes 983048 | tf_op jit(solution)/shard_map/ppermute | solution.py:69
  453.1 24.2 %collective-permute-start.39 = (bf16[256,640]{1,0:T(8,128)(2,1)S(1)}, bf16[256,640]{1,0:T(8,128)(2,1)S(1)}, u32[]{:S(2)}, u32[]{:S(2)}) collective-permute-start(bf16[256,640]{1,0:T(8,128)(2,1)S(1)} %pad_maximum_fusion.2.refs_0_), channel_id=1, source_target_pairs={{0,4},{2,6},{4,8},{6,10},{8,12},{10,14},{12,0},{14,2},{1,5},{3,7},... | collective-permute-start | bytes 983048 | tf_op jit(solution)/shard_map/ppermute | solution.py:50
  455.8 21.5 %collective-permute-start.40 = (bf16[256,640]{1,0:T(8,128)(2,1)S(1)}, bf16[256,640]{1,0:T(8,128)(2,1)S(1)}, u32[]{:S(2)}, u32[]{:S(2)}) collective-permute-start(bf16[256,640]{1,0:T(8,128)(2,1)S(1)} %pad_maximum_fusion.2.refs_0_), channel_id=1, source_target_pairs={{0,12},{2,14},{4,0},{6,2},{8,4},{10,6},{12,8},{14,10},{1,13},{3,15... | collective-permute-start | bytes 983048 | tf_op jit(solution)/shard_map/ppermute | solution.py:54
  456.4 23.1 %collective-permute-start.46 = (bf16[256,640]{1,0:T(8,128)(2,1)S(1)}, bf16[256,640]{1,0:T(8,128)(2,1)S(1)}, u32[]{:S(2)}, u32[]{:S(2)}) collective-permute-start(bf16[256,640]{1,0:T(8,128)(2,1)S(1)} %collective-permute-done.41.refs_4_), channel_id=1, source_target_pairs={{0,4},{2,6},{4,8},{6,10},{8,12},{10,14},{12,0},{14,2},{1,5},{3,7},... | collective-permute-start | bytes 983048 | tf_op jit(solution)/shard_map/ppermute | solution.py:50
  457.8 21.7 %collective-permute-start.47 = (bf16[256,640]{1,0:T(8,128)(2,1)S(1)}, bf16[256,640]{1,0:T(8,128)(2,1)S(1)}, u32[]{:S(2)}, u32[]{:S(2)}) collective-permute-start(bf16[256,640]{1,0:T(8,128)(2,1)S(1)} %collective-permute-done.41.refs_4_), channel_id=1, source_target_pairs={{0,12},{2,14},{4,0},{6,2},{8,4},{10,6},{12,8},{14,10},{1,13},{3,15... | collective-permute-start | bytes 983048 | tf_op jit(solution)/shard_map/ppermute | solution.py:54
  459.6 19.9 %collective-permute-start.48 = (bf16[256,640]{1,0:T(8,128)(2,1)S(1)}, bf16[256,640]{1,0:T(8,128)(2,1)S(1)}, u32[]{:S(2)}, u32[]{:S(2)}) collective-permute-start(bf16[256,640]{1,0:T(8,128)(2,1)S(1)} %collective-permute-done.42.refs_3_), channel_id=1, source_target_pairs={{0,2},{2,0},{4,6},{6,4},{8,10},{10,8},{12,14},{14,12},{1,3},{3,1},... | collective-permute-start | bytes 983048 | tf_op jit(solution)/shard_map/ppermute | solution.py:58
  477.3 13.6 %collective-permute-start.43 = (bf16[128,2048]{1,0:T(8,128)(2,1)S(1)}, bf16[128,2048]{1,0:T(8,128)(2,1)S(1)}, u32[]{:S(2)}, u32[]{:S(2)}) collective-permute-start(bf16[128,2048]{1,0:T(8,128)(2,1)S(1)} %copy-done.24), channel_id=1, source_target_pairs={{0,1},{1,0},{2,3},{3,2},{4,5},{5,4},{6,7},{7,6},{8,9},{9,8},{10,11... | collective-permute-start | bytes 1572872 | tf_op jit(solution)/shard_map/ppermute | solution.py:141
  (42 other events, 201.3 us)
Sparse Core Ops, SparseCore 0:
  13.1 43.5 all-gather.5
  59.6 69.9 all-gather.7
  131.3 67.7 all-gather.9
  209.5 75.3 reduce-scatter.3
  310.0 38.5 reduce-scatter.5
  359.0 36.6 reduce-scatter.7

commit v4 on v3

--- a/solution.py
+++ b/solution.py
@@ -1,3 +1,5 @@
+import functools
+
 import jax
 import jax.numpy as jnp
 import numpy as np
@@ -277,9 +279,10 @@
 UNIT_ROWS = 16
 
 
-def units_kernel(*refs):
+def units_kernel(half, *refs):
     x_hbm, g_hbm = refs[:4], refs[4:8]
     small_ref, mine_ref, weight_hbm = refs[8:11]
+    refs = refs[:11] + refs[11 + 2 * half :]
     d_hbm, back_hbm, hidden_hbm = refs[11:15], refs[15], refs[16]
     weight_ref, x_ref, g_ref, tail_ref, gate_ref, up_ref, down_ref = refs[17:24]
     back_ref, hidden_ref, turned_ref, flat_ref, d_ref, sems = refs[24:]
@@ -354,8 +357,9 @@
     middle, last = expert_units // UNIT_ROWS, units // UNIT_ROWS
     expert_sum = lax.fori_loop(0, middle, unit_rows(combine), zeros)
     shared_sum = lax.fori_loop(middle, last, unit_rows(shared_gate), zeros)
-    start("out", hidden_ref, hidden_hbm)
-    start("out", back_ref, back_hbm)
+    columns = pl.ds(half * tokens, tokens)
+    start("out", hidden_ref, hidden_hbm.at[:, columns])
+    start("out", back_ref, back_hbm.at[:, columns])
     expert_sum = jnp.sum(expert_sum, axis=0, keepdims=True)
     shared_sum = jnp.sum(shared_sum, axis=0, keepdims=True)
     sums = mine * expert_sum + jnp.where(places == 8, shared_sum, 0.0)
@@ -384,21 +388,22 @@
     finish("out")
 
 
-def units_forward_back(x_blocks, g_blocks, small_rows, mine, weights):
+def units_forward_back(x_blocks, g_blocks, small_rows, mine, weights, earlier):
     rows, width = x_blocks[0].shape
     tokens = 4 * rows
     units = weights.shape[1] // 3
     vmem = pl.BlockSpec(memory_space=pltpu.VMEM)
     anywhere = pl.BlockSpec(memory_space=pl.ANY)
     return pl.pallas_call(
-        units_kernel,
-        in_specs=[anywhere] * 8 + [vmem] * 2 + [anywhere],
+        functools.partial(units_kernel, len(earlier) // 2),
+        in_specs=[anywhere] * 8 + [vmem] * 2 + [anywhere] * (1 + len(earlier)),
         out_specs=[anywhere] * 6,
         out_shape=[jax.ShapeDtypeStruct((rows, 2 * width + 128), LOW)] * 4
         + [
-            jax.ShapeDtypeStruct((2 * units, tokens), LOW),
-            jax.ShapeDtypeStruct((units, tokens), LOW),
+            jax.ShapeDtypeStruct((2 * units, 2 * tokens), LOW),
+            jax.ShapeDtypeStruct((units, 2 * tokens), LOW),
         ],
+        input_output_aliases={11 + index: 4 + index for index in range(len(earlier))},
         scratch_shapes=[
             pltpu.VMEM((3 * units, width), LOW),
             pltpu.VMEM((tokens, width), LOW),
@@ -417,48 +422,36 @@
         compiler_params=params(),
         cost_estimate=estimate(11_000_000_000, 20_000_000),
         name="units",
-    )(*x_blocks, *g_blocks, small_rows, mine, weights)
+    )(*x_blocks, *g_blocks, small_rows, mine, weights, *earlier)
 
 
 def outer_kernel(*refs):
-    back_refs, hidden_refs, x_refs, g_refs, out_ref = (
-        refs[:2],
-        refs[2:4],
-        refs[4:12],
-        refs[12:20],
-        refs[20],
-    )
-    units = hidden_refs[0].shape[0]
-
-    def product(lefts, rights):
-        halves = [
-            jnp.concatenate([ref[...] for ref in rights[half : half + 4]], axis=0)
-            for half in (0, 4)
-        ]
-        return low(dot_plain(lefts[0][...], halves[0]) + dot_plain(lefts[1][...], halves[1]))
-
-    back, hidden = product(back_refs, x_refs), product(hidden_refs, g_refs)
+    back_ref, hidden_ref, x_refs, g_refs, out_ref = refs[0], refs[1], refs[2:10], refs[10:18], refs[18]
+    units = hidden_ref.shape[0]
+    rights = [jnp.concatenate([ref[...] for ref in part], axis=0) for part in (x_refs, g_refs)]
+    back = low(dot_plain(back_ref[...], rights[0]))
+    hidden = low(dot_plain(hidden_ref[...], rights[1]))
     for index in range(out_ref.shape[0]):
         columns = slice(index * 256, (index + 1) * 256)
         out_ref[index, : 2 * units] = back[:, columns]
         out_ref[index, 2 * units :] = hidden[:, columns]
 
 
-def outer_products(backs, hiddens, x_blocks, g_blocks):
-    units, tokens = hiddens[0].shape
+def outer_products(back, hidden, x_blocks, g_blocks):
+    units = hidden.shape[0]
     rows = x_blocks[0].shape[0]
     whole = lambda value: pl.BlockSpec(value.shape, lambda step: (0, 0))
     return pl.pallas_call(
         outer_kernel,
         grid=(4,),
-        in_specs=[whole(value) for value in (*backs, *hiddens)]
+        in_specs=[whole(back), whole(hidden)]
         + [pl.BlockSpec((rows, 512), lambda step: (0, step))] * 16,
         out_specs=pl.BlockSpec((2, 3 * units, 256), lambda step: (step, 0, 0)),
         out_shape=jax.ShapeDtypeStruct((8, 3 * units, 256), LOW),
         compiler_params=params(),
         cost_estimate=estimate(units * 2 * 1024 * 2048, 10_000_000),
         name="outer",
-    )(*backs, *hiddens, *x_blocks, *g_blocks)
+    )(back, hidden, *x_blocks, *g_blocks)
 
 
 def pack_kernel(here_ref, qkv_ref, out_weight_ref, small_ref, out_ref):
@@ -786,29 +779,31 @@
     pick = lambda blocks, half: [blocks[index] for index in half]
     results = []
     for half in (first_half, second_half):
-        mine_here = after(mine, [result[5] for result in results])
         results.append(
             units_forward_back(
-                pick(n_blocks, half), pick(g_blocks, half), small_rows, mine_here, unit_weights
+                pick(n_blocks, half),
+                pick(g_blocks, half),
+                small_rows,
+                mine,
+                unit_weights,
+                results[0][4:] if results else (),
             )
         )
     d_blocks = [None] * 8
     for half, result in zip((first_half, second_half), results):
         for place, index in enumerate(half):
             d_blocks[index] = result[place]
-    (back_first, hidden_first), (back_second, hidden_second) = (
-        results[0][4:],
-        results[1][4:],
-    )
+    back, hidden = results[1][4:]
     in_halves = lambda blocks: pick(blocks, first_half) + pick(blocks, second_half)
     weight_qkv_all = lax.all_gather(
         after(w_qkv.transpose(1, 0, 2), branch), "fsdp", axis=0, tiled=False
     )
     d_first = scatter_first(d_blocks)
+    d_blocks[1:3] = after(d_blocks[1:3], (n_second, g_second))
     d_second = scatter_second(d_blocks, d_first)
     unit_part = outer_products(
-        (back_first, back_second),
-        (hidden_first, hidden_second),
+        after(back, d_second[2:]),
+        hidden,
         in_halves(n_blocks),
         in_halves(g_blocks),
     )

time: 508 us -> 502 us (0.988)
    ppermute x11, waiting for transfers between devices: 24.8 us -> 46 us  [swap(): return lax.ppermute(values, 'ctx', PAIR)]
    ppermute x14, waiting for transfers between devices: 53.9 us -> 36.1 us  [up(): return lax.ppermute(values, 'ctx', ring(2))]
    all_to_all x1, waiting for transfers between devices: 21 us -> 12.6 us  [body(): lax.all_to_all(grad_attended.reshape(rows, heads, head_size).transpose(1,...]
    unnamed x110 -> x112, local copies, waits for them, and re-layouts: 11.8 us -> 9.96 us
  transfers between devices with their start and end apart: 58 -> 58, of which waited for: 15 -> 14; matrix products, arithmetic and copies ran while one was open for 17% -> 17% of each run, Pallas kernels for 26% -> 26%
where the time goes in v4:
time: 502 us; the launch traced here: 496 us
  waiting for transfers between devices  149 us (30%)
  Pallas kernels  131 us (26%)
  starting transfers between devices  94.1 us (19%)
  local copies, waits for them, and re-layouts  48.4 us (10%)
  other arithmetic  35.7 us (7%)
  between operations  15.4 us (3%)
  blocking collectives  11.7 us (2%)
  matrix products  10.4 us (2%)
    ppermute x11, waiting for transfers between devices, swap(): return lax.ppermute(values, 'ctx', PAIR)  46 us
    pallas_call x2, Pallas kernels, units_forward_back(): pl.pallas_call(functools.partial(units_kernel, len(earlier) // 2), in_spe...  44.5 us
    ppermute x14, waiting for transfers between devices, up(): return lax.ppermute(values, 'ctx', ring(2))  36.1 us
    ppermute x14, starting transfers between devices, down(): return lax.ppermute(values, 'ctx', ring(-2))  30.8 us
    pallas_call x1, Pallas kernels, outer_products(): pl.pallas_call(outer_kernel, grid=(4,), in_specs=[whole(back), whole(hidd...  20.1 us
    ppermute x4, waiting for transfers between devices, add_halves(): return wide(mine) + wide(lax.ppermute(mine, 'tp', [(0, 1), (1, 0)]))  19.9 us
    ppermute x5, waiting for transfers between devices, across(): return lax.ppermute(values, 'ctx', ring(4))  16.9 us
    ppermute x11, starting transfers between devices, swap(): return lax.ppermute(values, 'ctx', PAIR)  16.4 us
  transfers between devices with their start and end apart: 58, of which 14 were waited for; matrix products, arithmetic and copies ran while one was open for 17% of the time, Pallas kernels for 26%

profile of v4, /device:TPU:0, one launch (start us, length us, event | category | flops | bytes accessed | tf_op | source)
XLA Modules:
  0.0 495.5 jit_solution(279052866300421277)
XLA Ops:
  10.9 2.1 pack.1
  16.4 1.9 collective-permute-start.2
  21.2 2.0 multiply_convert_fusion.2
  23.2 8.0 %collective-permute-done.3.refs_4_ = bf16[128,2048]{1,0:T(8,128)(2,1)} collective-permute-done((bf16[128,2048]{1,0:T(8,128)(2,1)S(1)}, bf16[128,2048]{1,0:T(8,128)(2,1)}, u32[]{:S(2)}, u32[]{:S(2)}) %collective-permute-start.3) | collective-permute-done | bytes 524320 | tf_op jit(solution)/shard_map/ppermute | solution.py:60
  31.8 2.6 collective-permute-start.5
  34.4 7.2 %collective-permute-done.2.refs_3_ = bf16[128,2048]{1,0:T(8,128)(2,1)} collective-permute-done((bf16[128,2048]{1,0:T(8,128)(2,1)S(1)}, bf16[128,2048]{1,0:T(8,128)(2,1)}, u32[]{:S(2)}, u32[]{:S(2)}) %collective-permute-start.2) | collective-permute-done | bytes 524320 | tf_op jit(solution)/shard_map/ppermute | solution.py:71
  44.0 1.9 fusion.8.refs_4_.refs_10_
  45.9 5.7 %collective-permute-done.4.refs_5_ = bf16[128,2048]{1,0:T(8,128)(2,1)} collective-permute-done((bf16[128,2048]{1,0:T(8,128)(2,1)}, bf16[128,2048]{1,0:T(8,128)(2,1)}, u32[]{:S(2)}, u32[]{:S(2)}) %collective-permute-start.4) | collective-permute-done | bytes 524320 | tf_op jit(solution)/shard_map/ppermute | solution.py:52
  51.7 1.9 collective-permute-done.6.refs_7_
  61.3 2.3 collective-permute-start.8
  67.9 12.5 %attend.1 = (bf16[1024,128]{1,0:T(8,128)(2,1)}, bf16[1024,128]{1,0:T(8,128)(2,1)}, bf16[1024,128]{1,0:T(8,128)(2,1)}, bf16[1024,128]{1,0:T(8,128)(2,1)}, bf16[1024,2048]{1,0:T(8,128)(2,1)}) custom-call(s32[8]{0:T(128)} %stack.39.places_ref, bf16[128,2048]{1,0:T(8,128)(2,1)} %refs_0_.1, bf16[128,2048]{1,0:T(8,128)(2,1)} %collective-permute-done.refs_1_, ...), custom_call_target="tpu_custom_call" | custom-call | flops 9000000 | bytes 12000 | tf_op jit(solution)/shard_map/attend/pallas_call | solution.py:219
  80.3 11.7 %all_to_all.34 = bf16[8,128,128]{2,1,0:T(8,128)(2,1)S(1)} all-to-all(bf16[8,128,128]{2,1,0:T(8,128)(2,1)} %bitcast.134), channel_id=1, replica_groups=mesh['fsdp'=8,'ctx'=8,'tp'=2] {'ctx'}, dimensions={0} | all-to-all | bytes 524288 | tf_op jit(solution)/shard_map/all_to_all | solution.py:768
  92.9 4.9 branch.1
  97.9 3.0 collective-permute-start.11
  101.2 8.4 %collective-permute-done.11 = bf16[128,2048]{1,0:T(8,128)(2,1)S(1)} collective-permute-done((bf16[128,2048]{1,0:T(8,128)(2,1)}, bf16[128,2048]{1,0:T(8,128)(2,1)S(1)}, u32[]{:S(2)}, u32[]{:S(2)}) %collective-permute-start.11) | collective-permute-done | bytes 524320 | tf_op jit(solution)/shard_map/ppermute | solution.py:143
  114.0 2.4 collective-permute-start.12
  118.7 9.8 %collective-permute-done.15.refs_0_.refs_6_ = bf16[128,2048]{1,0:T(8,128)(2,1)} collective-permute-done((bf16[128,2048]{1,0:T(8,128)(2,1)S(1)}, bf16[128,2048]{1,0:T(8,128)(2,1)}, u32[]{:S(2)}, u32[]{:S(2)}) %collective-permute-start.15) | collective-permute-done | bytes 524320 | tf_op jit(solution)/shard_map/ppermute | solution.py:71
  130.5 6.5 %collective-permute-done.12.refs_1_.refs_3_ = bf16[128,2048]{1,0:T(8,128)(2,1)S(1)} collective-permute-done((bf16[128,2048]{1,0:T(8,128)(2,1)S(1)}, bf16[128,2048]{1,0:T(8,128)(2,1)S(1)}, u32[]{:S(2)}, u32[]{:S(2)}) %collective-permute-start.12) | collective-permute-done | bytes 524320 | tf_op jit(solution)/shard_map/ppermute | solution.py:52
  137.0 3.2 collective-permute-start.17
  143.6 22.3 %units.2 = (bf16[128,4224]{1,0:T(8,128)(2,1)}, bf16[128,4224]{1,0:T(8,128)(2,1)}, bf16[128,4224]{1,0:T(8,128)(2,1)}, bf16[128,4224]{1,0:T(8,128)(2,1)}, bf16[211...) custom-call(bf16[128,2048]{1,0:T(8,128)(2,1)} %copy-done.3, bf16[128,2048]{1,0:T(8,128)(2,1)} %copy-done.21, ...), custom_call_target="tpu_custom_call" | custom-call | flops 11000000 | bytes 20000 | tf_op jit(solution)/shard_map/units/pallas_call | solution.py:397
  166.9 2.6 collective-permute-start.28
  169.5 22.1 %units.3 = (bf16[128,4224]{1,0:T(8,128)(2,1)}, bf16[128,4224]{1,0:T(8,128)(2,1)}, bf16[128,4224]{1,0:T(8,128)(2,1)}, bf16[128,4224]{1,0:T(8,128)(2,1)}, bf16[211...) custom-call(bf16[128,2048]{1,0:T(8,128)(2,1)} %collective-permute-done.15.refs_0_.r, ...), custom_call_target="tpu_custom_call", output_to_operand_aliasing={{4}: (11, {}), {5}: (12, {})} | custom-call | flops 11000000 | bytes 20000 | tf_op jit(solution)/shard_map/units/pallas_call | solution.py:397
  191.6 20.1 %outer.1 = bf16[8,3168,256]{2,1,0:T(8,128)(2,1)} custom-call(bf16[2112,1024]{1,0:T(8,128)(2,1)} %get-tuple-element.77.refs_0_, bf16[1056,1024]{1,0:T(8,128)(2,1)} %get-tuple-element.78.refs_1_, bf16[128,2048]{1,0:T(8,128)(2,1)} %copy-done.3, bf16[128,2048]{1,0:T(8,128)(2,1)} %copy-done.21, bf16[128,2048]{1,0:T(8,128)(2,1)} %copy-done.22, ...), custom_call_target="tpu_custom_call" | custom-call | flops 4429185 | bytes 10000 | tf_op jit(solution)/shard_map/outer/pallas_call | solution.py:444
  215.2 17.6 %collective-permute-done.22 = bf16[128,4224]{1,0:T(8,128)(2,1)S(1)} collective-permute-done((bf16[128,4224]{1,0:T(8,128)(2,1)}, bf16[128,4224]{1,0:T(8,128)(2,1)S(1)}, u32[]{:S(2)}, u32[]{:S(2)}) %collective-permute-start.22) | collective-permute-done | bytes 1081376 | tf_op jit(solution)/shard_map/ppermute | solution.py:60
  236.0 23.9 %collective-permute-done.24 = bf16[128,4224]{1,0:T(8,128)(2,1)S(1)} collective-permute-done((bf16[128,4224]{1,0:T(8,128)(2,1)}, bf16[128,4224]{1,0:T(8,128)(2,1)S(1)}, u32[]{:S(2)}, u32[]{:S(2)}) %collective-permute-start.24) | collective-permute-done | bytes 1081376 | tf_op jit(solution)/shard_map/ppermute | solution.py:52
  262.1 18.4 %collective-permute-done.26 = bf16[128,4224]{1,0:T(8,128)(2,1)} collective-permute-done((bf16[128,4224]{1,0:T(8,128)(2,1)}, bf16[128,4224]{1,0:T(8,128)(2,1)}, u32[]{:S(2)}, u32[]{:S(2)}) %collective-permute-start.26) | collective-permute-done | bytes 1081376 | tf_op jit(solution)/shard_map/ppermute | solution.py:60
  280.5 3.3 convert_add_fusion
  287.0 11.5 %collective-permute-done.29 = bf16[128,2176]{1,0:T(8,128)(2,1)} collective-permute-done((bf16[128,2176]{1,0:T(8,128)(2,1)}, bf16[128,2176]{1,0:T(8,128)(2,1)}, u32[]{:S(2)}, u32[]{:S(2)}) %collective-permute-start.29) | collective-permute-done | bytes 557088 | tf_op jit(solution)/shard_map/ppermute | solution.py:143
  302.6 1.8 multiply_reduce_fusion
  305.9 3.3 convolution_convert_fusion
  309.3 3.2 collective-permute-start.31
  312.5 3.7 collective-permute-start.32
  316.2 4.6 branch_back.1
  322.5 3.4 all-to-all-start.1
  326.2 12.6 %all-to-all-done.1 = bf16[8,128,128]{2,1,0:T(8,128)(2,1)S(1)} async-done(((bf16[8,128,128]{2,1,0:T(8,128)(2,1)}), bf16[8,128,128]{2,1,0:T(8,128)(2,1)S(1)}, u32[]{:S(2)}, u32[]{:S(2)}) %all-to-all-start.1) | async-done | bytes 262176 | tf_op jit(solution)/shard_map/all_to_all | solution.py:836
  339.4 6.1 %attend_back.1 = (bf16[1024,384]{1,0:T(8,128)(2,1)}, f32[1,384]{1,0:T(1,128)}) custom-call(bf16[1024,128]{1,0:T(8,128)(2,1)} %get-tuple-element.86.q_ref, bf16[1024,128]{1,0:T(8,128)(2,1)} %get-tuple-element.87.k_ref, bf16[1024,128]{1,0:T(8,128)(2,1)} %get-tuple-element.88.v_ref, bf16[1024,128]{1,0:T(8,128)(2,1)} %bitcast.128, ...), custom_call_target="tpu_custom_call" | custom-call | flops 7000000 | bytes 6000 | tf_op jit(solution)/shard_map/attend_back/pallas_call | solution.py:266
  346.8 4.8 convolution_convert_fusion.1
  353.3 3.2 collective-permute-start.37
  358.3 1.9 slice.147
  360.2 1.9 bitcast_bitcast_fusion
  362.6 4.1 all-to-all-start.3
  367.6 2.1 slice.154
  369.7 2.1 collective-permute-start.34
  371.7 2.1 slice.155
  375.2 1.9 copy.202
  377.8 2.3 copy.195
  380.1 15.9 %all-to-all-done.3 = bf16[8,256,128]{2,1,0:T(8,128)(2,1)} async-done(((bf16[8,256,128]{2,1,0:T(8,128)(2,1)}), bf16[8,256,128]{2,1,0:T(8,128)(2,1)}, u32[]{:S(2)}, u32[]{:S(2)}) %all-to-all-start.3) | async-done | bytes 524320 | tf_op jit(solution)/shard_map/all_to_all | solution.py:848
  396.0 4.2 all-to-all-start.2
  402.5 3.6 collective-permute-start.38
  406.2 2.2 multiply_convert_fusion
  409.4 1.9 collective-permute-start.44
  411.3 2.1 slice.160
  417.6 3.7 collective-permute-start.42
  421.3 2.6 pad_maximum_fusion.refs_0_
  424.0 7.8 %place_units.2 = (f32[8,2,704,256]{3,2,1,0:T(8,128)}, f32[8,704,256]{2,1,0:T(8,128)}, bf16[3,8,352,256]{3,2,1,0:T(8,128)(2,1)}) custom-call(s32[4]{0:T(128)} %gather_fusion.1, bf16[3168,256]{1,0:T(8,128)(2,1)} %bitcast.121, bf16[3168,256]{1,0:T(8,128)(2,1)} %collective-permute-done.30.refs_1_, bf16[3168,256]{1,0:T(8,128)(2,1)} %collective-permute-done.31.refs_2_, ...), custom_call_target="tpu_custom_call" | custom-call | flops 1 | bytes 1 | tf_op jit(solution)/shard_map/place_units/pallas_call | solution.py:608
  435.7 10.1 %first_back.1 = bf16[128,2048]{1,0:T(8,128)(2,1)} custom-call(bf16[3,128,1024]{2,1,0:T(8,128)(2,1)} %reshape.197.left_ref, bf16[8,3,256,1024]{3,2,1,0:T(8,128)(2,1)} %bitcast.112), custom_call_target="tpu_custom_call" | custom-call | flops 1700000 | bytes 13000 | tf_op jit(solution)/shard_map/first_back/pallas_call | solution.py:537
  445.9 3.2 collective-permute-start.40
  449.1 3.2 collective-permute-start.47
  452.3 1.9 collective-permute-start.48
  454.3 2.6 pad_maximum_fusion.1.refs_3_
  456.9 7.9 %place_units.3 = (f32[8,2,704,256]{3,2,1,0:T(8,128)}, f32[8,704,256]{2,1,0:T(8,128)}, bf16[3,8,352,256]{3,2,1,0:T(8,128)(2,1)}) custom-call(s32[4]{0:T(128)} %gather_fusion, bf16[3168,256]{1,0:T(8,128)(2,1)} %pad_maximum_fusion.refs_0_, bf16[3168,256]{1,0:T(8,128)(2,1)} %copy-done.12, ...), custom_call_target="tpu_custom_call", output_to_operand_aliasing={{0}: (5, {}), {1}: (6, {}), {2}: (7, {})} | custom-call | flops 1 | bytes 1 | tf_op jit(solution)/shard_map/place_units/pallas_call | solution.py:608
  464.8 5.9 %flip.1 = (f32[256,2,2816]{2,1,0:T(2,128)}, f32[256,2816]{1,0:T(8,128)}) custom-call(bf16[256,256]{1,0:T(8,128)(2,1)} %fusion.11.one_ref, bf16[3,2816,256]{2,1,0:T(8,128)(2,1)} %bitcast.111), custom_call_target="tpu_custom_call" | custom-call | flops 1 | bytes 1 | tf_op jit(solution)/shard_map/flip/pallas_call | solution.py:646
  470.8 3.8 collective-permute-start.43
  476.2 4.6 place.1
  (291 shorter events, 87.5 us)
Async XLA Ops:
  7.2 46.4 %copy-start = (bf16[256,2,2816]{2,1,0:T(2,128)(2,1)S(1)}, bf16[256,2,2816]{2,1,0:T(2,128)(2,1)}, u32[]{:S(2)}) copy-start(bf16[256,2,2816]{2,1,0:T(2,128)(2,1)} %param.27) | copy-start | bytes 8650756
  7.2 58.2 %all-gather.6.cloned.1.call-start = ((), (), s32[]{:S(2)}) async-start(), calls=%async_computation.7 | async-start | bytes 7077888 | tf_op jit(solution)/shard_map/all_gather | solution.py:716
  13.0 130.6 %all-gather.8.cloned.1.call-start = ((), (), s32[]{:S(2)}) async-start(), calls=%async_computation.11 | async-start | bytes 14598144 | tf_op jit(solution)/shard_map/all_gather | solution.py:748
  13.1 32.9 %collective-permute-start = (bf16[128,2048]{1,0:T(8,128)(2,1)S(1)}, bf16[128,2048]{1,0:T(8,128)(2,1)}, u32[]{:S(2)}, u32[]{:S(2)}) collective-permute-start(bf16[128,2048]{1,0:T(8,128)(2,1)S(1)} %copy-done.5), channel_id=1, source_target_pairs={{0,4},{2,6},{4,8},{6,10},{8,12},{10,14},{12,0},{14,2},{1,5},{3,7},... | collective-permute-start | bytes 1572872 | tf_op jit(solution)/shard_map/ppermute | solution.py:52
  14.7 31.2 %collective-permute-start.1 = (bf16[128,2048]{1,0:T(8,128)(2,1)S(1)}, bf16[128,2048]{1,0:T(8,128)(2,1)}, u32[]{:S(2)}, u32[]{:S(2)}) collective-permute-start(bf16[128,2048]{1,0:T(8,128)(2,1)S(1)} %copy-done.5), channel_id=1, source_target_pairs={{0,12},{2,14},{4,0},{6,2},{8,4},{10,6},{12,8},{14,10},{1,13},{3,15... | collective-permute-start | bytes 1572872 | tf_op jit(solution)/shard_map/ppermute | solution.py:56
  16.4 25.2 %collective-permute-start.2 = (bf16[128,2048]{1,0:T(8,128)(2,1)S(1)}, bf16[128,2048]{1,0:T(8,128)(2,1)}, u32[]{:S(2)}, u32[]{:S(2)}) collective-permute-start(bf16[128,2048]{1,0:T(8,128)(2,1)S(1)} %copy-done.5), channel_id=1, source_target_pairs={{0,8},{2,10},{4,12},{6,14},{8,0},{10,2},{12,4},{14,6},{1,9},{3,11}... | collective-permute-start | bytes 1572872 | tf_op jit(solution)/shard_map/ppermute | solution.py:71
  18.3 12.9 %collective-permute-start.3 = (bf16[128,2048]{1,0:T(8,128)(2,1)S(1)}, bf16[128,2048]{1,0:T(8,128)(2,1)}, u32[]{:S(2)}, u32[]{:S(2)}) collective-permute-start(bf16[128,2048]{1,0:T(8,128)(2,1)S(1)} %copy-done.5), channel_id=1, source_target_pairs={{0,2},{2,0},{4,6},{6,4},{8,10},{10,8},{12,14},{14,12},{1,3},{3,1},... | collective-permute-start | bytes 1572872 | tf_op jit(solution)/shard_map/ppermute | solution.py:60
  31.2 20.5 %collective-permute-start.4 = (bf16[128,2048]{1,0:T(8,128)(2,1)}, bf16[128,2048]{1,0:T(8,128)(2,1)}, u32[]{:S(2)}, u32[]{:S(2)}) collective-permute-start(bf16[128,2048]{1,0:T(8,128)(2,1)} %collective-permute-done.3.refs_4_), channel_id=1, source_target_pairs={{0,4},{2,6},{4,8},{6,10},{8,12},{10,14},{12,0},{14,2},{1,5},{3,7},... | collective-permute-start | bytes 1572872 | tf_op jit(solution)/shard_map/ppermute | solution.py:52
  31.8 19.9 %collective-permute-start.5 = (bf16[128,2048]{1,0:T(8,128)(2,1)}, bf16[128,2048]{1,0:T(8,128)(2,1)}, u32[]{:S(2)}, u32[]{:S(2)}) collective-permute-start(bf16[128,2048]{1,0:T(8,128)(2,1)} %collective-permute-done.3.refs_4_), channel_id=1, source_target_pairs={{0,12},{2,14},{4,0},{6,2},{8,4},{10,6},{12,8},{14,10},{1,13},{3,15... | collective-permute-start | bytes 1572872 | tf_op jit(solution)/shard_map/ppermute | solution.py:56
  41.6 12.0 %collective-permute-start.6 = (bf16[128,2048]{1,0:T(8,128)(2,1)}, bf16[128,2048]{1,0:T(8,128)(2,1)}, u32[]{:S(2)}, u32[]{:S(2)}) collective-permute-start(bf16[128,2048]{1,0:T(8,128)(2,1)} %collective-permute-done.2.refs_3_), channel_id=1, source_target_pairs={{0,2},{2,0},{4,6},{6,4},{8,10},{10,8},{12,14},{14,12},{1,3},{3,1},... | collective-permute-start | bytes 1572872 | tf_op jit(solution)/shard_map/ppermute | solution.py:60
  59.5 202.6 %all-gather.10.cloned.1.call-start = ((), (), s32[]{:S(2)}) async-start(), calls=%async_computation.12 | async-start | bytes 14155776 | tf_op jit(solution)/shard_map/all_gather | solution.py:798
  60.2 249.0 %reduce-scatter.4.cloned.1.call-start = ((), (), s32[]{:S(2)}) async-start(), calls=%async_computation.8 | async-start | bytes 14598144 | tf_op jit(solution)/shard_map/reduce_scatter | solution.py:810
  60.3 37.5 %collective-permute-start.7 = (bf16[128,2176]{1,0:T(8,128)(2,1)S(1)}, bf16[128,2176]{1,0:T(8,128)(2,1)S(1)}, u32[]{:S(2)}, u32[]{:S(2)}) collective-permute-start(bf16[128,2176]{1,0:T(8,128)(2,1)S(1)} %copy-done.9), channel_id=1, source_target_pairs={{0,4},{2,6},{4,8},{6,10},{8,12},{10,14},{12,0},{14,2},{1,5},{3,7},... | collective-permute-start | bytes 1671176 | tf_op jit(solution)/shard_map/ppermute | solution.py:52
  61.3 36.6 %collective-permute-start.8 = (bf16[128,2176]{1,0:T(8,128)(2,1)S(1)}, bf16[128,2176]{1,0:T(8,128)(2,1)S(1)}, u32[]{:S(2)}, u32[]{:S(2)}) collective-permute-start(bf16[128,2176]{1,0:T(8,128)(2,1)S(1)} %copy-done.9), channel_id=1, source_target_pairs={{0,12},{2,14},{4,0},{6,2},{8,4},{10,6},{12,8},{14,10},{1,13},{3,15... | collective-permute-start | bytes 1671176 | tf_op jit(solution)/shard_map/ppermute | solution.py:56
  63.6 34.2 %collective-permute-start.9 = (bf16[128,2176]{1,0:T(8,128)(2,1)S(1)}, bf16[128,2176]{1,0:T(8,128)(2,1)}, u32[]{:S(2)}, u32[]{:S(2)}) collective-permute-start(bf16[128,2176]{1,0:T(8,128)(2,1)S(1)} %copy-done.9), channel_id=1, source_target_pairs={{0,2},{2,0},{4,6},{6,4},{8,10},{10,8},{12,14},{14,12},{1,3},{3,1},... | collective-permute-start | bytes 1671176 | tf_op jit(solution)/shard_map/ppermute | solution.py:60
  65.2 32.7 %collective-permute-start.10 = (bf16[128,2176]{1,0:T(8,128)(2,1)S(1)}, bf16[128,2176]{1,0:T(8,128)(2,1)}, u32[]{:S(2)}, u32[]{:S(2)}) collective-permute-start(bf16[128,2176]{1,0:T(8,128)(2,1)S(1)} %copy-done.9), channel_id=1, source_target_pairs={{0,8},{2,10},{4,12},{6,14},{8,0},{10,2},{12,4},{14,6},{1,9},{3,11}... | collective-permute-start | bytes 1671176 | tf_op jit(solution)/shard_map/ppermute | solution.py:71
  97.9 11.8 %collective-permute-start.11 = (bf16[128,2048]{1,0:T(8,128)(2,1)}, bf16[128,2048]{1,0:T(8,128)(2,1)S(1)}, u32[]{:S(2)}, u32[]{:S(2)}) collective-permute-start(bf16[128,2048]{1,0:T(8,128)(2,1)} %branch.1), channel_id=1, source_target_pairs={{0,1},{1,0},{2,3},{3,2},{4,5},{5,4},{6,7},{7,6},{8,9},{9,8},{10,11... | collective-permute-start | bytes 1572872 | tf_op jit(solution)/shard_map/ppermute | solution.py:143
  100.9 16.4 %collective-permute-start.19 = (bf16[128,2176]{1,0:T(8,128)(2,1)}, bf16[128,2176]{1,0:T(8,128)(2,1)S(1)}, u32[]{:S(2)}, u32[]{:S(2)}) collective-permute-start(bf16[128,2176]{1,0:T(8,128)(2,1)} %collective-permute-done.9.refs_7_.refs_13_), channel_id=1, source_target_pairs={{0,4},{2,6},{4,8},{6,10},{8,12},{10,14},{12,0},{14,2},{1,5},{3,7},... | collective-permute-start | bytes 1671176 | tf_op jit(solution)/shard_map/ppermute | solution.py:52
  111.5 54.4 %copy-start.41 = (f32[128]{0:T(128)}, f32[128]{0:T(128)S(1)}, u32[]{:S(2)}) copy-start(f32[128]{0:T(128)S(1)} %get-tuple-element.202) | copy-start | bytes 1540
  111.7 31.9 %copy-start.3 = (bf16[128,2048]{1,0:T(8,128)(2,1)}, bf16[128,2048]{1,0:T(8,128)(2,1)S(1)}, u32[]{:S(2)}) copy-start(bf16[128,2048]{1,0:T(8,128)(2,1)S(1)} %multiply_convert_fusion.1.refs_0_.refs_2_) | copy-start | bytes 1572868
  111.7 16.7 %collective-permute-start.15 = (bf16[128,2048]{1,0:T(8,128)(2,1)S(1)}, bf16[128,2048]{1,0:T(8,128)(2,1)}, u32[]{:S(2)}, u32[]{:S(2)}) collective-permute-start(bf16[128,2048]{1,0:T(8,128)(2,1)S(1)} %multiply_convert_fusion.1.refs_0_.refs_2_), channel_id=1, source_target_pairs={{0,8},{2,10},{4,12},{6,14},{8,0},{10,2},{12,4},{14,6},{1,9},{3,11}... | collective-permute-start | bytes 1572872 | tf_op jit(solution)/shard_map/ppermute | solution.py:71
  113.3 16.1 %collective-permute-start.14 = (bf16[128,2048]{1,0:T(8,128)(2,1)S(1)}, bf16[128,2048]{1,0:T(8,128)(2,1)}, u32[]{:S(2)}, u32[]{:S(2)}) collective-permute-start(bf16[128,2048]{1,0:T(8,128)(2,1)S(1)} %multiply_convert_fusion.1.refs_0_.refs_2_), channel_id=1, source_target_pairs={{0,2},{2,0},{4,6},{6,4},{8,10},{10,8},{12,14},{14,12},{1,3},{3,1},... | collective-permute-start | bytes 1572872 | tf_op jit(solution)/shard_map/ppermute | solution.py:60
  114.0 23.0 %collective-permute-start.12 = (bf16[128,2048]{1,0:T(8,128)(2,1)S(1)}, bf16[128,2048]{1,0:T(8,128)(2,1)S(1)}, u32[]{:S(2)}, u32[]{:S(2)}) collective-permute-start(bf16[128,2048]{1,0:T(8,128)(2,1)S(1)} %multiply_convert_fusion.1.refs_0_.refs_2_), channel_id=1, source_target_pairs={{0,4},{2,6},{4,8},{6,10},{8,12},{10,14},{12,0},{14,2},{1,5},{3,7},... | collective-permute-start | bytes 1572872 | tf_op jit(solution)/shard_map/ppermute | solution.py:52
  116.4 23.7 %collective-permute-start.13 = (bf16[128,2048]{1,0:T(8,128)(2,1)S(1)}, bf16[128,2048]{1,0:T(8,128)(2,1)S(1)}, u32[]{:S(2)}, u32[]{:S(2)}) collective-permute-start(bf16[128,2048]{1,0:T(8,128)(2,1)S(1)} %multiply_convert_fusion.1.refs_0_.refs_2_), channel_id=1, source_target_pairs={{0,12},{2,14},{4,0},{6,2},{8,4},{10,6},{12,8},{14,10},{1,13},{3,15... | collective-permute-start | bytes 1572872 | tf_op jit(solution)/shard_map/ppermute | solution.py:56
  117.2 22.9 %copy-start.18 = (bf16[128,2176]{1,0:T(8,128)(2,1)}, bf16[128,2176]{1,0:T(8,128)(2,1)S(1)}, u32[]{:S(2)}) copy-start(bf16[128,2176]{1,0:T(8,128)(2,1)S(1)} %collective-permute-done.19.refs_5_.refs_15_) | copy-start | bytes 1671172
  117.2 48.7 %collective-permute-start.20 = (bf16[128,2176]{1,0:T(8,128)(2,1)}, bf16[128,2176]{1,0:T(8,128)(2,1)S(1)}, u32[]{:S(2)}, u32[]{:S(2)}) collective-permute-start(bf16[128,2176]{1,0:T(8,128)(2,1)} %collective-permute-done.9.refs_7_.refs_13_), channel_id=1, source_target_pairs={{0,12},{2,14},{4,0},{6,2},{8,4},{10,6},{12,8},{14,10},{1,13},{3,15... | collective-permute-start | bytes 1671176 | tf_op jit(solution)/shard_map/ppermute | solution.py:56
  128.4 37.5 %collective-permute-start.21 = (bf16[128,2176]{1,0:T(8,128)(2,1)}, bf16[128,2176]{1,0:T(8,128)(2,1)S(1)}, u32[]{:S(2)}, u32[]{:S(2)}) collective-permute-start(bf16[128,2176]{1,0:T(8,128)(2,1)} %collective-permute-done.10.refs_4_.refs_14_), channel_id=1, source_target_pairs={{0,2},{2,0},{4,6},{6,4},{8,10},{10,8},{12,14},{14,12},{1,3},{3,1},... | collective-permute-start | bytes 1671176 | tf_op jit(solution)/shard_map/ppermute | solution.py:60
  129.4 36.6 %collective-permute-start.16 = (bf16[128,2048]{1,0:T(8,128)(2,1)}, bf16[128,2048]{1,0:T(8,128)(2,1)}, u32[]{:S(2)}, u32[]{:S(2)}) collective-permute-start(bf16[128,2048]{1,0:T(8,128)(2,1)} %collective-permute-done.14.refs_3_.refs_5_), channel_id=1, source_target_pairs={{0,4},{2,6},{4,8},{6,10},{8,12},{10,14},{12,0},{14,2},{1,5},{3,7},... | collective-permute-start | bytes 1572872 | tf_op jit(solution)/shard_map/ppermute | solution.py:52
  137.0 29.0 %collective-permute-start.17 = (bf16[128,2048]{1,0:T(8,128)(2,1)}, bf16[128,2048]{1,0:T(8,128)(2,1)}, u32[]{:S(2)}, u32[]{:S(2)}) collective-permute-start(bf16[128,2048]{1,0:T(8,128)(2,1)} %collective-permute-done.14.refs_3_.refs_5_), channel_id=1, source_target_pairs={{0,12},{2,14},{4,0},{6,2},{8,4},{10,6},{12,8},{14,10},{1,13},{3,15... | collective-permute-start | bytes 1572872 | tf_op jit(solution)/shard_map/ppermute | solution.py:56
  141.0 25.1 %collective-permute-start.18 = (bf16[128,2048]{1,0:T(8,128)(2,1)}, bf16[128,2048]{1,0:T(8,128)(2,1)}, u32[]{:S(2)}, u32[]{:S(2)}) collective-permute-start(bf16[128,2048]{1,0:T(8,128)(2,1)} %collective-permute-done.15.refs_0_.refs_6_), channel_id=1, source_target_pairs={{0,2},{2,0},{4,6},{6,4},{8,10},{10,8},{12,14},{14,12},{1,3},{3,1},... | collective-permute-start | bytes 1572872 | tf_op jit(solution)/shard_map/ppermute | solution.py:60
  166.0 25.6 %collective-permute-start.27 = (bf16[128,4224]{1,0:T(8,128)(2,1)}, bf16[128,4224]{1,0:T(8,128)(2,1)}, u32[]{:S(2)}, u32[]{:S(2)}) collective-permute-start(bf16[128,4224]{1,0:T(8,128)(2,1)} %get-tuple-element.74), channel_id=1, source_target_pairs={{0,4},{2,6},{4,8},{6,10},{8,12},{10,14},{12,0},{14,2},{1,5},{3,7},... | collective-permute-start | bytes 3244040 | tf_op jit(solution)/shard_map/ppermute | solution.py:52
  166.9 24.7 %collective-permute-start.28 = (bf16[128,4224]{1,0:T(8,128)(2,1)}, bf16[128,4224]{1,0:T(8,128)(2,1)}, u32[]{:S(2)}, u32[]{:S(2)}) collective-permute-start(bf16[128,4224]{1,0:T(8,128)(2,1)} %get-tuple-element.75), channel_id=1, source_target_pairs={{0,12},{2,14},{4,0},{6,2},{8,4},{10,6},{12,8},{14,10},{1,13},{3,15... | collective-permute-start | bytes 3244040 | tf_op jit(solution)/shard_map/ppermute | solution.py:56
  211.7 148.5 %reduce-scatter.6.cloned.1.call-start = ((), (), s32[]{:S(2)}) async-start(), calls=%async_computation.9 | async-start | bytes 4718592 | tf_op jit(solution)/shard_map/reduce_scatter | solution.py:843
  211.8 21.1 %collective-permute-start.22 = (bf16[128,4224]{1,0:T(8,128)(2,1)}, bf16[128,4224]{1,0:T(8,128)(2,1)S(1)}, u32[]{:S(2)}, u32[]{:S(2)}) collective-permute-start(bf16[128,4224]{1,0:T(8,128)(2,1)} %get-tuple-element.68), channel_id=1, source_target_pairs={{0,2},{2,0},{4,6},{6,4},{8,10},{10,8},{12,14},{14,12},{1,3},{3,1},... | collective-permute-start | bytes 3244040 | tf_op jit(solution)/shard_map/ppermute | solution.py:60
  213.2 22.8 %collective-permute-start.25 = (bf16[128,4224]{1,0:T(8,128)(2,1)}, bf16[128,4224]{1,0:T(8,128)(2,1)S(1)}, u32[]{:S(2)}, u32[]{:S(2)}) collective-permute-start(bf16[128,4224]{1,0:T(8,128)(2,1)} %get-tuple-element.71), channel_id=1, source_target_pairs={{0,12},{2,14},{4,0},{6,2},{8,4},{10,6},{12,8},{14,10},{1,13},{3,15... | collective-permute-start | bytes 3244040 | tf_op jit(solution)/shard_map/ppermute | solution.py:56
  213.8 46.1 %collective-permute-start.24 = (bf16[128,4224]{1,0:T(8,128)(2,1)}, bf16[128,4224]{1,0:T(8,128)(2,1)S(1)}, u32[]{:S(2)}, u32[]{:S(2)}) collective-permute-start(bf16[128,4224]{1,0:T(8,128)(2,1)} %get-tuple-element.70), channel_id=1, source_target_pairs={{0,4},{2,6},{4,8},{6,10},{8,12},{10,14},{12,0},{14,2},{1,5},{3,7},... | collective-permute-start | bytes 3244040 | tf_op jit(solution)/shard_map/ppermute | solution.py:52
  232.8 27.0 %copy-start.28 = (bf16[128,4224]{1,0:T(8,128)(2,1)S(1)}, bf16[128,4224]{1,0:T(8,128)(2,1)}, u32[]{:S(2)}) copy-start(bf16[128,4224]{1,0:T(8,128)(2,1)} %get-tuple-element.69) | copy-start | bytes 3244036
  234.1 28.1 %collective-permute-start.23 = (bf16[128,4224]{1,0:T(8,128)(2,1)}, bf16[128,4224]{1,0:T(8,128)(2,1)S(1)}, u32[]{:S(2)}, u32[]{:S(2)}) collective-permute-start(bf16[128,4224]{1,0:T(8,128)(2,1)} %add_convert_fusion.1), channel_id=1, source_target_pairs={{0,8},{2,10},{4,12},{6,14},{8,0},{10,2},{12,4},{14,6},{1,9},{3,11}... | collective-permute-start | bytes 3244040 | tf_op jit(solution)/shard_map/ppermute | solution.py:71
  261.2 19.3 %collective-permute-start.26 = (bf16[128,4224]{1,0:T(8,128)(2,1)}, bf16[128,4224]{1,0:T(8,128)(2,1)}, u32[]{:S(2)}, u32[]{:S(2)}) collective-permute-start(bf16[128,4224]{1,0:T(8,128)(2,1)} %add_convert_fusion), channel_id=1, source_target_pairs={{0,2},{2,0},{4,6},{6,4},{8,10},{10,8},{12,14},{14,12},{1,3},{3,1},... | collective-permute-start | bytes 3244040 | tf_op jit(solution)/shard_map/ppermute | solution.py:60
  284.8 13.7 %collective-permute-start.29 = (bf16[128,2176]{1,0:T(8,128)(2,1)}, bf16[128,2176]{1,0:T(8,128)(2,1)}, u32[]{:S(2)}, u32[]{:S(2)}) collective-permute-start(bf16[128,2176]{1,0:T(8,128)(2,1)} %slice.203), channel_id=1, source_target_pairs={{0,1},{1,0},{2,3},{3,2},{4,5},{5,4},{6,7},{7,6},{8,9},{9,8},{10,11... | collective-permute-start | bytes 1671176 | tf_op jit(solution)/shard_map/ppermute | solution.py:143
  309.2 29.5 %collective-permute-start.30 = (bf16[3168,256]{1,0:T(8,128)(2,1)}, bf16[3168,256]{1,0:T(8,128)(2,1)}, u32[]{:S(2)}, u32[]{:S(2)}) collective-permute-start(bf16[3168,256]{1,0:T(8,128)(2,1)} %bitcast.118), channel_id=1, source_target_pairs={{0,4},{2,6},{4,8},{6,10},{8,12},{10,14},{12,0},{14,2},{1,5},{3,7},... | collective-permute-start | bytes 4866056 | tf_op jit(solution)/shard_map/ppermute | solution.py:52
  309.3 29.4 %collective-permute-start.31 = (bf16[3168,256]{1,0:T(8,128)(2,1)}, bf16[3168,256]{1,0:T(8,128)(2,1)}, u32[]{:S(2)}, u32[]{:S(2)}) collective-permute-start(bf16[3168,256]{1,0:T(8,128)(2,1)} %bitcast.119), channel_id=1, source_target_pairs={{0,12},{2,14},{4,0},{6,2},{8,4},{10,6},{12,8},{14,10},{1,13},{3,15... | collective-permute-start | bytes 4866056 | tf_op jit(solution)/shard_map/ppermute | solution.py:56
  312.5 26.2 %collective-permute-start.32 = (bf16[3168,256]{1,0:T(8,128)(2,1)}, bf16[3168,256]{1,0:T(8,128)(2,1)}, u32[]{:S(2)}, u32[]{:S(2)}) collective-permute-start(bf16[3168,256]{1,0:T(8,128)(2,1)} %bitcast.120), channel_id=1, source_target_pairs={{0,2},{2,0},{4,6},{6,4},{8,10},{10,8},{12,14},{14,12},{1,3},{3,1},... | collective-permute-start | bytes 4866056 | tf_op jit(solution)/shard_map/ppermute | solution.py:60
  322.5 16.2 %all-to-all-start.1 = ((bf16[8,128,128]{2,1,0:T(8,128)(2,1)}), bf16[8,128,128]{2,1,0:T(8,128)(2,1)S(1)}, u32[]{:S(2)}, u32[]{:S(2)}) async-start(bf16[8,128,128]{2,1,0:T(8,128)(2,1)} %bitcast_bitcast_fusion.1), calls=%async_computation.1 | async-start | bytes 524288 | tf_op jit(solution)/shard_map/all_to_all | solution.py:836
  325.9 75.5 %reduce-scatter.8.cloned.1.call-start = ((), (), s32[]{:S(2)}) async-start(), calls=%async_computation.10 | async-start | bytes 2359296 | tf_op jit(solution)/shard_map/reduce_scatter | solution.py:863
  353.2 55.2 %collective-permute-start.36 = (bf16[3168,256]{1,0:T(8,128)(2,1)}, bf16[3168,256]{1,0:T(8,128)(2,1)S(1)}, u32[]{:S(2)}, u32[]{:S(2)}) collective-permute-start(bf16[3168,256]{1,0:T(8,128)(2,1)} %collective-permute-done.32.refs_3_), channel_id=1, source_target_pairs={{0,4},{2,6},{4,8},{6,10},{8,12},{10,14},{12,0},{14,2},{1,5},{3,7},... | collective-permute-start | bytes 4866056 | tf_op jit(solution)/shard_map/ppermute | solution.py:52
  353.3 58.0 %collective-permute-start.37 = (bf16[3168,256]{1,0:T(8,128)(2,1)}, bf16[3168,256]{1,0:T(8,128)(2,1)}, u32[]{:S(2)}, u32[]{:S(2)}) collective-permute-start(bf16[3168,256]{1,0:T(8,128)(2,1)} %collective-permute-done.32.refs_3_), channel_id=1, source_target_pairs={{0,12},{2,14},{4,0},{6,2},{8,4},{10,6},{12,8},{14,10},{1,13},{3,15... | collective-permute-start | bytes 4866056 | tf_op jit(solution)/shard_map/ppermute | solution.py:56
  362.2 40.4 %collective-permute-start.33 = (bf16[128,2048]{1,0:T(8,128)(2,1)}, bf16[128,2048]{1,0:T(8,128)(2,1)}, u32[]{:S(2)}, u32[]{:S(2)}) collective-permute-start(bf16[128,2048]{1,0:T(8,128)(2,1)} %slice.147), channel_id=1, source_target_pairs={{0,1},{1,0},{2,3},{3,2},{4,5},{5,4},{6,7},{7,6},{8,9},{9,8},{10,11... | collective-permute-start | bytes 1572872 | tf_op jit(solution)/shard_map/ppermute | solution.py:143
  362.6 33.4 %all-to-all-start.3 = ((bf16[8,256,128]{2,1,0:T(8,128)(2,1)}), bf16[8,256,128]{2,1,0:T(8,128)(2,1)}, u32[]{:S(2)}, u32[]{:S(2)}) async-start(bf16[8,256,128]{2,1,0:T(8,128)(2,1)} %bitcast_bitcast_fusion), calls=%async_computation.5 | async-start | bytes 1048576 | tf_op jit(solution)/shard_map/all_to_all | solution.py:848
  369.7 45.1 %collective-permute-start.34 = (bf16[1584,256]{1,0:T(8,128)(2,1)}, bf16[1584,256]{1,0:T(8,128)(2,1)}, u32[]{:S(2)}, u32[]{:S(2)}) collective-permute-start(bf16[1584,256]{1,0:T(8,128)(2,1)} %slice.154), channel_id=1, source_target_pairs={{0,4},{2,6},{4,8},{6,10},{8,12},{10,14},{12,0},{14,2},{1,5},{3,7},... | collective-permute-start | bytes 2433032 | tf_op jit(solution)/shard_map/ppermute | solution.py:52
  373.8 40.9 %collective-permute-start.35 = (bf16[1584,256]{1,0:T(8,128)(2,1)}, bf16[1584,256]{1,0:T(8,128)(2,1)}, u32[]{:S(2)}, u32[]{:S(2)}) collective-permute-start(bf16[1584,256]{1,0:T(8,128)(2,1)} %slice.155), channel_id=1, source_target_pairs={{0,12},{2,14},{4,0},{6,2},{8,4},{10,6},{12,8},{14,10},{1,13},{3,15... | collective-permute-start | bytes 2433032 | tf_op jit(solution)/shard_map/ppermute | solution.py:56
  396.0 35.8 %all-to-all-start.2 = ((bf16[8,128,384]{1,2,0:T(8,128)(2,1)}), bf16[8,128,384]{1,2,0:T(8,128)(2,1)}, u32[]{:S(2)}, u32[]{:S(2)}) async-start(bf16[8,128,384]{1,2,0:T(8,128)(2,1)} %copy.195), calls=%async_computation.3 | async-start | bytes 1572864 | tf_op jit(solution)/shard_map/all_to_all | solution.py:850
  402.5 13.5 %collective-permute-start.38 = (f32[256]{0:T(256)S(1)}, f32[256]{0:T(256)S(1)}, u32[]{:S(2)}, u32[]{:S(2)}) collective-permute-start(f32[256]{0:T(256)S(1)} %multiply_reduce_fusion.3), channel_id=1, source_target_pairs={{0,1},{1,0},{2,3},{3,2},{4,5},{5,4},{6,7},{7,6},{8,9},{9,8},{10,11... | collective-permute-start | bytes 3080 | tf_op jit(solution)/shard_map/ppermute | solution.py:868
  409.4 36.4 %collective-permute-start.44 = (bf16[1584,256]{1,0:T(8,128)(2,1)}, bf16[1584,256]{1,0:T(8,128)(2,1)}, u32[]{:S(2)}, u32[]{:S(2)}) collective-permute-start(bf16[1584,256]{1,0:T(8,128)(2,1)} %slice.159), channel_id=1, source_target_pairs={{0,4},{2,6},{4,8},{6,10},{8,12},{10,14},{12,0},{14,2},{1,5},{3,7},... | collective-permute-start | bytes 2433032 | tf_op jit(solution)/shard_map/ppermute | solution.py:52
  413.4 35.7 %collective-permute-start.45 = (bf16[1584,256]{1,0:T(8,128)(2,1)}, bf16[1584,256]{1,0:T(8,128)(2,1)}, u32[]{:S(2)}, u32[]{:S(2)}) collective-permute-start(bf16[1584,256]{1,0:T(8,128)(2,1)} %slice.160), channel_id=1, source_target_pairs={{0,12},{2,14},{4,0},{6,2},{8,4},{10,6},{12,8},{14,10},{1,13},{3,15... | collective-permute-start | bytes 2433032 | tf_op jit(solution)/shard_map/ppermute | solution.py:56
  416.3 29.6 %copy-start.25 = (bf16[256,640]{1,0:T(8,128)(2,1)}, bf16[256,640]{1,0:T(8,128)(2,1)S(1)}, u32[]{:S(2)}) copy-start(bf16[256,640]{1,0:T(8,128)(2,1)S(1)} %pad_maximum_fusion.2.refs_0_) | copy-start | bytes 983044
  416.3 32.8 %collective-permute-start.41 = (bf16[256,640]{1,0:T(8,128)(2,1)S(1)}, bf16[256,640]{1,0:T(8,128)(2,1)S(1)}, u32[]{:S(2)}, u32[]{:S(2)}) collective-permute-start(bf16[256,640]{1,0:T(8,128)(2,1)S(1)} %pad_maximum_fusion.2.refs_0_), channel_id=1, source_target_pairs={{0,2},{2,0},{4,6},{6,4},{8,10},{10,8},{12,14},{14,12},{1,3},{3,1},... | collective-permute-start | bytes 983048 | tf_op jit(solution)/shard_map/ppermute | solution.py:60
  417.6 34.7 %collective-permute-start.42 = (bf16[256,640]{1,0:T(8,128)(2,1)S(1)}, bf16[256,640]{1,0:T(8,128)(2,1)S(1)}, u32[]{:S(2)}, u32[]{:S(2)}) collective-permute-start(bf16[256,640]{1,0:T(8,128)(2,1)S(1)} %pad_maximum_fusion.2.refs_0_), channel_id=1, source_target_pairs={{0,8},{2,10},{4,12},{6,14},{8,0},{10,2},{12,4},{14,6},{1,9},{3,11}... | collective-permute-start | bytes 983048 | tf_op jit(solution)/shard_map/ppermute | solution.py:71
  445.8 24.9 %collective-permute-start.39 = (bf16[256,640]{1,0:T(8,128)(2,1)S(1)}, bf16[256,640]{1,0:T(8,128)(2,1)S(1)}, u32[]{:S(2)}, u32[]{:S(2)}) collective-permute-start(bf16[256,640]{1,0:T(8,128)(2,1)S(1)} %pad_maximum_fusion.2.refs_0_), channel_id=1, source_target_pairs={{0,4},{2,6},{4,8},{6,10},{8,12},{10,14},{12,0},{14,2},{1,5},{3,7},... | collective-permute-start | bytes 983048 | tf_op jit(solution)/shard_map/ppermute | solution.py:52
  445.9 24.9 %collective-permute-start.40 = (bf16[256,640]{1,0:T(8,128)(2,1)S(1)}, bf16[256,640]{1,0:T(8,128)(2,1)S(1)}, u32[]{:S(2)}, u32[]{:S(2)}) collective-permute-start(bf16[256,640]{1,0:T(8,128)(2,1)S(1)} %pad_maximum_fusion.2.refs_0_), channel_id=1, source_target_pairs={{0,12},{2,14},{4,0},{6,2},{8,4},{10,6},{12,8},{14,10},{1,13},{3,15... | collective-permute-start | bytes 983048 | tf_op jit(solution)/shard_map/ppermute | solution.py:56
  449.1 25.5 %collective-permute-start.46 = (bf16[256,640]{1,0:T(8,128)(2,1)S(1)}, bf16[256,640]{1,0:T(8,128)(2,1)S(1)}, u32[]{:S(2)}, u32[]{:S(2)}) collective-permute-start(bf16[256,640]{1,0:T(8,128)(2,1)S(1)} %collective-permute-done.41.refs_4_), channel_id=1, source_target_pairs={{0,4},{2,6},{4,8},{6,10},{8,12},{10,14},{12,0},{14,2},{1,5},{3,7},... | collective-permute-start | bytes 983048 | tf_op jit(solution)/shard_map/ppermute | solution.py:52
  449.1 25.5 %collective-permute-start.47 = (bf16[256,640]{1,0:T(8,128)(2,1)S(1)}, bf16[256,640]{1,0:T(8,128)(2,1)S(1)}, u32[]{:S(2)}, u32[]{:S(2)}) collective-permute-start(bf16[256,640]{1,0:T(8,128)(2,1)S(1)} %collective-permute-done.41.refs_4_), channel_id=1, source_target_pairs={{0,12},{2,14},{4,0},{6,2},{8,4},{10,6},{12,8},{14,10},{1,13},{3,15... | collective-permute-start | bytes 983048 | tf_op jit(solution)/shard_map/ppermute | solution.py:56
  452.3 22.3 %collective-permute-start.48 = (bf16[256,640]{1,0:T(8,128)(2,1)S(1)}, bf16[256,640]{1,0:T(8,128)(2,1)S(1)}, u32[]{:S(2)}, u32[]{:S(2)}) collective-permute-start(bf16[256,640]{1,0:T(8,128)(2,1)S(1)} %collective-permute-done.42.refs_3_), channel_id=1, source_target_pairs={{0,2},{2,0},{4,6},{6,4},{8,10},{10,8},{12,14},{14,12},{1,3},{3,1},... | collective-permute-start | bytes 983048 | tf_op jit(solution)/shard_map/ppermute | solution.py:60
  470.8 15.3 %collective-permute-start.43 = (bf16[128,2048]{1,0:T(8,128)(2,1)S(1)}, bf16[128,2048]{1,0:T(8,128)(2,1)S(1)}, u32[]{:S(2)}, u32[]{:S(2)}) collective-permute-start(bf16[128,2048]{1,0:T(8,128)(2,1)S(1)} %copy-done.24), channel_id=1, source_target_pairs={{0,1},{1,0},{2,3},{3,2},{4,5},{5,4},{6,7},{7,6},{8,9},{9,8},{10,11... | collective-permute-start | bytes 1572872 | tf_op jit(solution)/shard_map/ppermute | solution.py:143
  (43 other events, 257.6 us)
Sparse Core Ops, SparseCore 0:
  13.1 43.5 all-gather.5
  59.6 69.9 all-gather.7
  131.3 67.8 all-gather.9
  211.8 74.3 reduce-scatter.3
  309.3 41.1 reduce-scatter.5
  353.4 34.3 reduce-scatter.7

commit v5 on v4

--- a/solution.py
+++ b/solution.py
@@ -178,7 +178,7 @@
     columns = lax.broadcasted_iota(jnp.int32, scores.shape, 1)
     scores = jnp.where(columns <= rows, scores, MASKED_SCORE)
     expons = jnp.exp(scores - jnp.max(scores, axis=-1, keepdims=True))
-    return expons / jnp.sum(expons, axis=-1, keepdims=True)
+    return expons * (1.0 / jnp.sum(expons, axis=-1, keepdims=True))
 
 
 def block_rows(place, rows):
@@ -739,7 +739,7 @@
         [grad_own, jnp.pad(low(chosen), ((0, 0), (0, 128 - experts)))], axis=1
     )
     here_late = after(here, (x_first, x_second, grad_pack, block_places))
-    shared_start = here_late * shared_units
+    shared_start = after(here, x_first) * shared_units
     shared_gu = lax.dynamic_slice(w_sgu, (0, 0, shared_start), (shard, 2, shared_units))
     shared_gu = shared_gu.transpose(1, 2, 0)
     shared_down = lax.dynamic_slice(w_sdown, (0, shared_start), (shard, shared_units)).T

time: 502 us -> 500 us (level)
  no operation moved by 1% of the time
where the time goes in v5:
time: 500 us; the launch traced here: 493 us
  waiting for transfers between devices  144 us (29%)
  Pallas kernels  131 us (26%)
  starting transfers between devices  96 us (19%)
  local copies, waits for them, and re-layouts  48.5 us (10%)
  other arithmetic  35.7 us (7%)
  between operations  15.3 us (3%)
  blocking collectives  11.9 us (2%)
  matrix products  10.3 us (2%)
    ppermute x11, waiting for transfers between devices, swap(): return lax.ppermute(values, 'ctx', PAIR)  45.9 us
    pallas_call x2, Pallas kernels, units_forward_back(): pl.pallas_call(functools.partial(units_kernel, len(earlier) // 2), in_spe...  45.1 us
    ppermute x14, waiting for transfers between devices, up(): return lax.ppermute(values, 'ctx', ring(2))  35 us
    ppermute x14, starting transfers between devices, down(): return lax.ppermute(values, 'ctx', ring(-2))  31.9 us
    pallas_call x1, Pallas kernels, outer_products(): pl.pallas_call(outer_kernel, grid=(4,), in_specs=[whole(back), whole(hidd...  20.1 us
    ppermute x4, waiting for transfers between devices, add_halves(): return wide(mine) + wide(lax.ppermute(mine, 'tp', [(0, 1), (1, 0)]))  19.8 us
    ppermute x5, waiting for transfers between devices, across(): return lax.ppermute(values, 'ctx', ring(4))  16.8 us
    pallas_call x2, Pallas kernels, place_units(): pl.pallas_call(place_units_kernel, grid_spec=pltpu.PrefetchScalarGridSpec...  15.7 us
  transfers between devices with their start and end apart: 58, of which 14 were waited for; matrix products, arithmetic and copies ran while one was open for 17% of the time, Pallas kernels for 26%

profile of v5, /device:TPU:0, one launch (start us, length us, event | category | flops | bytes accessed | tf_op | source)
XLA Modules:
  0.0 493.3 jit_solution(15396168457008431292)
XLA Ops:
  10.9 2.1 pack.1
  16.4 1.9 collective-permute-start.2
  21.1 2.0 multiply_convert_fusion.2
  24.0 7.2 %collective-permute-done.3.refs_4_ = bf16[128,2048]{1,0:T(8,128)(2,1)} collective-permute-done((bf16[128,2048]{1,0:T(8,128)(2,1)S(1)}, bf16[128,2048]{1,0:T(8,128)(2,1)}, u32[]{:S(2)}, u32[]{:S(2)}) %collective-permute-start.3) | collective-permute-done | bytes 524320 | tf_op jit(solution)/shard_map/ppermute | solution.py:60
  31.8 2.6 collective-permute-start.5
  34.4 7.2 %collective-permute-done.2.refs_3_ = bf16[128,2048]{1,0:T(8,128)(2,1)} collective-permute-done((bf16[128,2048]{1,0:T(8,128)(2,1)S(1)}, bf16[128,2048]{1,0:T(8,128)(2,1)}, u32[]{:S(2)}, u32[]{:S(2)}) %collective-permute-start.2) | collective-permute-done | bytes 524320 | tf_op jit(solution)/shard_map/ppermute | solution.py:71
  43.2 1.9 fusion.8.refs_4_.refs_10_
  47.5 4.1 collective-permute-done.4.refs_5_
  51.7 1.9 collective-permute-done.6.refs_7_
  58.7 2.5 collective-permute-start.8
  65.5 12.0 %attend.1 = (bf16[1024,128]{1,0:T(8,128)(2,1)}, bf16[1024,128]{1,0:T(8,128)(2,1)}, bf16[1024,128]{1,0:T(8,128)(2,1)}, bf16[1024,128]{1,0:T(8,128)(2,1)}, bf16[1024,2048]{1,0:T(8,128)(2,1)}) custom-call(s32[8]{0:T(128)} %stack.39.places_ref, bf16[128,2048]{1,0:T(8,128)(2,1)} %refs_0_.1, bf16[128,2048]{1,0:T(8,128)(2,1)} %collective-permute-done.refs_1_, ...), custom_call_target="tpu_custom_call" | custom-call | flops 9000000 | bytes 12000 | tf_op jit(solution)/shard_map/attend/pallas_call | solution.py:219
  77.5 11.9 %all_to_all.34 = bf16[8,128,128]{2,1,0:T(8,128)(2,1)S(1)} all-to-all(bf16[8,128,128]{2,1,0:T(8,128)(2,1)} %bitcast.134), channel_id=1, replica_groups=mesh['fsdp'=8,'ctx'=8,'tp'=2] {'ctx'}, dimensions={0} | all-to-all | bytes 524288 | tf_op jit(solution)/shard_map/all_to_all | solution.py:768
  90.1 4.9 %branch.1 = bf16[128,2048]{1,0:T(8,128)(2,1)} custom-call(bf16[128,1024]{1,0:T(8,128)(2,1)} %copy_bitcast_fusion.left_ref, bf16[2048,1536]{1,0:T(8,128)(2,1)} %all-gather.6.cloned.1.call-done.refs_8_.weight_ref), custom_call_target="tpu_custom_call" | custom-call | flops 600000 | bytes 5000 | tf_op jit(solution)/shard_map/branch/pallas_call | solution.py:493
  95.1 2.9 collective-permute-start.11
  98.3 8.8 %collective-permute-done.11 = bf16[128,2048]{1,0:T(8,128)(2,1)S(1)} collective-permute-done((bf16[128,2048]{1,0:T(8,128)(2,1)}, bf16[128,2048]{1,0:T(8,128)(2,1)S(1)}, u32[]{:S(2)}, u32[]{:S(2)}) %collective-permute-start.11) | collective-permute-done | bytes 524320 | tf_op jit(solution)/shard_map/ppermute | solution.py:143
  111.5 2.3 collective-permute-start.12
  116.2 9.7 %collective-permute-done.15.refs_0_.refs_6_ = bf16[128,2048]{1,0:T(8,128)(2,1)} collective-permute-done((bf16[128,2048]{1,0:T(8,128)(2,1)S(1)}, bf16[128,2048]{1,0:T(8,128)(2,1)}, u32[]{:S(2)}, u32[]{:S(2)}) %collective-permute-start.15) | collective-permute-done | bytes 524320 | tf_op jit(solution)/shard_map/ppermute | solution.py:71
  128.1 6.6 %collective-permute-done.12.refs_1_.refs_3_ = bf16[128,2048]{1,0:T(8,128)(2,1)S(1)} collective-permute-done((bf16[128,2048]{1,0:T(8,128)(2,1)S(1)}, bf16[128,2048]{1,0:T(8,128)(2,1)S(1)}, u32[]{:S(2)}, u32[]{:S(2)}) %collective-permute-start.12) | collective-permute-done | bytes 524320 | tf_op jit(solution)/shard_map/ppermute | solution.py:52
  134.6 3.0 collective-permute-start.17
  141.2 23.0 %units.2 = (bf16[128,4224]{1,0:T(8,128)(2,1)}, bf16[128,4224]{1,0:T(8,128)(2,1)}, bf16[128,4224]{1,0:T(8,128)(2,1)}, bf16[128,4224]{1,0:T(8,128)(2,1)}, bf16[211...) custom-call(bf16[128,2048]{1,0:T(8,128)(2,1)} %copy-done.3, bf16[128,2048]{1,0:T(8,128)(2,1)} %copy-done.21, ...), custom_call_target="tpu_custom_call" | custom-call | flops 11000000 | bytes 20000 | tf_op jit(solution)/shard_map/units/pallas_call | solution.py:397
  164.5 3.2 collective-permute-start.28
  167.7 22.1 %units.3 = (bf16[128,4224]{1,0:T(8,128)(2,1)}, bf16[128,4224]{1,0:T(8,128)(2,1)}, bf16[128,4224]{1,0:T(8,128)(2,1)}, bf16[128,4224]{1,0:T(8,128)(2,1)}, bf16[211...) custom-call(bf16[128,2048]{1,0:T(8,128)(2,1)} %collective-permute-done.15.refs_0_.r, ...), custom_call_target="tpu_custom_call", output_to_operand_aliasing={{4}: (11, {}), {5}: (12, {})} | custom-call | flops 11000000 | bytes 20000 | tf_op jit(solution)/shard_map/units/pallas_call | solution.py:397
  189.9 20.1 %outer.1 = bf16[8,3168,256]{2,1,0:T(8,128)(2,1)} custom-call(bf16[2112,1024]{1,0:T(8,128)(2,1)} %get-tuple-element.79.refs_0_, bf16[1056,1024]{1,0:T(8,128)(2,1)} %get-tuple-element.80.refs_1_, bf16[128,2048]{1,0:T(8,128)(2,1)} %copy-done.3, bf16[128,2048]{1,0:T(8,128)(2,1)} %copy-done.21, bf16[128,2048]{1,0:T(8,128)(2,1)} %copy-done.22, ...), custom_call_target="tpu_custom_call" | custom-call | flops 4429185 | bytes 10000 | tf_op jit(solution)/shard_map/outer/pallas_call | solution.py:444
  213.4 17.8 %collective-permute-done.22 = bf16[128,4224]{1,0:T(8,128)(2,1)S(1)} collective-permute-done((bf16[128,4224]{1,0:T(8,128)(2,1)}, bf16[128,4224]{1,0:T(8,128)(2,1)S(1)}, u32[]{:S(2)}, u32[]{:S(2)}) %collective-permute-start.22) | collective-permute-done | bytes 1081376 | tf_op jit(solution)/shard_map/ppermute | solution.py:60
  234.2 24.3 %collective-permute-done.24 = bf16[128,4224]{1,0:T(8,128)(2,1)S(1)} collective-permute-done((bf16[128,4224]{1,0:T(8,128)(2,1)}, bf16[128,4224]{1,0:T(8,128)(2,1)S(1)}, u32[]{:S(2)}, u32[]{:S(2)}) %collective-permute-start.24) | collective-permute-done | bytes 1081376 | tf_op jit(solution)/shard_map/ppermute | solution.py:52
  260.8 18.9 %collective-permute-done.26 = bf16[128,4224]{1,0:T(8,128)(2,1)} collective-permute-done((bf16[128,4224]{1,0:T(8,128)(2,1)}, bf16[128,4224]{1,0:T(8,128)(2,1)}, u32[]{:S(2)}, u32[]{:S(2)}) %collective-permute-start.26) | collective-permute-done | bytes 1081376 | tf_op jit(solution)/shard_map/ppermute | solution.py:60
  279.7 3.3 convert_add_fusion
  286.3 11.0 %collective-permute-done.29 = bf16[128,2176]{1,0:T(8,128)(2,1)} collective-permute-done((bf16[128,2176]{1,0:T(8,128)(2,1)}, bf16[128,2176]{1,0:T(8,128)(2,1)}, u32[]{:S(2)}, u32[]{:S(2)}) %collective-permute-start.29) | collective-permute-done | bytes 557088 | tf_op jit(solution)/shard_map/ppermute | solution.py:143
  304.7 3.3 convolution_convert_fusion
  308.1 3.2 collective-permute-start.31
  311.3 2.8 collective-permute-start.32
  314.2 4.6 branch_back.1
  320.4 3.4 all-to-all-start.1
  324.1 11.6 %all-to-all-done.1 = bf16[8,128,128]{2,1,0:T(8,128)(2,1)S(1)} async-done(((bf16[8,128,128]{2,1,0:T(8,128)(2,1)}), bf16[8,128,128]{2,1,0:T(8,128)(2,1)S(1)}, u32[]{:S(2)}, u32[]{:S(2)}) %all-to-all-start.1) | async-done | bytes 262176 | tf_op jit(solution)/shard_map/all_to_all | solution.py:836
  336.4 6.1 %attend_back.1 = (bf16[1024,384]{1,0:T(8,128)(2,1)}, f32[1,384]{1,0:T(1,128)}) custom-call(bf16[1024,128]{1,0:T(8,128)(2,1)} %get-tuple-element.88.q_ref, bf16[1024,128]{1,0:T(8,128)(2,1)} %get-tuple-element.89.k_ref, bf16[1024,128]{1,0:T(8,128)(2,1)} %get-tuple-element.90.v_ref, bf16[1024,128]{1,0:T(8,128)(2,1)} %bitcast.128, ...), custom_call_target="tpu_custom_call" | custom-call | flops 7000000 | bytes 6000 | tf_op jit(solution)/shard_map/attend_back/pallas_call | solution.py:266
  343.7 4.8 convolution_convert_fusion.1
  350.2 3.2 collective-permute-start.37
  355.2 1.9 slice.147
  357.2 1.9 bitcast_bitcast_fusion
  359.1 3.1 collective-permute-start.33
  362.2 4.1 all-to-all-start.3
  367.1 2.1 slice.154
  369.2 2.0 collective-permute-start.34
  371.3 2.1 slice.155
  374.7 1.9 copy.202
  377.3 2.3 copy.195
  379.6 14.2 %all-to-all-done.3 = bf16[8,256,128]{2,1,0:T(8,128)(2,1)} async-done(((bf16[8,256,128]{2,1,0:T(8,128)(2,1)}), bf16[8,256,128]{2,1,0:T(8,128)(2,1)}, u32[]{:S(2)}, u32[]{:S(2)}) %all-to-all-start.3) | async-done | bytes 524320 | tf_op jit(solution)/shard_map/all_to_all | solution.py:848
  393.8 4.2 all-to-all-start.2
  400.4 4.8 collective-permute-start.38
  405.1 2.2 multiply_convert_fusion
  408.4 1.9 collective-permute-start.44
  410.3 2.1 slice.160
  416.6 3.5 collective-permute-start.42
  420.2 2.6 pad_maximum_fusion.refs_0_
  422.8 7.8 %place_units.2 = (f32[8,2,704,256]{3,2,1,0:T(8,128)}, f32[8,704,256]{2,1,0:T(8,128)}, bf16[3,8,352,256]{3,2,1,0:T(8,128)(2,1)}) custom-call(s32[4]{0:T(128)} %gather_fusion.1, bf16[3168,256]{1,0:T(8,128)(2,1)} %bitcast.121, bf16[3168,256]{1,0:T(8,128)(2,1)} %collective-permute-done.30.refs_1_, bf16[3168,256]{1,0:T(8,128)(2,1)} %collective-permute-done.31.refs_2_, ...), custom_call_target="tpu_custom_call" | custom-call | flops 1 | bytes 1 | tf_op jit(solution)/shard_map/place_units/pallas_call | solution.py:608
  434.6 10.1 %first_back.1 = bf16[128,2048]{1,0:T(8,128)(2,1)} custom-call(bf16[3,128,1024]{2,1,0:T(8,128)(2,1)} %reshape.197.left_ref, bf16[8,3,256,1024]{3,2,1,0:T(8,128)(2,1)} %bitcast.112), custom_call_target="tpu_custom_call" | custom-call | flops 1700000 | bytes 13000 | tf_op jit(solution)/shard_map/first_back/pallas_call | solution.py:537
  444.7 3.2 collective-permute-start.40
  447.9 3.2 collective-permute-start.47
  451.2 1.9 collective-permute-start.48
  453.1 2.6 pad_maximum_fusion.1.refs_3_
  455.8 7.9 %place_units.3 = (f32[8,2,704,256]{3,2,1,0:T(8,128)}, f32[8,704,256]{2,1,0:T(8,128)}, bf16[3,8,352,256]{3,2,1,0:T(8,128)(2,1)}) custom-call(s32[4]{0:T(128)} %gather_fusion, bf16[3168,256]{1,0:T(8,128)(2,1)} %pad_maximum_fusion.refs_0_, bf16[3168,256]{1,0:T(8,128)(2,1)} %copy-done.12, ...), custom_call_target="tpu_custom_call", output_to_operand_aliasing={{0}: (5, {}), {1}: (6, {}), {2}: (7, {})} | custom-call | flops 1 | bytes 1 | tf_op jit(solution)/shard_map/place_units/pallas_call | solution.py:608
  463.6 5.9 %flip.1 = (f32[256,2,2816]{2,1,0:T(2,128)}, f32[256,2816]{1,0:T(8,128)}) custom-call(bf16[256,256]{1,0:T(8,128)(2,1)} %fusion.11.one_ref, bf16[3,2816,256]{2,1,0:T(8,128)(2,1)} %bitcast.111), custom_call_target="tpu_custom_call" | custom-call | flops 1 | bytes 1 | tf_op jit(solution)/shard_map/flip/pallas_call | solution.py:646
  469.6 2.8 collective-permute-start.43
  474.0 4.6 place.1
  (291 shorter events, 88.4 us)
Async XLA Ops:
  7.2 37.9 %copy-start = (bf16[256,2,2816]{2,1,0:T(2,128)(2,1)S(1)}, bf16[256,2,2816]{2,1,0:T(2,128)(2,1)}, u32[]{:S(2)}) copy-start(bf16[256,2,2816]{2,1,0:T(2,128)(2,1)} %param.27) | copy-start | bytes 8650756
  7.2 55.8 %all-gather.6.cloned.1.call-start = ((), (), s32[]{:S(2)}) async-start(), calls=%async_computation.7 | async-start | bytes 7077888 | tf_op jit(solution)/shard_map/all_gather | solution.py:716
  13.0 128.2 %all-gather.8.cloned.1.call-start = ((), (), s32[]{:S(2)}) async-start(), calls=%async_computation.11 | async-start | bytes 14598144 | tf_op jit(solution)/shard_map/all_gather | solution.py:748
  13.1 32.0 %collective-permute-start = (bf16[128,2048]{1,0:T(8,128)(2,1)S(1)}, bf16[128,2048]{1,0:T(8,128)(2,1)}, u32[]{:S(2)}, u32[]{:S(2)}) collective-permute-start(bf16[128,2048]{1,0:T(8,128)(2,1)S(1)} %copy-done.5), channel_id=1, source_target_pairs={{0,4},{2,6},{4,8},{6,10},{8,12},{10,14},{12,0},{14,2},{1,5},{3,7},... | collective-permute-start | bytes 1572872 | tf_op jit(solution)/shard_map/ppermute | solution.py:52
  14.7 30.4 %collective-permute-start.1 = (bf16[128,2048]{1,0:T(8,128)(2,1)S(1)}, bf16[128,2048]{1,0:T(8,128)(2,1)}, u32[]{:S(2)}, u32[]{:S(2)}) collective-permute-start(bf16[128,2048]{1,0:T(8,128)(2,1)S(1)} %copy-done.5), channel_id=1, source_target_pairs={{0,12},{2,14},{4,0},{6,2},{8,4},{10,6},{12,8},{14,10},{1,13},{3,15... | collective-permute-start | bytes 1572872 | tf_op jit(solution)/shard_map/ppermute | solution.py:56
  16.4 25.2 %collective-permute-start.2 = (bf16[128,2048]{1,0:T(8,128)(2,1)S(1)}, bf16[128,2048]{1,0:T(8,128)(2,1)}, u32[]{:S(2)}, u32[]{:S(2)}) collective-permute-start(bf16[128,2048]{1,0:T(8,128)(2,1)S(1)} %copy-done.5), channel_id=1, source_target_pairs={{0,8},{2,10},{4,12},{6,14},{8,0},{10,2},{12,4},{14,6},{1,9},{3,11}... | collective-permute-start | bytes 1572872 | tf_op jit(solution)/shard_map/ppermute | solution.py:71
  18.3 12.9 %collective-permute-start.3 = (bf16[128,2048]{1,0:T(8,128)(2,1)S(1)}, bf16[128,2048]{1,0:T(8,128)(2,1)}, u32[]{:S(2)}, u32[]{:S(2)}) collective-permute-start(bf16[128,2048]{1,0:T(8,128)(2,1)S(1)} %copy-done.5), channel_id=1, source_target_pairs={{0,2},{2,0},{4,6},{6,4},{8,10},{10,8},{12,14},{14,12},{1,3},{3,1},... | collective-permute-start | bytes 1572872 | tf_op jit(solution)/shard_map/ppermute | solution.py:60
  31.2 20.5 %collective-permute-start.4 = (bf16[128,2048]{1,0:T(8,128)(2,1)}, bf16[128,2048]{1,0:T(8,128)(2,1)}, u32[]{:S(2)}, u32[]{:S(2)}) collective-permute-start(bf16[128,2048]{1,0:T(8,128)(2,1)} %collective-permute-done.3.refs_4_), channel_id=1, source_target_pairs={{0,4},{2,6},{4,8},{6,10},{8,12},{10,14},{12,0},{14,2},{1,5},{3,7},... | collective-permute-start | bytes 1572872 | tf_op jit(solution)/shard_map/ppermute | solution.py:52
  31.8 19.9 %collective-permute-start.5 = (bf16[128,2048]{1,0:T(8,128)(2,1)}, bf16[128,2048]{1,0:T(8,128)(2,1)}, u32[]{:S(2)}, u32[]{:S(2)}) collective-permute-start(bf16[128,2048]{1,0:T(8,128)(2,1)} %collective-permute-done.3.refs_4_), channel_id=1, source_target_pairs={{0,12},{2,14},{4,0},{6,2},{8,4},{10,6},{12,8},{14,10},{1,13},{3,15... | collective-permute-start | bytes 1572872 | tf_op jit(solution)/shard_map/ppermute | solution.py:56
  41.6 12.0 %collective-permute-start.6 = (bf16[128,2048]{1,0:T(8,128)(2,1)}, bf16[128,2048]{1,0:T(8,128)(2,1)}, u32[]{:S(2)}, u32[]{:S(2)}) collective-permute-start(bf16[128,2048]{1,0:T(8,128)(2,1)} %collective-permute-done.2.refs_3_), channel_id=1, source_target_pairs={{0,2},{2,0},{4,6},{6,4},{8,10},{10,8},{12,14},{14,12},{1,3},{3,1},... | collective-permute-start | bytes 1572872 | tf_op jit(solution)/shard_map/ppermute | solution.py:60
  57.1 203.6 %all-gather.10.cloned.1.call-start = ((), (), s32[]{:S(2)}) async-start(), calls=%async_computation.12 | async-start | bytes 14155776 | tf_op jit(solution)/shard_map/all_gather | solution.py:798
  57.9 250.2 %reduce-scatter.4.cloned.1.call-start = ((), (), s32[]{:S(2)}) async-start(), calls=%async_computation.8 | async-start | bytes 14598144 | tf_op jit(solution)/shard_map/reduce_scatter | solution.py:810
  57.9 37.2 %collective-permute-start.7 = (bf16[128,2176]{1,0:T(8,128)(2,1)S(1)}, bf16[128,2176]{1,0:T(8,128)(2,1)S(1)}, u32[]{:S(2)}, u32[]{:S(2)}) collective-permute-start(bf16[128,2176]{1,0:T(8,128)(2,1)S(1)} %copy-done.9), channel_id=1, source_target_pairs={{0,4},{2,6},{4,8},{6,10},{8,12},{10,14},{12,0},{14,2},{1,5},{3,7},... | collective-permute-start | bytes 1671176 | tf_op jit(solution)/shard_map/ppermute | solution.py:52
  58.7 36.3 %collective-permute-start.8 = (bf16[128,2176]{1,0:T(8,128)(2,1)S(1)}, bf16[128,2176]{1,0:T(8,128)(2,1)S(1)}, u32[]{:S(2)}, u32[]{:S(2)}) collective-permute-start(bf16[128,2176]{1,0:T(8,128)(2,1)S(1)} %copy-done.9), channel_id=1, source_target_pairs={{0,12},{2,14},{4,0},{6,2},{8,4},{10,6},{12,8},{14,10},{1,13},{3,15... | collective-permute-start | bytes 1671176 | tf_op jit(solution)/shard_map/ppermute | solution.py:56
  61.2 33.9 %collective-permute-start.9 = (bf16[128,2176]{1,0:T(8,128)(2,1)S(1)}, bf16[128,2176]{1,0:T(8,128)(2,1)}, u32[]{:S(2)}, u32[]{:S(2)}) collective-permute-start(bf16[128,2176]{1,0:T(8,128)(2,1)S(1)} %copy-done.9), channel_id=1, source_target_pairs={{0,2},{2,0},{4,6},{6,4},{8,10},{10,8},{12,14},{14,12},{1,3},{3,1},... | collective-permute-start | bytes 1671176 | tf_op jit(solution)/shard_map/ppermute | solution.py:60
  62.8 32.4 %collective-permute-start.10 = (bf16[128,2176]{1,0:T(8,128)(2,1)S(1)}, bf16[128,2176]{1,0:T(8,128)(2,1)}, u32[]{:S(2)}, u32[]{:S(2)}) collective-permute-start(bf16[128,2176]{1,0:T(8,128)(2,1)S(1)} %copy-done.9), channel_id=1, source_target_pairs={{0,8},{2,10},{4,12},{6,14},{8,0},{10,2},{12,4},{14,6},{1,9},{3,11}... | collective-permute-start | bytes 1671176 | tf_op jit(solution)/shard_map/ppermute | solution.py:71
  95.1 12.0 %collective-permute-start.11 = (bf16[128,2048]{1,0:T(8,128)(2,1)}, bf16[128,2048]{1,0:T(8,128)(2,1)S(1)}, u32[]{:S(2)}, u32[]{:S(2)}) collective-permute-start(bf16[128,2048]{1,0:T(8,128)(2,1)} %branch.1), channel_id=1, source_target_pairs={{0,1},{1,0},{2,3},{3,2},{4,5},{5,4},{6,7},{7,6},{8,9},{9,8},{10,11... | collective-permute-start | bytes 1572872 | tf_op jit(solution)/shard_map/ppermute | solution.py:143
  98.0 16.8 %collective-permute-start.19 = (bf16[128,2176]{1,0:T(8,128)(2,1)}, bf16[128,2176]{1,0:T(8,128)(2,1)S(1)}, u32[]{:S(2)}, u32[]{:S(2)}) collective-permute-start(bf16[128,2176]{1,0:T(8,128)(2,1)} %collective-permute-done.9.refs_7_.refs_13_), channel_id=1, source_target_pairs={{0,4},{2,6},{4,8},{6,10},{8,12},{10,14},{12,0},{14,2},{1,5},{3,7},... | collective-permute-start | bytes 1671176 | tf_op jit(solution)/shard_map/ppermute | solution.py:52
  109.1 55.1 %copy-start.41 = (f32[128]{0:T(128)}, f32[128]{0:T(128)S(1)}, u32[]{:S(2)}) copy-start(f32[128]{0:T(128)S(1)} %get-tuple-element.204) | copy-start | bytes 1540
  109.3 31.9 %copy-start.3 = (bf16[128,2048]{1,0:T(8,128)(2,1)}, bf16[128,2048]{1,0:T(8,128)(2,1)S(1)}, u32[]{:S(2)}) copy-start(bf16[128,2048]{1,0:T(8,128)(2,1)S(1)} %multiply_convert_fusion.1.refs_0_.refs_2_) | copy-start | bytes 1572868
  109.3 16.6 %collective-permute-start.15 = (bf16[128,2048]{1,0:T(8,128)(2,1)S(1)}, bf16[128,2048]{1,0:T(8,128)(2,1)}, u32[]{:S(2)}, u32[]{:S(2)}) collective-permute-start(bf16[128,2048]{1,0:T(8,128)(2,1)S(1)} %multiply_convert_fusion.1.refs_0_.refs_2_), channel_id=1, source_target_pairs={{0,8},{2,10},{4,12},{6,14},{8,0},{10,2},{12,4},{14,6},{1,9},{3,11}... | collective-permute-start | bytes 1572872 | tf_op jit(solution)/shard_map/ppermute | solution.py:71
  110.9 16.1 %collective-permute-start.14 = (bf16[128,2048]{1,0:T(8,128)(2,1)S(1)}, bf16[128,2048]{1,0:T(8,128)(2,1)}, u32[]{:S(2)}, u32[]{:S(2)}) collective-permute-start(bf16[128,2048]{1,0:T(8,128)(2,1)S(1)} %multiply_convert_fusion.1.refs_0_.refs_2_), channel_id=1, source_target_pairs={{0,2},{2,0},{4,6},{6,4},{8,10},{10,8},{12,14},{14,12},{1,3},{3,1},... | collective-permute-start | bytes 1572872 | tf_op jit(solution)/shard_map/ppermute | solution.py:60
  111.5 23.1 %collective-permute-start.12 = (bf16[128,2048]{1,0:T(8,128)(2,1)S(1)}, bf16[128,2048]{1,0:T(8,128)(2,1)S(1)}, u32[]{:S(2)}, u32[]{:S(2)}) collective-permute-start(bf16[128,2048]{1,0:T(8,128)(2,1)S(1)} %multiply_convert_fusion.1.refs_0_.refs_2_), channel_id=1, source_target_pairs={{0,4},{2,6},{4,8},{6,10},{8,12},{10,14},{12,0},{14,2},{1,5},{3,7},... | collective-permute-start | bytes 1572872 | tf_op jit(solution)/shard_map/ppermute | solution.py:52
  113.9 24.0 %collective-permute-start.13 = (bf16[128,2048]{1,0:T(8,128)(2,1)S(1)}, bf16[128,2048]{1,0:T(8,128)(2,1)S(1)}, u32[]{:S(2)}, u32[]{:S(2)}) collective-permute-start(bf16[128,2048]{1,0:T(8,128)(2,1)S(1)} %multiply_convert_fusion.1.refs_0_.refs_2_), channel_id=1, source_target_pairs={{0,12},{2,14},{4,0},{6,2},{8,4},{10,6},{12,8},{14,10},{1,13},{3,15... | collective-permute-start | bytes 1572872 | tf_op jit(solution)/shard_map/ppermute | solution.py:56
  114.8 23.1 %copy-start.18 = (bf16[128,2176]{1,0:T(8,128)(2,1)}, bf16[128,2176]{1,0:T(8,128)(2,1)S(1)}, u32[]{:S(2)}) copy-start(bf16[128,2176]{1,0:T(8,128)(2,1)S(1)} %collective-permute-done.19.refs_5_.refs_15_) | copy-start | bytes 1671172
  114.8 49.4 %collective-permute-start.20 = (bf16[128,2176]{1,0:T(8,128)(2,1)}, bf16[128,2176]{1,0:T(8,128)(2,1)S(1)}, u32[]{:S(2)}, u32[]{:S(2)}) collective-permute-start(bf16[128,2176]{1,0:T(8,128)(2,1)} %collective-permute-done.9.refs_7_.refs_13_), channel_id=1, source_target_pairs={{0,12},{2,14},{4,0},{6,2},{8,4},{10,6},{12,8},{14,10},{1,13},{3,15... | collective-permute-start | bytes 1671176 | tf_op jit(solution)/shard_map/ppermute | solution.py:56
  125.9 38.3 %collective-permute-start.21 = (bf16[128,2176]{1,0:T(8,128)(2,1)}, bf16[128,2176]{1,0:T(8,128)(2,1)S(1)}, u32[]{:S(2)}, u32[]{:S(2)}) collective-permute-start(bf16[128,2176]{1,0:T(8,128)(2,1)} %collective-permute-done.10.refs_4_.refs_14_), channel_id=1, source_target_pairs={{0,2},{2,0},{4,6},{6,4},{8,10},{10,8},{12,14},{14,12},{1,3},{3,1},... | collective-permute-start | bytes 1671176 | tf_op jit(solution)/shard_map/ppermute | solution.py:60
  127.0 37.2 %collective-permute-start.16 = (bf16[128,2048]{1,0:T(8,128)(2,1)}, bf16[128,2048]{1,0:T(8,128)(2,1)}, u32[]{:S(2)}, u32[]{:S(2)}) collective-permute-start(bf16[128,2048]{1,0:T(8,128)(2,1)} %collective-permute-done.14.refs_3_.refs_5_), channel_id=1, source_target_pairs={{0,4},{2,6},{4,8},{6,10},{8,12},{10,14},{12,0},{14,2},{1,5},{3,7},... | collective-permute-start | bytes 1572872 | tf_op jit(solution)/shard_map/ppermute | solution.py:52
  134.6 29.6 %collective-permute-start.17 = (bf16[128,2048]{1,0:T(8,128)(2,1)}, bf16[128,2048]{1,0:T(8,128)(2,1)}, u32[]{:S(2)}, u32[]{:S(2)}) collective-permute-start(bf16[128,2048]{1,0:T(8,128)(2,1)} %collective-permute-done.14.refs_3_.refs_5_), channel_id=1, source_target_pairs={{0,12},{2,14},{4,0},{6,2},{8,4},{10,6},{12,8},{14,10},{1,13},{3,15... | collective-permute-start | bytes 1572872 | tf_op jit(solution)/shard_map/ppermute | solution.py:56
  138.6 25.6 %collective-permute-start.18 = (bf16[128,2048]{1,0:T(8,128)(2,1)}, bf16[128,2048]{1,0:T(8,128)(2,1)}, u32[]{:S(2)}, u32[]{:S(2)}) collective-permute-start(bf16[128,2048]{1,0:T(8,128)(2,1)} %collective-permute-done.15.refs_0_.refs_6_), channel_id=1, source_target_pairs={{0,2},{2,0},{4,6},{6,4},{8,10},{10,8},{12,14},{14,12},{1,3},{3,1},... | collective-permute-start | bytes 1572872 | tf_op jit(solution)/shard_map/ppermute | solution.py:60
  164.3 25.6 %collective-permute-start.27 = (bf16[128,4224]{1,0:T(8,128)(2,1)}, bf16[128,4224]{1,0:T(8,128)(2,1)}, u32[]{:S(2)}, u32[]{:S(2)}) collective-permute-start(bf16[128,4224]{1,0:T(8,128)(2,1)} %get-tuple-element.76), channel_id=1, source_target_pairs={{0,4},{2,6},{4,8},{6,10},{8,12},{10,14},{12,0},{14,2},{1,5},{3,7},... | collective-permute-start | bytes 3244040 | tf_op jit(solution)/shard_map/ppermute | solution.py:52
  164.5 25.4 %collective-permute-start.28 = (bf16[128,4224]{1,0:T(8,128)(2,1)}, bf16[128,4224]{1,0:T(8,128)(2,1)}, u32[]{:S(2)}, u32[]{:S(2)}) collective-permute-start(bf16[128,4224]{1,0:T(8,128)(2,1)} %get-tuple-element.77), channel_id=1, source_target_pairs={{0,12},{2,14},{4,0},{6,2},{8,4},{10,6},{12,8},{14,10},{1,13},{3,15... | collective-permute-start | bytes 3244040 | tf_op jit(solution)/shard_map/ppermute | solution.py:56
  210.0 147.2 %reduce-scatter.6.cloned.1.call-start = ((), (), s32[]{:S(2)}) async-start(), calls=%async_computation.9 | async-start | bytes 4718592 | tf_op jit(solution)/shard_map/reduce_scatter | solution.py:843
  210.0 21.2 %collective-permute-start.22 = (bf16[128,4224]{1,0:T(8,128)(2,1)}, bf16[128,4224]{1,0:T(8,128)(2,1)S(1)}, u32[]{:S(2)}, u32[]{:S(2)}) collective-permute-start(bf16[128,4224]{1,0:T(8,128)(2,1)} %get-tuple-element.70), channel_id=1, source_target_pairs={{0,2},{2,0},{4,6},{6,4},{8,10},{10,8},{12,14},{14,12},{1,3},{3,1},... | collective-permute-start | bytes 3244040 | tf_op jit(solution)/shard_map/ppermute | solution.py:60
  211.4 22.9 %collective-permute-start.25 = (bf16[128,4224]{1,0:T(8,128)(2,1)}, bf16[128,4224]{1,0:T(8,128)(2,1)S(1)}, u32[]{:S(2)}, u32[]{:S(2)}) collective-permute-start(bf16[128,4224]{1,0:T(8,128)(2,1)} %get-tuple-element.73), channel_id=1, source_target_pairs={{0,12},{2,14},{4,0},{6,2},{8,4},{10,6},{12,8},{14,10},{1,13},{3,15... | collective-permute-start | bytes 3244040 | tf_op jit(solution)/shard_map/ppermute | solution.py:56
  212.3 46.2 %collective-permute-start.24 = (bf16[128,4224]{1,0:T(8,128)(2,1)}, bf16[128,4224]{1,0:T(8,128)(2,1)S(1)}, u32[]{:S(2)}, u32[]{:S(2)}) collective-permute-start(bf16[128,4224]{1,0:T(8,128)(2,1)} %get-tuple-element.72), channel_id=1, source_target_pairs={{0,4},{2,6},{4,8},{6,10},{8,12},{10,14},{12,0},{14,2},{1,5},{3,7},... | collective-permute-start | bytes 3244040 | tf_op jit(solution)/shard_map/ppermute | solution.py:52
  231.2 27.3 %copy-start.28 = (bf16[128,4224]{1,0:T(8,128)(2,1)S(1)}, bf16[128,4224]{1,0:T(8,128)(2,1)}, u32[]{:S(2)}) copy-start(bf16[128,4224]{1,0:T(8,128)(2,1)} %get-tuple-element.71) | copy-start | bytes 3244036
  232.5 28.3 %collective-permute-start.23 = (bf16[128,4224]{1,0:T(8,128)(2,1)}, bf16[128,4224]{1,0:T(8,128)(2,1)S(1)}, u32[]{:S(2)}, u32[]{:S(2)}) collective-permute-start(bf16[128,4224]{1,0:T(8,128)(2,1)} %add_convert_fusion.1), channel_id=1, source_target_pairs={{0,8},{2,10},{4,12},{6,14},{8,0},{10,2},{12,4},{14,6},{1,9},{3,11}... | collective-permute-start | bytes 3244040 | tf_op jit(solution)/shard_map/ppermute | solution.py:71
  259.9 19.9 %collective-permute-start.26 = (bf16[128,4224]{1,0:T(8,128)(2,1)}, bf16[128,4224]{1,0:T(8,128)(2,1)}, u32[]{:S(2)}, u32[]{:S(2)}) collective-permute-start(bf16[128,4224]{1,0:T(8,128)(2,1)} %add_convert_fusion), channel_id=1, source_target_pairs={{0,2},{2,0},{4,6},{6,4},{8,10},{10,8},{12,14},{14,12},{1,3},{3,1},... | collective-permute-start | bytes 3244040 | tf_op jit(solution)/shard_map/ppermute | solution.py:60
  284.0 13.3 %collective-permute-start.29 = (bf16[128,2176]{1,0:T(8,128)(2,1)}, bf16[128,2176]{1,0:T(8,128)(2,1)}, u32[]{:S(2)}, u32[]{:S(2)}) collective-permute-start(bf16[128,2176]{1,0:T(8,128)(2,1)} %slice.203), channel_id=1, source_target_pairs={{0,1},{1,0},{2,3},{3,2},{4,5},{5,4},{6,7},{7,6},{8,9},{9,8},{10,11... | collective-permute-start | bytes 1671176 | tf_op jit(solution)/shard_map/ppermute | solution.py:143
  308.0 27.7 %collective-permute-start.30 = (bf16[3168,256]{1,0:T(8,128)(2,1)}, bf16[3168,256]{1,0:T(8,128)(2,1)}, u32[]{:S(2)}, u32[]{:S(2)}) collective-permute-start(bf16[3168,256]{1,0:T(8,128)(2,1)} %bitcast.118), channel_id=1, source_target_pairs={{0,4},{2,6},{4,8},{6,10},{8,12},{10,14},{12,0},{14,2},{1,5},{3,7},... | collective-permute-start | bytes 4866056 | tf_op jit(solution)/shard_map/ppermute | solution.py:52
  308.1 27.6 %collective-permute-start.31 = (bf16[3168,256]{1,0:T(8,128)(2,1)}, bf16[3168,256]{1,0:T(8,128)(2,1)}, u32[]{:S(2)}, u32[]{:S(2)}) collective-permute-start(bf16[3168,256]{1,0:T(8,128)(2,1)} %bitcast.119), channel_id=1, source_target_pairs={{0,12},{2,14},{4,0},{6,2},{8,4},{10,6},{12,8},{14,10},{1,13},{3,15... | collective-permute-start | bytes 4866056 | tf_op jit(solution)/shard_map/ppermute | solution.py:56
  311.3 24.4 %collective-permute-start.32 = (bf16[3168,256]{1,0:T(8,128)(2,1)}, bf16[3168,256]{1,0:T(8,128)(2,1)}, u32[]{:S(2)}, u32[]{:S(2)}) collective-permute-start(bf16[3168,256]{1,0:T(8,128)(2,1)} %bitcast.120), channel_id=1, source_target_pairs={{0,2},{2,0},{4,6},{6,4},{8,10},{10,8},{12,14},{14,12},{1,3},{3,1},... | collective-permute-start | bytes 4866056 | tf_op jit(solution)/shard_map/ppermute | solution.py:60
  320.4 15.3 %all-to-all-start.1 = ((bf16[8,128,128]{2,1,0:T(8,128)(2,1)}), bf16[8,128,128]{2,1,0:T(8,128)(2,1)S(1)}, u32[]{:S(2)}, u32[]{:S(2)}) async-start(bf16[8,128,128]{2,1,0:T(8,128)(2,1)} %bitcast_bitcast_fusion.1), calls=%async_computation.1 | async-start | bytes 524288 | tf_op jit(solution)/shard_map/all_to_all | solution.py:836
  323.9 75.3 %reduce-scatter.8.cloned.1.call-start = ((), (), s32[]{:S(2)}) async-start(), calls=%async_computation.10 | async-start | bytes 2359296 | tf_op jit(solution)/shard_map/reduce_scatter | solution.py:863
  350.2 57.2 %collective-permute-start.36 = (bf16[3168,256]{1,0:T(8,128)(2,1)}, bf16[3168,256]{1,0:T(8,128)(2,1)S(1)}, u32[]{:S(2)}, u32[]{:S(2)}) collective-permute-start(bf16[3168,256]{1,0:T(8,128)(2,1)} %collective-permute-done.32.refs_3_), channel_id=1, source_target_pairs={{0,4},{2,6},{4,8},{6,10},{8,12},{10,14},{12,0},{14,2},{1,5},{3,7},... | collective-permute-start | bytes 4866056 | tf_op jit(solution)/shard_map/ppermute | solution.py:52
  350.2 60.1 %collective-permute-start.37 = (bf16[3168,256]{1,0:T(8,128)(2,1)}, bf16[3168,256]{1,0:T(8,128)(2,1)}, u32[]{:S(2)}, u32[]{:S(2)}) collective-permute-start(bf16[3168,256]{1,0:T(8,128)(2,1)} %collective-permute-done.32.refs_3_), channel_id=1, source_target_pairs={{0,12},{2,14},{4,0},{6,2},{8,4},{10,6},{12,8},{14,10},{1,13},{3,15... | collective-permute-start | bytes 4866056 | tf_op jit(solution)/shard_map/ppermute | solution.py:56
  359.1 41.3 %collective-permute-start.33 = (bf16[128,2048]{1,0:T(8,128)(2,1)}, bf16[128,2048]{1,0:T(8,128)(2,1)}, u32[]{:S(2)}, u32[]{:S(2)}) collective-permute-start(bf16[128,2048]{1,0:T(8,128)(2,1)} %slice.147), channel_id=1, source_target_pairs={{0,1},{1,0},{2,3},{3,2},{4,5},{5,4},{6,7},{7,6},{8,9},{9,8},{10,11... | collective-permute-start | bytes 1572872 | tf_op jit(solution)/shard_map/ppermute | solution.py:143
  362.2 31.7 %all-to-all-start.3 = ((bf16[8,256,128]{2,1,0:T(8,128)(2,1)}), bf16[8,256,128]{2,1,0:T(8,128)(2,1)}, u32[]{:S(2)}, u32[]{:S(2)}) async-start(bf16[8,256,128]{2,1,0:T(8,128)(2,1)} %bitcast_bitcast_fusion), calls=%async_computation.5 | async-start | bytes 1048576 | tf_op jit(solution)/shard_map/all_to_all | solution.py:848
  369.2 44.5 %collective-permute-start.34 = (bf16[1584,256]{1,0:T(8,128)(2,1)}, bf16[1584,256]{1,0:T(8,128)(2,1)}, u32[]{:S(2)}, u32[]{:S(2)}) collective-permute-start(bf16[1584,256]{1,0:T(8,128)(2,1)} %slice.154), channel_id=1, source_target_pairs={{0,4},{2,6},{4,8},{6,10},{8,12},{10,14},{12,0},{14,2},{1,5},{3,7},... | collective-permute-start | bytes 2433032 | tf_op jit(solution)/shard_map/ppermute | solution.py:52
  373.4 40.4 %collective-permute-start.35 = (bf16[1584,256]{1,0:T(8,128)(2,1)}, bf16[1584,256]{1,0:T(8,128)(2,1)}, u32[]{:S(2)}, u32[]{:S(2)}) collective-permute-start(bf16[1584,256]{1,0:T(8,128)(2,1)} %slice.155), channel_id=1, source_target_pairs={{0,12},{2,14},{4,0},{6,2},{8,4},{10,6},{12,8},{14,10},{1,13},{3,15... | collective-permute-start | bytes 2433032 | tf_op jit(solution)/shard_map/ppermute | solution.py:56
  393.8 36.8 %all-to-all-start.2 = ((bf16[8,128,384]{1,2,0:T(8,128)(2,1)}), bf16[8,128,384]{1,2,0:T(8,128)(2,1)}, u32[]{:S(2)}, u32[]{:S(2)}) async-start(bf16[8,128,384]{1,2,0:T(8,128)(2,1)} %copy.195), calls=%async_computation.3 | async-start | bytes 1572864 | tf_op jit(solution)/shard_map/all_to_all | solution.py:850
  400.4 14.6 %collective-permute-start.38 = (f32[256]{0:T(256)S(1)}, f32[256]{0:T(256)S(1)}, u32[]{:S(2)}, u32[]{:S(2)}) collective-permute-start(f32[256]{0:T(256)S(1)} %multiply_reduce_fusion.3), channel_id=1, source_target_pairs={{0,1},{1,0},{2,3},{3,2},{4,5},{5,4},{6,7},{7,6},{8,9},{9,8},{10,11... | collective-permute-start | bytes 3080 | tf_op jit(solution)/shard_map/ppermute | solution.py:868
  408.4 36.3 %collective-permute-start.44 = (bf16[1584,256]{1,0:T(8,128)(2,1)}, bf16[1584,256]{1,0:T(8,128)(2,1)}, u32[]{:S(2)}, u32[]{:S(2)}) collective-permute-start(bf16[1584,256]{1,0:T(8,128)(2,1)} %slice.159), channel_id=1, source_target_pairs={{0,4},{2,6},{4,8},{6,10},{8,12},{10,14},{12,0},{14,2},{1,5},{3,7},... | collective-permute-start | bytes 2433032 | tf_op jit(solution)/shard_map/ppermute | solution.py:52
  412.4 35.5 %collective-permute-start.45 = (bf16[1584,256]{1,0:T(8,128)(2,1)}, bf16[1584,256]{1,0:T(8,128)(2,1)}, u32[]{:S(2)}, u32[]{:S(2)}) collective-permute-start(bf16[1584,256]{1,0:T(8,128)(2,1)} %slice.160), channel_id=1, source_target_pairs={{0,12},{2,14},{4,0},{6,2},{8,4},{10,6},{12,8},{14,10},{1,13},{3,15... | collective-permute-start | bytes 2433032 | tf_op jit(solution)/shard_map/ppermute | solution.py:56
  415.2 29.4 %copy-start.25 = (bf16[256,640]{1,0:T(8,128)(2,1)}, bf16[256,640]{1,0:T(8,128)(2,1)S(1)}, u32[]{:S(2)}) copy-start(bf16[256,640]{1,0:T(8,128)(2,1)S(1)} %pad_maximum_fusion.2.refs_0_) | copy-start | bytes 983044
  415.3 32.6 %collective-permute-start.41 = (bf16[256,640]{1,0:T(8,128)(2,1)S(1)}, bf16[256,640]{1,0:T(8,128)(2,1)S(1)}, u32[]{:S(2)}, u32[]{:S(2)}) collective-permute-start(bf16[256,640]{1,0:T(8,128)(2,1)S(1)} %pad_maximum_fusion.2.refs_0_), channel_id=1, source_target_pairs={{0,2},{2,0},{4,6},{6,4},{8,10},{10,8},{12,14},{14,12},{1,3},{3,1},... | collective-permute-start | bytes 983048 | tf_op jit(solution)/shard_map/ppermute | solution.py:60
  416.6 34.5 %collective-permute-start.42 = (bf16[256,640]{1,0:T(8,128)(2,1)S(1)}, bf16[256,640]{1,0:T(8,128)(2,1)S(1)}, u32[]{:S(2)}, u32[]{:S(2)}) collective-permute-start(bf16[256,640]{1,0:T(8,128)(2,1)S(1)} %pad_maximum_fusion.2.refs_0_), channel_id=1, source_target_pairs={{0,8},{2,10},{4,12},{6,14},{8,0},{10,2},{12,4},{14,6},{1,9},{3,11}... | collective-permute-start | bytes 983048 | tf_op jit(solution)/shard_map/ppermute | solution.py:71
  444.7 24.9 %collective-permute-start.39 = (bf16[256,640]{1,0:T(8,128)(2,1)S(1)}, bf16[256,640]{1,0:T(8,128)(2,1)S(1)}, u32[]{:S(2)}, u32[]{:S(2)}) collective-permute-start(bf16[256,640]{1,0:T(8,128)(2,1)S(1)} %pad_maximum_fusion.2.refs_0_), channel_id=1, source_target_pairs={{0,4},{2,6},{4,8},{6,10},{8,12},{10,14},{12,0},{14,2},{1,5},{3,7},... | collective-permute-start | bytes 983048 | tf_op jit(solution)/shard_map/ppermute | solution.py:52
  444.7 24.9 %collective-permute-start.40 = (bf16[256,640]{1,0:T(8,128)(2,1)S(1)}, bf16[256,640]{1,0:T(8,128)(2,1)S(1)}, u32[]{:S(2)}, u32[]{:S(2)}) collective-permute-start(bf16[256,640]{1,0:T(8,128)(2,1)S(1)} %pad_maximum_fusion.2.refs_0_), channel_id=1, source_target_pairs={{0,12},{2,14},{4,0},{6,2},{8,4},{10,6},{12,8},{14,10},{1,13},{3,15... | collective-permute-start | bytes 983048 | tf_op jit(solution)/shard_map/ppermute | solution.py:56
  447.9 24.5 %collective-permute-start.46 = (bf16[256,640]{1,0:T(8,128)(2,1)S(1)}, bf16[256,640]{1,0:T(8,128)(2,1)S(1)}, u32[]{:S(2)}, u32[]{:S(2)}) collective-permute-start(bf16[256,640]{1,0:T(8,128)(2,1)S(1)} %collective-permute-done.41.refs_4_), channel_id=1, source_target_pairs={{0,4},{2,6},{4,8},{6,10},{8,12},{10,14},{12,0},{14,2},{1,5},{3,7},... | collective-permute-start | bytes 983048 | tf_op jit(solution)/shard_map/ppermute | solution.py:52
  447.9 24.5 %collective-permute-start.47 = (bf16[256,640]{1,0:T(8,128)(2,1)S(1)}, bf16[256,640]{1,0:T(8,128)(2,1)S(1)}, u32[]{:S(2)}, u32[]{:S(2)}) collective-permute-start(bf16[256,640]{1,0:T(8,128)(2,1)S(1)} %collective-permute-done.41.refs_4_), channel_id=1, source_target_pairs={{0,12},{2,14},{4,0},{6,2},{8,4},{10,6},{12,8},{14,10},{1,13},{3,15... | collective-permute-start | bytes 983048 | tf_op jit(solution)/shard_map/ppermute | solution.py:56
  451.2 21.3 %collective-permute-start.48 = (bf16[256,640]{1,0:T(8,128)(2,1)S(1)}, bf16[256,640]{1,0:T(8,128)(2,1)S(1)}, u32[]{:S(2)}, u32[]{:S(2)}) collective-permute-start(bf16[256,640]{1,0:T(8,128)(2,1)S(1)} %collective-permute-done.42.refs_3_), channel_id=1, source_target_pairs={{0,2},{2,0},{4,6},{6,4},{8,10},{10,8},{12,14},{14,12},{1,3},{3,1},... | collective-permute-start | bytes 983048 | tf_op jit(solution)/shard_map/ppermute | solution.py:60
  469.6 14.3 %collective-permute-start.43 = (bf16[128,2048]{1,0:T(8,128)(2,1)S(1)}, bf16[128,2048]{1,0:T(8,128)(2,1)S(1)}, u32[]{:S(2)}, u32[]{:S(2)}) collective-permute-start(bf16[128,2048]{1,0:T(8,128)(2,1)S(1)} %copy-done.24), channel_id=1, source_target_pairs={{0,1},{1,0},{2,3},{3,2},{4,5},{5,4},{6,7},{7,6},{8,9},{9,8},{10,11... | collective-permute-start | bytes 1572872 | tf_op jit(solution)/shard_map/ppermute | solution.py:143
  (43 other events, 262.2 us)
Sparse Core Ops, SparseCore 0:
  13.1 43.5 all-gather.5
  59.0 69.1 all-gather.7
  129.9 67.7 all-gather.9
  210.1 73.8 reduce-scatter.3
  308.1 40.2 reduce-scatter.5
  351.4 33.1 reduce-scatter.7
